TPU v7x, 32 devices: a whole 2x2x4 slice. The times are simulated.
32 devices in a mesh: comp: 4 (over y, core), space: 8 (over z, x).
Axes of the slice: x: 2, y: 2, z: 4, core: 2. Of those that a mesh axis runs over, the one named last changes fastest.
Arguments:
- adjoint_forcing: float32 [384, 256, 1024], P('comp', 'space'), may hold values from -6 to 6
- forward_state: bfloat16 [384, 256, 1024], P(None, ('space', 'comp')), may hold values from -6 to 6
- wind_speed: float32 [256, 1024], P(('space', 'comp')), may hold values from 0.5 to 2
- cg_index: int32 [16, 256, 1024], P('comp', 'space'), may hold values from 0 to 7
- turn_index: int32 [16, 256, 1024], P('comp', 'space'), may hold values from 0 to 7
- sea_mask: int32 [256, 1024], P('space'), may hold values 0 or 1
- dir_sign: int32 [2, 24], replicated, may hold values from -1 to 1, as said below
- w_in: bfloat16 [1536, 384], replicated, may hold values from -0.3125 to 0.3125
- w_out: bfloat16 [384, 1536], replicated, may hold values from -0.15625 to 0.15625
- wind_weight: float32 [1536], replicated, may hold values from -6 to 6
Outputs:
- adjoint_start: float32 [384, 256, 1024], P('comp', 'space')
- wind_gradient: float32 [256, 1024], P(('space', 'comp'))
Inputs may be any that keep to these rules, and one draw needn't show every extreme that they name: `dir_sign`: every entry is -1 or 1.
All inputs are finite; a program needn't handle non-finite values. No bound on the sum of `sea_mask` on one device may be relied on, other than what follows from the above.
Results may differ from a plain program's by a relative error of at most 0.0035.
Values may be sent and summed in bfloat16 or wider, within the bound.
No kernel may reach another device: no remote copies, remote signals or barrier semaphores. Data moves between devices by JAX's collectives and lax.ppermute only.
A program may use at most 192 MiB of HBM per device.

v0:
```python
import math

import jax
import jax.numpy as jnp
from jax import lax
from jax.sharding import PartitionSpec as P

STEPS = 2


def extended(block, sides, width):
    for axis, dim in sides:
        count = lax.axis_size(axis)
        forward = [(i, i + 1) for i in range(count - 1)]
        backward = [(target, source) for source, target in forward]
        low = lax.ppermute(
            lax.slice_in_dim(block, block.shape[dim] - width, None, axis=dim), axis, forward
        )
        high = lax.ppermute(lax.slice_in_dim(block, 0, width, axis=dim), axis, backward)
        block = jnp.concatenate([low, block, high], axis=dim)
    return block


def direction_factors(dirs):
    angle = (jnp.arange(dirs, dtype=jnp.float32) + 0.5) * (2.0 * math.pi / dirs)
    return (0.5 * jnp.abs(jnp.cos(angle)), 0.5 * jnp.abs(jnp.sin(angle)))


def adjoint_step(costate, celerity, turning, turn_up, sea_land, sign_x, sign_y, along_x, along_y):
    cour_x = along_x * celerity
    cour_y = along_y * celerity
    masked = costate * sea_land
    retained = (1.0 - cour_x - cour_y - turning) * masked
    flux_x = cour_x * masked
    flux_y = cour_y * masked
    flux_t = turning * masked
    zero_col = jnp.zeros_like(flux_x[..., :1])
    from_right = jnp.concatenate([flux_x[..., 1:], zero_col], axis=-1)
    from_left = jnp.concatenate([zero_col, flux_x[..., :-1]], axis=-1)
    term_x = jnp.where(sign_x > 0, from_right, from_left)
    padded = extended(flux_y, (("space", 2),), 1)
    term_y = jnp.where(sign_y > 0, padded[:, :, 2:, :], padded[:, :, :-2, :])
    term_t = jnp.where(turn_up, jnp.roll(flux_t, -1, axis=-3), jnp.roll(flux_t, 1, axis=-3))
    return retained + term_x + term_y + term_t


def source_adjoint(cell_half, cell_state, cell_wind, w_in, w_out, wind_weight):
    pulled = lax.dot_general(
        w_out, cell_half, (((0,), (0,)), ((), ())), preferred_element_type=jnp.float32
    )
    forward = (
        jnp.dot(w_in, cell_state, preferred_element_type=jnp.float32)
        + wind_weight[:, None] * cell_wind[None, :]
    )
    squash = jnp.tanh(forward)
    weighted = (1.0 - squash * squash) * pulled
    increment = lax.dot_general(
        w_in,
        weighted.astype(jnp.bfloat16),
        (((0,), (0,)), ((), ())),
        preferred_element_type=jnp.float32,
    ).astype(jnp.bfloat16)
    wind_grad = jnp.sum(wind_weight[:, None] * weighted, axis=0)
    return (increment, wind_grad)


def shards(
    adjoint_forcing,
    forward_state,
    wind_speed,
    cg_index,
    turn_index,
    sea_mask,
    dir_sign,
    w_in,
    w_out,
    wind_weight,
):
    dirs = dir_sign.shape[1]
    comps, rows, cols = adjoint_forcing.shape
    freqs = comps // dirs
    total_comps = w_in.shape[1]
    along_x, along_y = direction_factors(dirs)
    along_x = along_x.reshape(1, dirs, 1, 1)
    along_y = along_y.reshape(1, dirs, 1, 1)
    sign_x = dir_sign[0].reshape(1, dirs, 1, 1)
    sign_y = dir_sign[1].reshape(1, dirs, 1, 1)
    sea_land = sea_mask.astype(jnp.float32)
    celerity = (0.1 + 0.8 * cg_index.astype(jnp.float32) / 7.0)[:, None]
    turning = (0.3 * jnp.abs(turn_index.astype(jnp.float32) - 3.5) / 3.5)[:, None]
    turn_up = (turn_index >= 4)[:, None]
    costate = adjoint_forcing.reshape(freqs, dirs, rows, cols)
    for sweep in range(STEPS):
        costate = adjoint_step(
            costate, celerity, turning, turn_up, sea_land, sign_x, sign_y, along_x, along_y
        )
    costate = costate.reshape(comps, rows, cols)
    cell_state = forward_state.reshape(total_comps, -1)
    cell_wind = wind_speed.reshape(-1)
    cell_costate = lax.all_to_all(costate, "comp", split_axis=1, concat_axis=0, tiled=True)
    increment, wind_grad = source_adjoint(
        cell_costate.reshape(total_comps, -1).astype(jnp.bfloat16),
        cell_state,
        cell_wind,
        w_in,
        w_out,
        wind_weight,
    )
    cell_start = cell_costate + increment.astype(jnp.float32).reshape(cell_costate.shape)
    adjoint_start = lax.all_to_all(cell_start, "comp", split_axis=0, concat_axis=1, tiled=True)
    return (adjoint_start, wind_grad.reshape(wind_speed.shape))


def solution(mesh):
    placed = (
        P("comp", "space", None),
        P(None, ("space", "comp"), None),
        P(("space", "comp"), None),
        P("comp", "space", None),
        P("comp", "space", None),
        P("space", None),
        P(),
        P(),
        P(),
        P(),
    )
    return jax.shard_map(
        shards,
        mesh=mesh,
        in_specs=placed,
        out_specs=(P("comp", "space", None), P(("space", "comp"), None)),
        check_vma=False,
    )
```

profile of v0, /device:TPU:0, one launch (start us, length us, event | category | flops | bytes accessed | tf_op | source)
XLA Modules:
  0.0 635.9 jit_solution(708877549982629993)
XLA Ops:
  0.6 0.0 copy-start
  0.7 1.2 multiply_add_fusion
  1.9 0.3 copy.20
  2.3 1.1 abs_multiply_fusion
  3.4 0.3 copy.21
  3.7 0.9 convert_element_type.28
  4.7 0.0 copy-start.1
  4.7 17.1 %multiply_multiply_fusion.3 = (f32[4,24,32,1024]{3,1,0,2:T(8,128)}, f32[4,24,32,1024]{3,1,0,2:T(8,128)}, f32[4,24,32,1024]{3,1,0,2:T(8,128)S(1)}) fusion(f32[4,24,32,1024]{3,2,1,0:T(8,128)} %bitcast.41, f32[32,1024]{1,0:T(8,128)S(1)} %convert_element_type.28, f32[4,32,1024]{2,0,1:T(4,128)S(1)} %copy.20, f32[24]{0:T(128)S(1)} %get-tuple-element.30, ...), kind=kLoop, calls=%fused_computation.8 | loop fusion | flops 18874368 | bytes 51511488 | tf_op jit(solution)/shard_map/mul | solution.py:34
  21.8 1.2 fusion.27
  23.0 1.3 collective-permute-start
  24.3 6.0 collective-permute-start.1
  30.3 0.0 copy-done.1
  30.3 0.1 broadcast_compare_fusion
  30.4 9.4 %fusion.28 = (f32[4,23,32,1024]{3,1,0,2:T(8,128)}, f32[4,23,32,1024]{3,1,0,2:T(8,128)}) fusion(f32[4,24,32,1024]{3,1,0,2:T(8,128)S(1)} %get-tuple-element.6), kind=kLoop, calls=%fused_computation.51 | loop fusion | bytes 48234496 | tf_op jit(solution)/shard_map/jit(_roll_static)/slice | solution.py:43
  39.8 19.3 %fusion.26 = (f32[4,24,32,1023]{3,1,0,2:T(8,128)}, f32[4,24,32,1023]{3,1,0,2:T(8,128)}) fusion(f32[4,24,32,1024]{3,1,0,2:T(8,128)} %get-tuple-element.4), kind=kLoop, calls=%fused_computation.49 | loop fusion | bytes 50282496 | tf_op jit(solution)/shard_map/slice | solution.py:38
  59.2 0.0 copy-done.4
  59.2 0.2 copy.23
  59.4 1.1 fusion.29
  60.5 0.0 collective-permute-done
  60.5 0.0 collective-permute-done.1
  60.5 39.0 %multiply_multiply_fusion.2 = (f32[4,24,32,1024]{3,1,0,2:T(8,128)}, f32[4,24,32,1024]{3,1,0,2:T(8,128)}) fusion(f32[4,32,1024]{2,0,1:T(4,128)S(1)} %copy.20, f32[24]{0:T(128)S(1)} %get-tuple-element.30, f32[4,23,32,1024]{3,1,0,2:T(8,128)} %get-tuple-element.22, f32[4,1,32,1024]{3,1,0,2:T(1,128)S(1)} %get-tuple-element.24, ...), kind=kLoop, calls=%fused_computation.7 | loop fusion | flops 59768832 | bytes 102736112 | tf_op jit(solution)/shard_map/mul | solution.py:34
  99.5 11.5 %broadcast_multiply_fusion = (f32[4,24,32,1024]{3,1,0,2:T(8,128)S(1)}, f32[4,24,32,1024]{3,1,0,2:T(8,128)}) fusion(f32[4,24,32,1024]{3,1,0,2:T(8,128)} %get-tuple-element.3, f32[4,32,1024]{2,0,1:T(4,128)S(1)} %copy.21, f32[4,32,1024]{2,0,1:T(4,128)S(1)} %copy.20, f32[24]{0:T(128)S(1)} %get-tuple-element.29), kind=kLoop, calls=%fused_computation.35 | loop fusion | flops 9437184 | bytes 38797408 | tf_op jit(solution)/shard_map/mul | solution.py:36
  111.1 9.4 %fusion.24 = (f32[4,23,32,1024]{3,1,0,2:T(8,128)}, f32[4,23,32,1024]{3,1,0,2:T(8,128)}) fusion(f32[4,24,32,1024]{3,1,0,2:T(8,128)S(1)} %get-tuple-element.13), kind=kLoop, calls=%fused_computation.47 | loop fusion | bytes 48234496 | tf_op jit(solution)/shard_map/jit(_roll_static)/slice | solution.py:43
  120.5 1.2 fusion.25
  121.6 1.3 collective-permute-start.2
  122.9 6.4 %collective-permute-start.3 = (f32[4,24,1,1024]{3,1,0,2:T(8,128)S(1)}, f32[4,24,1,1024]{3,1,0,2:T(8,128)}, u32[]{:S(2)}, u32[]{:S(2)}) collective-permute-start(f32[4,24,1,1024]{3,1,0,2:T(8,128)S(1)} %get-tuple-element.16), channel_id=1, source_target_pairs={{0,1},{1,2},{2,3},{3,4},{4,5},{5,6},{6,7},{8,9},{9,10},{10,11},{11... | collective-permute-start | bytes 1179656 | tf_op jit(solution)/shard_map/ppermute | solution.py:16
  129.3 19.3 %fusion.22 = (f32[4,24,32,1023]{3,1,0,2:T(8,128)}, f32[4,24,32,1023]{3,1,0,2:T(8,128)}) fusion(f32[4,24,32,1024]{3,1,0,2:T(8,128)} %get-tuple-element.2), kind=kLoop, calls=%fused_computation.45 | loop fusion | bytes 50282496 | tf_op jit(solution)/shard_map/slice | solution.py:38
  148.7 1.1 fusion.23
  149.8 0.0 collective-permute-done.2
  149.8 0.0 collective-permute-done.3
  149.8 35.0 %fusion.11 = f32[4,24,32,1024]{3,1,0,2:T(8,128)} fusion(f32[4,24,32,1024]{3,1,0,2:T(8,128)} %get-tuple-element.3, f32[4,24,32,1024]{3,1,0,2:T(8,128)} %get-tuple-element.14, f32[4,24,1,1024]{3,1,0,2:T(8,128)} %collective-permute-done.3, f32[4,24,1,1024]{3,1,0,2:T(8,128)} %collective-permute-done.2, f32[4,1,32,1024]{3,1,0,2:T(1,128)S(1)} %get-tuple-element.10, ...), kind=kLoop, calls=%fused_computation.19 | loop fusion | flops 50331648 | bytes 90022128 | tf_op jit(solution)/shard_map/add | solution.py:44
  184.8 6.5 %all-to-all-start = ((f32[96,32,1024]{2,0,1:T(8,128)}), f32[96,32,1024]{2,0,1:T(8,128)}, u32[]{:S(2)}, u32[]{:S(2)}) async-start(f32[96,32,1024]{2,0,1:T(8,128)} %bitcast.40), calls=%async_computation | async-start | bytes 25165824 | tf_op jit(solution)/shard_map/all_to_all | solution.py:100
  191.3 0.0 copy-start.3
  191.4 12.7 %copy.30 = bf16[48,8,8,1024]{3,1,2,0:T(8,128)(2,1)} copy(bf16[48,8,8,1024]{3,2,1,0:T(8,128)(2,1)} %bitcast.48) | data formatting | bytes 12582912
  204.0 125.2 %all-to-all-done = f32[96,32,1024]{2,0,1:T(8,128)} async-done(((f32[96,32,1024]{2,0,1:T(8,128)}), f32[96,32,1024]{2,0,1:T(8,128)}, u32[]{:S(2)}, u32[]{:S(2)}) %all-to-all-start) | async-done | bytes 12582944 | tf_op jit(solution)/shard_map/all_to_all | solution.py:100
  329.2 14.4 %copy.46 = bf16[96,32,1024]{2,1,0:T(8,128)(2,1)} copy(f32[96,32,1024]{2,0,1:T(8,128)} %all-to-all-done) | data formatting | bytes 18874368 | tf_op jit(solution)/shard_map/all_to_all | solution.py:100
  343.6 3.6 copy.26
  347.2 10.0 %copy.32 = bf16[48,8,8,1024]{3,1,2,0:T(8,128)(2,1)} copy(bf16[48,8,8,1024]{3,2,1,0:T(8,128)(2,1)S(1)} %bitcast.44) | data formatting | bytes 12582912
  357.2 23.5 %fusion.30 = f32[8192,1536]{0,1:T(8,128)} fusion(bf16[384,8192]{1,0:T(8,128)(2,1)} %bitcast.43, bf16[384,1536]{1,0:T(8,128)(2,1)S(1)} %copy-done.2), kind=kOutput, calls=%fused_computation.53 | convolution fusion | flops 9663676416 | bytes 57802752 | tf_op jit(solution)/shard_map/dot_general | solution.py:48
  380.7 33.0 %multiply_reduce_fusion = (f32[8192]{0:T(1024)S(1)}, bf16[1536,8192]{1,0:T(8,128)(2,1)}) fusion(f32[1536]{0:T(1024)S(1)} %copy-done.5, f32[8192,1536]{0,1:T(8,128)} %fusion.30, f32[8192]{0:T(1024)S(1)} %bitcast.51, bf16[1536,384]{1,0:T(8,128)(2,1)S(1)} %copy-done, bf16[384,8192]{1,0:T(8,128)(2,1)} %bitcast.49), kind=kOutput, calls=%fused_computation.1 | convolution fusion | flops 9764331520 | bytes 83040256 | tf_op jit(solution)/shard_map/dot_general | solution.py:52
  413.7 21.0 %fusion.17 = f32[8192,384]{1,0:T(8,128)} fusion(bf16[1536,384]{1,0:T(8,128)(2,1)S(1)} %copy-done, bf16[1536,8192]{1,0:T(8,128)(2,1)} %get-tuple-element.28), kind=kOutput, calls=%fused_computation.33 | convolution fusion | flops 9669967872 | bytes 38928384 | tf_op jit(solution)/shard_map/dot_general | solution.py:57
  434.7 12.9 %copy.27 = f32[384,8,1024]{2,1,0:T(8,128)} copy(f32[384,8,1024]{0,2,1:T(8,128)} %bitcast.47) | data formatting | bytes 25165824 | tf_op jit(solution)/shard_map/reshape | solution.py:109
  447.6 16.6 %copy.25 = f32[4,96,8,1024]{3,2,1,0:T(8,128)} copy(f32[4,96,8,1024]{3,1,2,0:T(8,128)} %bitcast.6) | data formatting | bytes 25165824 | tf_op jit(solution)/shard_map/all_to_all | solution.py:100
  464.2 14.9 %bitcast_add_fusion = f32[384,8,1024]{2,1,0:T(8,128)} fusion(f32[384,8,1024]{2,1,0:T(8,128)} %copy.27, f32[4,96,8,1024]{3,2,1,0:T(8,128)} %copy.25), kind=kLoop, calls=%fused_computation.29 | loop fusion | flops 3145728 | bytes 37748736 | tf_op jit(solution)/shard_map/add | solution.py:109
  479.1 6.3 all-to-all-start.1
  485.4 0.6 reshape.69
  486.1 137.5 %all-to-all-done.1 = f32[384,8,1024]{2,1,0:T(8,128)} async-done(((f32[384,8,1024]{2,1,0:T(8,128)}), f32[384,8,1024]{2,1,0:T(8,128)}, u32[]{:S(2)}, u32[]{:S(2)}) %all-to-all-start.1) | async-done | bytes 12582944 | tf_op jit(solution)/shard_map/all_to_all | solution.py:110
  623.5 12.1 %copy.47 = f32[96,4,8,1024]{3,2,1,0:T(8,128)} copy(f32[96,4,8,1024]{3,2,0,1:T(8,128)} %bitcast.13) | data formatting | bytes 25165824 | tf_op jit(solution)/shard_map/all_to_all | solution.py:110
  (10 shorter events, 0.1 us)
Async XLA Ops:
  0.6 380.0 %copy-start = (bf16[1536,384]{1,0:T(8,128)(2,1)S(1)}, bf16[1536,384]{1,0:T(8,128)(2,1)}, u32[]{:S(2)}) copy-start(bf16[1536,384]{1,0:T(8,128)(2,1)} %param.17) | copy-start | bytes 3538948
  4.7 25.6 %copy-start.1 = (s32[4,32,1024]{2,1,0:T(8,128)S(1)}, s32[4,32,1024]{2,1,0:T(8,128)}, u32[]{:S(2)}) copy-start(s32[4,32,1024]{2,1,0:T(8,128)} %param.14) | copy-start | bytes 1572868
  23.0 37.6 %collective-permute-start = (f32[4,24,1,1024]{3,1,0,2:T(8,128)S(1)}, f32[4,24,1,1024]{3,1,0,2:T(8,128)S(1)}, u32[]{:S(2)}, u32[]{:S(2)}) collective-permute-start(f32[4,24,1,1024]{3,1,0,2:T(8,128)S(1)} %get-tuple-element.19), channel_id=1, source_target_pairs={{1,0},{2,1},{3,2},{4,3},{5,4},{6,5},{7,6},{9,8},{10,9},{11,10},{12... | collective-permute-start | bytes 1179656 | tf_op jit(solution)/shard_map/ppermute | solution.py:19
  24.3 36.3 %collective-permute-start.1 = (f32[4,24,1,1024]{3,1,0,2:T(8,128)S(1)}, f32[4,24,1,1024]{3,1,0,2:T(8,128)S(1)}, u32[]{:S(2)}, u32[]{:S(2)}) collective-permute-start(f32[4,24,1,1024]{3,1,0,2:T(8,128)S(1)} %get-tuple-element.20), channel_id=1, source_target_pairs={{0,1},{1,2},{2,3},{3,4},{4,5},{5,6},{6,7},{8,9},{9,10},{10,11},{11... | collective-permute-start | bytes 1179656 | tf_op jit(solution)/shard_map/ppermute | solution.py:16
  39.8 19.4 %copy-start.4 = (s32[2,24]{1,0:T(2,128)S(1)}, s32[2,24]{1,0:T(2,128)}, u32[]{:S(2)}) copy-start(s32[2,24]{1,0:T(2,128)} %param.16) | copy-start | bytes 580
  121.6 28.2 %collective-permute-start.2 = (f32[4,24,1,1024]{3,1,0,2:T(8,128)S(1)}, f32[4,24,1,1024]{3,1,0,2:T(8,128)}, u32[]{:S(2)}, u32[]{:S(2)}) collective-permute-start(f32[4,24,1,1024]{3,1,0,2:T(8,128)S(1)} %get-tuple-element.15), channel_id=1, source_target_pairs={{1,0},{2,1},{3,2},{4,3},{5,4},{6,5},{7,6},{9,8},{10,9},{11,10},{12... | collective-permute-start | bytes 1179656 | tf_op jit(solution)/shard_map/ppermute | solution.py:19
  122.9 26.9 %collective-permute-start.3 = (f32[4,24,1,1024]{3,1,0,2:T(8,128)S(1)}, f32[4,24,1,1024]{3,1,0,2:T(8,128)}, u32[]{:S(2)}, u32[]{:S(2)}) collective-permute-start(f32[4,24,1,1024]{3,1,0,2:T(8,128)S(1)} %get-tuple-element.16), channel_id=1, source_target_pairs={{0,1},{1,2},{2,3},{3,4},{4,5},{5,6},{6,7},{8,9},{9,10},{10,11},{11... | collective-permute-start | bytes 1179656 | tf_op jit(solution)/shard_map/ppermute | solution.py:16
  184.8 144.4 %all-to-all-start = ((f32[96,32,1024]{2,0,1:T(8,128)}), f32[96,32,1024]{2,0,1:T(8,128)}, u32[]{:S(2)}, u32[]{:S(2)}) async-start(f32[96,32,1024]{2,0,1:T(8,128)} %bitcast.40), calls=%async_computation | async-start | bytes 25165824 | tf_op jit(solution)/shard_map/all_to_all | solution.py:100
  191.3 12.7 %copy-start.3 = (f32[8,1024]{1,0:T(8,128)S(1)}, f32[8,1024]{1,0:T(8,128)}, u32[]{:S(2)}) copy-start(f32[8,1024]{1,0:T(8,128)} %param.12) | copy-start | bytes 98308
  343.6 13.6 %copy-start.2 = (bf16[384,1536]{1,0:T(8,128)(2,1)S(1)}, bf16[384,1536]{1,0:T(8,128)(2,1)}, u32[]{:S(2)}) copy-start(bf16[384,1536]{1,0:T(8,128)(2,1)} %param.18) | copy-start | bytes 3538948
  357.2 23.5 %copy-start.5 = (f32[1536]{0:T(1024)S(1)}, f32[1536]{0:T(1024)}, u32[]{:S(2)}) copy-start(f32[1536]{0:T(1024)} %param.19) | copy-start | bytes 18436
  479.1 144.4 %all-to-all-start.1 = ((f32[384,8,1024]{2,1,0:T(8,128)}), f32[384,8,1024]{2,1,0:T(8,128)}, u32[]{:S(2)}, u32[]{:S(2)}) async-start(f32[384,8,1024]{2,1,0:T(8,128)} %bitcast_add_fusion), calls=%async_computation.1 | async-start | bytes 25165824 | tf_op jit(solution)/shard_map/all_to_all | solution.py:110
where the time goes:
time: 640 us; the launch traced here: 636 us
  waiting for transfers between devices  263 us (41%)
  local copies, waits for them, and re-layouts  146 us (23%)
  other arithmetic  121 us (19%)
  matrix products  77.5 us (12%)
  starting transfers between devices  27.8 us (4%)
    all_to_all x1, waiting for transfers between devices, shards(): lax.all_to_all(cell_start, 'comp', split_axis=0, concat_axis=1, tiled=True)  137 us
    all_to_all x1, waiting for transfers between devices, shards(): lax.all_to_all(costate, 'comp', split_axis=1, concat_axis=0, tiled=True)  125 us
    mul x2, other arithmetic, adjoint_step(): flux_x = cour_x * masked  56.1 us
    slice x2, local copies, waits for them, and re-layouts, adjoint_step(): from_right = jnp.concatenate([flux_x[..., 1:], zero_col], axis=-1)  38.7 us
    add x1, other arithmetic, adjoint_step(): return retained + term_x + term_y + term_t  35 us
    dot_general x1, matrix products, source_adjoint(): jnp.dot(w_in, cell_state, preferred_element_type=jnp.float32)  33 us
    all_to_all x2, local copies, waits for them, and re-layouts, shards(): lax.all_to_all(costate, 'comp', split_axis=1, concat_axis=0, tiled=True)  31 us
    dot_general x1, matrix products, source_adjoint(): lax.dot_general(w_out, cell_half, (((0,), (0,)), ((), ())), preferred_ele...  23.5 us
  transfers between devices with their start and end apart: 6, of which 2 were waited for; matrix products, arithmetic and copies ran while one was open for 10% of the time, Pallas kernels for 0%

commit v1 on v0

--- a/solution.py
+++ b/solution.py
@@ -95,20 +95,33 @@
             costate, celerity, turning, turn_up, sea_land, sign_x, sign_y, along_x, along_y
         )
     costate = costate.reshape(comps, rows, cols)
-    cell_state = forward_state.reshape(total_comps, -1)
-    cell_wind = wind_speed.reshape(-1)
-    cell_costate = lax.all_to_all(costate, "comp", split_axis=1, concat_axis=0, tiled=True)
-    increment, wind_grad = source_adjoint(
-        cell_costate.reshape(total_comps, -1).astype(jnp.bfloat16),
-        cell_state,
-        cell_wind,
-        w_in,
-        w_out,
-        wind_weight,
-    )
-    cell_start = cell_costate + increment.astype(jnp.float32).reshape(cell_costate.shape)
-    adjoint_start = lax.all_to_all(cell_start, "comp", split_axis=0, concat_axis=1, tiled=True)
-    return (adjoint_start, wind_grad.reshape(wind_speed.shape))
+    parts = lax.axis_size("comp")
+    local = rows // parts
+    chunks = 2
+    width = cols // chunks
+    starts, grads = [], []
+    for c in range(chunks):
+        here = slice(c * width, (c + 1) * width)
+        home = costate[:, :, here]
+        half = home.astype(jnp.bfloat16).reshape(comps, parts, local, width)
+        half = jnp.transpose(half, (1, 2, 0, 3))
+        got = lax.all_to_all(half, "comp", split_axis=0, concat_axis=0, tiled=True)
+        cell = jnp.transpose(got, (0, 2, 1, 3)).reshape(total_comps, local * width)
+        increment, wind_grad = source_adjoint(
+            cell,
+            forward_state[:, :, here].reshape(total_comps, -1),
+            wind_speed[:, here].reshape(-1),
+            w_in,
+            w_out,
+            wind_weight,
+        )
+        back = increment.reshape(parts, comps, local, width)
+        back = jnp.transpose(back, (0, 2, 1, 3))
+        back = lax.all_to_all(back, "comp", split_axis=0, concat_axis=0, tiled=True)
+        back = jnp.transpose(back, (2, 0, 1, 3)).reshape(comps, rows, width)
+        starts.append(home + back.astype(jnp.float32))
+        grads.append(wind_grad.reshape(local, width))
+    return (jnp.concatenate(starts, axis=-1), jnp.concatenate(grads, axis=-1))
 
 
 def solution(mesh):

time: 640 us -> 468 us (0.73)
  waiting for transfers between devices: 263 us -> 82.6 us
  local copies, waits for them, and re-layouts: 146 us -> 115 us
  matrix products: 77.5 us -> 97.5 us
  other arithmetic: 121 us -> 130 us
    all_to_all x2 -> x4, waiting for transfers between devices: 263 us -> 82.6 us  [the longest x2 50.6 us: shards(): back = lax.all_to_all(back, 'comp', split_axis=0, concat_axis=0, tiled=True)]
    all_to_all x3 -> x0, local copies, waits for them, and re-layouts: 43.1 us -> none  [the longest x2 31 us: shards(): lax.all_to_all(costate, 'comp', split_axis=1, concat_axis=0, tiled=True)]
    dot_general x1 -> x2, matrix products: 23.5 us -> 48.4 us  [source_adjoint(): lax.dot_general(w_out, cell_half, (((0,), (0,)), ((), ())), preferred_ele...]
    concatenate x0 -> x2, other arithmetic: none -> 12.5 us  [shards(): return (jnp.concatenate(starts, axis=-1), jnp.concatenate(grads, axis=-1))]
    dot_general x1 -> x2, matrix products: 33 us -> 25.4 us  [source_adjoint(): jnp.dot(w_in, cell_state, preferred_element_type=jnp.float32)]
    all_to_all x2 -> x4, starting transfers between devices: 12.8 us -> 19.2 us  [the longest x2 9.63 us: shards(): got = lax.all_to_all(half, 'comp', split_axis=0, concat_axis=0, tiled=True)]
    add x2 -> x1, other arithmetic: 16.1 us -> 10.9 us  [shards(): starts.append(home + back.astype(jnp.float32))]
    dot_general x1 -> x2, matrix products: 21 us -> 23.7 us  [source_adjoint(): lax.dot_general(w_in, weighted.astype(jnp.bfloat16), (((0,), (0,)), ((),...]
  transfers between devices with their start and end apart: 6 -> 8, of which waited for: 2 -> 4; matrix products, arithmetic and copies ran while one was open for 10% -> 27% of each run, Pallas kernels for 0% -> 0%
where the time goes in v1:
time: 468 us; the launch traced here: 460 us
  other arithmetic  130 us (28%)
  local copies, waits for them, and re-layouts  115 us (25%)
  matrix products  97.5 us (21%)
  waiting for transfers between devices  82.6 us (18%)
  starting transfers between devices  33.9 us (7%)
    mul x2, other arithmetic, adjoint_step(): flux_x = cour_x * masked  57.4 us
    all_to_all x2, waiting for transfers between devices, shards(): back = lax.all_to_all(back, 'comp', split_axis=0, concat_axis=0, tiled=True)  50.6 us
    dot_general x2, matrix products, source_adjoint(): lax.dot_general(w_out, cell_half, (((0,), (0,)), ((), ())), preferred_ele...  48.4 us
    slice x2, local copies, waits for them, and re-layouts, adjoint_step(): from_right = jnp.concatenate([flux_x[..., 1:], zero_col], axis=-1)  38.7 us
    add x1, other arithmetic, adjoint_step(): return retained + term_x + term_y + term_t  35 us
    all_to_all x2, waiting for transfers between devices, shards(): got = lax.all_to_all(half, 'comp', split_axis=0, concat_axis=0, tiled=True)  32 us
    dot_general x2, matrix products, source_adjoint(): jnp.dot(w_in, cell_state, preferred_element_type=jnp.float32)  25.4 us
    dot_general x2, matrix products, source_adjoint(): lax.dot_general(w_in, weighted.astype(jnp.bfloat16), (((0,), (0,)), ((),...  23.7 us
  transfers between devices with their start and end apart: 8, of which 4 were waited for; matrix products, arithmetic and copies ran while one was open for 27% of the time, Pallas kernels for 0%

profile of v1, /device:TPU:0, one launch (start us, length us, event | category | flops | bytes accessed | tf_op | source)
XLA Modules:
  0.0 459.9 jit_solution(12245860592154657163)
XLA Ops:
  0.7 1.0 convert_element_type.53
  1.7 1.4 abs_multiply_fusion
  3.1 14.3 %multiply_multiply_fusion.3 = (f32[4,24,32,1024]{3,2,1,0:T(8,128)}, f32[4,24,32,1024]{3,2,1,0:T(8,128)}, f32[4,24,32,1024]{3,2,1,0:T(8,128)S(1)}) fusion(f32[4,24,32,1024]{3,2,1,0:T(8,128)} %bitcast.79, f32[32,1024]{1,0:T(8,128)S(1)} %convert_element_type.53, f32[4,32,1024]{2,1,0:T(8,128)S(1)} %get-tuple-element.39, f32[24]{0:T(128)S(1)} %get-tuple-element.41, ...), kind=kLoop, calls=%fused_computation.8 | loop fusion | flops 18874368 | bytes 51511488 | tf_op jit(solution)/shard_map/mul | solution.py:34
  17.4 3.7 fusion.36
  21.1 1.3 collective-permute-start
  22.4 6.2 %collective-permute-start.1 = (f32[4,24,1,1024]{3,2,1,0:T(1,128)S(1)}, f32[4,24,1,1024]{3,2,1,0:T(1,128)}, u32[]{:S(2)}, u32[]{:S(2)}) collective-permute-start(f32[4,24,1,1024]{3,2,1,0:T(1,128)S(1)} %get-tuple-element.26), channel_id=1, source_target_pairs={{0,1},{1,2},{2,3},{3,4},{4,5},{5,6},{6,7},{8,9},{9,10},{10,11},{11... | collective-permute-start | bytes 1179656 | tf_op jit(solution)/shard_map/ppermute | solution.py:16
  28.7 8.9 %fusion.37 = (f32[4,23,32,1024]{3,2,1,0:T(8,128)}, f32[4,23,32,1024]{3,2,1,0:T(8,128)}) fusion(f32[4,24,32,1024]{3,2,1,0:T(8,128)S(1)} %get-tuple-element.8), kind=kLoop, calls=%fused_computation.68 | loop fusion | bytes 48234496 | tf_op jit(solution)/shard_map/jit(_roll_static)/slice | solution.py:43
  37.6 19.3 %fusion.35 = (f32[4,24,32,1023]{3,2,1,0:T(8,128)}, f32[4,24,32,1023]{3,2,1,0:T(8,128)}) fusion(f32[4,24,32,1024]{3,2,1,0:T(8,128)} %get-tuple-element.6), kind=kLoop, calls=%fused_computation.66 | loop fusion | bytes 50282496 | tf_op jit(solution)/shard_map/slice | solution.py:38
  57.0 43.1 %multiply_multiply_fusion.2 = (f32[4,24,32,1024]{3,2,1,0:T(8,128)}, f32[4,24,32,1024]{3,2,1,0:T(8,128)}) fusion(f32[4,32,1024]{2,1,0:T(8,128)S(1)} %get-tuple-element.39, f32[24]{0:T(128)S(1)} %get-tuple-element.41, f32[4,23,32,1024]{3,2,1,0:T(8,128)} %get-tuple-element.28, f32[4,1,32,1024]{3,2,1,0:T(8,128)S(1)} %get-tuple-element.30, ...), kind=kLoop, calls=%fused_computation.7 | loop fusion | flops 59768832 | bytes 102736112 | tf_op jit(solution)/shard_map/mul | solution.py:34
  100.1 11.7 %broadcast_multiply_fusion = (f32[4,24,32,1024]{3,2,1,0:T(8,128)S(1)}, f32[4,24,32,1024]{3,2,1,0:T(8,128)}) fusion(f32[4,24,32,1024]{3,2,1,0:T(8,128)} %get-tuple-element.5, f32[4,32,1024]{2,1,0:T(8,128)S(1)} %get-tuple-element.38, f32[4,32,1024]{2,1,0:T(8,128)S(1)} %get-tuple-element.39, f32[24]{0:T(128)S(1)} %get-tuple-element.40), kind=kLoop, calls=%fused_computation.38 | loop fusion | flops 9437184 | bytes 38797408 | tf_op jit(solution)/shard_map/mul | solution.py:36
  111.9 3.7 fusion.34
  115.5 1.3 collective-permute-start.2
  116.8 5.9 %collective-permute-start.3 = (f32[4,24,1,1024]{3,2,1,0:T(1,128)S(1)}, f32[4,24,1,1024]{3,2,1,0:T(1,128)}, u32[]{:S(2)}, u32[]{:S(2)}) collective-permute-start(f32[4,24,1,1024]{3,2,1,0:T(1,128)S(1)} %get-tuple-element.22), channel_id=1, source_target_pairs={{0,1},{1,2},{2,3},{3,4},{4,5},{5,6},{6,7},{8,9},{9,10},{10,11},{11... | collective-permute-start | bytes 1179656 | tf_op jit(solution)/shard_map/ppermute | solution.py:16
  122.8 19.3 %fusion.31 = (f32[4,24,32,1023]{3,2,1,0:T(8,128)}, f32[4,24,32,1023]{3,2,1,0:T(8,128)}) fusion(f32[4,24,32,1024]{3,2,1,0:T(8,128)} %get-tuple-element.4), kind=kLoop, calls=%fused_computation.62 | loop fusion | bytes 50282496 | tf_op jit(solution)/shard_map/slice | solution.py:38
  142.1 8.9 %fusion.33 = (f32[4,23,32,1024]{3,2,1,0:T(8,128)}, f32[4,23,32,1024]{3,2,1,0:T(8,128)}) fusion(f32[4,24,32,1024]{3,2,1,0:T(8,128)S(1)} %get-tuple-element.19), kind=kLoop, calls=%fused_computation.64 | loop fusion | bytes 48234496 | tf_op jit(solution)/shard_map/jit(_roll_static)/slice | solution.py:43
  151.0 0.1 fusion.32
  151.1 35.0 %fusion.9 = f32[4,24,32,1024]{3,2,1,0:T(8,128)} fusion(f32[4,24,32,1024]{3,2,1,0:T(8,128)} %get-tuple-element.5, f32[4,24,32,1024]{3,2,1,0:T(8,128)} %get-tuple-element.20, f32[4,24,1,1024]{3,2,1,0:T(1,128)} %collective-permute-done.3, f32[4,24,1,1024]{3,2,1,0:T(1,128)} %collective-permute-done.2, f32[4,1,32,1024]{3,2,1,0:T(8,128)S(1)} %get-tuple-element.16, ...), kind=kLoop, calls=%fused_computation.19 | loop fusion | flops 50331648 | bytes 90022128 | tf_op jit(solution)/shard_map/add | solution.py:44
  186.2 7.3 %fusion.28 = (bf16[96,4,8,512]{3,2,1,0:T(8,128)(2,1)}, bf16[96,4,8,512]{3,2,1,0:T(8,128)(2,1)S(1)}) fusion(f32[96,32,1024]{2,1,0:T(8,128)} %bitcast.77), kind=kLoop, calls=%fused_computation.45 | loop fusion | bytes 12582912 | tf_op jit(solution)/shard_map/reshape | solution.py:106
  193.5 1.9 copy.36
  195.4 4.8 %all-to-all-start.2 = ((bf16[4,8,96,512]{3,1,2,0:T(8,128)(2,1)}), bf16[4,8,96,512]{3,1,2,0:T(8,128)(2,1)}, u32[]{:S(2)}, u32[]{:S(2)}) async-start(bf16[4,8,96,512]{3,1,2,0:T(8,128)(2,1)} %bitcast.84), calls=%async_computation.2 | async-start | bytes 6291456 | tf_op jit(solution)/shard_map/all_to_all | solution.py:108
  200.2 3.4 fusion.39
  203.6 3.0 copy.28
  206.7 3.1 copy.24
  209.8 2.0 copy.37
  211.8 25.4 %all-to-all-done.2 = bf16[4,8,96,512]{3,1,2,0:T(8,128)(2,1)} async-done(((bf16[4,8,96,512]{3,1,2,0:T(8,128)(2,1)}), bf16[4,8,96,512]{3,1,2,0:T(8,128)(2,1)}, u32[]{:S(2)}, u32[]{:S(2)}) %all-to-all-start.2) | async-done | bytes 3145760 | tf_op jit(solution)/shard_map/all_to_all | solution.py:108
  237.2 4.8 %all-to-all-start = ((bf16[4,8,96,512]{3,1,2,0:T(8,128)(2,1)}), bf16[4,8,96,512]{3,1,2,0:T(8,128)(2,1)}, u32[]{:S(2)}, u32[]{:S(2)}) async-start(bf16[4,8,96,512]{3,1,2,0:T(8,128)(2,1)} %bitcast.85), calls=%async_computation | async-start | bytes 6291456 | tf_op jit(solution)/shard_map/all_to_all | solution.py:108
  242.1 13.7 %fusion.41 = f32[1536,4096]{1,0:T(8,128)} fusion(bf16[1536,384]{1,0:T(8,128)(2,1)S(1)} %copy-done, bf16[384,4096]{1,0:T(8,128)(2,1)} %bitcast.82), kind=kOutput, calls=%fused_computation.72 | convolution fusion | flops 4831838208 | bytes 29491200 | tf_op jit(solution)/shard_map/dot_general | solution.py:52
  255.8 11.7 %fusion.40 = f32[1536,4096]{1,0:T(8,128)} fusion(bf16[1536,384]{1,0:T(8,128)(2,1)S(1)} %copy-done, bf16[384,4096]{1,0:T(8,128)(2,1)S(1)} %bitcast.83), kind=kOutput, calls=%fused_computation.71 | convolution fusion | flops 4831838208 | bytes 29491200 | tf_op jit(solution)/shard_map/dot_general | solution.py:52
  267.4 5.0 %copy.30 = bf16[48,8,8,512]{3,1,2,0:T(8,128)(2,1)} copy(bf16[48,8,8,512]{3,2,1,0:T(8,128)(2,1)} %bitcast.35) | data formatting | bytes 6291456
  272.5 6.5 %all-to-all-done = bf16[4,8,96,512]{3,1,2,0:T(8,128)(2,1)} async-done(((bf16[4,8,96,512]{3,1,2,0:T(8,128)(2,1)}), bf16[4,8,96,512]{3,1,2,0:T(8,128)(2,1)}, u32[]{:S(2)}, u32[]{:S(2)}) %all-to-all-start) | async-done | bytes 3145760 | tf_op jit(solution)/shard_map/all_to_all | solution.py:108
  279.0 4.9 %copy.26 = bf16[48,8,8,512]{3,1,2,0:T(8,128)(2,1)} copy(bf16[48,8,8,512]{3,2,1,0:T(8,128)(2,1)} %bitcast.25) | data formatting | bytes 6291456
  284.0 23.4 %bitcast_multiply_fusion = f32[1536,4096]{1,0:T(8,128)} fusion(f32[1536,4096]{1,0:T(8,128)} %fusion.41, bf16[384,4096]{1,0:T(8,128)(2,1)} %bitcast.81, bf16[384,1536]{1,0:T(8,128)(2,1)S(1)} %copy-done.4, f32[4096]{0:T(1024)S(1)} %bitcast.93, f32[1536]{0:T(1024)S(1)} %copy-done.6), kind=kOutput, calls=%fused_computation | convolution fusion | flops 4863295488 | bytes 54679552 | tf_op jit(solution)/shard_map/dot_general | solution.py:48
  307.4 25.0 %multiply_reduce_fusion.1 = (f32[4096]{0:T(1024)S(1)}, f32[4096]{0:T(1024)S(1)}, bf16[1536,4096]{1,0:T(8,128)(2,1)}) fusion(f32[1536]{0:T(1024)S(1)} %copy-done.6, f32[1536,4096]{1,0:T(8,128)} %bitcast_multiply_fusion, bf16[384,4096]{1,0:T(8,128)(2,1)} %bitcast.92, bf16[384,1536]{1,0:T(8,128)(2,1)S(1)} %copy-done.4, f32[1536,4096]{1,0:T(8,128)} %fusion.40, ...), kind=kOutput, calls=%fused_computation.3 | convolution fusion | flops 4894744576 | bytes 67295232 | tf_op jit(solution)/shard_map/dot_general | solution.py:48
  332.4 10.9 %fusion.25 = bf16[384,4096]{0,1:T(8,128)(2,1)} fusion(bf16[1536,384]{1,0:T(8,128)(2,1)S(1)} %copy-done, bf16[1536,4096]{1,0:T(8,128)(2,1)} %get-tuple-element.37), kind=kOutput, calls=%fused_computation.44 | convolution fusion | flops 4833411072 | bytes 16908288 | tf_op jit(solution)/shard_map/dot_general | solution.py:57
  343.3 4.7 %copy.19 = bf16[384,4096]{1,0:T(8,128)(2,1)} copy(bf16[384,4096]{0,1:T(8,128)(2,1)} %fusion.25) | data formatting | bytes 6291456 | tf_op jit(solution)/shard_map/convert_element_type | solution.py:62
  348.0 3.3 copy.27
  351.3 1.9 bitcast_bitcast_fusion.1
  353.1 4.9 %all-to-all-start.1 = ((bf16[4,8,96,512]{3,1,2,0:T(8,128)(2,1)}), bf16[4,8,96,512]{3,1,2,0:T(8,128)(2,1)}, u32[]{:S(2)}, u32[]{:S(2)}) async-start(bf16[4,8,96,512]{3,1,2,0:T(8,128)(2,1)} %bitcast_bitcast_fusion.1), calls=%async_computation.1 | async-start | bytes 6291456 | tf_op jit(solution)/shard_map/all_to_all | solution.py:120
  358.1 12.8 %fusion.22 = bf16[384,4096]{0,1:T(8,128)(2,1)} fusion(bf16[1536,384]{1,0:T(8,128)(2,1)S(1)} %copy-done, f32[1536,4096]{1,0:T(8,128)} %bitcast_multiply_fusion), kind=kOutput, calls=%fused_computation.43 | convolution fusion | flops 4839702528 | bytes 29491200 | tf_op jit(solution)/shard_map/dot_general | solution.py:57
  370.9 4.7 %copy.22 = bf16[384,4096]{1,0:T(8,128)(2,1)} copy(bf16[384,4096]{0,1:T(8,128)(2,1)} %fusion.22) | data formatting | bytes 6291456 | tf_op jit(solution)/shard_map/convert_element_type | solution.py:62
  375.7 3.3 copy.31
  379.0 1.8 bitcast_bitcast_fusion
  380.8 14.3 %all-to-all-done.1 = bf16[4,8,96,512]{3,1,2,0:T(8,128)(2,1)} async-done(((bf16[4,8,96,512]{3,1,2,0:T(8,128)(2,1)}), bf16[4,8,96,512]{3,1,2,0:T(8,128)(2,1)}, u32[]{:S(2)}, u32[]{:S(2)}) %all-to-all-start.1) | async-done | bytes 3145760 | tf_op jit(solution)/shard_map/all_to_all | solution.py:120
  395.1 4.7 %all-to-all-start.3 = ((bf16[4,8,96,512]{3,1,2,0:T(8,128)(2,1)}), bf16[4,8,96,512]{3,1,2,0:T(8,128)(2,1)}, u32[]{:S(2)}, u32[]{:S(2)}) async-start(bf16[4,8,96,512]{3,1,2,0:T(8,128)(2,1)} %bitcast_bitcast_fusion), calls=%async_computation.3 | async-start | bytes 6291456 | tf_op jit(solution)/shard_map/all_to_all | solution.py:120
  399.8 0.6 pad_maximum_fusion.5
  400.4 36.4 %all-to-all-done.3 = bf16[4,8,96,512]{3,1,2,0:T(8,128)(2,1)} async-done(((bf16[4,8,96,512]{3,1,2,0:T(8,128)(2,1)}), bf16[4,8,96,512]{3,1,2,0:T(8,128)(2,1)}, u32[]{:S(2)}, u32[]{:S(2)}) %all-to-all-start.3) | async-done | bytes 3145760 | tf_op jit(solution)/shard_map/all_to_all | solution.py:120
  436.7 10.9 %bitcast_add_fusion.1 = (f32[96,32,512]{2,1,0:T(8,128)}, f32[96,32,512]{2,1,0:T(8,128)}) fusion(f32[96,32,1024]{2,1,0:T(8,128)} %bitcast.78, bf16[4,8,96,512]{3,1,2,0:T(8,128)(2,1)} %all-to-all-done.3, bf16[4,8,96,512]{3,1,2,0:T(8,128)(2,1)} %all-to-all-done.1), kind=kLoop, calls=%fused_computation.35 | loop fusion | flops 6291456 | bytes 31457280 | tf_op jit(solution)/shard_map/add | solution.py:122
  447.7 11.8 %pad_maximum_fusion.4 = f32[96,32,1024]{2,1,0:T(8,128)} fusion(f32[96,32,512]{2,1,0:T(8,128)} %get-tuple-element.10, f32[96,32,512]{2,1,0:T(8,128)} %get-tuple-element.9), kind=kLoop, calls=%fused_computation.28 | loop fusion | flops 3145728 | bytes 25165824 | tf_op jit(solution)/shard_map/concatenate | solution.py:124
  (29 shorter events, 0.3 us)
Async XLA Ops:
  0.6 241.4 %copy-start = (bf16[1536,384]{1,0:T(8,128)(2,1)S(1)}, bf16[1536,384]{1,0:T(8,128)(2,1)}, u32[]{:S(2)}) copy-start(bf16[1536,384]{1,0:T(8,128)(2,1)} %param.17) | copy-start | bytes 3538948
  3.1 25.5 %copy-start.3 = (s32[4,32,1024]{2,1,0:T(8,128)S(1)}, s32[4,32,1024]{2,1,0:T(8,128)}, u32[]{:S(2)}) copy-start(s32[4,32,1024]{2,1,0:T(8,128)} %param.14) | copy-start | bytes 1572868
  21.1 36.0 %collective-permute-start = (f32[4,24,1,1024]{3,2,1,0:T(1,128)S(1)}, f32[4,24,1,1024]{3,2,1,0:T(1,128)}, u32[]{:S(2)}, u32[]{:S(2)}) collective-permute-start(f32[4,24,1,1024]{3,2,1,0:T(1,128)S(1)} %get-tuple-element.25), channel_id=1, source_target_pairs={{1,0},{2,1},{3,2},{4,3},{5,4},{6,5},{7,6},{9,8},{10,9},{11,10},{12... | collective-permute-start | bytes 1179656 | tf_op jit(solution)/shard_map/ppermute | solution.py:19
  22.4 34.7 %collective-permute-start.1 = (f32[4,24,1,1024]{3,2,1,0:T(1,128)S(1)}, f32[4,24,1,1024]{3,2,1,0:T(1,128)}, u32[]{:S(2)}, u32[]{:S(2)}) collective-permute-start(f32[4,24,1,1024]{3,2,1,0:T(1,128)S(1)} %get-tuple-element.26), channel_id=1, source_target_pairs={{0,1},{1,2},{2,3},{3,4},{4,5},{5,6},{6,7},{8,9},{9,10},{10,11},{11... | collective-permute-start | bytes 1179656 | tf_op jit(solution)/shard_map/ppermute | solution.py:16
  37.6 19.4 %copy-start.7 = (s32[2,24]{1,0:T(2,128)S(1)}, s32[2,24]{1,0:T(2,128)}, u32[]{:S(2)}) copy-start(s32[2,24]{1,0:T(2,128)} %param.16) | copy-start | bytes 580
  115.5 35.6 %collective-permute-start.2 = (f32[4,24,1,1024]{3,2,1,0:T(1,128)S(1)}, f32[4,24,1,1024]{3,2,1,0:T(1,128)}, u32[]{:S(2)}, u32[]{:S(2)}) collective-permute-start(f32[4,24,1,1024]{3,2,1,0:T(1,128)S(1)} %get-tuple-element.21), channel_id=1, source_target_pairs={{1,0},{2,1},{3,2},{4,3},{5,4},{6,5},{7,6},{9,8},{10,9},{11,10},{12... | collective-permute-start | bytes 1179656 | tf_op jit(solution)/shard_map/ppermute | solution.py:19
  116.8 34.3 %collective-permute-start.3 = (f32[4,24,1,1024]{3,2,1,0:T(1,128)S(1)}, f32[4,24,1,1024]{3,2,1,0:T(1,128)}, u32[]{:S(2)}, u32[]{:S(2)}) collective-permute-start(f32[4,24,1,1024]{3,2,1,0:T(1,128)S(1)} %get-tuple-element.22), channel_id=1, source_target_pairs={{0,1},{1,2},{2,3},{3,4},{4,5},{5,6},{6,7},{8,9},{9,10},{10,11},{11... | collective-permute-start | bytes 1179656 | tf_op jit(solution)/shard_map/ppermute | solution.py:16
  195.4 11.3 %copy-start.5 = (f32[8,1024]{1,0:T(8,128)S(1)}, f32[8,1024]{1,0:T(8,128)}, u32[]{:S(2)}) copy-start(f32[8,1024]{1,0:T(8,128)} %param.12) | copy-start | bytes 98308
  195.4 41.8 %all-to-all-start.2 = ((bf16[4,8,96,512]{3,1,2,0:T(8,128)(2,1)}), bf16[4,8,96,512]{3,1,2,0:T(8,128)(2,1)}, u32[]{:S(2)}, u32[]{:S(2)}) async-start(bf16[4,8,96,512]{3,1,2,0:T(8,128)(2,1)} %bitcast.84), calls=%async_computation.2 | async-start | bytes 6291456 | tf_op jit(solution)/shard_map/all_to_all | solution.py:108
  200.2 9.6 %copy-start.2 = (bf16[96,4,8,512]{3,2,1,0:T(8,128)(2,1)S(1)}, bf16[96,4,8,512]{3,2,1,0:T(8,128)(2,1)}, u32[]{:S(2)}) copy-start(bf16[96,4,8,512]{3,2,1,0:T(8,128)(2,1)} %get-tuple-element.11) | copy-start | bytes 9437188
  237.2 41.8 %all-to-all-start = ((bf16[4,8,96,512]{3,1,2,0:T(8,128)(2,1)}), bf16[4,8,96,512]{3,1,2,0:T(8,128)(2,1)}, u32[]{:S(2)}, u32[]{:S(2)}) async-start(bf16[4,8,96,512]{3,1,2,0:T(8,128)(2,1)} %bitcast.85), calls=%async_computation | async-start | bytes 6291456 | tf_op jit(solution)/shard_map/all_to_all | solution.py:108
  242.1 13.7 %copy-start.1 = (bf16[48,8,8,512]{3,1,2,0:T(8,128)(2,1)S(1)}, bf16[48,8,8,512]{3,1,2,0:T(8,128)(2,1)}, u32[]{:S(2)}) copy-start(bf16[48,8,8,512]{3,1,2,0:T(8,128)(2,1)} %copy.24) | copy-start | bytes 9437188
  267.4 16.5 %copy-start.4 = (bf16[384,1536]{1,0:T(8,128)(2,1)S(1)}, bf16[384,1536]{1,0:T(8,128)(2,1)}, u32[]{:S(2)}) copy-start(bf16[384,1536]{1,0:T(8,128)(2,1)} %param.18) | copy-start | bytes 3538948
  267.4 16.5 %copy-start.6 = (f32[1536]{0:T(1024)S(1)}, f32[1536]{0:T(1024)}, u32[]{:S(2)}) copy-start(f32[1536]{0:T(1024)} %param.19) | copy-start | bytes 18436
  353.1 41.9 %all-to-all-start.1 = ((bf16[4,8,96,512]{3,1,2,0:T(8,128)(2,1)}), bf16[4,8,96,512]{3,1,2,0:T(8,128)(2,1)}, u32[]{:S(2)}, u32[]{:S(2)}) async-start(bf16[4,8,96,512]{3,1,2,0:T(8,128)(2,1)} %bitcast_bitcast_fusion.1), calls=%async_computation.1 | async-start | bytes 6291456 | tf_op jit(solution)/shard_map/all_to_all | solution.py:120
  395.1 41.7 %all-to-all-start.3 = ((bf16[4,8,96,512]{3,1,2,0:T(8,128)(2,1)}), bf16[4,8,96,512]{3,1,2,0:T(8,128)(2,1)}, u32[]{:S(2)}, u32[]{:S(2)}) async-start(bf16[4,8,96,512]{3,1,2,0:T(8,128)(2,1)} %bitcast_bitcast_fusion), calls=%async_computation.3 | async-start | bytes 6291456 | tf_op jit(solution)/shard_map/all_to_all | solution.py:120

commit v2 on v0

v2 whole, which is shorter than its diff:
```python
import functools
import math

import jax
import jax.numpy as jnp
from jax import lax
from jax.experimental import pallas as pl
from jax.experimental.pallas import tpu as pltpu
from jax.sharding import PartitionSpec as P

HALO = 2
TILE = 8
LANES = 128
MIB = 1 << 20
VMEM_LIMIT = 56 * MIB


def direction_factors(dirs):
    angle = (jnp.arange(dirs, dtype=jnp.float32) + 0.5) * (2.0 * math.pi / dirs)
    return (0.5 * jnp.abs(jnp.cos(angle)), 0.5 * jnp.abs(jnp.sin(angle)))


def chunk_row(owner, j, half, late):
    return jnp.where((owner == 0) != late, half + j, j)


UNREAD = pl.BlockSpec(memory_space=pl.ANY)


def lane_tiles(cols):
    return [pl.ds(c * LANES, LANES) for c in range(cols // LANES)]


def propagate_kernel(parts, local, chunks, window, keep, *refs):
    refs = list(refs)
    own_ref, sign_ref, along_ref, _, forcing_ref, cg_ref, turn_ref, mask_ref = refs[:8]
    refs = refs[8:]
    wcg_ref = wturn_ref = wmask_ref = None
    if window:
        above_ref, below_ref, wcg_ref, wturn_ref, wmask_ref = refs[:5]
        refs = refs[5:]
    if keep:
        home_ref = refs.pop(0)
    sends = parts * len(chunks)
    send_refs = refs[:sends]
    cel_ref, base_ref, trn_ref, first_ref, swap_ref = refs[sends : sends + 5]
    dirs, rows, cols = forcing_ref.shape[1:]
    pitch = dirs + 1
    tiles = rows // TILE
    count = tiles + (1 if window else 0)
    lanes = lane_tiles(cols)

    def span(t):
        return pl.ds(t * TILE, TILE)

    def level(main, side, t, *lead):
        return main[(*lead, span(t), slice(None))] if t < tiles else side[(*lead, slice(None), slice(None))]

    for t in range(count):
        sea = level(mask_ref, wmask_ref, t).astype(jnp.float32)
        celerity = 0.1 + 0.8 * level(cg_ref, wcg_ref, t, 0).astype(jnp.float32) / 7.0
        turning = 0.3 * jnp.abs(level(turn_ref, wturn_ref, t, 0).astype(jnp.float32) - 3.5) / 3.5
        cel_ref[span(t), :] = celerity * sea
        base_ref[span(t), :] = (1.0 - turning) * sea
        trn_ref[span(t), :] = turning * sea

    if window:
        side_ref, edge_ref = refs[sends + 5 :]
        edge_ref[...] = jnp.zeros_like(edge_ref)
        for r in range(HALO):
            for c, here in enumerate(lanes):
                edge_ref[c, pl.ds(r * pitch, dirs), :] = above_ref[r, 0, :, here].astype(jnp.float32)
                low = (TILE - HALO + r) * pitch
                edge_ref[c, pl.ds(low, dirs), :] = below_ref[r, 0, :, here].astype(jnp.float32)

        def gather(d, carry):
            for c, here in enumerate(lanes):
                side_ref[d, :, here] = edge_ref[c, pl.ds(d, TILE, stride=pitch), :]
            return carry

        lax.fori_loop(0, dirs, gather, 0)

    row = lax.broadcasted_iota(jnp.int32, (TILE, LANES), 0)
    lane = lax.broadcasted_iota(jnp.int32, (TILE, LANES), 1)
    nothing = jnp.zeros((TILE, LANES), jnp.float32)

    def sweep(load, store, final):
        def one(d, carry):
            following = jnp.where(d == dirs - 1, 0, d + 1)
            previous = jnp.where(d == 0, dirs - 1, d - 1)
            ax = along_ref[0, d]
            ay = along_ref[1, d]
            both = ax + ay
            right = sign_ref[0, d] > 0
            high = sign_ref[1, d] > 0
            shift_x = jnp.where(right, LANES - 1, 1)
            shift_y = jnp.where(high, TILE - 1, 1)
            at_right = lane == jnp.where(right, LANES - 1, LANES)
            at_left = lane == jnp.where(right, LANES, 0)
            at_high = row == jnp.where(high, TILE - 1, TILE)
            at_low = row == jnp.where(high, TILE, 0)

            def column(c):
                here = [load(t, d, lanes[c]) for t in range(count)]
                flow = [cel_ref[span(t), lanes[c]] * here[t] for t in range(count)]
                return here, flow, [pltpu.roll(f, shift_x, 1) for f in flow]

            before = [nothing] * count
            here, flow, moved = column(0)
            for c in range(len(lanes)):
                beyond = [nothing] * count
                if c + 1 < len(lanes):
                    later = column(c + 1)
                    beyond = later[2]
                lifted = [pltpu.roll(f, shift_y, 0) for f in flow]
                side = None
                for t in reversed(range(count)):
                    above = lifted[t + 1] if t + 1 < tiles else nothing
                    below = lifted[t - 1] if 0 < t < tiles else nothing
                    flow_x = jnp.where(at_right, beyond[t], jnp.where(at_left, before[t], moved[t]))
                    flow_y = jnp.where(at_high, above, jnp.where(at_low, below, lifted[t]))
                    up = level(turn_ref, wturn_ref, t, 0)[:, c * LANES : (c + 1) * LANES] >= 4
                    turned = jnp.where(up, load(t, following, lanes[c]), load(t, previous, lanes[c]))
                    total = (base_ref[span(t), lanes[c]] - both * cel_ref[span(t), lanes[c]]) * here[t]
                    total = total + ax * flow_x + ay * flow_y + trn_ref[span(t), lanes[c]] * turned
                    if final and window:
                        if t == tiles:
                            side = total
                            continue
                        if t == 0:
                            total = total + jnp.where(row < HALO, pltpu.roll(side, TILE - HALO, 0), 0.0)
                        if t == tiles - 1:
                            total = total + jnp.where(row >= TILE - HALO, pltpu.roll(side, HALO, 0), 0.0)
                    store(t, d, c, total)
                if c + 1 < len(lanes):
                    before = moved
                    here, flow, moved = later
            return carry

        lax.fori_loop(0, dirs, one, 0, unroll=2)

    def load_input(t, d, lanes_here):
        return forcing_ref[0, d, span(t), lanes_here] if t < tiles else side_ref[d, :, lanes_here]

    def load_first(t, d, lanes_here):
        return first_ref[d, span(t), lanes_here]

    def store_first(t, d, c, value):
        first_ref[d, span(t), lanes[c]] = value

    def store_last(t, d, c, value):
        if keep:
            home_ref[0, d, span(t), lanes[c]] = value
        swap_ref[c, pl.ds(t * TILE * pitch + d, TILE, stride=pitch), :] = value

    sweep(load_input, store_first, False)
    sweep(load_first, store_last, True)

    own = own_ref[0]
    half = local // 2
    for i, late in enumerate(chunks):
        for k in range(parts):
            owner = own ^ k
            for j in range(half):
                start = (owner * local + chunk_row(owner, j, half, late)) * pitch
                for c, here in enumerate(lanes):
                    piece = swap_ref[c, pl.ds(start, dirs), :]
                    send_refs[i * parts + k][j, 0, :, here] = piece.astype(jnp.bfloat16)


def propagate(own, signs, along, after, forcing, cg, turn, mask, side, parts, chunks, keep, group):
    freqs, dirs, rows, cols = forcing.shape
    begin, many = group
    local = rows // parts
    half = local // 2
    window = side is not None
    smem = pl.BlockSpec(memory_space=pltpu.SMEM)
    levels = pl.BlockSpec((1, rows, cols), lambda f: (begin + f, 0, 0))
    block = pl.BlockSpec((1, dirs, rows, cols), lambda f: (begin + f, 0, 0, 0))
    in_specs = [smem, smem, smem, UNREAD, block, levels, levels, pl.BlockSpec((rows, cols), lambda f: (0, 0))]
    args = [own, signs, along, after, forcing, cg, turn, mask]
    if window:
        edge = pl.BlockSpec((HALO, 1, dirs, cols), lambda f: (0, begin + f, 0, 0))
        near = pl.BlockSpec((1, TILE, cols), lambda f: (begin + f, 0, 0))
        in_specs += [edge, edge, near, near, pl.BlockSpec((TILE, cols), lambda f: (0, 0))]
        args += list(side)
    out_specs, out_shape = [], []
    if keep:
        out_specs.append(pl.BlockSpec((1, dirs, rows, cols), lambda f: (f, 0, 0, 0)))
        out_shape.append(jax.ShapeDtypeStruct((many, dirs, rows, cols), jnp.float32))
    for _ in range(parts * len(chunks)):
        out_specs.append(pl.BlockSpec((half, 1, dirs, cols), lambda f: (0, f, 0, 0)))
        out_shape.append(jax.ShapeDtypeStruct((half, many, dirs, cols), jnp.bfloat16))
    deep = rows + (TILE if window else 0)
    coefs = pltpu.VMEM((deep, cols), jnp.float32)
    scratch = [
        coefs,
        coefs,
        coefs,
        pltpu.VMEM((dirs, deep, cols), jnp.float32),
        pltpu.VMEM((cols // LANES, rows * (dirs + 1), LANES), jnp.float32),
    ]
    if window:
        scratch.append(pltpu.VMEM((dirs, TILE, cols), jnp.float32))
        scratch.append(pltpu.VMEM((cols // LANES, TILE * (dirs + 1), LANES), jnp.float32))
    size = many * dirs * rows * cols
    outs = pl.pallas_call(
        functools.partial(propagate_kernel, parts, local, chunks, window, keep),
        grid=(many,),
        in_specs=in_specs,
        out_specs=out_specs,
        out_shape=out_shape,
        scratch_shapes=scratch,
        compiler_params=pltpu.CompilerParams(vmem_limit_bytes=VMEM_LIMIT),
        cost_estimate=pl.CostEstimate(flops=40 * size, bytes_accessed=(8 if keep else 4) * size, transcendentals=0),
    )(*args)
    outs = list(outs)
    home = outs.pop(0) if keep else None
    return home, [outs[i * parts : (i + 1) * parts] for i in range(len(chunks))]


def edges_kernel(_, top_ref, bottom_ref, first_ref, last_ref, swap_ref):
    dirs, _, cols = top_ref.shape[1:]
    pitch = dirs + 1
    lanes = lane_tiles(cols)

    for ref, out_ref, low in ((top_ref, first_ref, 0), (bottom_ref, last_ref, TILE - HALO)):

        def body(d, carry, ref=ref):
            for c, here in enumerate(lanes):
                swap_ref[c, pl.ds(d, TILE, stride=pitch), :] = ref[0, d, :, here]
            return carry

        lax.fori_loop(0, dirs, body, 0, unroll=2)
        for r in range(HALO):
            for c, here in enumerate(lanes):
                out_ref[r, 0, :, here] = swap_ref[c, pl.ds((low + r) * pitch, dirs), :].astype(jnp.bfloat16)


def edges(after, forcing):
    freqs, dirs, rows, cols = forcing.shape
    out = pl.BlockSpec((HALO, 1, dirs, cols), lambda f: (0, f, 0, 0))
    shape = jax.ShapeDtypeStruct((HALO, freqs, dirs, cols), jnp.bfloat16)
    return pl.pallas_call(
        edges_kernel,
        grid=(freqs,),
        in_specs=[
            UNREAD,
            pl.BlockSpec((1, dirs, TILE, cols), lambda f: (f, 0, 0, 0)),
            pl.BlockSpec((1, dirs, TILE, cols), lambda f: (f, 0, rows // TILE - 1, 0)),
        ],
        out_specs=[out, out],
        out_shape=[shape, shape],
        scratch_shapes=[pltpu.VMEM((cols // LANES, TILE * (dirs + 1), LANES), jnp.float32)],
        compiler_params=pltpu.CompilerParams(vmem_limit_bytes=VMEM_LIMIT),
        cost_estimate=pl.CostEstimate(
            flops=freqs * dirs * TILE * cols, bytes_accessed=8 * freqs * dirs * TILE * cols, transcendentals=0
        ),
    )(after, forcing, forcing)


def by_row_kernel(_, state_ref, out_ref, swap_ref):
    deep, local, _ = state_ref.shape
    pitch = deep + 1

    def body(d, carry):
        swap_ref[pl.ds(d, local, stride=pitch), :] = state_ref[d].astype(jnp.float32)
        return carry

    lax.fori_loop(0, deep, body, 0, unroll=8)
    for r in range(local):
        out_ref[r] = swap_ref[pl.ds(r * pitch, deep), :].astype(jnp.bfloat16)


def by_row(after, state):
    deep, local, cols = state.shape
    return pl.pallas_call(
        by_row_kernel,
        grid=(cols // LANES,),
        in_specs=[UNREAD, pl.BlockSpec((deep, local, LANES), lambda c: (0, 0, c))],
        out_specs=pl.BlockSpec((local, deep, LANES), lambda c: (0, 0, c)),
        out_shape=jax.ShapeDtypeStruct((local, deep, cols), jnp.bfloat16),
        scratch_shapes=[pltpu.VMEM((local * (deep + 1), LANES), jnp.float32)],
        compiler_params=pltpu.CompilerParams(vmem_limit_bytes=VMEM_LIMIT),
        cost_estimate=pl.CostEstimate(flops=4 * state.size, bytes_accessed=4 * state.size, transcendentals=0),
    )(after, state)


def turned_kernel(_, w_in_ref, w_out_ref, in_t_ref, out_t_ref):
    in_t_ref[...] = w_in_ref[...].T
    out_t_ref[...] = w_out_ref[...].T


def turned(after, w_in, w_out):
    hidden, total = w_in.shape
    step = 512
    tall = pl.BlockSpec((step, total), lambda h: (h, 0))
    wide = pl.BlockSpec((total, step), lambda h: (0, h))
    return pl.pallas_call(
        turned_kernel,
        grid=(hidden // step,),
        in_specs=[UNREAD, tall, wide],
        out_specs=[wide, tall],
        out_shape=[jax.ShapeDtypeStruct((total, hidden), w_in.dtype), jax.ShapeDtypeStruct((hidden, total), w_in.dtype)],
        compiler_params=pltpu.CompilerParams(vmem_limit_bytes=VMEM_LIMIT),
        cost_estimate=pl.CostEstimate(flops=4 * w_in.size, bytes_accessed=8 * w_in.size, transcendentals=0),
    )(after, w_in, w_out)


def source_kernel(parts, groups, step, own_ref, _, state_ref, wind_ref, w_in_ref, out_t_ref, in_t_ref, weight_ref, *refs):
    pieces = parts * groups
    cell_refs = refs[:pieces]
    grad_ref = refs[pieces]
    back_refs = refs[pieces + 1 : 2 * pieces + 1]
    cell_ref, weighted_ref, grown_ref = refs[2 * pieces + 1 :]
    many, dirs, width = cell_refs[0].shape[1:]
    comps = many * dirs
    hidden = w_in_ref.shape[0]
    own = own_ref[0]

    def place(k, g):
        return pl.ds(pl.multiple_of(((own ^ k) * groups + g) * comps, TILE), comps)

    for k in range(parts):
        for g in range(groups):
            cell_ref[place(k, g), :] = cell_refs[g * parts + k][0].astype(jnp.float32).reshape(comps, width)
    cell = cell_ref[...].astype(jnp.bfloat16)
    state = state_ref[0]
    wind = wind_ref[0]
    grad = jnp.zeros((TILE, width), jnp.float32)
    for h in range(0, hidden, step):
        some = pl.ds(h, step)
        weight = weight_ref[some, :]
        forward = jnp.dot(w_in_ref[some, :], state, preferred_element_type=jnp.float32) + weight * wind
        squash = jnp.tanh(forward)
        pulled = jnp.dot(out_t_ref[some, :], cell, preferred_element_type=jnp.float32)
        weighted = (1.0 - squash * squash) * pulled
        weighted_ref[some, :] = weighted.astype(jnp.bfloat16)
        grad = grad + jnp.sum((weight * weighted).reshape(step // TILE, TILE, width), axis=0)
    grad_ref[0] = jnp.sum(grad, axis=0, keepdims=True)
    grown_ref[...] = jnp.dot(in_t_ref[...], weighted_ref[...], preferred_element_type=jnp.float32)
    for k in range(parts):
        for g in range(groups):
            back_refs[g * parts + k][0] = grown_ref[place(k, g), :].reshape(many, dirs, width).astype(jnp.bfloat16)


def source_term(own, after, state, wind, w_in, out_t, in_t, weight, cells, late):
    groups, parts = len(cells), len(cells[0])
    half, many, dirs, cols = cells[0][0].shape
    hidden, total = w_in.shape
    width = min(cols, 512)

    def row_of(j, own_ref):
        return chunk_row(own_ref[0], j, half, late)

    def whole(shape):
        return pl.BlockSpec(shape, lambda j, c, own_ref: (0, 0))

    piece = pl.BlockSpec((1, many, dirs, width), lambda j, c, own_ref: (j, 0, 0, c))
    line = pl.BlockSpec((1, 1, width), lambda j, c, own_ref: (j, 0, c))
    pieces = groups * parts
    outs = pl.pallas_call(
        functools.partial(source_kernel, parts, groups, 256),
        grid_spec=pltpu.PrefetchScalarGridSpec(
            num_scalar_prefetch=1,
            grid=(half, cols // width),
            in_specs=[
                UNREAD,
                pl.BlockSpec((1, total, width), lambda j, c, own_ref: (row_of(j, own_ref), 0, c)),
                pl.BlockSpec((1, 1, width), lambda j, c, own_ref: (row_of(j, own_ref), 0, c)),
                whole((hidden, total)),
                whole((hidden, total)),
                whole((total, hidden)),
                whole((hidden, 1)),
            ]
            + [piece] * pieces,
            out_specs=[line] + [piece] * pieces,
            scratch_shapes=[
                pltpu.VMEM((total, width), jnp.float32),
                pltpu.VMEM((hidden, width), jnp.bfloat16),
                pltpu.VMEM((total, width), jnp.float32),
            ],
        ),
        out_shape=[jax.ShapeDtypeStruct((half, 1, cols), jnp.float32)]
        + [jax.ShapeDtypeStruct(cells[0][0].shape, jnp.bfloat16)] * pieces,
        compiler_params=pltpu.CompilerParams(vmem_limit_bytes=VMEM_LIMIT),
        cost_estimate=pl.CostEstimate(
            flops=6 * half * cols * hidden * total,
            bytes_accessed=6 * half * cols * total,
            transcendentals=half * cols * hidden,
        ),
    )(own, after, state, wind, w_in, out_t, in_t, weight, *[cell for group in cells for cell in group])
    return outs[0].reshape(half, cols), [outs[1 + g * parts : 1 + (g + 1) * parts] for g in range(groups)]


def join_kernel(parts, own_ref, _, home_ref, *refs):
    back_refs = refs[: 2 * parts]
    out_ref, swap_ref = refs[2 * parts :]
    dirs, rows, cols = home_ref.shape[1:]
    pitch = dirs + 1
    local = rows // parts
    half = local // 2
    own = own_ref[0]
    lanes = lane_tiles(cols)
    for late in (False, True):
        for k in range(parts):
            owner = own ^ k
            for j in range(half):
                start = (owner * local + chunk_row(owner, j, half, late)) * pitch
                for c, here in enumerate(lanes):
                    piece = back_refs[late * parts + k][j, 0, :, here]
                    swap_ref[c, pl.ds(start, dirs), :] = piece.astype(jnp.float32)

    def body(d, carry):
        for t in range(rows // TILE):
            for c, here in enumerate(lanes):
                grown = swap_ref[c, pl.ds(t * TILE * pitch + d, TILE, stride=pitch), :]
                out_ref[0, d, pl.ds(t * TILE, TILE), here] = home_ref[0, d, pl.ds(t * TILE, TILE), here] + grown
        return carry

    lax.fori_loop(0, dirs, body, 0, unroll=2)


def join(own, into, home, early, late, freqs, begin):
    parts = len(early)
    many, dirs, rows, cols = home.shape
    half = early[0].shape[0]
    block = pl.BlockSpec((1, dirs, rows, cols), lambda f: (f, 0, 0, 0))
    piece = pl.BlockSpec((half, 1, dirs, cols), lambda f: (0, f, 0, 0))
    return pl.pallas_call(
        functools.partial(join_kernel, parts),
        grid=(many,),
        in_specs=[pl.BlockSpec(memory_space=pltpu.SMEM), UNREAD, block] + [piece] * (2 * parts),
        out_specs=pl.BlockSpec((1, dirs, rows, cols), lambda f: (begin + f, 0, 0, 0)),
        out_shape=jax.ShapeDtypeStruct((freqs, dirs, rows, cols), jnp.float32),
        scratch_shapes=[pltpu.VMEM((cols // LANES, rows * (dirs + 1), LANES), jnp.float32)],
        input_output_aliases={} if begin == 0 else {1: 0},
        compiler_params=pltpu.CompilerParams(vmem_limit_bytes=VMEM_LIMIT),
        cost_estimate=pl.CostEstimate(flops=home.size, bytes_accessed=10 * home.size, transcendentals=0),
    )(own, into, home, *early, *late)


def swapped(pieces):
    parts = len(pieces)
    moved = {k: lax.ppermute(pieces[k], "comp", [(i, i ^ k) for i in range(parts)]) for k in range(parts - 1, 0, -1)}
    return [pieces[0]] + [moved[k] for k in range(1, parts)]


def across(low, high):
    count = lax.axis_size("space")
    up = [(i, i + 1) for i in range(count - 1)]
    down = [(i + 1, i) for i in range(count - 1)]
    return lax.ppermute(high, "space", up), lax.ppermute(low, "space", down)


def near_levels(cg, turn, mask):
    freqs, rows, _ = cg.shape
    levels = jnp.concatenate([cg, turn, mask[None]], axis=0)
    low, high = levels[:, :HALO], levels[:, rows - HALO :]
    above, below = across(low, high)
    near = jnp.concatenate([above, low, high, below], axis=1)
    return (near[:freqs], near[freqs : 2 * freqs], near[2 * freqs])


def shards(
    adjoint_forcing,
    forward_state,
    wind_speed,
    cg_index,
    turn_index,
    sea_mask,
    dir_sign,
    w_in,
    w_out,
    wind_weight,
):
    parts = lax.axis_size("comp")
    own_place = lax.axis_index("comp")
    own = own_place.astype(jnp.int32).reshape(1)
    dirs = dir_sign.shape[1]
    comps, rows, cols = adjoint_forcing.shape
    freqs = comps // dirs
    half = rows // parts // 2
    along = jnp.stack(direction_factors(dirs))
    forcing = adjoint_forcing.reshape(freqs, dirs, rows, cols)
    weight = wind_weight[:, None]
    wind = wind_speed[:, None]
    many = freqs // 2 if freqs % 2 == 0 else freqs
    groups = [(begin, many) for begin in range(0, freqs, many)]

    def spread(after, side, chunks, keep, group):
        fields = (forcing, cg_index, turn_index, sea_mask)
        return propagate(own, dir_sign, along, after, *fields, side, parts, chunks, keep, group)

    near = near_levels(cg_index, turn_index, sea_mask)
    early, late, homes = [], [], []
    after = wind
    if half >= HALO:
        _, [pieces] = spread(after, None, (False,), False, groups[0])
        early.append(swapped(pieces))
        after = pieces[-1]
    low, high = edges(after, forcing)
    side = (*across(low, high), *near)
    after = high
    if half >= HALO:
        for group in groups[1:]:
            _, [pieces] = spread(after, None, (False,), False, group)
            early.append(swapped(pieces))
            after = pieces[-1]
    state = by_row(after, forward_state)
    in_t, out_t = turned(state, w_in, w_out)
    after = in_t
    for group in groups:
        home, pieces = spread(after, side, (True,) if half >= HALO else (False, True), True, group)
        if half < HALO:
            early.append(swapped(pieces[0]))
        late.append(swapped(pieces[-1]))
        homes.append(home)
        after = pieces[-1][-1]
    early_grad, early_back = source_term(own, after, state, wind, w_in, out_t, in_t, weight, early, False)
    after = early_back[-1][-1]
    early_back = [swapped(pieces) for pieces in early_back]
    late_grad, late_back = source_term(own, after, state, wind, w_in, out_t, in_t, weight, late, True)
    start = late_back[-1][-1]
    late_back = [swapped(pieces) for pieces in late_back]
    for g, (begin, _) in enumerate(groups):
        start = join(own, start, homes[g], early_back[g], late_back[g], freqs, begin)
    first = jnp.where(own_place == 0, late_grad, early_grad)
    second = jnp.where(own_place == 0, early_grad, late_grad)
    return (start.reshape(comps, rows, cols), jnp.concatenate([first, second], axis=0))


def solution(mesh):
    placed = (
        P("comp", "space", None),
        P(None, ("space", "comp"), None),
        P(("space", "comp"), None),
        P("comp", "space", None),
        P("comp", "space", None),
        P("space", None),
        P(),
        P(),
        P(),
        P(),
    )
    return jax.shard_map(
        shards,
        mesh=mesh,
        in_specs=placed,
        out_specs=(P("comp", "space", None), P(("space", "comp"), None)),
        check_vma=False,
    )
```

time: 640 us -> 229 us (0.36)
  waiting for transfers between devices: 263 us -> 52.9 us
  local copies, waits for them, and re-layouts: 146 us -> 4.89 us
  Pallas kernels: 0 us -> 134 us
  other arithmetic: 121 us -> 3.96 us
  matrix products: 77.5 us -> 0 us
    all_to_all x2 -> x0, waiting for transfers between devices: 263 us -> none  [the longest x1 137 us: shards(): lax.all_to_all(cell_start, 'comp', split_axis=0, concat_axis=1, tiled=True)]
    pallas_call x0 -> x11, Pallas kernels: none -> 134 us  [the longest x4 53.7 us: propagate(): pl.pallas_call(functools.partial(propagate_kernel, parts, local, chunks,...]
    dot_general x3 -> x0, matrix products: 77.5 us -> none  [the longest x1 33 us: source_adjoint(): jnp.dot(w_in, cell_state, preferred_element_type=jnp.float32)]
    mul x3 -> x0, other arithmetic: 67.6 us -> none  [the longest x2 56.1 us: adjoint_step(): flux_x = cour_x * masked]
    slice x8 -> x1, local copies, waits for them, and re-layouts: 62.2 us -> 0.71 us  [near_levels(): return (near[:freqs], near[freqs:2 * freqs], near[2 * freqs])]
    ppermute x4 -> x28, waiting for transfers between devices: 0.01 us -> 52.9 us  [the longest x24 42.7 us: swapped(): lax.ppermute(pieces[k], 'comp', [(i, i ^ k) for i in range(parts)])]
    add x3 -> x0, other arithmetic: 51.1 us -> none  [the longest x1 35 us: adjoint_step(): return retained + term_x + term_y + term_t]
    all_to_all x3 -> x0, local copies, waits for them, and re-layouts: 43.1 us -> none  [the longest x2 31 us: shards(): lax.all_to_all(costate, 'comp', split_axis=1, concat_axis=0, tiled=True)]
  transfers between devices with their start and end apart: 6 -> 28, of which waited for: 2 -> 7; matrix products, arithmetic and copies ran while one was open for 10% -> 3% of each run, Pallas kernels for 0% -> 56%
where the time goes in v2:
time: 229 us; the launch traced here: 228 us
  Pallas kernels  134 us (59%)
  waiting for transfers between devices  52.9 us (23%)
  starting transfers between devices  31.3 us (14%)
  local copies, waits for them, and re-layouts  4.89 us (2%)
  other arithmetic  3.96 us (2%)
    pallas_call x4, Pallas kernels, propagate(): pl.pallas_call(functools.partial(propagate_kernel, parts, local, chunks,...  53.7 us
    pallas_call x2, Pallas kernels, source_term(): pl.pallas_call(functools.partial(source_kernel, parts, groups, 256), grid...  50.2 us
    ppermute x24, waiting for transfers between devices, swapped(): lax.ppermute(pieces[k], 'comp', [(i, i ^ k) for i in range(parts)])  42.7 us
    ppermute x24, starting transfers between devices, swapped(): lax.ppermute(pieces[k], 'comp', [(i, i ^ k) for i in range(parts)])  19.2 us
    ppermute x4, starting transfers between devices, across(): return (lax.ppermute(high, 'space', up), lax.ppermute(low, 'space', down))  12.2 us
    pallas_call x2, Pallas kernels, join(): pl.pallas_call(functools.partial(join_kernel, parts), grid=(many,), in_sp...  11.9 us
    ppermute x4, waiting for transfers between devices, across(): return (lax.ppermute(high, 'space', up), lax.ppermute(low, 'space', down))  10.2 us
    pallas_call x1, Pallas kernels, by_row(): pl.pallas_call(by_row_kernel, grid=(cols // LANES,), in_specs=[UNREAD, pl...  9.04 us
  transfers between devices with their start and end apart: 28, of which 7 were waited for; matrix products, arithmetic and copies ran while one was open for 3% of the time, Pallas kernels for 56%

profile of v2, /device:TPU:0, one launch (start us, length us, event | category | flops | bytes accessed | tf_op | source)
XLA Modules:
  0.0 227.7 jit_solution(10247286879993922695)
XLA Ops:
  0.6 1.2 pad_add_fusion.3
  1.8 4.8 %collective-permute-start.2 = (s32[9,2,1024]{2,1,0:T(2,128)S(1)}, s32[9,2,1024]{2,1,0:T(2,128)S(1)}, u32[]{:S(2)}, u32[]{:S(2)}) collective-permute-start(s32[9,2,1024]{2,1,0:T(2,128)S(1)} %get-tuple-element.82), channel_id=1, source_target_pairs={{0,1},{1,2},{2,3},{3,4},{4,5},{5,6},{6,7},{8,9},{9,10},{10,11},{11... | collective-permute-start | bytes 221192 | tf_op jit(solution)/shard_map/ppermute | solution.py:453
  6.7 1.3 collective-permute-start.3
  8.0 1.4 broadcast_in_dim.9.refs_3_.wind_ref
  9.4 0.6 pad_maximum_fusion.1.refs_2_
  10.0 11.6 %shard_map.113 = (bf16[4,2,24,1024]{3,2,1,0:T(8,128)(2,1)}, bf16[4,2,24,1024]{3,2,1,0:T(8,128)(2,1)}, bf16[4,2,24,1024]{3,2,1,0:T(8,128)(2,1)}, bf16[4,2,24,1024]{3,2,1,0:T(8,128)(2,1)}) custom-call(s32[1]{0:T(128)} %bitcast.refs_0_.own_ref, s32[2,24]{1,0:T(2,128)} %refs_1_.7, f32[2,24]{1,0:T(2,128)} %pad_maximum_fusion.1.refs_2_, ...), custom_call_target="tpu_custom_call" | custom-call | flops 62914560 | bytes 6291456 | tf_op jit(solution)/shard_map/pallas_call | solution.py:207
  21.7 1.6 collective-permute-start.6
  23.3 4.7 %shard_map.114 = (bf16[2,4,24,1024]{3,2,1,0:T(8,128)(2,1)}, bf16[2,4,24,1024]{3,2,1,0:T(8,128)(2,1)}) custom-call(bf16[4,2,24,1024]{3,2,1,0:T(8,128)(2,1)} %get-tuple-element.42._, f32[4,24,32,1024]{3,2,1,0:T(8,128)} %bitcast.12, f32[4,24,32,1024]{3,2,1,0:T(8,128)} %bitcast.13), custom_call_target="tpu_custom_call" | custom-call | flops 786432 | bytes 6291456 | tf_op jit(solution)/shard_map/pallas_call | solution.py:244
  28.0 4.6 %collective-permute-start = (bf16[2,4,24,1024]{3,2,1,0:T(8,128)(2,1)}, bf16[2,4,24,1024]{3,2,1,0:T(8,128)(2,1)S(1)}, u32[]{:S(2)}, u32[]{:S(2)}) collective-permute-start(bf16[2,4,24,1024]{3,2,1,0:T(8,128)(2,1)} %get-tuple-element.43.refs_3_), channel_id=1, source_target_pairs={{0,1},{1,2},{2,3},{3,4},{4,5},{5,6},{6,7},{8,9},{9,10},{10,11},{11... | collective-permute-start | bytes 1179656 | tf_op jit(solution)/shard_map/ppermute | solution.py:453
  32.6 11.7 %shard_map.115 = (bf16[4,2,24,1024]{3,2,1,0:T(8,128)(2,1)}, bf16[4,2,24,1024]{3,2,1,0:T(8,128)(2,1)}, bf16[4,2,24,1024]{3,2,1,0:T(8,128)(2,1)}, bf16[4,2,24,1024]{3,2,1,0:T(8,128)(2,1)}) custom-call(s32[1]{0:T(128)} %bitcast.refs_0_.own_ref, s32[2,24]{1,0:T(2,128)} %refs_1_.7, f32[2,24]{1,0:T(2,128)} %pad_maximum_fusion.1.refs_2_, ...), custom_call_target="tpu_custom_call" | custom-call | flops 62914560 | bytes 6291456 | tf_op jit(solution)/shard_map/pallas_call | solution.py:207
  44.2 9.0 %shard_map.116._.state_ref = bf16[8,384,1024]{2,1,0:T(8,128)(2,1)} custom-call(bf16[4,2,24,1024]{3,2,1,0:T(8,128)(2,1)} %get-tuple-element.44._, bf16[384,8,1024]{2,1,0:T(8,128)(2,1)} %state_ref.1), custom_call_target="tpu_custom_call" | custom-call | flops 12582912 | bytes 12582912 | tf_op jit(solution)/shard_map/pallas_call | solution.py:277
  53.3 4.1 %shard_map.117 = (bf16[384,1536]{1,0:T(8,128)(2,1)}, bf16[1536,384]{1,0:T(8,128)(2,1)}) custom-call(bf16[8,384,1024]{2,1,0:T(8,128)(2,1)} %shard_map.116._.state_ref, bf16[1536,384]{1,0:T(8,128)(2,1)} %w_in_ref.5, bf16[384,1536]{1,0:T(8,128)(2,1)} %w_out_ref.1), custom_call_target="tpu_custom_call" | custom-call | flops 2359296 | bytes 4718592 | tf_op jit(solution)/shard_map/pallas_call | solution.py:299
  57.4 0.6 collective-permute-start.5
  58.0 1.5 collective-permute-start.1
  59.5 0.6 add_bitcast_fusion.refs_12_
  60.2 0.7 fusion.1
  61.0 10.2 %collective-permute-done.1.refs_9_ = bf16[2,4,24,1024]{3,2,1,0:T(8,128)(2,1)S(1)} collective-permute-done((bf16[2,4,24,1024]{3,2,1,0:T(8,128)(2,1)S(1)}, bf16[2,4,24,1024]{3,2,1,0:T(8,128)(2,1)S(1)}, u32[]{:S(2)}, u32[]{:S(2)}) %collective-permute-start.1) | collective-permute-done | bytes 393248 | tf_op jit(solution)/shard_map/ppermute | solution.py:453
  71.2 1.6 collective-permute-start.8
  72.8 15.3 %shard_map.118 = (f32[2,24,32,1024]{3,2,1,0:T(8,128)}, bf16[4,2,24,1024]{3,2,1,0:T(8,128)(2,1)}, bf16[4,2,24,1024]{3,2,1,0:T(8,128)(2,1)}, bf16[4,2,24,1024]{3,2,1,0:T(8,128)(2,1)}, bf16[4,2,24,1024]{3,2,1,0:T(8,128)(2,1)}) custom-call(s32[1]{0:T(128)} %bitcast.refs_0_.own_ref, s32[2,24]{1,0:T(2,128)} %refs_1_.7, f32[2,24]{1,0:T(2,128)} %pad_maximum_fusion.1.refs_2_, ...), custom_call_target="tpu_custom_call" | custom-call | flops 62914560 | bytes 12582912 | tf_op jit(solution)/shard_map/pallas_call | solution.py:207
  88.1 0.8 collective-permute-start.9
  89.0 1.2 broadcast_in_dim.12.weight_ref
  90.2 15.2 %shard_map.119 = (f32[2,24,32,1024]{3,2,1,0:T(8,128)}, bf16[4,2,24,1024]{3,2,1,0:T(8,128)(2,1)}, bf16[4,2,24,1024]{3,2,1,0:T(8,128)(2,1)}, bf16[4,2,24,1024]{3,2,1,0:T(8,128)(2,1)}, bf16[4,2,24,1024]{3,2,1,0:T(8,128)(2,1)}) custom-call(s32[1]{0:T(128)} %bitcast.refs_0_.own_ref, s32[2,24]{1,0:T(2,128)} %refs_1_.7, f32[2,24]{1,0:T(2,128)} %pad_maximum_fusion.1.refs_2_, ...), custom_call_target="tpu_custom_call" | custom-call | flops 62914560 | bytes 12582912 | tf_op jit(solution)/shard_map/pallas_call | solution.py:207
  105.4 1.1 collective-permute-start.12
  106.5 1.0 collective-permute-start.11
  107.6 1.2 collective-permute-start.14
  108.7 0.7 collective-permute-start.15
  109.4 25.1 %shard_map.120 = (f32[4,1,1024]{2,1,0:T(1,128)}, bf16[4,2,24,1024]{3,2,1,0:T(8,128)(2,1)}, bf16[4,2,24,1024]{3,2,1,0:T(8,128)(2,1)}, bf16[4,2,24,1024]{3,2,1,0:T...) custom-call(s32[1]{0:T(128)} %bitcast.refs_0_.own_ref, ...), custom_call_target="tpu_custom_call" | custom-call | flops 14495514624 | bytes 9437184 | tf_op jit(solution)/shard_map/pallas_call | solution.py:362
  135.0 1.1 collective-permute-start.17
  136.5 0.6 collective-permute-start.22
  137.1 4.6 %collective-permute-done.15.refs_7_ = bf16[4,2,24,1024]{3,2,1,0:T(8,128)(2,1)S(1)} collective-permute-done((bf16[4,2,24,1024]{3,2,1,0:T(8,128)(2,1)}, bf16[4,2,24,1024]{3,2,1,0:T(8,128)(2,1)S(1)}, u32[]{:S(2)}, u32[]{:S(2)}) %collective-permute-start.15) | collective-permute-done | bytes 393248 | tf_op jit(solution)/shard_map/ppermute | solution.py:445
  141.7 0.8 copy-done.35
  142.5 25.1 %shard_map.121 = (f32[4,1,1024]{2,1,0:T(1,128)}, bf16[4,2,24,1024]{3,2,1,0:T(8,128)(2,1)}, bf16[4,2,24,1024]{3,2,1,0:T(8,128)(2,1)}, bf16[4,2,24,1024]{3,2,1,0:T...) custom-call(s32[1]{0:T(128)} %bitcast.refs_0_.own_ref, ...), custom_call_target="tpu_custom_call" | custom-call | flops 14495514624 | bytes 9437184 | tf_op jit(solution)/shard_map/pallas_call | solution.py:362
  167.6 0.8 collective-permute-start.19
  168.4 1.1 collective-permute-start.20
  169.9 1.4 collective-permute-start.24
  171.3 1.0 collective-permute-start.23
  172.3 8.2 %collective-permute-done.20.refs_6_ = bf16[4,2,24,1024]{3,2,1,0:T(8,128)(2,1)S(1)} collective-permute-done((bf16[4,2,24,1024]{3,2,1,0:T(8,128)(2,1)}, bf16[4,2,24,1024]{3,2,1,0:T(8,128)(2,1)S(1)}, u32[]{:S(2)}, u32[]{:S(2)}) %collective-permute-start.20) | collective-permute-done | bytes 393248 | tf_op jit(solution)/shard_map/ppermute | solution.py:445
  180.6 1.1 collective-permute-start.26
  181.6 6.0 %collective-permute-done.21.refs_7_ = bf16[4,2,24,1024]{3,2,1,0:T(8,128)(2,1)S(1)} collective-permute-done((bf16[4,2,24,1024]{3,2,1,0:T(8,128)(2,1)}, bf16[4,2,24,1024]{3,2,1,0:T(8,128)(2,1)S(1)}, u32[]{:S(2)}, u32[]{:S(2)}) %collective-permute-start.21) | collective-permute-done | bytes 393248 | tf_op jit(solution)/shard_map/ppermute | solution.py:445
  187.7 2.1 collective-permute-start.27
  189.8 0.7 fusion
  190.6 0.6 pad_maximum_fusion
  191.2 5.9 %shard_map.122._ = f32[4,24,32,1024]{3,2,1,0:T(8,128)} custom-call(s32[1]{0:T(128)} %bitcast.refs_0_.own_ref, bf16[4,2,24,1024]{3,2,1,0:T(8,128)(2,1)} %get-tuple-element.63._, f32[2,24,32,1024]{3,2,1,0:T(8,128)} %get-tuple-element.64.home_ref, bf16[4,2,24,1024]{3,2,1,0:T(8,128)(2,1)} %get-tuple-element.65.refs_0_, bf16[4,2,24,1024]{3,2,1,0:T(8,128)(2,1)} %copy-done.9, ...), custom_call_target="tpu_custom_call" | custom-call | flops 1572864 | bytes 15728640 | tf_op jit(solution)/shard_map/pallas_call | solution.py:430
  197.2 8.7 %collective-permute-done.23.refs_2_ = bf16[4,2,24,1024]{3,2,1,0:T(8,128)(2,1)S(1)} collective-permute-done((bf16[4,2,24,1024]{3,2,1,0:T(8,128)(2,1)S(1)}, bf16[4,2,24,1024]{3,2,1,0:T(8,128)(2,1)S(1)}, u32[]{:S(2)}, u32[]{:S(2)}) %collective-permute-start.23) | collective-permute-done | bytes 393248 | tf_op jit(solution)/shard_map/ppermute | solution.py:445
  205.9 8.4 %collective-permute-done.26.refs_6_ = bf16[4,2,24,1024]{3,2,1,0:T(8,128)(2,1)S(1)} collective-permute-done((bf16[4,2,24,1024]{3,2,1,0:T(8,128)(2,1)}, bf16[4,2,24,1024]{3,2,1,0:T(8,128)(2,1)S(1)}, u32[]{:S(2)}, u32[]{:S(2)}) %collective-permute-start.26) | collective-permute-done | bytes 393248 | tf_op jit(solution)/shard_map/ppermute | solution.py:445
  214.3 6.7 %collective-permute-done.27.refs_7_ = bf16[4,2,24,1024]{3,2,1,0:T(8,128)(2,1)S(1)} collective-permute-done((bf16[4,2,24,1024]{3,2,1,0:T(8,128)(2,1)}, bf16[4,2,24,1024]{3,2,1,0:T(8,128)(2,1)S(1)}, u32[]{:S(2)}, u32[]{:S(2)}) %collective-permute-start.27) | collective-permute-done | bytes 393248 | tf_op jit(solution)/shard_map/ppermute | solution.py:445
  221.0 0.7 copy-done.7
  221.7 5.9 %shard_map.123 = f32[4,24,32,1024]{3,2,1,0:T(8,128)} custom-call(s32[1]{0:T(128)} %bitcast.refs_0_.own_ref, f32[4,24,32,1024]{3,2,1,0:T(8,128)} %shard_map.122._, f32[2,24,32,1024]{3,2,1,0:T(8,128)} %get-tuple-element.73.home_ref, bf16[4,2,24,1024]{3,2,1,0:T(8,128)(2,1)} %get-tuple-element.74.refs_0_, ...), custom_call_target="tpu_custom_call", output_to_operand_aliasing={{}: (1, {})} | custom-call | flops 1572864 | bytes 15728640 | tf_op jit(solution)/shard_map/pallas_call | solution.py:430
  (105 shorter events, 1.8 us)
Async XLA Ops:
  1.8 55.6 %collective-permute-start.2 = (s32[9,2,1024]{2,1,0:T(2,128)S(1)}, s32[9,2,1024]{2,1,0:T(2,128)S(1)}, u32[]{:S(2)}, u32[]{:S(2)}) collective-permute-start(s32[9,2,1024]{2,1,0:T(2,128)S(1)} %get-tuple-element.82), channel_id=1, source_target_pairs={{0,1},{1,2},{2,3},{3,4},{4,5},{5,6},{6,7},{8,9},{9,10},{10,11},{11... | collective-permute-start | bytes 221192 | tf_op jit(solution)/shard_map/ppermute | solution.py:453
  6.7 51.3 %collective-permute-start.3 = (s32[9,2,1024]{2,1,0:T(2,128)S(1)}, s32[9,2,1024]{2,1,0:T(2,128)S(1)}, u32[]{:S(2)}, u32[]{:S(2)}) collective-permute-start(s32[9,2,1024]{2,1,0:T(2,128)S(1)} %get-tuple-element.83), channel_id=1, source_target_pairs={{1,0},{2,1},{3,2},{4,3},{5,4},{6,5},{7,6},{9,8},{10,9},{11,10},{12... | collective-permute-start | bytes 221192 | tf_op jit(solution)/shard_map/ppermute | solution.py:453
  21.7 66.4 %collective-permute-start.4 = (bf16[4,2,24,1024]{3,2,1,0:T(8,128)(2,1)}, bf16[4,2,24,1024]{3,2,1,0:T(8,128)(2,1)S(1)}, u32[]{:S(2)}, u32[]{:S(2)}) collective-permute-start(bf16[4,2,24,1024]{3,2,1,0:T(8,128)(2,1)} %get-tuple-element.51), channel_id=1, source_target_pairs={{0,8},{8,0},{16,24},{24,16},{1,9},{9,1},{17,25},{25,17},{2,10},{10... | collective-permute-start | bytes 1179656 | tf_op jit(solution)/shard_map/ppermute | solution.py:445
  21.7 83.7 %collective-permute-start.6 = (bf16[4,2,24,1024]{3,2,1,0:T(8,128)(2,1)}, bf16[4,2,24,1024]{3,2,1,0:T(8,128)(2,1)S(1)}, u32[]{:S(2)}, u32[]{:S(2)}) collective-permute-start(bf16[4,2,24,1024]{3,2,1,0:T(8,128)(2,1)} %get-tuple-element.42._), channel_id=1, source_target_pairs={{0,24},{8,16},{16,8},{24,0},{1,25},{9,17},{17,9},{25,1},{2,26},{10... | collective-permute-start | bytes 1179656 | tf_op jit(solution)/shard_map/ppermute | solution.py:445
  28.0 43.1 %collective-permute-start = (bf16[2,4,24,1024]{3,2,1,0:T(8,128)(2,1)}, bf16[2,4,24,1024]{3,2,1,0:T(8,128)(2,1)S(1)}, u32[]{:S(2)}, u32[]{:S(2)}) collective-permute-start(bf16[2,4,24,1024]{3,2,1,0:T(8,128)(2,1)} %get-tuple-element.43.refs_3_), channel_id=1, source_target_pairs={{0,1},{1,2},{2,3},{3,4},{4,5},{5,6},{6,7},{8,9},{9,10},{10,11},{11... | collective-permute-start | bytes 1179656 | tf_op jit(solution)/shard_map/ppermute | solution.py:453
  53.3 17.8 %copy-start.30 = (bf16[4,2,24,1024]{3,2,1,0:T(8,128)(2,1)S(1)}, bf16[4,2,24,1024]{3,2,1,0:T(8,128)(2,1)}, u32[]{:S(2)}) copy-start(bf16[4,2,24,1024]{3,2,1,0:T(8,128)(2,1)} %get-tuple-element.54) | copy-start | bytes 1179652
  53.3 17.8 %copy-start.26 = (bf16[4,2,24,1024]{3,2,1,0:T(8,128)(2,1)S(1)}, bf16[4,2,24,1024]{3,2,1,0:T(8,128)(2,1)}, u32[]{:S(2)}) copy-start(bf16[4,2,24,1024]{3,2,1,0:T(8,128)(2,1)} %get-tuple-element.55) | copy-start | bytes 1179652
  57.4 31.4 %collective-permute-start.5 = (bf16[4,2,24,1024]{3,2,1,0:T(8,128)(2,1)S(1)}, bf16[4,2,24,1024]{3,2,1,0:T(8,128)(2,1)S(1)}, u32[]{:S(2)}, u32[]{:S(2)}) collective-permute-start(bf16[4,2,24,1024]{3,2,1,0:T(8,128)(2,1)S(1)} %copy-done.33), channel_id=1, source_target_pairs={{0,16},{8,24},{16,0},{24,8},{1,17},{9,25},{17,1},{25,9},{2,18},{10... | collective-permute-start | bytes 1179656 | tf_op jit(solution)/shard_map/ppermute | solution.py:445
  58.0 13.1 %collective-permute-start.1 = (bf16[2,4,24,1024]{3,2,1,0:T(8,128)(2,1)S(1)}, bf16[2,4,24,1024]{3,2,1,0:T(8,128)(2,1)S(1)}, u32[]{:S(2)}, u32[]{:S(2)}) collective-permute-start(bf16[2,4,24,1024]{3,2,1,0:T(8,128)(2,1)S(1)} %copy-done.36), channel_id=1, source_target_pairs={{1,0},{2,1},{3,2},{4,3},{5,4},{6,5},{7,6},{9,8},{10,9},{11,10},{12... | collective-permute-start | bytes 1179656 | tf_op jit(solution)/shard_map/ppermute | solution.py:453
  71.1 35.4 %collective-permute-start.7 = (bf16[4,2,24,1024]{3,2,1,0:T(8,128)(2,1)S(1)}, bf16[4,2,24,1024]{3,2,1,0:T(8,128)(2,1)S(1)}, u32[]{:S(2)}, u32[]{:S(2)}) collective-permute-start(bf16[4,2,24,1024]{3,2,1,0:T(8,128)(2,1)S(1)} %copy-done.30), channel_id=1, source_target_pairs={{0,8},{8,0},{16,24},{24,16},{1,9},{9,1},{17,25},{25,17},{2,10},{10... | collective-permute-start | bytes 1179656 | tf_op jit(solution)/shard_map/ppermute | solution.py:445
  71.2 36.4 %collective-permute-start.8 = (bf16[4,2,24,1024]{3,2,1,0:T(8,128)(2,1)S(1)}, bf16[4,2,24,1024]{3,2,1,0:T(8,128)(2,1)S(1)}, u32[]{:S(2)}, u32[]{:S(2)}) collective-permute-start(bf16[4,2,24,1024]{3,2,1,0:T(8,128)(2,1)S(1)} %copy-done.26), channel_id=1, source_target_pairs={{0,16},{8,24},{16,0},{24,8},{1,17},{9,25},{17,1},{25,9},{2,18},{10... | collective-permute-start | bytes 1179656 | tf_op jit(solution)/shard_map/ppermute | solution.py:445
  72.7 15.3 %copy-start.8 = (bf16[4,2,24,1024]{3,2,1,0:T(8,128)(2,1)S(1)}, bf16[4,2,24,1024]{3,2,1,0:T(8,128)(2,1)}, u32[]{:S(2)}) copy-start(bf16[4,2,24,1024]{3,2,1,0:T(8,128)(2,1)} %get-tuple-element.44._) | copy-start | bytes 1179652
  72.7 16.3 %copy-start.17 = (f32[1536]{0:T(1024)S(1)}, f32[1536]{0:T(1024)}, u32[]{:S(2)}) copy-start(f32[1536]{0:T(1024)} %param.19) | copy-start | bytes 18436
  88.1 17.3 %copy-start.20 = (bf16[4,2,24,1024]{3,2,1,0:T(8,128)(2,1)}, bf16[4,2,24,1024]{3,2,1,0:T(8,128)(2,1)S(1)}, u32[]{:S(2)}) copy-start(bf16[4,2,24,1024]{3,2,1,0:T(8,128)(2,1)S(1)} %collective-permute-done.4.refs_1_) | copy-start | bytes 1179652
  88.1 19.5 %collective-permute-start.9 = (bf16[4,2,24,1024]{3,2,1,0:T(8,128)(2,1)S(1)}, bf16[4,2,24,1024]{3,2,1,0:T(8,128)(2,1)S(1)}, u32[]{:S(2)}, u32[]{:S(2)}) collective-permute-start(bf16[4,2,24,1024]{3,2,1,0:T(8,128)(2,1)S(1)} %copy-done.8), channel_id=1, source_target_pairs={{0,24},{8,16},{16,8},{24,0},{1,25},{9,17},{17,9},{25,1},{2,26},{10... | collective-permute-start | bytes 1179656 | tf_op jit(solution)/shard_map/ppermute | solution.py:445
  88.9 16.5 %copy-start.22 = (bf16[4,2,24,1024]{3,2,1,0:T(8,128)(2,1)}, bf16[4,2,24,1024]{3,2,1,0:T(8,128)(2,1)S(1)}, u32[]{:S(2)}) copy-start(bf16[4,2,24,1024]{3,2,1,0:T(8,128)(2,1)S(1)} %collective-permute-done.5.refs_2_) | copy-start | bytes 1179652
  88.9 19.8 %collective-permute-start.10 = (bf16[4,2,24,1024]{3,2,1,0:T(8,128)(2,1)}, bf16[4,2,24,1024]{3,2,1,0:T(8,128)(2,1)S(1)}, u32[]{:S(2)}, u32[]{:S(2)}) collective-permute-start(bf16[4,2,24,1024]{3,2,1,0:T(8,128)(2,1)} %get-tuple-element.58), channel_id=1, source_target_pairs={{0,8},{8,0},{16,24},{24,16},{1,9},{9,1},{17,25},{25,17},{2,10},{10... | collective-permute-start | bytes 1179656 | tf_op jit(solution)/shard_map/ppermute | solution.py:445
  90.2 15.2 %copy-start.12 = (bf16[4,2,24,1024]{3,2,1,0:T(8,128)(2,1)S(1)}, bf16[4,2,24,1024]{3,2,1,0:T(8,128)(2,1)}, u32[]{:S(2)}) copy-start(bf16[4,2,24,1024]{3,2,1,0:T(8,128)(2,1)} %get-tuple-element.47.refs_3_) | copy-start | bytes 1179652
  90.2 16.3 %copy-start.29 = (bf16[4,2,24,1024]{3,2,1,0:T(8,128)(2,1)S(1)}, bf16[4,2,24,1024]{3,2,1,0:T(8,128)(2,1)}, u32[]{:S(2)}) copy-start(bf16[4,2,24,1024]{3,2,1,0:T(8,128)(2,1)} %get-tuple-element.59) | copy-start | bytes 1179652
  105.4 29.6 %collective-permute-start.12 = (bf16[4,2,24,1024]{3,2,1,0:T(8,128)(2,1)S(1)}, bf16[4,2,24,1024]{3,2,1,0:T(8,128)(2,1)S(1)}, u32[]{:S(2)}, u32[]{:S(2)}) collective-permute-start(bf16[4,2,24,1024]{3,2,1,0:T(8,128)(2,1)S(1)} %copy-done.12), channel_id=1, source_target_pairs={{0,24},{8,16},{16,8},{24,0},{1,25},{9,17},{17,9},{25,1},{2,26},{10... | collective-permute-start | bytes 1179656 | tf_op jit(solution)/shard_map/ppermute | solution.py:445
  106.5 28.0 %collective-permute-start.11 = (bf16[4,2,24,1024]{3,2,1,0:T(8,128)(2,1)S(1)}, bf16[4,2,24,1024]{3,2,1,0:T(8,128)(2,1)S(1)}, u32[]{:S(2)}, u32[]{:S(2)}) collective-permute-start(bf16[4,2,24,1024]{3,2,1,0:T(8,128)(2,1)S(1)} %copy-done.29), channel_id=1, source_target_pairs={{0,16},{8,24},{16,0},{24,8},{1,17},{9,25},{17,1},{25,9},{2,18},{10... | collective-permute-start | bytes 1179656 | tf_op jit(solution)/shard_map/ppermute | solution.py:445
  107.5 28.5 %collective-permute-start.13 = (bf16[4,2,24,1024]{3,2,1,0:T(8,128)(2,1)}, bf16[4,2,24,1024]{3,2,1,0:T(8,128)(2,1)S(1)}, u32[]{:S(2)}, u32[]{:S(2)}) collective-permute-start(bf16[4,2,24,1024]{3,2,1,0:T(8,128)(2,1)} %get-tuple-element.61), channel_id=1, source_target_pairs={{0,8},{8,0},{16,24},{24,16},{1,9},{9,1},{17,25},{25,17},{2,10},{10... | collective-permute-start | bytes 1179656 | tf_op jit(solution)/shard_map/ppermute | solution.py:445
  107.6 28.9 %collective-permute-start.14 = (bf16[4,2,24,1024]{3,2,1,0:T(8,128)(2,1)}, bf16[4,2,24,1024]{3,2,1,0:T(8,128)(2,1)S(1)}, u32[]{:S(2)}, u32[]{:S(2)}) collective-permute-start(bf16[4,2,24,1024]{3,2,1,0:T(8,128)(2,1)} %get-tuple-element.62), channel_id=1, source_target_pairs={{0,16},{8,24},{16,0},{24,8},{1,17},{9,25},{17,1},{25,9},{2,18},{10... | collective-permute-start | bytes 1179656 | tf_op jit(solution)/shard_map/ppermute | solution.py:445
  108.7 25.8 %copy-start.23 = (bf16[4,2,24,1024]{3,2,1,0:T(8,128)(2,1)}, bf16[4,2,24,1024]{3,2,1,0:T(8,128)(2,1)S(1)}, u32[]{:S(2)}) copy-start(bf16[4,2,24,1024]{3,2,1,0:T(8,128)(2,1)S(1)} %collective-permute-done.10.refs_1_) | copy-start | bytes 1179652
  108.7 33.0 %collective-permute-start.15 = (bf16[4,2,24,1024]{3,2,1,0:T(8,128)(2,1)}, bf16[4,2,24,1024]{3,2,1,0:T(8,128)(2,1)S(1)}, u32[]{:S(2)}, u32[]{:S(2)}) collective-permute-start(bf16[4,2,24,1024]{3,2,1,0:T(8,128)(2,1)} %get-tuple-element.48._), channel_id=1, source_target_pairs={{0,24},{8,16},{16,8},{24,0},{1,25},{9,17},{17,9},{25,1},{2,26},{10... | collective-permute-start | bytes 1179656 | tf_op jit(solution)/shard_map/ppermute | solution.py:445
  134.6 33.8 %collective-permute-start.16 = (bf16[4,2,24,1024]{3,2,1,0:T(8,128)(2,1)}, bf16[4,2,24,1024]{3,2,1,0:T(8,128)(2,1)S(1)}, u32[]{:S(2)}, u32[]{:S(2)}) collective-permute-start(bf16[4,2,24,1024]{3,2,1,0:T(8,128)(2,1)} %get-tuple-element.66), channel_id=1, source_target_pairs={{0,8},{8,0},{16,24},{24,16},{1,9},{9,1},{17,25},{25,17},{2,10},{10... | collective-permute-start | bytes 1179656 | tf_op jit(solution)/shard_map/ppermute | solution.py:445
  135.0 34.5 %collective-permute-start.17 = (bf16[4,2,24,1024]{3,2,1,0:T(8,128)(2,1)}, bf16[4,2,24,1024]{3,2,1,0:T(8,128)(2,1)S(1)}, u32[]{:S(2)}, u32[]{:S(2)}) collective-permute-start(bf16[4,2,24,1024]{3,2,1,0:T(8,128)(2,1)} %get-tuple-element.67), channel_id=1, source_target_pairs={{0,16},{8,24},{16,0},{24,8},{1,17},{9,25},{17,1},{25,9},{2,18},{10... | collective-permute-start | bytes 1179656 | tf_op jit(solution)/shard_map/ppermute | solution.py:445
  136.1 33.8 %collective-permute-start.18 = (bf16[4,2,24,1024]{3,2,1,0:T(8,128)(2,1)}, bf16[4,2,24,1024]{3,2,1,0:T(8,128)(2,1)S(1)}, u32[]{:S(2)}, u32[]{:S(2)}) collective-permute-start(bf16[4,2,24,1024]{3,2,1,0:T(8,128)(2,1)} %get-tuple-element.68), channel_id=1, source_target_pairs={{0,24},{8,16},{16,8},{24,0},{1,25},{9,17},{17,9},{25,1},{2,26},{10... | collective-permute-start | bytes 1179656 | tf_op jit(solution)/shard_map/ppermute | solution.py:445
  136.5 34.8 %collective-permute-start.22 = (bf16[4,2,24,1024]{3,2,1,0:T(8,128)(2,1)}, bf16[4,2,24,1024]{3,2,1,0:T(8,128)(2,1)S(1)}, u32[]{:S(2)}, u32[]{:S(2)}) collective-permute-start(bf16[4,2,24,1024]{3,2,1,0:T(8,128)(2,1)} %get-tuple-element.75), channel_id=1, source_target_pairs={{0,8},{8,0},{16,24},{24,16},{1,9},{9,1},{17,25},{25,17},{2,10},{10... | collective-permute-start | bytes 1179656 | tf_op jit(solution)/shard_map/ppermute | solution.py:445
  142.5 27.4 %copy-start.18 = (bf16[4,2,24,1024]{3,2,1,0:T(8,128)(2,1)S(1)}, bf16[4,2,24,1024]{3,2,1,0:T(8,128)(2,1)}, u32[]{:S(2)}) copy-start(bf16[4,2,24,1024]{3,2,1,0:T(8,128)(2,1)} %get-tuple-element.56._) | copy-start | bytes 1179652
  142.5 28.8 %copy-start.19 = (bf16[4,2,24,1024]{3,2,1,0:T(8,128)(2,1)S(1)}, bf16[4,2,24,1024]{3,2,1,0:T(8,128)(2,1)}, u32[]{:S(2)}) copy-start(bf16[4,2,24,1024]{3,2,1,0:T(8,128)(2,1)} %get-tuple-element.76) | copy-start | bytes 1179652
  142.5 47.3 %copy-start.16 = (f32[4,1,1024]{2,1,0:T(1,128)S(1)}, f32[4,1,1024]{2,1,0:T(1,128)}, u32[]{:S(2)}) copy-start(f32[4,1,1024]{2,1,0:T(1,128)} %get-tuple-element.81) | copy-start | bytes 49156
  167.6 4.7 %collective-permute-start.19 = (bf16[4,2,24,1024]{3,2,1,0:T(8,128)(2,1)}, bf16[4,2,24,1024]{3,2,1,0:T(8,128)(2,1)S(1)}, u32[]{:S(2)}, u32[]{:S(2)}) collective-permute-start(bf16[4,2,24,1024]{3,2,1,0:T(8,128)(2,1)} %get-tuple-element.70), channel_id=1, source_target_pairs={{0,8},{8,0},{16,24},{24,16},{1,9},{9,1},{17,25},{25,17},{2,10},{10... | collective-permute-start | bytes 1179656 | tf_op jit(solution)/shard_map/ppermute | solution.py:445
  168.4 22.8 %copy-start.9 = (bf16[4,2,24,1024]{3,2,1,0:T(8,128)(2,1)}, bf16[4,2,24,1024]{3,2,1,0:T(8,128)(2,1)S(1)}, u32[]{:S(2)}) copy-start(bf16[4,2,24,1024]{3,2,1,0:T(8,128)(2,1)S(1)} %collective-permute-done.16.refs_1_) | copy-start | bytes 1179652
  168.4 12.2 %collective-permute-start.20 = (bf16[4,2,24,1024]{3,2,1,0:T(8,128)(2,1)}, bf16[4,2,24,1024]{3,2,1,0:T(8,128)(2,1)S(1)}, u32[]{:S(2)}, u32[]{:S(2)}) collective-permute-start(bf16[4,2,24,1024]{3,2,1,0:T(8,128)(2,1)} %get-tuple-element.71), channel_id=1, source_target_pairs={{0,16},{8,24},{16,0},{24,8},{1,17},{9,25},{17,1},{25,9},{2,18},{10... | collective-permute-start | bytes 1179656 | tf_op jit(solution)/shard_map/ppermute | solution.py:445
  169.5 21.7 %copy-start.10 = (bf16[4,2,24,1024]{3,2,1,0:T(8,128)(2,1)}, bf16[4,2,24,1024]{3,2,1,0:T(8,128)(2,1)S(1)}, u32[]{:S(2)}) copy-start(bf16[4,2,24,1024]{3,2,1,0:T(8,128)(2,1)S(1)} %collective-permute-done.17.refs_2_) | copy-start | bytes 1179652
  169.5 18.2 %collective-permute-start.21 = (bf16[4,2,24,1024]{3,2,1,0:T(8,128)(2,1)}, bf16[4,2,24,1024]{3,2,1,0:T(8,128)(2,1)S(1)}, u32[]{:S(2)}, u32[]{:S(2)}) collective-permute-start(bf16[4,2,24,1024]{3,2,1,0:T(8,128)(2,1)} %get-tuple-element.72), channel_id=1, source_target_pairs={{0,24},{8,16},{16,8},{24,0},{1,25},{9,17},{17,9},{25,1},{2,26},{10... | collective-permute-start | bytes 1179656 | tf_op jit(solution)/shard_map/ppermute | solution.py:445
  169.9 21.3 %copy-start.11 = (bf16[4,2,24,1024]{3,2,1,0:T(8,128)(2,1)}, bf16[4,2,24,1024]{3,2,1,0:T(8,128)(2,1)S(1)}, u32[]{:S(2)}) copy-start(bf16[4,2,24,1024]{3,2,1,0:T(8,128)(2,1)S(1)} %collective-permute-done.18.refs_3_) | copy-start | bytes 1179652
  169.9 36.0 %collective-permute-start.24 = (bf16[4,2,24,1024]{3,2,1,0:T(8,128)(2,1)S(1)}, bf16[4,2,24,1024]{3,2,1,0:T(8,128)(2,1)S(1)}, u32[]{:S(2)}, u32[]{:S(2)}) collective-permute-start(bf16[4,2,24,1024]{3,2,1,0:T(8,128)(2,1)S(1)} %copy-done.18), channel_id=1, source_target_pairs={{0,24},{8,16},{16,8},{24,0},{1,25},{9,17},{17,9},{25,1},{2,26},{10... | collective-permute-start | bytes 1179656 | tf_op jit(solution)/shard_map/ppermute | solution.py:445
  171.3 25.9 %copy-start.2 = (bf16[4,2,24,1024]{3,2,1,0:T(8,128)(2,1)}, bf16[4,2,24,1024]{3,2,1,0:T(8,128)(2,1)S(1)}, u32[]{:S(2)}) copy-start(bf16[4,2,24,1024]{3,2,1,0:T(8,128)(2,1)S(1)} %collective-permute-done.22.refs_1_) | copy-start | bytes 1179652
  171.3 34.6 %collective-permute-start.23 = (bf16[4,2,24,1024]{3,2,1,0:T(8,128)(2,1)S(1)}, bf16[4,2,24,1024]{3,2,1,0:T(8,128)(2,1)S(1)}, u32[]{:S(2)}, u32[]{:S(2)}) collective-permute-start(bf16[4,2,24,1024]{3,2,1,0:T(8,128)(2,1)S(1)} %copy-done.19), channel_id=1, source_target_pairs={{0,16},{8,24},{16,0},{24,8},{1,17},{9,25},{17,1},{25,9},{2,18},{10... | collective-permute-start | bytes 1179656 | tf_op jit(solution)/shard_map/ppermute | solution.py:445
  172.3 18.9 %copy-start.13 = (bf16[4,2,24,1024]{3,2,1,0:T(8,128)(2,1)}, bf16[4,2,24,1024]{3,2,1,0:T(8,128)(2,1)S(1)}, u32[]{:S(2)}) copy-start(bf16[4,2,24,1024]{3,2,1,0:T(8,128)(2,1)S(1)} %collective-permute-done.19.refs_5_) | copy-start | bytes 1179652
  172.3 33.5 %collective-permute-start.25 = (bf16[4,2,24,1024]{3,2,1,0:T(8,128)(2,1)}, bf16[4,2,24,1024]{3,2,1,0:T(8,128)(2,1)S(1)}, u32[]{:S(2)}, u32[]{:S(2)}) collective-permute-start(bf16[4,2,24,1024]{3,2,1,0:T(8,128)(2,1)} %get-tuple-element.78), channel_id=1, source_target_pairs={{0,8},{8,0},{16,24},{24,16},{1,9},{9,1},{17,25},{25,17},{2,10},{10... | collective-permute-start | bytes 1179656 | tf_op jit(solution)/shard_map/ppermute | solution.py:445
  180.6 33.7 %collective-permute-start.26 = (bf16[4,2,24,1024]{3,2,1,0:T(8,128)(2,1)}, bf16[4,2,24,1024]{3,2,1,0:T(8,128)(2,1)S(1)}, u32[]{:S(2)}, u32[]{:S(2)}) collective-permute-start(bf16[4,2,24,1024]{3,2,1,0:T(8,128)(2,1)} %get-tuple-element.79), channel_id=1, source_target_pairs={{0,16},{8,24},{16,0},{24,8},{1,17},{9,25},{17,1},{25,9},{2,18},{10... | collective-permute-start | bytes 1179656 | tf_op jit(solution)/shard_map/ppermute | solution.py:445
  187.7 33.3 %collective-permute-start.27 = (bf16[4,2,24,1024]{3,2,1,0:T(8,128)(2,1)}, bf16[4,2,24,1024]{3,2,1,0:T(8,128)(2,1)S(1)}, u32[]{:S(2)}, u32[]{:S(2)}) collective-permute-start(bf16[4,2,24,1024]{3,2,1,0:T(8,128)(2,1)} %get-tuple-element.63._), channel_id=1, source_target_pairs={{0,24},{8,16},{16,8},{24,0},{1,25},{9,17},{17,9},{25,1},{2,26},{10... | collective-permute-start | bytes 1179656 | tf_op jit(solution)/shard_map/ppermute | solution.py:445
  205.9 15.2 %copy-start.4 = (bf16[4,2,24,1024]{3,2,1,0:T(8,128)(2,1)}, bf16[4,2,24,1024]{3,2,1,0:T(8,128)(2,1)S(1)}, u32[]{:S(2)}) copy-start(bf16[4,2,24,1024]{3,2,1,0:T(8,128)(2,1)S(1)} %collective-permute-done.23.refs_2_) | copy-start | bytes 1179652
  205.9 15.1 %copy-start.3 = (bf16[4,2,24,1024]{3,2,1,0:T(8,128)(2,1)}, bf16[4,2,24,1024]{3,2,1,0:T(8,128)(2,1)S(1)}, u32[]{:S(2)}) copy-start(bf16[4,2,24,1024]{3,2,1,0:T(8,128)(2,1)S(1)} %collective-permute-done.24.refs_3_) | copy-start | bytes 1179652
  205.9 15.1 %copy-start.5 = (bf16[4,2,24,1024]{3,2,1,0:T(8,128)(2,1)}, bf16[4,2,24,1024]{3,2,1,0:T(8,128)(2,1)S(1)}, u32[]{:S(2)}) copy-start(bf16[4,2,24,1024]{3,2,1,0:T(8,128)(2,1)S(1)} %collective-permute-done.25.refs_5_) | copy-start | bytes 1179652
  (17 other events, 70.0 us)

commit v3 on v0

v3 whole, which is shorter than its diff:
```python
import functools
import math

import jax
import jax.numpy as jnp
from jax import lax
from jax.experimental import pallas as pl
from jax.experimental.pallas import tpu as pltpu
from jax.sharding import PartitionSpec as P

HALO = 2
TILE = 8
LANES = 128
MIB = 1 << 20
VMEM_LIMIT = 60 * MIB
COST = pl.CostEstimate(flops=1, bytes_accessed=1, transcendentals=0)


def direction_factors(dirs):
    angle = (jnp.arange(dirs, dtype=jnp.float32) + 0.5) * (2.0 * math.pi / dirs)
    return (0.5 * jnp.abs(jnp.cos(angle)), 0.5 * jnp.abs(jnp.sin(angle)))


def chunk_row(owner, j, half, late):
    return jnp.where((owner == 0) != late, half + j, j)


UNREAD = pl.BlockSpec(memory_space=pl.ANY)


def lane_tiles(cols):
    return [pl.ds(c * LANES, LANES) for c in range(cols // LANES)]


def coefficients(cel_ref, base_ref, trn_ref, here, cg, turn, sea):
    sea = sea.astype(jnp.float32)
    celerity = 0.1 + 0.8 * cg.astype(jnp.float32) / 7.0
    turning = 0.3 * jnp.abs(turn.astype(jnp.float32) - 3.5) / 3.5
    cel_ref[here, :] = celerity * sea
    base_ref[here, :] = (1.0 - turning) * sea
    trn_ref[here, :] = turning * sea


def sweep(dirs, tiles, lanes, sign_ref, along_ref, coefs, turns_up, load, store):
    cel_ref, base_ref, trn_ref = coefs
    row = lax.broadcasted_iota(jnp.int32, (TILE, LANES), 0)
    lane = lax.broadcasted_iota(jnp.int32, (TILE, LANES), 1)
    nothing = jnp.zeros((TILE, LANES), jnp.float32)

    def span(t):
        return pl.ds(t * TILE, TILE)

    def pair(i, carry):
        ds = (2 * i, 2 * i + 1)
        around = (jnp.where(i == 0, dirs - 1, 2 * i - 1), jnp.where(i == dirs // 2 - 1, 0, 2 * i + 2))
        right = [sign_ref[0, d] > 0 for d in ds]
        high = [sign_ref[1, d] > 0 for d in ds]
        ax = [along_ref[0, d] for d in ds]
        ay = [along_ref[1, d] for d in ds]
        shift_x = [jnp.where(r, LANES - 1, 1) for r in right]
        shift_y = [jnp.where(h, TILE - 1, 1) for h in high]
        at_right = [lane == jnp.where(r, LANES - 1, LANES) for r in right]
        at_left = [lane == jnp.where(r, LANES, 0) for r in right]
        at_high = [row == jnp.where(h, TILE - 1, TILE) for h in high]
        at_low = [row == jnp.where(h, TILE, 0) for h in high]

        def column(c):
            flow = [[None] * tiles, [None] * tiles]
            for t in range(tiles):
                cel = cel_ref[span(t), lanes[c]]
                for n in range(2):
                    flow[n][t] = cel * load(t, ds[n], lanes[c])
            return flow, [[pltpu.roll(f, shift_x[n], 1) for f in flow[n]] for n in range(2)]

        before = [[nothing] * tiles] * 2
        flow, moved = column(0)
        for c in range(len(lanes)):
            beyond = [[nothing] * tiles] * 2
            if c + 1 < len(lanes):
                later = column(c + 1)
                beyond = later[1]
            lifted = [[pltpu.roll(f, shift_y[n], 0) for f in flow[n]] for n in range(2)]
            for t in range(tiles):
                up = turns_up(t, c)
                base = base_ref[span(t), lanes[c]]
                trn = trn_ref[span(t), lanes[c]]
                here = [load(t, d, lanes[c]) for d in ds]
                aside = [load(t, d, lanes[c]) for d in around]
                turned = (jnp.where(up, here[1], aside[0]), jnp.where(up, aside[1], here[0]))
                for n in range(2):
                    above = lifted[n][t + 1] if t + 1 < tiles else nothing
                    below = lifted[n][t - 1] if t > 0 else nothing
                    flow_x = jnp.where(at_right[n], beyond[n][t], jnp.where(at_left[n], before[n][t], moved[n][t]))
                    flow_y = jnp.where(at_high[n], above, jnp.where(at_low[n], below, lifted[n][t]))
                    total = base * here[n] + ax[n] * (flow_x - flow[n][t])
                    total = total + ay[n] * (flow_y - flow[n][t]) + trn * turned[n]
                    store(t, ds[n], c, total)
            if c + 1 < len(lanes):
                before = moved
                flow, moved = later
        return carry

    lax.fori_loop(0, dirs // 2, pair, 0, unroll=1 if tiles > 1 else 3)


def emit(own, parts, local, chunks, dirs, lanes, swap_ref, send_refs):
    half = local // 2
    for i, late in enumerate(chunks):
        for k in range(parts):
            owner = own ^ k
            for j in range(half):
                start = (owner * local + chunk_row(owner, j, half, late)) * (dirs + 1)
                for c, here in enumerate(lanes):
                    piece = swap_ref[c, pl.ds(start, dirs), :]
                    send_refs[i * parts + k][j, 0, :, here] = piece.astype(jnp.bfloat16)


def inner_kernel(parts, local, chunks, into, own_ref, sign_ref, along_ref, _, forcing_ref, cg_ref, turn_ref, mask_ref, *refs):
    refs = refs[1:] if into else refs
    home_ref = refs[0]
    sends = parts * len(chunks)
    cel_ref, base_ref, trn_ref, first_ref, swap_ref = refs[sends + 1 :]
    dirs, rows, _ = forcing_ref.shape[1:]
    pitch = dirs + 1
    lanes = lane_tiles(forcing_ref.shape[3])
    tiles = rows // TILE

    def span(t):
        return pl.ds(t * TILE, TILE)

    for t in range(tiles):
        levels = (cg_ref[0, span(t), :], turn_ref[0, span(t), :], mask_ref[span(t), :])
        coefficients(cel_ref, base_ref, trn_ref, span(t), *levels)

    def turns_up(t, c):
        return turn_ref[0, span(t), lanes[c]] >= 4

    def store_first(t, d, c, value):
        first_ref[d, span(t), lanes[c]] = value

    def store_last(t, d, c, value):
        home_ref[0, d, span(t), lanes[c]] = value
        if chunks:
            swap_ref[c, pl.ds(t * TILE * pitch + d, TILE, stride=pitch), :] = value

    step = functools.partial(sweep, dirs, tiles, lanes, sign_ref, along_ref, (cel_ref, base_ref, trn_ref), turns_up)
    step(lambda t, d, here: forcing_ref[0, d, span(t), here], store_first)
    step(lambda t, d, here: first_ref[d, span(t), here], store_last)
    emit(own_ref[0], parts, local, chunks, dirs, lanes, swap_ref, refs[1 : sends + 1])


def inner(own, signs, along, after, forcing, cg, turn, mask, into, parts, chunks, group):
    freqs, dirs, rows, cols = forcing.shape
    begin, many = group
    local = rows // parts
    half = local // 2
    smem = pl.BlockSpec(memory_space=pltpu.SMEM)
    levels = pl.BlockSpec((1, rows, cols), lambda f: (begin + f, 0, 0))
    block = pl.BlockSpec((1, dirs, rows, cols), lambda f: (begin + f, 0, 0, 0))
    coefs = pltpu.VMEM((rows, cols), jnp.float32)
    sends = parts * len(chunks)
    outs = pl.pallas_call(
        functools.partial(inner_kernel, parts, local, chunks, into is not None),
        grid=(many,),
        in_specs=[smem, smem, smem, UNREAD, block, levels, levels, pl.BlockSpec((rows, cols), lambda f: (0, 0))]
        + ([] if into is None else [UNREAD]),
        out_specs=[block] + [pl.BlockSpec((half, 1, dirs, cols), lambda f: (0, f, 0, 0))] * sends,
        out_shape=[jax.ShapeDtypeStruct(forcing.shape, jnp.float32)]
        + [jax.ShapeDtypeStruct((half, many, dirs, cols), jnp.bfloat16)] * sends,
        scratch_shapes=[
            coefs,
            coefs,
            coefs,
            pltpu.VMEM((dirs, rows, cols), jnp.float32),
            pltpu.VMEM((cols // LANES, rows * (dirs + 1), LANES), jnp.float32),
        ],
        input_output_aliases={} if into is None else {8: 0},
        compiler_params=pltpu.CompilerParams(vmem_limit_bytes=VMEM_LIMIT),
        cost_estimate=COST,
    )(own, signs, along, after, forcing, cg, turn, mask, *([] if into is None else [into]))
    return outs[0], list(outs[1:])


def outer_kernel(parts, local, chunks, *refs):
    own_ref, sign_ref, along_ref, _, above_ref, below_ref, above_lev_ref, below_lev_ref = refs[:8]
    cg_ref, turn_ref, mask_ref, home_ref, share_ref = refs[8:13]
    sends = parts * len(chunks)
    send_refs = refs[13 : 13 + sends]
    cel_ref, base_ref, trn_ref, lev_ref, near_ref, first_ref, side_ref, edge_ref, swap_ref = refs[13 + sends :]
    dirs, rows, cols = home_ref.shape[1:]
    pitch = dirs + 1
    lanes = lane_tiles(cols)
    tiles = rows // TILE
    f, freqs = pl.program_id(0), pl.num_programs(0)

    for i, (ref, r) in enumerate(((above_lev_ref, 0), (above_lev_ref, 1), (below_lev_ref, 0), (below_lev_ref, 1))):
        lev_ref[pl.ds(i * dirs, dirs), :] = ref[r, 0].astype(jnp.float32)
    kinds = ((f, cg_ref[0]), (freqs + f, turn_ref[0]), (2 * freqs, mask_ref[...]))
    for q, (place, mine) in enumerate(kinds):
        for i in range(HALO):
            near_ref[q * TILE + i : q * TILE + i + 1, :] = lev_ref[pl.ds(i * dirs + place, 1), :]
            low = q * TILE + TILE - HALO + i
            near_ref[low : low + 1, :] = lev_ref[pl.ds((HALO + i) * dirs + place, 1), :]
        near_ref[q * TILE + HALO : q * TILE + 2 * HALO, :] = mine[:HALO].astype(jnp.float32)
        near_ref[q * TILE + 2 * HALO : q * TILE + 3 * HALO, :] = mine[rows - HALO :].astype(jnp.float32)
    near = [near_ref[pl.ds(q * TILE, TILE), :] for q in range(3)]
    coefficients(cel_ref, base_ref, trn_ref, pl.ds(0, TILE), *near)

    edge_ref[...] = jnp.zeros_like(edge_ref)
    for r in range(HALO):
        for c, here in enumerate(lanes):
            edge_ref[c, pl.ds(r * pitch, dirs), :] = above_ref[r, 0, :, here].astype(jnp.float32)
            edge_ref[c, pl.ds((TILE - HALO + r) * pitch, dirs), :] = below_ref[r, 0, :, here].astype(jnp.float32)

    def gather(d, carry):
        for c, here in enumerate(lanes):
            side_ref[d, :, here] = edge_ref[c, pl.ds(d, TILE, stride=pitch), :]
        return carry

    lax.fori_loop(0, dirs, gather, 0, unroll=4)

    def turns_up(t, c):
        return near_ref[pl.ds(TILE, TILE), lanes[c]] >= 4.0

    def store_first(t, d, c, value):
        first_ref[d, :, lanes[c]] = value

    def store_last(t, d, c, value):
        share_ref[0, d, :, lanes[c]] = value

    step = functools.partial(sweep, dirs, 1, lanes, sign_ref, along_ref, (cel_ref, base_ref, trn_ref), turns_up)
    step(lambda t, d, here: side_ref[d, :, here], store_first)
    step(lambda t, d, here: first_ref[d, :, here], store_last)

    def whole(d, carry):
        for t in range(tiles):
            for c, here in enumerate(lanes):
                value = with_share(home_ref[0, d, pl.ds(t * TILE, TILE), here], share_ref, d, here, t, tiles)
                swap_ref[c, pl.ds(t * TILE * pitch + d, TILE, stride=pitch), :] = value
        return carry

    lax.fori_loop(0, dirs, whole, 0, unroll=2)
    emit(own_ref[0], parts, local, chunks, dirs, lanes, swap_ref, send_refs)


def with_share(value, share_ref, d, here, t, tiles):
    row = lax.broadcasted_iota(jnp.int32, value.shape, 0)
    if t == 0:
        value = value + jnp.where(row < HALO, pltpu.roll(share_ref[0, d, :, here], TILE - HALO, 0), 0.0)
    if t == tiles - 1:
        value = value + jnp.where(row >= TILE - HALO, pltpu.roll(share_ref[0, d, :, here], HALO, 0), 0.0)
    return value


def outer(own, signs, along, after, above, below, cg, turn, mask, home, parts, chunks):
    freqs, dirs, rows, cols = home.shape
    local = rows // parts
    half = local // 2
    smem = pl.BlockSpec(memory_space=pltpu.SMEM)
    edge = pl.BlockSpec((HALO, 1, dirs, cols), lambda f: (0, f, 0, 0))
    last = pl.BlockSpec((HALO, 1, dirs, cols), lambda f: (0, freqs, 0, 0))
    levels = pl.BlockSpec((1, rows, cols), lambda f: (f, 0, 0))
    sends = parts * len(chunks)
    tile = pltpu.VMEM((TILE, cols), jnp.float32)
    outs = pl.pallas_call(
        functools.partial(outer_kernel, parts, local, chunks),
        grid=(freqs,),
        in_specs=[smem, smem, smem, UNREAD, edge, edge, last, last, levels, levels]
        + [pl.BlockSpec((rows, cols), lambda f: (0, 0)), pl.BlockSpec((1, dirs, rows, cols), lambda f: (f, 0, 0, 0))],
        out_specs=[pl.BlockSpec((1, dirs, TILE, cols), lambda f: (f, 0, 0, 0))]
        + [pl.BlockSpec((half, 1, dirs, cols), lambda f: (0, f, 0, 0))] * sends,
        out_shape=[jax.ShapeDtypeStruct((freqs, dirs, TILE, cols), jnp.float32)]
        + [jax.ShapeDtypeStruct((half, freqs, dirs, cols), jnp.bfloat16)] * sends,
        scratch_shapes=[
            tile,
            tile,
            tile,
            pltpu.VMEM((2 * HALO * dirs, cols), jnp.float32),
            pltpu.VMEM((3 * TILE, cols), jnp.float32),
            pltpu.VMEM((dirs, TILE, cols), jnp.float32),
            pltpu.VMEM((dirs, TILE, cols), jnp.float32),
            pltpu.VMEM((cols // LANES, TILE * (dirs + 1), LANES), jnp.float32),
            pltpu.VMEM((cols // LANES, rows * (dirs + 1), LANES), jnp.float32),
        ],
        compiler_params=pltpu.CompilerParams(vmem_limit_bytes=VMEM_LIMIT),
        cost_estimate=COST,
    )(own, signs, along, after, above, below, above, below, cg, turn, mask, home)
    return outs[0], [list(outs[1 + i * parts : 1 + (i + 1) * parts]) for i in range(len(chunks))]


def edges_kernel(freqs, _, *refs):
    swap_ref, lev_ref = refs[-2:]
    dirs, _, cols = refs[0].shape[1:]
    pitch = dirs + 1
    lanes = lane_tiles(cols)
    f = pl.program_id(0)

    for side, low in ((0, 0), (1, TILE - HALO)):
        forcing_ref, cg_ref, turn_ref, mask_ref = refs[4 * side : 4 * side + 4]
        out_ref = refs[8 + side]

        @pl.when(f < freqs)
        def _(forcing_ref=forcing_ref, out_ref=out_ref, low=low):
            def body(d, carry):
                for c, here in enumerate(lanes):
                    swap_ref[c, pl.ds(d, TILE, stride=pitch), :] = forcing_ref[0, d, :, here]
                return carry

            lax.fori_loop(0, dirs, body, 0, unroll=2)
            for r in range(HALO):
                for c, here in enumerate(lanes):
                    out_ref[r, 0, :, here] = swap_ref[c, pl.ds((low + r) * pitch, dirs), :].astype(jnp.bfloat16)

        @pl.when(f == freqs)
        def _(cg_ref=cg_ref, turn_ref=turn_ref, mask_ref=mask_ref, out_ref=out_ref, low=low):
            lev_ref[...] = jnp.zeros_like(lev_ref)
            for r in range(low, low + HALO):
                for n in range(freqs):
                    lev_ref[n : n + 1, :] = cg_ref[n, r : r + 1, :].astype(jnp.float32)
                    lev_ref[freqs + n : freqs + n + 1, :] = turn_ref[n, r : r + 1, :].astype(jnp.float32)
                lev_ref[2 * freqs : 2 * freqs + 1, :] = mask_ref[r : r + 1, :].astype(jnp.float32)
                out_ref[r - low, 0] = lev_ref[...].astype(jnp.bfloat16)


def edges(after, forcing, cg, turn, mask):
    freqs, dirs, rows, cols = forcing.shape
    assert 2 * freqs + 1 <= dirs
    out = pl.BlockSpec((HALO, 1, dirs, cols), lambda f: (0, f, 0, 0))
    shape = jax.ShapeDtypeStruct((HALO, freqs + 1, dirs, cols), jnp.bfloat16)
    in_specs = [UNREAD]
    for t in (0, rows // TILE - 1):
        in_specs += [
            pl.BlockSpec((1, dirs, TILE, cols), lambda f, t=t: (jnp.minimum(f, freqs - 1), 0, t, 0)),
            pl.BlockSpec((freqs, TILE, cols), lambda f, t=t: (0, t, 0)),
            pl.BlockSpec((freqs, TILE, cols), lambda f, t=t: (0, t, 0)),
            pl.BlockSpec((TILE, cols), lambda f, t=t: (t, 0)),
        ]
    return pl.pallas_call(
        functools.partial(edges_kernel, freqs),
        grid=(freqs + 1,),
        in_specs=in_specs,
        out_specs=[out, out],
        out_shape=[shape, shape],
        scratch_shapes=[
            pltpu.VMEM((cols // LANES, TILE * (dirs + 1), LANES), jnp.float32),
            pltpu.VMEM((dirs, cols), jnp.float32),
        ],
        compiler_params=pltpu.CompilerParams(vmem_limit_bytes=VMEM_LIMIT),
        cost_estimate=COST,
    )(after, *(2 * [forcing, cg, turn, mask]))


def by_row_kernel(_, state_ref, out_ref, swap_ref):
    deep, local, _ = state_ref.shape
    pitch = deep + 1

    def body(d, carry):
        swap_ref[pl.ds(d, local, stride=pitch), :] = state_ref[d].astype(jnp.float32)
        return carry

    lax.fori_loop(0, deep, body, 0, unroll=16)
    for r in range(local):
        out_ref[r] = swap_ref[pl.ds(r * pitch, deep), :].astype(jnp.bfloat16)


def by_row(after, state):
    deep, local, cols = state.shape
    return pl.pallas_call(
        by_row_kernel,
        grid=(cols // LANES,),
        in_specs=[UNREAD, pl.BlockSpec((deep, local, LANES), lambda c: (0, 0, c))],
        out_specs=pl.BlockSpec((local, deep, LANES), lambda c: (0, 0, c)),
        out_shape=jax.ShapeDtypeStruct((local, deep, cols), jnp.bfloat16),
        scratch_shapes=[pltpu.VMEM((local * (deep + 1), LANES), jnp.float32)],
        compiler_params=pltpu.CompilerParams(vmem_limit_bytes=VMEM_LIMIT),
        cost_estimate=COST,
    )(after, state)


def turned_kernel(_, w_in_ref, w_out_ref, in_t_ref, out_t_ref):
    in_t_ref[...] = w_in_ref[...].T
    out_t_ref[...] = w_out_ref[...].T


def turned(after, w_in, w_out):
    hidden, total = w_in.shape
    step = 512
    tall = pl.BlockSpec((step, total), lambda h: (h, 0))
    wide = pl.BlockSpec((total, step), lambda h: (0, h))
    return pl.pallas_call(
        turned_kernel,
        grid=(hidden // step,),
        in_specs=[UNREAD, tall, wide],
        out_specs=[wide, tall],
        out_shape=[jax.ShapeDtypeStruct((total, hidden), w_in.dtype), jax.ShapeDtypeStruct((hidden, total), w_in.dtype)],
        compiler_params=pltpu.CompilerParams(vmem_limit_bytes=VMEM_LIMIT),
        cost_estimate=COST,
    )(after, w_in, w_out)


def source_kernel(parts, got, sent, dirs, step, own_ref, _, state_ref, wind_ref, w_in_ref, out_t_ref, in_t_ref, weight_ref, *refs):
    cell_refs = refs[: parts * len(got)]
    grad_ref = refs[parts * len(got)]
    back_refs = refs[parts * len(got) + 1 : -3]
    cell_ref, weighted_ref, grown_ref = refs[-3:]
    freqs = sum(many for _, many in got)
    hidden, width = weighted_ref.shape
    own = own_ref[0]

    def place(k, group):
        begin, many = group
        return pl.ds(pl.multiple_of(((own ^ k) * freqs + begin) * dirs, TILE), many * dirs)

    for g, group in enumerate(got):
        for k in range(parts):
            piece = cell_refs[g * parts + k][0].astype(jnp.float32)
            cell_ref[place(k, group), :] = piece.reshape(group[1] * dirs, width)
    cell = cell_ref[...].astype(jnp.bfloat16)
    state = state_ref[0]
    wind = wind_ref[0]
    grad = jnp.zeros((TILE, width), jnp.float32)
    for h in range(0, hidden, step):
        some = pl.ds(h, step)
        weight = weight_ref[some, :]
        forward = jnp.dot(w_in_ref[some, :], state, preferred_element_type=jnp.float32) + weight * wind
        squash = jnp.tanh(forward)
        pulled = jnp.dot(out_t_ref[some, :], cell, preferred_element_type=jnp.float32)
        weighted = (1.0 - squash * squash) * pulled
        weighted_ref[some, :] = weighted.astype(jnp.bfloat16)
        grad = grad + jnp.sum((weight * weighted).reshape(step // TILE, TILE, width), axis=0)
    grad_ref[0] = jnp.sum(grad, axis=0, keepdims=True)
    grown_ref[...] = jnp.dot(in_t_ref[...], weighted_ref[...], preferred_element_type=jnp.float32)
    for g, group in enumerate(sent):
        for k in range(parts):
            grown = grown_ref[place(k, group), :].reshape(group[1], dirs, width)
            back_refs[g * parts + k][0] = grown.astype(jnp.bfloat16)


def source_term(own, after, state, wind, w_in, out_t, in_t, weight, cells, got, sent, rows, late):
    parts = len(cells[0])
    half, _, dirs, cols = cells[0][0].shape
    first, count = rows
    hidden, total = w_in.shape
    width = min(cols, 512)

    def row_of(j, own_ref):
        return chunk_row(own_ref[0], first + j, half, late)

    def whole(shape):
        return pl.BlockSpec(shape, lambda j, c, own_ref: (0, 0))

    cell_specs = [
        pl.BlockSpec((1, many, dirs, width), lambda j, c, own_ref: (first + j, 0, 0, c)) for _, many in got for _ in range(parts)
    ]
    back_specs = [pl.BlockSpec((1, many, dirs, width), lambda j, c, own_ref: (j, 0, 0, c)) for _, many in sent for _ in range(parts)]
    outs = pl.pallas_call(
        functools.partial(source_kernel, parts, got, sent, dirs, 256),
        grid_spec=pltpu.PrefetchScalarGridSpec(
            num_scalar_prefetch=1,
            grid=(count, cols // width),
            in_specs=[
                UNREAD,
                pl.BlockSpec((1, total, width), lambda j, c, own_ref: (row_of(j, own_ref), 0, c)),
                pl.BlockSpec((1, 1, width), lambda j, c, own_ref: (row_of(j, own_ref), 0, c)),
                whole((hidden, total)),
                whole((hidden, total)),
                whole((total, hidden)),
                whole((hidden, 1)),
            ]
            + cell_specs,
            out_specs=[pl.BlockSpec((1, 1, width), lambda j, c, own_ref: (j, 0, c))] + back_specs,
            scratch_shapes=[
                pltpu.VMEM((total, width), jnp.float32),
                pltpu.VMEM((hidden, width), jnp.bfloat16),
                pltpu.VMEM((total, width), jnp.float32),
            ],
        ),
        out_shape=[jax.ShapeDtypeStruct((count, 1, cols), jnp.float32)]
        + [jax.ShapeDtypeStruct((count, many, dirs, cols), jnp.bfloat16) for _, many in sent for _ in range(parts)],
        compiler_params=pltpu.CompilerParams(vmem_limit_bytes=VMEM_LIMIT),
        cost_estimate=COST,
    )(own, after, state, wind, w_in, out_t, in_t, weight, *[cell for group in cells for cell in group])
    return outs[0].reshape(count, cols), [list(outs[1 + g * parts : 1 + (g + 1) * parts]) for g in range(len(sent))]


def join_kernel(parts, spans, own_ref, _, home_ref, share_ref, *refs):
    out_ref, swap_ref = refs[-2:]
    dirs, rows, cols = home_ref.shape[1:]
    pitch = dirs + 1
    local = rows // parts
    half = local // 2
    own = own_ref[0]
    lanes = lane_tiles(cols)
    tiles = rows // TILE
    for i, (first, count, late) in enumerate(spans):
        for k in range(parts):
            owner = own ^ k
            for j in range(count):
                start = (owner * local + chunk_row(owner, first + j, half, late)) * pitch
                for c, here in enumerate(lanes):
                    swap_ref[c, pl.ds(start, dirs), :] = refs[i * parts + k][j, 0, :, here].astype(jnp.float32)

    def body(d, carry):
        for t in range(tiles):
            for c, here in enumerate(lanes):
                grown = swap_ref[c, pl.ds(t * TILE * pitch + d, TILE, stride=pitch), :]
                value = with_share(home_ref[0, d, pl.ds(t * TILE, TILE), here], share_ref, d, here, t, tiles)
                out_ref[0, d, pl.ds(t * TILE, TILE), here] = value + grown
        return carry

    lax.fori_loop(0, dirs, body, 0, unroll=2)


def join(own, into, home, share, early, late, rows_of, group):
    begin, many = group
    parts = len(late)
    _, dirs, rows, cols = home.shape
    half = late[0].shape[0]
    spans = [(*span, False) for span in rows_of] + [(0, half, True)]
    block = pl.BlockSpec((1, dirs, rows, cols), lambda f: (begin + f, 0, 0, 0))
    specs = [
        pl.BlockSpec((count, 1, dirs, cols), lambda f: (0, begin + f, 0, 0)) for _, count in rows_of for _ in range(parts)
    ] + [pl.BlockSpec((half, 1, dirs, cols), lambda f: (0, f, 0, 0))] * parts
    return pl.pallas_call(
        functools.partial(join_kernel, parts, spans),
        grid=(many,),
        in_specs=[pl.BlockSpec(memory_space=pltpu.SMEM), UNREAD, block]
        + [pl.BlockSpec((1, dirs, TILE, cols), lambda f: (begin + f, 0, 0, 0))]
        + specs,
        out_specs=block,
        out_shape=jax.ShapeDtypeStruct(home.shape, jnp.float32),
        scratch_shapes=[pltpu.VMEM((cols // LANES, rows * (dirs + 1), LANES), jnp.float32)],
        input_output_aliases={} if begin == 0 else {1: 0},
        compiler_params=pltpu.CompilerParams(vmem_limit_bytes=VMEM_LIMIT),
        cost_estimate=COST,
    )(own, into, home, share, *[piece for pieces in early for piece in pieces], *late)


def swapped(pieces):
    parts = len(pieces)
    moved = {k: lax.ppermute(pieces[k], "comp", [(i, i ^ k) for i in range(parts)]) for k in range(parts - 1, 0, -1)}
    return [pieces[0]] + [moved[k] for k in range(1, parts)]


def across(low, high):
    count = lax.axis_size("space")
    up = [(i, i + 1) for i in range(count - 1)]
    down = [(i + 1, i) for i in range(count - 1)]
    return lax.ppermute(high, "space", up), lax.ppermute(low, "space", down)


def halves(count):
    spans, begin = [], 0
    while begin < count:
        many = max(1, (count - begin) // 2)
        spans.append((begin, many))
        begin += many
    return spans


def shards(
    adjoint_forcing,
    forward_state,
    wind_speed,
    cg_index,
    turn_index,
    sea_mask,
    dir_sign,
    w_in,
    w_out,
    wind_weight,
):
    parts = lax.axis_size("comp")
    own_place = lax.axis_index("comp")
    own = own_place.astype(jnp.int32).reshape(1)
    dirs = dir_sign.shape[1]
    comps, rows, cols = adjoint_forcing.shape
    freqs = comps // dirs
    half = rows // parts // 2
    along = jnp.stack(direction_factors(dirs))
    forcing = adjoint_forcing.reshape(freqs, dirs, rows, cols)
    weight = wind_weight[:, None]
    wind = wind_speed[:, None]
    everything = [(0, freqs)]
    many = freqs // 2 if freqs % 2 == 0 else freqs
    groups = [(begin, many) for begin in range(0, freqs, many)]
    sent = halves(freqs)
    rows_of = [(0, half // 2), (half // 2, half // 2)] if half % 2 == 0 else [(0, half)]
    levels = (cg_index, turn_index, sea_mask)
    clear = half >= HALO

    early, home, after = [], None, wind
    for g, group in enumerate(groups):
        into = home
        home, pieces = inner(own, dir_sign, along, after, forcing, *levels, into, parts, (False,) if clear else (), group)
        after = home
        if clear:
            early.append(swapped(pieces))
            after = pieces[-1]
        if g == 0:
            low, high = edges(after, forcing, *levels)
            above, below = across(low, high)
            after = high
    share, pieces = outer(own, dir_sign, along, after, above, below, *levels, home, parts, (True,) if clear else (False, True))
    if not clear:
        early.append(swapped(pieces[0]))
    late = swapped(pieces[-1])
    state = by_row(share, forward_state)
    in_t, out_t = turned(state, w_in, w_out)
    term = functools.partial(source_term, own)
    fixed = (state, wind, w_in, out_t, in_t, weight)
    after, early_grads, early_back = in_t, [], []
    for span in rows_of:
        grad, [back] = term(after, *fixed, early, groups if clear else everything, everything, span, False)
        after = grad
        early_grads.append(grad)
        early_back.append(swapped(back))
    late_grad, late_back = term(after, *fixed, [late], everything, sent, (0, half), True)
    start = late_grad
    late_back = [swapped(pieces) for pieces in late_back]
    for group, back in zip(sent, late_back, strict=True):
        start = join(own, start, home, share, early_back, back, rows_of, group)
    early_grad = jnp.concatenate(early_grads, axis=0)
    first = jnp.where(own_place == 0, late_grad, early_grad)
    second = jnp.where(own_place == 0, early_grad, late_grad)
    return (start.reshape(comps, rows, cols), jnp.concatenate([first, second], axis=0))


def solution(mesh):
    placed = (
        P("comp", "space", None),
        P(None, ("space", "comp"), None),
        P(("space", "comp"), None),
        P("comp", "space", None),
        P("comp", "space", None),
        P("space", None),
        P(),
        P(),
        P(),
        P(),
    )
    return jax.shard_map(
        shards,
        mesh=mesh,
        in_specs=placed,
        out_specs=(P("comp", "space", None), P(("space", "comp"), None)),
        check_vma=False,
    )
```

time: 640 us -> 185 us (0.29)
  waiting for transfers between devices: 263 us -> 18.6 us
  local copies, waits for them, and re-layouts: 146 us -> 8.71 us
  Pallas kernels: 0 us -> 127 us
  other arithmetic: 121 us -> 1.97 us
  matrix products: 77.5 us -> 0 us
    all_to_all x2 -> x0, waiting for transfers between devices: 263 us -> none  [the longest x1 137 us: shards(): lax.all_to_all(cell_start, 'comp', split_axis=0, concat_axis=1, tiled=True)]
    pallas_call x0 -> x12, Pallas kernels: none -> 127 us  [the longest x3 53.3 us: source_term(): pl.pallas_call(functools.partial(source_kernel, parts, got, sent, dirs, 2...]
    dot_general x3 -> x0, matrix products: 77.5 us -> none  [the longest x1 33 us: source_adjoint(): jnp.dot(w_in, cell_state, preferred_element_type=jnp.float32)]
    mul x3 -> x0, other arithmetic: 67.6 us -> none  [the longest x2 56.1 us: adjoint_step(): flux_x = cour_x * masked]
    slice x8 -> x0, local copies, waits for them, and re-layouts: 62.2 us -> none  [the longest x2 38.7 us: adjoint_step(): from_right = jnp.concatenate([flux_x[..., 1:], zero_col], axis=-1)]
    add x3 -> x0, other arithmetic: 51.1 us -> none  [the longest x1 35 us: adjoint_step(): return retained + term_x + term_y + term_t]
    all_to_all x3 -> x0, local copies, waits for them, and re-layouts: 43.1 us -> none  [the longest x2 31 us: shards(): lax.all_to_all(costate, 'comp', split_axis=1, concat_axis=0, tiled=True)]
    ppermute x4 -> x26, waiting for transfers between devices: 0.01 us -> 18.6 us  [the longest x24 16.9 us: swapped(): lax.ppermute(pieces[k], 'comp', [(i, i ^ k) for i in range(parts)])]
  transfers between devices with their start and end apart: 6 -> 26, of which waited for: 2 -> 6; matrix products, arithmetic and copies ran while one was open for 10% -> 3% of each run, Pallas kernels for 0% -> 56%
where the time goes in v3:
time: 185 us; the launch traced here: 184 us
  Pallas kernels  127 us (69%)
  starting transfers between devices  26.5 us (14%)
  waiting for transfers between devices  18.6 us (10%)
  local copies, waits for them, and re-layouts  8.71 us (5%)
  other arithmetic  1.97 us (1%)
    pallas_call x3, Pallas kernels, source_term(): pl.pallas_call(functools.partial(source_kernel, parts, got, sent, dirs, 2...  53.3 us
    pallas_call x2, Pallas kernels, inner(): pl.pallas_call(functools.partial(inner_kernel, parts, local, chunks, into...  28.2 us
    ppermute x24, starting transfers between devices, swapped(): lax.ppermute(pieces[k], 'comp', [(i, i ^ k) for i in range(parts)])  19.7 us
    ppermute x24, waiting for transfers between devices, swapped(): lax.ppermute(pieces[k], 'comp', [(i, i ^ k) for i in range(parts)])  16.9 us
    pallas_call x3, Pallas kernels, join(): pl.pallas_call(functools.partial(join_kernel, parts, spans), grid=(many,)...  16.3 us
    pallas_call x1, Pallas kernels, outer(): pl.pallas_call(functools.partial(outer_kernel, parts, local, chunks), gri...  11.9 us
    pallas_call x1, Pallas kernels, by_row(): pl.pallas_call(by_row_kernel, grid=(cols // LANES,), in_specs=[UNREAD, pl...  8.63 us
    ppermute x2, starting transfers between devices, across(): return (lax.ppermute(high, 'space', up), lax.ppermute(low, 'space', down))  6.78 us
  transfers between devices with their start and end apart: 26, of which 6 were waited for; matrix products, arithmetic and copies ran while one was open for 3% of the time, Pallas kernels for 56%

profile of v3, /device:TPU:0, one launch (start us, length us, event | category | flops | bytes accessed | tf_op | source)
XLA Modules:
  0.0 184.2 jit_solution(229627072111566651)
XLA Ops:
  0.7 1.4 broadcast_in_dim.6._.wind_ref
  2.1 0.6 pad_maximum_fusion.2.along_ref.refs_2_
  2.7 14.1 %shard_map.113 = (f32[4,24,32,1024]{3,2,1,0:T(8,128)}, bf16[4,2,24,1024]{3,2,1,0:T(8,128)(2,1)}, bf16[4,2,24,1024]{3,2,1,0:T(8,128)(2,1)}, bf16[4,2,24,1024]{3,2,1,0:T(8,128)(2,1)}, bf16[4,2,24,1024]{3,2,1,0:T(8,128)(2,1)}) custom-call(s32[1]{0:T(128)} %bitcast.own_ref.refs_0_, s32[2,24]{1,0:T(2,128)} %refs_1_.3, ...), custom_call_target="tpu_custom_call" | custom-call | flops 1 | bytes 1 | tf_op jit(solution)/shard_map/pallas_call | solution.py:162
  16.7 5.1 %shard_map.114 = (bf16[2,5,24,1024]{3,2,1,0:T(8,128)(2,1)}, bf16[2,5,24,1024]{3,2,1,0:T(8,128)(2,1)}) custom-call(bf16[4,2,24,1024]{3,2,1,0:T(8,128)(2,1)} %get-tuple-element.44._, f32[4,24,32,1024]{3,2,1,0:T(8,128)} %bitcast.17, s32[4,32,1024]{2,1,0:T(8,128)} %refs_8_.1, s32[4,32,1024]{2,1,0:T(8,128)} %refs_9_.1, s32[32,1024]{1,0:T(8,128)} %refs_10_.1, ...), custom_call_target="tpu_custom_call" | custom-call | flops 1 | bytes 1 | tf_op jit(solution)/shard_map/pallas_call | solution.py:338
  21.8 1.3 collective-permute-start.1
  23.1 5.5 %collective-permute-start = (bf16[2,5,24,1024]{3,2,1,0:T(8,128)(2,1)}, bf16[2,5,24,1024]{3,2,1,0:T(8,128)(2,1)S(1)}, u32[]{:S(2)}, u32[]{:S(2)}) collective-permute-start(bf16[2,5,24,1024]{3,2,1,0:T(8,128)(2,1)} %get-tuple-element.45._), channel_id=1, source_target_pairs={{0,1},{1,2},{2,3},{3,4},{4,5},{5,6},{6,7},{8,9},{9,10},{10,11},{11... | collective-permute-start | bytes 1474568 | tf_op jit(solution)/shard_map/ppermute | solution.py:549
  28.7 2.1 %collective-permute-start.3 = (bf16[4,2,24,1024]{3,2,1,0:T(8,128)(2,1)S(1)}, bf16[4,2,24,1024]{3,2,1,0:T(8,128)(2,1)S(1)}, u32[]{:S(2)}, u32[]{:S(2)}) collective-permute-start(bf16[4,2,24,1024]{3,2,1,0:T(8,128)(2,1)S(1)} %copy-done.26), channel_id=1, source_target_pairs={{0,16},{8,24},{16,0},{24,8},{1,17},{9,25},{17,1},{25,9},{2,18},{10... | collective-permute-start | bytes 1179656 | tf_op jit(solution)/shard_map/ppermute | solution.py:541
  30.9 14.1 %shard_map.115 = (f32[4,24,32,1024]{3,2,1,0:T(8,128)}, bf16[4,2,24,1024]{3,2,1,0:T(8,128)(2,1)}, bf16[4,2,24,1024]{3,2,1,0:T(8,128)(2,1)}, bf16[4,2,24,1024]{3,2,1,0:T(8,128)(2,1)}, bf16[4,2,24,1024]{3,2,1,0:T(8,128)(2,1)}) custom-call(s32[1]{0:T(128)} %bitcast.own_ref.refs_0_, s32[2,24]{1,0:T(2,128)} %refs_1_.3, ...), custom_call_target="tpu_custom_call", output_to_operand_aliasing={{0}: (8, {})} | custom-call | flops 1 | bytes 1 | tf_op jit(solution)/shard_map/pallas_call | solution.py:162
  45.3 1.9 %collective-permute-start.6 = (bf16[4,2,24,1024]{3,2,1,0:T(8,128)(2,1)}, bf16[4,2,24,1024]{3,2,1,0:T(8,128)(2,1)S(1)}, u32[]{:S(2)}, u32[]{:S(2)}) collective-permute-start(bf16[4,2,24,1024]{3,2,1,0:T(8,128)(2,1)} %get-tuple-element.58), channel_id=1, source_target_pairs={{0,16},{8,24},{16,0},{24,8},{1,17},{9,25},{17,1},{25,9},{2,18},{10... | collective-permute-start | bytes 1179656 | tf_op jit(solution)/shard_map/ppermute | solution.py:541
  47.2 1.7 collective-permute-done.refs_4_.refs_6_
  48.9 1.1 collective-permute-start.7
  50.0 11.9 %shard_map.116 = (f32[4,24,8,1024]{3,2,1,0:T(8,128)}, bf16[4,4,24,1024]{3,2,1,0:T(8,128)(2,1)}, bf16[4,4,24,1024]{3,2,1,0:T(8,128)(2,1)}, bf16[4,4,24,1024]{3,2,1,0:T(8,128)(2,1)}, bf16[4,4,24,1024]{3,2,1,0:T(8,128)(2,1)}) custom-call(s32[1]{0:T(128)} %bitcast.own_ref.refs_0_, s32[2,24]{1,0:T(2,128)} %refs_1_.3, ...), custom_call_target="tpu_custom_call" | custom-call | flops 1 | bytes 1 | tf_op jit(solution)/shard_map/pallas_call | solution.py:265
  61.9 0.6 collective-permute-start.8
  62.5 0.7 collective-permute-start.9
  63.2 1.1 broadcast_in_dim.8.weight_ref
  64.4 8.6 %shard_map.117._.state_ref = bf16[8,384,1024]{2,1,0:T(8,128)(2,1)} custom-call(f32[4,24,8,1024]{3,2,1,0:T(8,128)} %get-tuple-element.50._.share_ref, bf16[384,8,1024]{2,1,0:T(8,128)(2,1)} %state_ref.1), custom_call_target="tpu_custom_call" | custom-call | flops 1 | bytes 1 | tf_op jit(solution)/shard_map/pallas_call | solution.py:368
  73.0 4.2 %shard_map.118 = (bf16[384,1536]{1,0:T(8,128)(2,1)}, bf16[1536,384]{1,0:T(8,128)(2,1)}) custom-call(bf16[8,384,1024]{2,1,0:T(8,128)(2,1)} %shard_map.117._.state_ref, bf16[1536,384]{1,0:T(8,128)(2,1)} %w_in_ref.7, bf16[384,1536]{1,0:T(8,128)(2,1)} %w_out_ref.1), custom_call_target="tpu_custom_call" | custom-call | flops 1 | bytes 1 | tf_op jit(solution)/shard_map/pallas_call | solution.py:390
  77.2 0.8 collective-permute-start.10
  78.0 0.7 copy-done.12
  78.9 14.1 %shard_map.119 = (f32[2,1,1024]{2,1,0:T(1,128)}, bf16[2,4,24,1024]{3,2,1,0:T(8,128)(2,1)}, bf16[2,4,24,1024]{3,2,1,0:T(8,128)(2,1)}, bf16[2,4,24,1024]{3,2,1,0:T(8,128)(2,1)}, bf16[2,4,24,1024]{3,2,1,0:T(8,128)(2,1)}) custom-call(s32[1]{0:T(128)} %bitcast.own_ref.refs_0_, bf16[384,1536]{1,0:T(8,128)(2,1)} %get-tuple-element.51._.in_t_ref, ...), custom_call_target="tpu_custom_call" | custom-call | flops 1 | bytes 1 | tf_op jit(solution)/shard_map/pallas_call | solution.py:456
  92.9 1.3 copy.30
  94.2 14.1 %shard_map.120 = (f32[2,1,1024]{2,1,0:T(1,128)}, bf16[2,4,24,1024]{3,2,1,0:T(8,128)(2,1)}, bf16[2,4,24,1024]{3,2,1,0:T(8,128)(2,1)}, bf16[2,4,24,1024]{3,2,1,0:T(8,128)(2,1)}, bf16[2,4,24,1024]{3,2,1,0:T(8,128)(2,1)}) custom-call(s32[1]{0:T(128)} %bitcast.own_ref.refs_0_, f32[2,1024]{1,0:T(2,128)} %bitcast.21, bf16[8,384,1024]{2,1,0:T(8,128)(2,1)} %shard_map.117._.state_ref, ...), custom_call_target="tpu_custom_call" | custom-call | flops 1 | bytes 1 | tf_op jit(solution)/shard_map/pallas_call | solution.py:456
  108.4 0.8 collective-permute-start.14
  109.1 0.7 collective-permute-start.15
  109.9 0.8 collective-permute-done.14.refs_5_
  110.7 0.7 collective-permute-start.16
  111.6 1.3 collective-permute-start.12
  112.9 1.3 copy.29
  114.2 0.4 collective-permute-start.13
  114.6 25.0 %shard_map.121 = (f32[4,1,1024]{2,1,0:T(1,128)}, bf16[4,2,24,1024]{3,2,1,0:T(8,128)(2,1)}, bf16[4,2,24,1024]{3,2,1,0:T(8,128)(2,1)}, bf16[4,2,24,1024]{3,2,1,0:T...) custom-call(s32[1]{0:T(128)} %bitcast.own_ref.refs_0_, ...), custom_call_target="tpu_custom_call" | custom-call | flops 1 | bytes 1 | tf_op jit(solution)/shard_map/pallas_call | solution.py:456
  139.7 0.5 collective-permute-start.17
  140.2 1.3 collective-permute-start.18
  141.7 0.7 collective-permute-start.20
  142.4 2.6 %collective-permute-done.13.refs_3_ = bf16[2,4,24,1024]{3,2,1,0:T(8,128)(2,1)S(1)} collective-permute-done((bf16[2,4,24,1024]{3,2,1,0:T(8,128)(2,1)}, bf16[2,4,24,1024]{3,2,1,0:T(8,128)(2,1)S(1)}, u32[]{:S(2)}, u32[]{:S(2)}) %collective-permute-start.13) | collective-permute-done | bytes 393248 | tf_op jit(solution)/shard_map/ppermute | solution.py:541
  145.0 1.3 collective-permute-start.21
  146.3 1.5 collective-permute-start.22
  147.8 7.2 %collective-permute-done.18.refs_10_ = bf16[4,2,24,1024]{3,2,1,0:T(8,128)(2,1)S(1)} collective-permute-done((bf16[4,2,24,1024]{3,2,1,0:T(8,128)(2,1)}, bf16[4,2,24,1024]{3,2,1,0:T(8,128)(2,1)S(1)}, u32[]{:S(2)}, u32[]{:S(2)}) %collective-permute-start.18) | collective-permute-done | bytes 393248 | tf_op jit(solution)/shard_map/ppermute | solution.py:541
  155.0 0.7 collective-permute-start.24
  155.8 6.0 %collective-permute-done.19.refs_11_ = bf16[4,2,24,1024]{3,2,1,0:T(8,128)(2,1)S(1)} collective-permute-done((bf16[4,2,24,1024]{3,2,1,0:T(8,128)(2,1)}, bf16[4,2,24,1024]{3,2,1,0:T(8,128)(2,1)S(1)}, u32[]{:S(2)}, u32[]{:S(2)}) %collective-permute-start.19) | collective-permute-done | bytes 393248 | tf_op jit(solution)/shard_map/ppermute | solution.py:541
  161.8 1.8 collective-permute-start.25
  163.6 0.7 fusion.1
  164.4 1.3 copy.28
  165.7 0.6 pad_maximum_fusion
  166.4 6.6 %shard_map.122._ = f32[4,24,32,1024]{3,2,1,0:T(8,128)} custom-call(s32[1]{0:T(128)} %bitcast.own_ref.refs_0_, f32[4,1024]{1,0:T(4,128)} %bitcast.25, f32[4,24,32,1024]{3,2,1,0:T(8,128)} %get-tuple-element.49.refs_11_.home_ref, f32[4,24,8,1024]{3,2,1,0:T(8,128)} %get-tuple-element.50._.share_ref, bf16[2,4,24,1024]{3,2,1,0:T(8,128)(2,1)} %get-tuple-element.66.refs_0_, ...), custom_call_target="tpu_custom_call" | custom-call | flops 1 | bytes 1 | tf_op jit(solution)/shard_map/pallas_call | solution.py:524
  173.0 0.7 copy-done.21
  173.6 4.9 %shard_map.123._ = f32[4,24,32,1024]{3,2,1,0:T(8,128)} custom-call(s32[1]{0:T(128)} %bitcast.own_ref.refs_0_, f32[4,24,32,1024]{3,2,1,0:T(8,128)} %shard_map.122._, f32[4,24,32,1024]{3,2,1,0:T(8,128)} %get-tuple-element.49.refs_11_.home_ref, f32[4,24,8,1024]{3,2,1,0:T(8,128)} %get-tuple-element.50._.share_ref, ...), custom_call_target="tpu_custom_call", output_to_operand_aliasing={{}: (1, {})} | custom-call | flops 1 | bytes 1 | tf_op jit(solution)/shard_map/pallas_call | solution.py:524
  178.7 0.5 copy-done.18
  179.3 4.9 %shard_map.124 = f32[4,24,32,1024]{3,2,1,0:T(8,128)} custom-call(s32[1]{0:T(128)} %bitcast.own_ref.refs_0_, f32[4,24,32,1024]{3,2,1,0:T(8,128)} %shard_map.123._, f32[4,24,32,1024]{3,2,1,0:T(8,128)} %get-tuple-element.49.refs_11_.home_ref, f32[4,24,8,1024]{3,2,1,0:T(8,128)} %get-tuple-element.50._.share_ref, ...), custom_call_target="tpu_custom_call", output_to_operand_aliasing={{}: (1, {})} | custom-call | flops 1 | bytes 1 | tf_op jit(solution)/shard_map/pallas_call | solution.py:524
  (81 shorter events, 1.3 us)
Async XLA Ops:
  16.7 11.9 %copy-start.27 = (bf16[4,2,24,1024]{3,2,1,0:T(8,128)(2,1)S(1)}, bf16[4,2,24,1024]{3,2,1,0:T(8,128)(2,1)}, u32[]{:S(2)}) copy-start(bf16[4,2,24,1024]{3,2,1,0:T(8,128)(2,1)} %get-tuple-element.54) | copy-start | bytes 1179652
  16.7 12.0 %copy-start.26 = (bf16[4,2,24,1024]{3,2,1,0:T(8,128)(2,1)S(1)}, bf16[4,2,24,1024]{3,2,1,0:T(8,128)(2,1)}, u32[]{:S(2)}) copy-start(bf16[4,2,24,1024]{3,2,1,0:T(8,128)(2,1)} %get-tuple-element.55) | copy-start | bytes 1179652
  21.8 23.4 %collective-permute-start.1 = (bf16[2,5,24,1024]{3,2,1,0:T(8,128)(2,1)}, bf16[2,5,24,1024]{3,2,1,0:T(8,128)(2,1)S(1)}, u32[]{:S(2)}, u32[]{:S(2)}) collective-permute-start(bf16[2,5,24,1024]{3,2,1,0:T(8,128)(2,1)} %get-tuple-element.48), channel_id=1, source_target_pairs={{1,0},{2,1},{3,2},{4,3},{5,4},{6,5},{7,6},{9,8},{10,9},{11,10},{12... | collective-permute-start | bytes 1474568 | tf_op jit(solution)/shard_map/ppermute | solution.py:549
  23.1 25.8 %collective-permute-start = (bf16[2,5,24,1024]{3,2,1,0:T(8,128)(2,1)}, bf16[2,5,24,1024]{3,2,1,0:T(8,128)(2,1)S(1)}, u32[]{:S(2)}, u32[]{:S(2)}) collective-permute-start(bf16[2,5,24,1024]{3,2,1,0:T(8,128)(2,1)} %get-tuple-element.45._), channel_id=1, source_target_pairs={{0,1},{1,2},{2,3},{3,4},{4,5},{5,6},{6,7},{8,9},{9,10},{10,11},{11... | collective-permute-start | bytes 1474568 | tf_op jit(solution)/shard_map/ppermute | solution.py:549
  28.6 16.4 %collective-permute-start.2 = (bf16[4,2,24,1024]{3,2,1,0:T(8,128)(2,1)S(1)}, bf16[4,2,24,1024]{3,2,1,0:T(8,128)(2,1)S(1)}, u32[]{:S(2)}, u32[]{:S(2)}) collective-permute-start(bf16[4,2,24,1024]{3,2,1,0:T(8,128)(2,1)S(1)} %copy-done.27), channel_id=1, source_target_pairs={{0,8},{8,0},{16,24},{24,16},{1,9},{9,1},{17,25},{25,17},{2,10},{10... | collective-permute-start | bytes 1179656 | tf_op jit(solution)/shard_map/ppermute | solution.py:541
  28.7 33.2 %collective-permute-start.3 = (bf16[4,2,24,1024]{3,2,1,0:T(8,128)(2,1)S(1)}, bf16[4,2,24,1024]{3,2,1,0:T(8,128)(2,1)S(1)}, u32[]{:S(2)}, u32[]{:S(2)}) collective-permute-start(bf16[4,2,24,1024]{3,2,1,0:T(8,128)(2,1)S(1)} %copy-done.26), channel_id=1, source_target_pairs={{0,16},{8,24},{16,0},{24,8},{1,17},{9,25},{17,1},{25,9},{2,18},{10... | collective-permute-start | bytes 1179656 | tf_op jit(solution)/shard_map/ppermute | solution.py:541
  30.8 31.6 %collective-permute-start.4 = (bf16[4,2,24,1024]{3,2,1,0:T(8,128)(2,1)}, bf16[4,2,24,1024]{3,2,1,0:T(8,128)(2,1)S(1)}, u32[]{:S(2)}, u32[]{:S(2)}) collective-permute-start(bf16[4,2,24,1024]{3,2,1,0:T(8,128)(2,1)} %get-tuple-element.44._), channel_id=1, source_target_pairs={{0,24},{8,16},{16,8},{24,0},{1,25},{9,17},{17,9},{25,1},{2,26},{10... | collective-permute-start | bytes 1179656 | tf_op jit(solution)/shard_map/ppermute | solution.py:541
  45.0 32.1 %copy-start.8 = (bf16[4,2,24,1024]{3,2,1,0:T(8,128)(2,1)}, bf16[4,2,24,1024]{3,2,1,0:T(8,128)(2,1)S(1)}, u32[]{:S(2)}) copy-start(bf16[4,2,24,1024]{3,2,1,0:T(8,128)(2,1)S(1)} %collective-permute-done.2.refs_1_) | copy-start | bytes 1179652
  45.0 32.1 %collective-permute-start.5 = (bf16[4,2,24,1024]{3,2,1,0:T(8,128)(2,1)}, bf16[4,2,24,1024]{3,2,1,0:T(8,128)(2,1)S(1)}, u32[]{:S(2)}, u32[]{:S(2)}) collective-permute-start(bf16[4,2,24,1024]{3,2,1,0:T(8,128)(2,1)} %get-tuple-element.57), channel_id=1, source_target_pairs={{0,8},{8,0},{16,24},{24,16},{1,9},{9,1},{17,25},{25,17},{2,10},{10... | collective-permute-start | bytes 1179656 | tf_op jit(solution)/shard_map/ppermute | solution.py:541
  45.3 4.8 %copy-start.6 = (bf16[2,5,24,1024]{3,2,1,0:T(8,128)(2,1)}, bf16[2,5,24,1024]{3,2,1,0:T(8,128)(2,1)S(1)}, u32[]{:S(2)}) copy-start(bf16[2,5,24,1024]{3,2,1,0:T(8,128)(2,1)S(1)} %collective-permute-done.1.refs_5_.refs_7_) | copy-start | bytes 1474564
  45.3 32.7 %collective-permute-start.6 = (bf16[4,2,24,1024]{3,2,1,0:T(8,128)(2,1)}, bf16[4,2,24,1024]{3,2,1,0:T(8,128)(2,1)S(1)}, u32[]{:S(2)}, u32[]{:S(2)}) collective-permute-start(bf16[4,2,24,1024]{3,2,1,0:T(8,128)(2,1)} %get-tuple-element.58), channel_id=1, source_target_pairs={{0,16},{8,24},{16,0},{24,8},{1,17},{9,25},{17,1},{25,9},{2,18},{10... | collective-permute-start | bytes 1179656 | tf_op jit(solution)/shard_map/ppermute | solution.py:541
  48.9 1.1 copy-start.7
  48.9 29.1 %collective-permute-start.7 = (bf16[4,2,24,1024]{3,2,1,0:T(8,128)(2,1)}, bf16[4,2,24,1024]{3,2,1,0:T(8,128)(2,1)S(1)}, u32[]{:S(2)}, u32[]{:S(2)}) collective-permute-start(bf16[4,2,24,1024]{3,2,1,0:T(8,128)(2,1)} %get-tuple-element.47.refs_3_), channel_id=1, source_target_pairs={{0,24},{8,16},{16,8},{24,0},{1,25},{9,17},{17,9},{25,1},{2,26},{10... | collective-permute-start | bytes 1179656 | tf_op jit(solution)/shard_map/ppermute | solution.py:541
  50.0 13.2 %copy-start.24 = (f32[1536]{0:T(1024)S(1)}, f32[1536]{0:T(1024)}, u32[]{:S(2)}) copy-start(f32[1536]{0:T(1024)} %param.19) | copy-start | bytes 18436
  61.9 11.1 %copy-start.9 = (bf16[4,2,24,1024]{3,2,1,0:T(8,128)(2,1)}, bf16[4,2,24,1024]{3,2,1,0:T(8,128)(2,1)S(1)}, u32[]{:S(2)}) copy-start(bf16[4,2,24,1024]{3,2,1,0:T(8,128)(2,1)S(1)} %collective-permute-done.3.refs_2_) | copy-start | bytes 1179652
  61.9 49.5 %collective-permute-start.8 = (bf16[4,4,24,1024]{3,2,1,0:T(8,128)(2,1)}, bf16[4,4,24,1024]{3,2,1,0:T(8,128)(2,1)S(1)}, u32[]{:S(2)}, u32[]{:S(2)}) collective-permute-start(bf16[4,4,24,1024]{3,2,1,0:T(8,128)(2,1)} %get-tuple-element.62), channel_id=1, source_target_pairs={{0,8},{8,0},{16,24},{24,16},{1,9},{9,1},{17,25},{25,17},{2,10},{10... | collective-permute-start | bytes 2359304 | tf_op jit(solution)/shard_map/ppermute | solution.py:541
  62.5 10.5 %copy-start.10 = (bf16[4,2,24,1024]{3,2,1,0:T(8,128)(2,1)}, bf16[4,2,24,1024]{3,2,1,0:T(8,128)(2,1)S(1)}, u32[]{:S(2)}) copy-start(bf16[4,2,24,1024]{3,2,1,0:T(8,128)(2,1)S(1)} %collective-permute-done.4.refs_3_) | copy-start | bytes 1179652
  62.5 49.1 %collective-permute-start.9 = (bf16[4,4,24,1024]{3,2,1,0:T(8,128)(2,1)}, bf16[4,4,24,1024]{3,2,1,0:T(8,128)(2,1)}, u32[]{:S(2)}, u32[]{:S(2)}) collective-permute-start(bf16[4,4,24,1024]{3,2,1,0:T(8,128)(2,1)} %get-tuple-element.63), channel_id=1, source_target_pairs={{0,16},{8,24},{16,0},{24,8},{1,17},{9,25},{17,1},{25,9},{2,18},{10... | collective-permute-start | bytes 2359304 | tf_op jit(solution)/shard_map/ppermute | solution.py:541
  73.0 4.2 %copy-start.25 = (bf16[4,4,24,1024]{3,2,1,0:T(8,128)(2,1)S(1)}, bf16[4,4,24,1024]{3,2,1,0:T(8,128)(2,1)}, u32[]{:S(2)}) copy-start(bf16[4,4,24,1024]{3,2,1,0:T(8,128)(2,1)} %get-tuple-element.64) | copy-start | bytes 2359300
  77.2 37.0 %collective-permute-start.10 = (bf16[4,4,24,1024]{3,2,1,0:T(8,128)(2,1)S(1)}, bf16[4,4,24,1024]{3,2,1,0:T(8,128)(2,1)}, u32[]{:S(2)}, u32[]{:S(2)}) collective-permute-start(bf16[4,4,24,1024]{3,2,1,0:T(8,128)(2,1)S(1)} %copy-done.25), channel_id=1, source_target_pairs={{0,24},{8,16},{16,8},{24,0},{1,25},{9,17},{17,9},{25,1},{2,26},{10... | collective-permute-start | bytes 2359304 | tf_op jit(solution)/shard_map/ppermute | solution.py:541
  108.4 2.3 %collective-permute-start.14 = (bf16[2,4,24,1024]{3,2,1,0:T(8,128)(2,1)}, bf16[2,4,24,1024]{3,2,1,0:T(8,128)(2,1)S(1)}, u32[]{:S(2)}, u32[]{:S(2)}) collective-permute-start(bf16[2,4,24,1024]{3,2,1,0:T(8,128)(2,1)} %get-tuple-element.71), channel_id=1, source_target_pairs={{0,8},{8,0},{16,24},{24,16},{1,9},{9,1},{17,25},{25,17},{2,10},{10... | collective-permute-start | bytes 1179656 | tf_op jit(solution)/shard_map/ppermute | solution.py:541
  109.1 30.5 %collective-permute-start.15 = (bf16[2,4,24,1024]{3,2,1,0:T(8,128)(2,1)}, bf16[2,4,24,1024]{3,2,1,0:T(8,128)(2,1)S(1)}, u32[]{:S(2)}, u32[]{:S(2)}) collective-permute-start(bf16[2,4,24,1024]{3,2,1,0:T(8,128)(2,1)} %get-tuple-element.72), channel_id=1, source_target_pairs={{0,16},{8,24},{16,0},{24,8},{1,17},{9,25},{17,1},{25,9},{2,18},{10... | collective-permute-start | bytes 1179656 | tf_op jit(solution)/shard_map/ppermute | solution.py:541
  110.7 28.9 %copy-start = (bf16[2,4,24,1024]{3,2,1,0:T(8,128)(2,1)}, bf16[2,4,24,1024]{3,2,1,0:T(8,128)(2,1)S(1)}, u32[]{:S(2)}) copy-start(bf16[2,4,24,1024]{3,2,1,0:T(8,128)(2,1)S(1)} %collective-permute-done.14.refs_5_) | copy-start | bytes 1179652
  110.7 29.5 %collective-permute-start.16 = (bf16[2,4,24,1024]{3,2,1,0:T(8,128)(2,1)}, bf16[2,4,24,1024]{3,2,1,0:T(8,128)(2,1)S(1)}, u32[]{:S(2)}, u32[]{:S(2)}) collective-permute-start(bf16[2,4,24,1024]{3,2,1,0:T(8,128)(2,1)} %get-tuple-element.73), channel_id=1, source_target_pairs={{0,24},{8,16},{16,8},{24,0},{1,25},{9,17},{17,9},{25,1},{2,26},{10... | collective-permute-start | bytes 1179656 | tf_op jit(solution)/shard_map/ppermute | solution.py:541
  111.4 3.2 %copy-start.14 = (bf16[4,4,24,1024]{3,2,1,0:T(8,128)(2,1)}, bf16[4,4,24,1024]{3,2,1,0:T(8,128)(2,1)S(1)}, u32[]{:S(2)}) copy-start(bf16[4,4,24,1024]{3,2,1,0:T(8,128)(2,1)S(1)} %collective-permute-done.8.refs_1_) | copy-start | bytes 2359300
  111.4 30.0 %collective-permute-start.11 = (bf16[2,4,24,1024]{3,2,1,0:T(8,128)(2,1)}, bf16[2,4,24,1024]{3,2,1,0:T(8,128)(2,1)S(1)}, u32[]{:S(2)}, u32[]{:S(2)}) collective-permute-start(bf16[2,4,24,1024]{3,2,1,0:T(8,128)(2,1)} %get-tuple-element.67), channel_id=1, source_target_pairs={{0,8},{8,0},{16,24},{24,16},{1,9},{9,1},{17,25},{25,17},{2,10},{10... | collective-permute-start | bytes 1179656 | tf_op jit(solution)/shard_map/ppermute | solution.py:541
  111.6 30.1 %collective-permute-start.12 = (bf16[2,4,24,1024]{3,2,1,0:T(8,128)(2,1)}, bf16[2,4,24,1024]{3,2,1,0:T(8,128)(2,1)S(1)}, u32[]{:S(2)}, u32[]{:S(2)}) collective-permute-start(bf16[2,4,24,1024]{3,2,1,0:T(8,128)(2,1)} %get-tuple-element.68), channel_id=1, source_target_pairs={{0,16},{8,24},{16,0},{24,8},{1,17},{9,25},{17,1},{25,9},{2,18},{10... | collective-permute-start | bytes 1179656 | tf_op jit(solution)/shard_map/ppermute | solution.py:541
  114.2 30.8 %collective-permute-start.13 = (bf16[2,4,24,1024]{3,2,1,0:T(8,128)(2,1)}, bf16[2,4,24,1024]{3,2,1,0:T(8,128)(2,1)S(1)}, u32[]{:S(2)}, u32[]{:S(2)}) collective-permute-start(bf16[2,4,24,1024]{3,2,1,0:T(8,128)(2,1)} %get-tuple-element.69), channel_id=1, source_target_pairs={{0,24},{8,16},{16,8},{24,0},{1,25},{9,17},{17,9},{25,1},{2,26},{10... | collective-permute-start | bytes 1179656 | tf_op jit(solution)/shard_map/ppermute | solution.py:541
  114.6 49.0 %copy-start.22 = (f32[2,1,1024]{2,0,1:T(2,128)S(1)}, f32[2,1,1024]{2,0,1:T(2,128)}, u32[]{:S(2)}) copy-start(f32[2,1,1024]{2,0,1:T(2,128)} %copy.30) | copy-start | bytes 24580
  114.6 49.0 %copy-start.23 = (f32[2,1,1024]{2,0,1:T(2,128)S(1)}, f32[2,1,1024]{2,0,1:T(2,128)}, u32[]{:S(2)}) copy-start(f32[2,1,1024]{2,0,1:T(2,128)} %copy.29) | copy-start | bytes 24580
  139.7 26.6 %copy-start.1 = (bf16[2,4,24,1024]{3,2,1,0:T(8,128)(2,1)}, bf16[2,4,24,1024]{3,2,1,0:T(8,128)(2,1)S(1)}, u32[]{:S(2)}) copy-start(bf16[2,4,24,1024]{3,2,1,0:T(8,128)(2,1)S(1)} %collective-permute-done.15.refs_6_) | copy-start | bytes 1179652
  139.7 8.1 %collective-permute-start.17 = (bf16[4,2,24,1024]{3,2,1,0:T(8,128)(2,1)}, bf16[4,2,24,1024]{3,2,1,0:T(8,128)(2,1)S(1)}, u32[]{:S(2)}, u32[]{:S(2)}) collective-permute-start(bf16[4,2,24,1024]{3,2,1,0:T(8,128)(2,1)} %get-tuple-element.75), channel_id=1, source_target_pairs={{0,8},{8,0},{16,24},{24,16},{1,9},{9,1},{17,25},{25,17},{2,10},{10... | collective-permute-start | bytes 1179656 | tf_op jit(solution)/shard_map/ppermute | solution.py:541
  140.2 26.1 %copy-start.2 = (bf16[2,4,24,1024]{3,2,1,0:T(8,128)(2,1)}, bf16[2,4,24,1024]{3,2,1,0:T(8,128)(2,1)S(1)}, u32[]{:S(2)}) copy-start(bf16[2,4,24,1024]{3,2,1,0:T(8,128)(2,1)S(1)} %collective-permute-done.16.refs_7_) | copy-start | bytes 1179652
  140.2 14.8 %collective-permute-start.18 = (bf16[4,2,24,1024]{3,2,1,0:T(8,128)(2,1)}, bf16[4,2,24,1024]{3,2,1,0:T(8,128)(2,1)S(1)}, u32[]{:S(2)}, u32[]{:S(2)}) collective-permute-start(bf16[4,2,24,1024]{3,2,1,0:T(8,128)(2,1)} %get-tuple-element.76), channel_id=1, source_target_pairs={{0,16},{8,24},{16,0},{24,8},{1,17},{9,25},{17,1},{25,9},{2,18},{10... | collective-permute-start | bytes 1179656 | tf_op jit(solution)/shard_map/ppermute | solution.py:541
  141.5 24.8 %copy-start.3 = (bf16[2,4,24,1024]{3,2,1,0:T(8,128)(2,1)}, bf16[2,4,24,1024]{3,2,1,0:T(8,128)(2,1)S(1)}, u32[]{:S(2)}) copy-start(bf16[2,4,24,1024]{3,2,1,0:T(8,128)(2,1)S(1)} %collective-permute-done.11.refs_1_) | copy-start | bytes 1179652
  141.5 20.3 %collective-permute-start.19 = (bf16[4,2,24,1024]{3,2,1,0:T(8,128)(2,1)}, bf16[4,2,24,1024]{3,2,1,0:T(8,128)(2,1)S(1)}, u32[]{:S(2)}, u32[]{:S(2)}) collective-permute-start(bf16[4,2,24,1024]{3,2,1,0:T(8,128)(2,1)} %get-tuple-element.77), channel_id=1, source_target_pairs={{0,24},{8,16},{16,8},{24,0},{1,25},{9,17},{17,9},{25,1},{2,26},{10... | collective-permute-start | bytes 1179656 | tf_op jit(solution)/shard_map/ppermute | solution.py:541
  141.7 24.7 %copy-start.4 = (bf16[2,4,24,1024]{3,2,1,0:T(8,128)(2,1)}, bf16[2,4,24,1024]{3,2,1,0:T(8,128)(2,1)S(1)}, u32[]{:S(2)}) copy-start(bf16[2,4,24,1024]{3,2,1,0:T(8,128)(2,1)S(1)} %collective-permute-done.12.refs_2_) | copy-start | bytes 1179652
  141.7 4.6 %collective-permute-start.20 = (bf16[4,1,24,1024]{3,2,1,0:T(8,128)(2,1)}, bf16[4,1,24,1024]{3,2,1,0:T(8,128)(2,1)S(1)}, u32[]{:S(2)}, u32[]{:S(2)}) collective-permute-start(bf16[4,1,24,1024]{3,2,1,0:T(8,128)(2,1)} %get-tuple-element.79), channel_id=1, source_target_pairs={{0,8},{8,0},{16,24},{24,16},{1,9},{9,1},{17,25},{25,17},{2,10},{10... | collective-permute-start | bytes 589832 | tf_op jit(solution)/shard_map/ppermute | solution.py:541
  145.0 21.4 %copy-start.5 = (bf16[2,4,24,1024]{3,2,1,0:T(8,128)(2,1)}, bf16[2,4,24,1024]{3,2,1,0:T(8,128)(2,1)S(1)}, u32[]{:S(2)}) copy-start(bf16[2,4,24,1024]{3,2,1,0:T(8,128)(2,1)S(1)} %collective-permute-done.13.refs_3_) | copy-start | bytes 1179652
  145.0 28.0 %collective-permute-start.21 = (bf16[4,1,24,1024]{3,2,1,0:T(8,128)(2,1)}, bf16[4,1,24,1024]{3,2,1,0:T(8,128)(2,1)S(1)}, u32[]{:S(2)}, u32[]{:S(2)}) collective-permute-start(bf16[4,1,24,1024]{3,2,1,0:T(8,128)(2,1)} %get-tuple-element.80), channel_id=1, source_target_pairs={{0,16},{8,24},{16,0},{24,8},{1,17},{9,25},{17,1},{25,9},{2,18},{10... | collective-permute-start | bytes 589832 | tf_op jit(solution)/shard_map/ppermute | solution.py:541
  146.3 26.7 %copy-start.19 = (bf16[4,1,24,1024]{3,2,1,0:T(8,128)(2,1)}, bf16[4,1,24,1024]{3,2,1,0:T(8,128)(2,1)S(1)}, u32[]{:S(2)}) copy-start(bf16[4,1,24,1024]{3,2,1,0:T(8,128)(2,1)S(1)} %collective-permute-done.20.refs_9_) | copy-start | bytes 589828
  146.3 26.7 %collective-permute-start.22 = (bf16[4,1,24,1024]{3,2,1,0:T(8,128)(2,1)}, bf16[4,1,24,1024]{3,2,1,0:T(8,128)(2,1)}, u32[]{:S(2)}, u32[]{:S(2)}) collective-permute-start(bf16[4,1,24,1024]{3,2,1,0:T(8,128)(2,1)} %get-tuple-element.81), channel_id=1, source_target_pairs={{0,24},{8,16},{16,8},{24,0},{1,25},{9,17},{17,9},{25,1},{2,26},{10... | collective-permute-start | bytes 589832 | tf_op jit(solution)/shard_map/ppermute | solution.py:541
  147.8 18.5 %copy-start.15 = (bf16[4,2,24,1024]{3,2,1,0:T(8,128)(2,1)}, bf16[4,2,24,1024]{3,2,1,0:T(8,128)(2,1)S(1)}, u32[]{:S(2)}) copy-start(bf16[4,2,24,1024]{3,2,1,0:T(8,128)(2,1)S(1)} %collective-permute-done.17.refs_9_) | copy-start | bytes 1179652
  147.8 30.7 %collective-permute-start.23 = (bf16[4,1,24,1024]{3,2,1,0:T(8,128)(2,1)}, bf16[4,1,24,1024]{3,2,1,0:T(8,128)(2,1)S(1)}, u32[]{:S(2)}, u32[]{:S(2)}) collective-permute-start(bf16[4,1,24,1024]{3,2,1,0:T(8,128)(2,1)} %get-tuple-element.83), channel_id=1, source_target_pairs={{0,8},{8,0},{16,24},{24,16},{1,9},{9,1},{17,25},{25,17},{2,10},{10... | collective-permute-start | bytes 589832 | tf_op jit(solution)/shard_map/ppermute | solution.py:541
  155.0 11.3 %copy-start.16 = (bf16[4,2,24,1024]{3,2,1,0:T(8,128)(2,1)}, bf16[4,2,24,1024]{3,2,1,0:T(8,128)(2,1)S(1)}, u32[]{:S(2)}) copy-start(bf16[4,2,24,1024]{3,2,1,0:T(8,128)(2,1)S(1)} %collective-permute-done.18.refs_10_) | copy-start | bytes 1179652
  155.0 23.5 %collective-permute-start.24 = (bf16[4,1,24,1024]{3,2,1,0:T(8,128)(2,1)}, bf16[4,1,24,1024]{3,2,1,0:T(8,128)(2,1)S(1)}, u32[]{:S(2)}, u32[]{:S(2)}) collective-permute-start(bf16[4,1,24,1024]{3,2,1,0:T(8,128)(2,1)} %get-tuple-element.84), channel_id=1, source_target_pairs={{0,16},{8,24},{16,0},{24,8},{1,17},{9,25},{17,1},{25,9},{2,18},{10... | collective-permute-start | bytes 589832 | tf_op jit(solution)/shard_map/ppermute | solution.py:541
  161.8 4.5 %copy-start.17 = (bf16[4,2,24,1024]{3,2,1,0:T(8,128)(2,1)}, bf16[4,2,24,1024]{3,2,1,0:T(8,128)(2,1)S(1)}, u32[]{:S(2)}) copy-start(bf16[4,2,24,1024]{3,2,1,0:T(8,128)(2,1)S(1)} %collective-permute-done.19.refs_11_) | copy-start | bytes 1179652
  161.8 16.8 %collective-permute-start.25 = (bf16[4,1,24,1024]{3,2,1,0:T(8,128)(2,1)}, bf16[4,1,24,1024]{3,2,1,0:T(8,128)(2,1)}, u32[]{:S(2)}, u32[]{:S(2)}) collective-permute-start(bf16[4,1,24,1024]{3,2,1,0:T(8,128)(2,1)} %get-tuple-element.85), channel_id=1, source_target_pairs={{0,24},{8,16},{16,8},{24,0},{1,25},{9,17},{17,9},{25,1},{2,26},{10... | collective-permute-start | bytes 589832 | tf_op jit(solution)/shard_map/ppermute | solution.py:541
  (6 other events, 4.6 us)

commit v4 on v3

v4 whole, which is shorter than its diff:
```python
import functools
import math

import jax
import jax.numpy as jnp
import numpy as np
from jax import lax
from jax.experimental import pallas as pl
from jax.experimental.pallas import tpu as pltpu
from jax.sharding import PartitionSpec as P

HALO = 2
TILE = 8
LANES = 128
MIB = 1 << 20
VMEM_LIMIT = 60 * MIB
COST = pl.CostEstimate(flops=1, bytes_accessed=1, transcendentals=0)
LONG = pl.CostEstimate(flops=10**11, bytes_accessed=100 * MIB, transcendentals=0)


def direction_factors(dirs):
    angle = (np.arange(dirs, dtype=np.float32) + np.float32(0.5)) * np.float32(2.0 * math.pi / dirs)
    return np.stack([np.float32(0.5) * np.abs(np.cos(angle)), np.float32(0.5) * np.abs(np.sin(angle))])


def chunk_row(owner, j, chunk):
    return jnp.where(owner == 0, chunk[0], chunk[1]) + j


UNREAD = pl.BlockSpec(memory_space=pl.ANY)


def lane_tiles(cols):
    return [pl.ds(c * LANES, LANES) for c in range(cols // LANES)]


def coefficients(cel_ref, base_ref, trn_ref, here, cg, turn, sea):
    sea = sea.astype(jnp.float32)
    celerity = 0.1 + 0.8 * cg.astype(jnp.float32) / 7.0
    turning = 0.3 * jnp.abs(turn.astype(jnp.float32) - 3.5) / 3.5
    cel_ref[here, :] = celerity * sea
    base_ref[here, :] = (1.0 - turning) * sea
    trn_ref[here, :] = turning * sea


def sweep(dirs, tiles, alone, lanes, sign_ref, along_ref, coefs, turns_up, load, store):
    cel_ref, base_ref, trn_ref = coefs
    row = lax.broadcasted_iota(jnp.int32, (TILE, LANES), 0)
    lane = lax.broadcasted_iota(jnp.int32, (TILE, LANES), 1)
    nothing = jnp.zeros((TILE, LANES), jnp.float32)

    def span(t):
        return pl.ds(t * TILE, TILE)

    def one(d, carry):
        following = jnp.where(d == dirs - 1, 0, d + 1)
        previous = jnp.where(d == 0, dirs - 1, d - 1)
        ax = along_ref[0, d]
        ay = along_ref[1, d]
        right = sign_ref[0, d] > 0
        high = sign_ref[1, d] > 0
        shift_x = jnp.where(right, LANES - 1, 1)
        shift_y = jnp.where(high, TILE - 1, 1)
        at_right = lane == jnp.where(right, LANES - 1, LANES)
        at_left = lane == jnp.where(right, LANES, 0)
        at_high = row == jnp.where(high, TILE - 1, TILE)
        at_low = row == jnp.where(high, TILE, 0)
        at_edge = row == jnp.where(high, TILE - 1, 0)

        def column(c):
            here = [load(t, d, lanes[c]) for t in range(tiles)]
            flow = [cel_ref[span(t), lanes[c]] * here[t] for t in range(tiles)]
            return here, flow, [pltpu.roll(f, shift_x, 1) for f in flow]

        before = [nothing] * tiles
        here, flow, moved = column(0)
        for c in range(len(lanes)):
            beyond = [nothing] * tiles
            if c + 1 < len(lanes):
                later = column(c + 1)
                beyond = later[2]
            lifted = [pltpu.roll(f, shift_y, 0) for f in flow]
            for t in range(tiles):
                flow_x = jnp.where(at_right, beyond[t], jnp.where(at_left, before[t], moved[t]))
                if alone:
                    flow_y = jnp.where(at_edge, nothing, lifted[t])
                else:
                    above = lifted[t + 1] if t + 1 < tiles else nothing
                    below = lifted[t - 1] if t > 0 else nothing
                    flow_y = jnp.where(at_high, above, jnp.where(at_low, below, lifted[t]))
                turned = jnp.where(turns_up(t, c), load(t, following, lanes[c]), load(t, previous, lanes[c]))
                total = base_ref[span(t), lanes[c]] * here[t] + ax * (flow_x - flow[t])
                total = total + ay * (flow_y - flow[t]) + trn_ref[span(t), lanes[c]] * turned
                store(t, d, c, total)
            if c + 1 < len(lanes):
                before = moved
                here, flow, moved = later
        return carry

    lax.fori_loop(0, dirs, one, 0, unroll=6)


def emit(own, parts, local, chunk, dirs, lanes, swap_ref, send_refs):
    for k in range(parts):
        owner = own ^ k
        for j in range(chunk[2]):
            start = (owner * local + chunk_row(owner, j, chunk)) * (dirs + 1)
            for c, here in enumerate(lanes):
                send_refs[k][j, 0, :, here] = swap_ref[c, pl.ds(start, dirs), :].astype(jnp.bfloat16)


def inner_kernel(parts, local, chunk, into, own_ref, sign_ref, along_ref, _, forcing_ref, cg_ref, turn_ref, mask_ref, *refs):
    refs = refs[3:] if into else refs
    home_ref, first_out, last_out = refs[:3]
    sends = parts if chunk else 0
    cel_ref, base_ref, trn_ref, first_ref, swap_ref, edge_ref = refs[sends + 3 :]
    dirs, rows, cols = forcing_ref.shape[1:]
    pitch = dirs + 1
    lanes = lane_tiles(cols)
    tiles = rows // TILE

    def span(t):
        return pl.ds(t * TILE, TILE)

    for t in range(tiles):
        levels = (cg_ref[0, span(t), :], turn_ref[0, span(t), :], mask_ref[span(t), :])
        coefficients(cel_ref, base_ref, trn_ref, span(t), *levels)

    def outermost(d, carry):
        for side, t in enumerate((0, tiles - 1)):
            for c, here in enumerate(lanes):
                swap_ref[c, pl.ds(side * TILE * pitch + d, TILE, stride=pitch), :] = forcing_ref[0, d, span(t), here]
        return carry

    lax.fori_loop(0, dirs, outermost, 0, unroll=8)
    edge_ref[...] = jnp.zeros_like(edge_ref)
    for out_ref, low, at in ((first_out, 0, 0), (last_out, rows - HALO, 2 * TILE - HALO)):
        for r in range(HALO):
            for c, here in enumerate(lanes):
                edge_ref[:dirs, here] = swap_ref[c, pl.ds((at + r) * pitch, dirs), :]
            for n, level in enumerate((cg_ref[0], turn_ref[0], mask_ref[...])):
                edge_ref[dirs + n : dirs + n + 1, :] = level[low + r : low + r + 1].astype(jnp.float32)
            out_ref[r, 0] = edge_ref[...].astype(jnp.bfloat16)

    def turns_up(t, c):
        return turn_ref[0, span(t), lanes[c]] >= 4

    def store_first(t, d, c, value):
        first_ref[d, span(t), lanes[c]] = value

    def store_last(t, d, c, value):
        home_ref[0, d, span(t), lanes[c]] = value
        if chunk:
            swap_ref[c, pl.ds(t * TILE * pitch + d, TILE, stride=pitch), :] = value

    step = functools.partial(sweep, dirs, tiles, False, lanes, sign_ref, along_ref, (cel_ref, base_ref, trn_ref), turns_up)
    step(lambda t, d, here: forcing_ref[0, d, span(t), here], store_first)
    step(lambda t, d, here: first_ref[d, span(t), here], store_last)
    if chunk:
        emit(own_ref[0], parts, local, chunk, dirs, lanes, swap_ref, refs[3 : sends + 3])


def inner(own, signs, along, after, forcing, cg, turn, mask, into, parts, chunk, group):
    freqs, dirs, rows, cols = forcing.shape
    begin, many = group
    local = rows // parts
    smem = pl.BlockSpec(memory_space=pltpu.SMEM)
    levels = pl.BlockSpec((1, rows, cols), lambda f: (begin + f, 0, 0))
    block = pl.BlockSpec((1, dirs, rows, cols), lambda f: (begin + f, 0, 0, 0))
    edge = pl.BlockSpec((HALO, 1, dirs + TILE, cols), lambda f: (0, begin + f, 0, 0))
    edge_shape = jax.ShapeDtypeStruct((HALO, freqs, dirs + TILE, cols), jnp.bfloat16)
    coefs = pltpu.VMEM((rows, cols), jnp.float32)
    sends = parts if chunk else 0
    count = chunk[2] if chunk else 0
    outs = pl.pallas_call(
        functools.partial(inner_kernel, parts, local, chunk, into is not None),
        grid=(many,),
        in_specs=[smem, smem, smem, UNREAD, block, levels, levels, pl.BlockSpec((rows, cols), lambda f: (0, 0))]
        + ([] if into is None else [UNREAD] * 3),
        out_specs=[block, edge, edge] + [pl.BlockSpec((count, 1, dirs, cols), lambda f: (0, f, 0, 0))] * sends,
        out_shape=[jax.ShapeDtypeStruct(forcing.shape, jnp.float32), edge_shape, edge_shape]
        + [jax.ShapeDtypeStruct((count, many, dirs, cols), jnp.bfloat16)] * sends,
        scratch_shapes=[
            coefs,
            coefs,
            coefs,
            pltpu.VMEM((dirs, rows, cols), jnp.float32),
            pltpu.VMEM((cols // LANES, rows * (dirs + 1), LANES), jnp.float32),
            pltpu.VMEM((dirs + TILE, cols), jnp.float32),
        ],
        input_output_aliases={} if into is None else {8: 0, 9: 1, 10: 2},
        compiler_params=pltpu.CompilerParams(vmem_limit_bytes=VMEM_LIMIT),
        cost_estimate=COST,
    )(own, signs, along, after, forcing, cg, turn, mask, *([] if into is None else into))
    return outs[:3], list(outs[3:])


def outer_kernel(parts, local, chunk, *refs):
    own_ref, sign_ref, along_ref, _, above_ref, below_ref, cg_ref, turn_ref, mask_ref, home_ref, share_ref = refs[:11]
    send_refs = refs[11 : 11 + parts]
    cel_ref, base_ref, trn_ref, up_ref, lev_ref, near_ref, first_ref, side_ref, edge_ref, swap_ref = refs[11 + parts :]
    dirs, rows, cols = home_ref.shape[1:]
    freqs = share_ref.shape[0]
    pitch = dirs + 1
    lanes = lane_tiles(cols)
    tiles = rows // TILE
    f = pl.program_id(0)

    def span(t):
        return pl.ds(t * TILE, TILE)

    @pl.when(f == 0)
    def _():
        edge_ref[...] = jnp.zeros_like(edge_ref)
        beyond = ((above_ref, 0, 0), (above_ref, 1, 1), (below_ref, 0, TILE - HALO), (below_ref, 1, TILE - 1))
        for n in range(freqs):
            for i, (ref, r, low) in enumerate(beyond):
                for c, here in enumerate(lanes):
                    piece = ref[r, n, :, here].astype(jnp.float32)
                    edge_ref[c, pl.ds(low * pitch, dirs), :] = piece[:dirs]
                    lev_ref[i * TILE : (i + 1) * TILE, here] = piece[dirs:]

            def gather(d, carry, n=n):
                for c, here in enumerate(lanes):
                    side_ref[d, span(n), here] = edge_ref[c, pl.ds(d, TILE, stride=pitch), :]
                return carry

            lax.fori_loop(0, dirs, gather, 0, unroll=12)
            for q, mine in enumerate((cg_ref[n], turn_ref[n], mask_ref[...])):
                for i, (_, _, low) in enumerate(beyond):
                    near_ref[q * TILE + low : q * TILE + low + 1, :] = lev_ref[i * TILE + q : i * TILE + q + 1, :]
                near_ref[q * TILE + HALO : q * TILE + 2 * HALO, :] = mine[:HALO].astype(jnp.float32)
                near_ref[q * TILE + 2 * HALO : q * TILE + 3 * HALO, :] = mine[rows - HALO :].astype(jnp.float32)
            coefficients(cel_ref, base_ref, trn_ref, span(n), *[near_ref[span(q), :] for q in range(3)])
            up_ref[span(n), :] = near_ref[span(1), :]

        def turns_up(t, c):
            return up_ref[span(t), lanes[c]] >= 4.0

        def store_first(t, d, c, value):
            first_ref[d, span(t), lanes[c]] = value

        def store_last(t, d, c, value):
            share_ref[t, d, :, lanes[c]] = value

        step = functools.partial(sweep, dirs, freqs, True, lanes, sign_ref, along_ref, (cel_ref, base_ref, trn_ref), turns_up)
        step(lambda t, d, here: side_ref[d, span(t), here], store_first)
        step(lambda t, d, here: first_ref[d, span(t), here], store_last)

    def whole(d, carry):
        for t in range(tiles):
            for c, here in enumerate(lanes):
                value = with_share(home_ref[0, d, span(t), here], share_ref, f, d, here, t, tiles)
                swap_ref[c, pl.ds(t * TILE * pitch + d, TILE, stride=pitch), :] = value
        return carry

    lax.fori_loop(0, dirs, whole, 0, unroll=4)
    emit(own_ref[0], parts, local, chunk, dirs, lanes, swap_ref, send_refs)


def with_share(value, share_ref, f, d, here, t, tiles):
    row = lax.broadcasted_iota(jnp.int32, value.shape, 0)
    if t == 0:
        value = value + jnp.where(row < HALO, pltpu.roll(share_ref[f, d, :, here], TILE - HALO, 0), 0.0)
    if t == tiles - 1:
        value = value + jnp.where(row >= TILE - HALO, pltpu.roll(share_ref[f, d, :, here], HALO, 0), 0.0)
    return value


def outer(own, signs, along, after, above, below, cg, turn, mask, home, parts, chunk):
    freqs, dirs, rows, cols = home.shape
    local = rows // parts
    smem = pl.BlockSpec(memory_space=pltpu.SMEM)
    edge = pl.BlockSpec((HALO, freqs, dirs + TILE, cols), lambda f: (0, 0, 0, 0))
    levels = pl.BlockSpec((freqs, rows, cols), lambda f: (0, 0, 0))
    tall = pltpu.VMEM((freqs * TILE, cols), jnp.float32)
    outs = pl.pallas_call(
        functools.partial(outer_kernel, parts, local, chunk),
        grid=(freqs,),
        in_specs=[smem, smem, smem, UNREAD, edge, edge, levels, levels]
        + [pl.BlockSpec((rows, cols), lambda f: (0, 0)), pl.BlockSpec((1, dirs, rows, cols), lambda f: (f, 0, 0, 0))],
        out_specs=[pl.BlockSpec((freqs, dirs, TILE, cols), lambda f: (0, 0, 0, 0))]
        + [pl.BlockSpec((chunk[2], 1, dirs, cols), lambda f: (0, f, 0, 0))] * parts,
        out_shape=[jax.ShapeDtypeStruct((freqs, dirs, TILE, cols), jnp.float32)]
        + [jax.ShapeDtypeStruct((chunk[2], freqs, dirs, cols), jnp.bfloat16)] * parts,
        scratch_shapes=[
            tall,
            tall,
            tall,
            tall,
            pltpu.VMEM((2 * HALO * TILE, cols), jnp.float32),
            pltpu.VMEM((3 * TILE, cols), jnp.float32),
            pltpu.VMEM((dirs, freqs * TILE, cols), jnp.float32),
            pltpu.VMEM((dirs, freqs * TILE, cols), jnp.float32),
            pltpu.VMEM((cols // LANES, TILE * (dirs + 1), LANES), jnp.float32),
            pltpu.VMEM((cols // LANES, rows * (dirs + 1), LANES), jnp.float32),
        ],
        compiler_params=pltpu.CompilerParams(vmem_limit_bytes=VMEM_LIMIT),
        cost_estimate=LONG,
    )(own, signs, along, after, above, below, cg, turn, mask, home)
    return outs[0], list(outs[1:])


def by_row_kernel(_, state_ref, out_ref, swap_ref):
    deep, local, _ = state_ref.shape
    pitch = deep + 1

    def body(d, carry):
        swap_ref[pl.ds(d, local, stride=pitch), :] = state_ref[d].astype(jnp.float32)
        return carry

    lax.fori_loop(0, deep, body, 0, unroll=64)
    for r in range(local):
        out_ref[r] = swap_ref[pl.ds(r * pitch, deep), :].astype(jnp.bfloat16)


def by_row(after, state):
    deep, local, cols = state.shape
    return pl.pallas_call(
        by_row_kernel,
        grid=(cols // LANES,),
        in_specs=[UNREAD, pl.BlockSpec((deep, local, LANES), lambda c: (0, 0, c))],
        out_specs=pl.BlockSpec((local, deep, LANES), lambda c: (0, 0, c)),
        out_shape=jax.ShapeDtypeStruct((local, deep, cols), jnp.bfloat16),
        scratch_shapes=[pltpu.VMEM((local * (deep + 1), LANES), jnp.float32)],
        compiler_params=pltpu.CompilerParams(vmem_limit_bytes=VMEM_LIMIT),
        cost_estimate=COST,
    )(after, state)


def turned_kernel(_, w_in_ref, w_out_ref, in_t_ref, out_t_ref):
    in_t_ref[...] = w_in_ref[...].T
    out_t_ref[...] = w_out_ref[...].T


def turned(after, w_in, w_out):
    hidden, total = w_in.shape
    step = 512
    tall = pl.BlockSpec((step, total), lambda h: (h, 0))
    wide = pl.BlockSpec((total, step), lambda h: (0, h))
    return pl.pallas_call(
        turned_kernel,
        grid=(hidden // step,),
        in_specs=[UNREAD, tall, wide],
        out_specs=[wide, tall],
        out_shape=[jax.ShapeDtypeStruct((total, hidden), w_in.dtype), jax.ShapeDtypeStruct((hidden, total), w_in.dtype)],
        compiler_params=pltpu.CompilerParams(vmem_limit_bytes=VMEM_LIMIT),
        cost_estimate=COST,
    )(after, w_in, w_out)


def source_kernel(parts, got, sent, dirs, step, own_ref, _, state_ref, wind_ref, w_in_ref, out_t_ref, in_t_ref, weight_ref, *refs):
    cell_refs = refs[: parts * len(got)]
    grad_ref = refs[parts * len(got)]
    back_refs = refs[parts * len(got) + 1 : -3]
    cell_ref, weighted_ref, grown_ref = refs[-3:]
    freqs = sum(many for _, many in got)
    hidden, width = weighted_ref.shape
    own = own_ref[0]

    def place(k, group):
        begin, many = group
        return pl.ds(pl.multiple_of(((own ^ k) * freqs + begin) * dirs, TILE), many * dirs)

    for g, group in enumerate(got):
        for k in range(parts):
            piece = cell_refs[g * parts + k][0].astype(jnp.float32)
            cell_ref[place(k, group), :] = piece.reshape(group[1] * dirs, width)
    cell = cell_ref[...].astype(jnp.bfloat16)
    state = state_ref[0]
    wind = wind_ref[0]
    grad = jnp.zeros((TILE, width), jnp.float32)
    for h in range(0, hidden, step):
        some = pl.ds(h, step)
        weight = weight_ref[some, :]
        forward = jnp.dot(w_in_ref[some, :], state, preferred_element_type=jnp.float32) + weight * wind
        squash = jnp.tanh(forward)
        pulled = jnp.dot(out_t_ref[some, :], cell, preferred_element_type=jnp.float32)
        weighted = (1.0 - squash * squash) * pulled
        weighted_ref[some, :] = weighted.astype(jnp.bfloat16)
        grad = grad + jnp.sum((weight * weighted).reshape(step // TILE, TILE, width), axis=0)
    grad_ref[0] = jnp.sum(grad, axis=0, keepdims=True)
    grown_ref[...] = jnp.dot(in_t_ref[...], weighted_ref[...], preferred_element_type=jnp.float32)
    for g, group in enumerate(sent):
        for k in range(parts):
            grown = grown_ref[place(k, group), :].reshape(group[1], dirs, width)
            back_refs[g * parts + k][0] = grown.astype(jnp.bfloat16)


def source_term(own, after, state, wind, w_in, out_t, in_t, weight, cells, got, sent, rows, chunk):
    parts = len(cells[0])
    _, _, dirs, cols = cells[0][0].shape
    first, count = rows
    hidden, total = w_in.shape
    width = min(cols, 512)

    def row_of(j, own_ref):
        return chunk_row(own_ref[0], first + j, chunk)

    def whole(shape):
        return pl.BlockSpec(shape, lambda j, c, own_ref: (0, 0))

    cell_specs = [
        pl.BlockSpec((1, many, dirs, width), lambda j, c, own_ref: (first + j, 0, 0, c)) for _, many in got for _ in range(parts)
    ]
    back_specs = [pl.BlockSpec((1, many, dirs, width), lambda j, c, own_ref: (j, 0, 0, c)) for _, many in sent for _ in range(parts)]
    outs = pl.pallas_call(
        functools.partial(source_kernel, parts, got, sent, dirs, 256),
        grid_spec=pltpu.PrefetchScalarGridSpec(
            num_scalar_prefetch=1,
            grid=(count, cols // width),
            in_specs=[
                UNREAD,
                pl.BlockSpec((1, total, width), lambda j, c, own_ref: (row_of(j, own_ref), 0, c)),
                pl.BlockSpec((1, 1, width), lambda j, c, own_ref: (row_of(j, own_ref), 0, c)),
                whole((hidden, total)),
                whole((hidden, total)),
                whole((total, hidden)),
                whole((hidden, 1)),
            ]
            + cell_specs,
            out_specs=[pl.BlockSpec((1, 1, width), lambda j, c, own_ref: (j, 0, c))] + back_specs,
            scratch_shapes=[
                pltpu.VMEM((total, width), jnp.float32),
                pltpu.VMEM((hidden, width), jnp.bfloat16),
                pltpu.VMEM((total, width), jnp.float32),
            ],
        ),
        out_shape=[jax.ShapeDtypeStruct((count, 1, cols), jnp.float32)]
        + [jax.ShapeDtypeStruct((count, many, dirs, cols), jnp.bfloat16) for _, many in sent for _ in range(parts)],
        compiler_params=pltpu.CompilerParams(vmem_limit_bytes=VMEM_LIMIT),
        cost_estimate=COST,
    )(own, after, state, wind, w_in, out_t, in_t, weight, *[cell for group in cells for cell in group])
    return outs[0], [list(outs[1 + g * parts : 1 + (g + 1) * parts]) for g in range(len(sent))]


def join_kernel(parts, spans, own_ref, _, home_ref, share_ref, *refs):
    out_ref, swap_ref = refs[-2:]
    dirs, rows, cols = home_ref.shape[1:]
    pitch = dirs + 1
    local = rows // parts
    own = own_ref[0]
    lanes = lane_tiles(cols)
    tiles = rows // TILE
    for i, (first, count, chunk) in enumerate(spans):
        for k in range(parts):
            owner = own ^ k
            for j in range(count):
                start = (owner * local + chunk_row(owner, first + j, chunk)) * pitch
                for c, here in enumerate(lanes):
                    swap_ref[c, pl.ds(start, dirs), :] = refs[i * parts + k][j, 0, :, here].astype(jnp.float32)

    def body(d, carry):
        for t in range(tiles):
            for c, here in enumerate(lanes):
                grown = swap_ref[c, pl.ds(t * TILE * pitch + d, TILE, stride=pitch), :]
                value = with_share(home_ref[0, d, pl.ds(t * TILE, TILE), here], share_ref, 0, d, here, t, tiles)
                out_ref[0, d, pl.ds(t * TILE, TILE), here] = value + grown
        return carry

    lax.fori_loop(0, dirs, body, 0, unroll=12)


def join(own, into, home, share, early, late, rows_of, chunks, group):
    begin, many = group
    parts = len(late)
    _, dirs, rows, cols = home.shape
    last = late[0].shape[0]
    spans = [(*span, chunks[0]) for span in rows_of] + [(0, last, chunks[-1])]
    width = min(cols, 256)
    block = pl.BlockSpec((1, dirs, rows, width), lambda f, c: (begin + f, 0, 0, c))
    specs = [
        pl.BlockSpec((count, 1, dirs, width), lambda f, c: (0, begin + f, 0, c)) for _, count in rows_of for _ in range(parts)
    ] + [pl.BlockSpec((last, 1, dirs, width), lambda f, c: (0, f, 0, c))] * parts
    return pl.pallas_call(
        functools.partial(join_kernel, parts, spans),
        grid=(many, cols // width),
        in_specs=[pl.BlockSpec(memory_space=pltpu.SMEM), UNREAD, block]
        + [pl.BlockSpec((1, dirs, TILE, width), lambda f, c: (begin + f, 0, 0, c))]
        + specs,
        out_specs=block,
        out_shape=jax.ShapeDtypeStruct(home.shape, jnp.float32),
        scratch_shapes=[pltpu.VMEM((width // LANES, rows * (dirs + 1), LANES), jnp.float32)],
        input_output_aliases={} if begin == 0 else {1: 0},
        compiler_params=pltpu.CompilerParams(vmem_limit_bytes=VMEM_LIMIT),
        cost_estimate=COST,
    )(own, into, home, share, *[piece for pieces in early for piece in pieces], *late)


def arrived_kernel(held, *refs):
    refs[-1][...] = jnp.zeros_like(refs[-1])


def arrived(after, pieces, held=()):
    outs = pl.pallas_call(
        functools.partial(arrived_kernel, len(held)),
        in_specs=[UNREAD] * (1 + len(pieces) + len(held)),
        out_specs=[UNREAD] * len(held) + [pl.BlockSpec(memory_space=pltpu.VMEM)],
        out_shape=[jax.ShapeDtypeStruct(h.shape, h.dtype) for h in held] + [jax.ShapeDtypeStruct((TILE, LANES), jnp.float32)],
        input_output_aliases={1 + len(pieces) + i: i for i in range(len(held))},
        cost_estimate=COST,
    )(after, *pieces, *held)
    return outs[-1], list(outs[:-1])


def swapped(pieces):
    parts = len(pieces)
    moved = {k: lax.ppermute(pieces[k], "comp", [(i, i ^ k) for i in range(parts)]) for k in range(parts - 1, 0, -1)}
    return [pieces[0]] + [moved[k] for k in range(1, parts)]


def across(low, high):
    count = lax.axis_size("space")
    up = [(i, i + 1) for i in range(count - 1)]
    down = [(i + 1, i) for i in range(count - 1)]
    return lax.ppermute(high, "space", up), lax.ppermute(low, "space", down)


def halves(count):
    spans, begin = [], 0
    while begin < count:
        many = max(1, (count - begin) // 2)
        spans.append((begin, many))
        begin += many
    return spans


def shards(
    adjoint_forcing,
    forward_state,
    wind_speed,
    cg_index,
    turn_index,
    sea_mask,
    dir_sign,
    w_in,
    w_out,
    wind_weight,
):
    parts = lax.axis_size("comp")
    own_place = lax.axis_index("comp")
    own = own_place.astype(jnp.int32).reshape(1)
    dirs = dir_sign.shape[1]
    comps, rows, cols = adjoint_forcing.shape
    freqs = comps // dirs
    local = rows // parts
    along = jnp.asarray(direction_factors(dirs))
    forcing = adjoint_forcing.reshape(freqs, dirs, rows, cols)
    weight = wind_weight[:, None]
    wind = wind_speed[:, None]
    everything = [(0, freqs)]
    many = freqs // 2 if freqs % 2 == 0 else freqs
    groups = [(begin, many) for begin in range(0, freqs, many)]
    sent = halves(freqs)
    levels = (cg_index, turn_index, sea_mask)
    if local > HALO:
        chunks = [(HALO, 0, local - HALO), (0, local - HALO, HALO)]
    else:
        chunks = [(0, 0, local)]
    ahead = chunks[0] if len(chunks) > 1 else None

    early, into, after = [], None, sea_mask
    for group in groups:
        into, pieces = inner(own, dir_sign, along, after, forcing, *levels, into, parts, ahead, group)
        if ahead:
            early.append(swapped(pieces))
    home, low, high = into
    above, below = across(low, high)
    after = arrived(home, early[0][1:])[0] if len(early) > 1 else home
    state = by_row(after, forward_state)
    in_t, out_t = turned(state, w_in, w_out)
    share, pieces = outer(own, dir_sign, along, in_t, above, below, *levels, home, parts, chunks[-1])
    late = swapped(pieces)
    term = functools.partial(source_term, own)
    fixed = (state, wind, w_in, out_t, in_t, weight)
    after, grads, early_back, rows_of = share, [], [], []
    if ahead:
        count = ahead[2]
        rows_of = [(0, count // 2), (count // 2, count - count // 2)] if count > 1 else [(0, count)]
    for span in rows_of:
        grad, [back] = term(after, *fixed, early, groups, everything, span, ahead)
        after = grad
        if not grads:
            after, rest = arrived(grad, late[1:], back[1:])
            back = [back[0], *rest]
        grads.append(grad)
        early_back.append(swapped(back))
    late_grad, late_back = term(after, *fixed, [late], everything, sent, (0, chunks[-1][2]), chunks[-1])
    start, returned = late_grad, []
    for g, pieces in enumerate(late_back):
        if g < len(early_back):
            rest = [piece for group in late_back[g:] for piece in group[1:]]
            start, rest = arrived(start, early_back[g][1:], rest)
            for n, group in enumerate(late_back[g:]):
                late_back[g + n] = [group[0], *rest[n * (parts - 1) : (n + 1) * (parts - 1)]]
        returned.append(swapped(late_back[g]))
    late_back = returned
    for group, back in zip(sent, late_back, strict=True):
        start = join(own, start, home, share, early_back, back, rows_of, chunks, group)
    gradient = jnp.where(
        own_place == 0, jnp.concatenate([late_grad, *grads], axis=0), jnp.concatenate([*grads, late_grad], axis=0)
    )
    return (start.reshape(comps, rows, cols), gradient.reshape(wind_speed.shape))


def solution(mesh):
    placed = (
        P("comp", "space", None),
        P(None, ("space", "comp"), None),
        P(("space", "comp"), None),
        P("comp", "space", None),
        P("comp", "space", None),
        P("space", None),
        P(),
        P(),
        P(),
        P(),
    )
    return jax.shard_map(
        shards,
        mesh=mesh,
        in_specs=placed,
        out_specs=(P("comp", "space", None), P(("space", "comp"), None)),
        check_vma=False,
    )
```

time: 185 us -> 187 us (1.011)
  waiting for transfers between devices: 18.6 us -> 24.3 us
    ppermute x24, waiting for transfers between devices: 16.9 us -> 24.3 us  [swapped(): lax.ppermute(pieces[k], 'comp', [(i, i ^ k) for i in range(parts)])]
    pallas_call x7 -> x10, Pallas kernels: 61.4 us -> 60.6 us  [the longest x2 27.1 us: inner(): pl.pallas_call(functools.partial(inner_kernel, parts, local, chunk, into...]
    unnamed x59 -> x56, local copies, waits for them, and re-layouts: 6.16 us -> 6.6 us
  transfers between devices with their start and end apart: 26 -> 26, of which waited for: 6 -> 5; matrix products, arithmetic and copies ran while one was open for 3% -> 2% of each run, Pallas kernels for 56% -> 57%
where the time goes in v4:
time: 187 us; the launch traced here: 186 us
  Pallas kernels  127 us (68%)
  starting transfers between devices  25.4 us (14%)
  waiting for transfers between devices  24.3 us (13%)
  local copies, waits for them, and re-layouts  8.4 us (4%)
    pallas_call x3, Pallas kernels, source_term(): pl.pallas_call(functools.partial(source_kernel, parts, got, sent, dirs, 2...  53.3 us
    pallas_call x2, Pallas kernels, inner(): pl.pallas_call(functools.partial(inner_kernel, parts, local, chunk, into...  27.1 us
    ppermute x24, waiting for transfers between devices, swapped(): lax.ppermute(pieces[k], 'comp', [(i, i ^ k) for i in range(parts)])  24.3 us
    ppermute x24, starting transfers between devices, swapped(): lax.ppermute(pieces[k], 'comp', [(i, i ^ k) for i in range(parts)])  19.7 us
    pallas_call x3, Pallas kernels, join(): pl.pallas_call(functools.partial(join_kernel, parts, spans), grid=(many,...  18.2 us
    pallas_call x1, Pallas kernels, outer(): pl.pallas_call(functools.partial(outer_kernel, parts, local, chunk), grid...  12.9 us
    pallas_call x1, Pallas kernels, by_row(): pl.pallas_call(by_row_kernel, grid=(cols // LANES,), in_specs=[UNREAD, pl...  8.64 us
    unnamed x56, local copies, waits for them, and re-layouts  6.6 us
  transfers between devices with their start and end apart: 26, of which 5 were waited for; matrix products, arithmetic and copies ran while one was open for 2% of the time, Pallas kernels for 57%

profile of v4, /device:TPU:0, one launch (start us, length us, event | category | flops | bytes accessed | tf_op | source)
XLA Modules:
  0.0 186.4 jit_solution(3699119049500270319)
XLA Ops:
  0.6 13.6 %shard_map.122 = (f32[4,24,32,1024]{3,2,1,0:T(8,128)}, bf16[2,4,32,1024]{3,2,1,0:T(8,128)(2,1)}, bf16[2,4,32,1024]{3,2,1,0:T(8,128)(2,1)}, bf16[6,2,24,1024]{3,2...) custom-call(s32[1]{0:T(128)} %bitcast.own_ref.refs_0_, ...), custom_call_target="tpu_custom_call" | custom-call | flops 1 | bytes 1 | tf_op jit(solution)/shard_map/pallas_call | solution.py:175
  14.7 2.6 %collective-permute-start.1 = (bf16[6,2,24,1024]{3,2,1,0:T(8,128)(2,1)}, bf16[6,2,24,1024]{3,2,1,0:T(8,128)(2,1)S(1)}, u32[]{:S(2)}, u32[]{:S(2)}) collective-permute-start(bf16[6,2,24,1024]{3,2,1,0:T(8,128)(2,1)} %get-tuple-element.72), channel_id=1, source_target_pairs={{0,16},{8,24},{16,0},{24,8},{1,17},{9,25},{17,1},{25,9},{2,18},{10... | collective-permute-start | bytes 1769480 | tf_op jit(solution)/shard_map/ppermute | solution.py:508
  17.4 13.5 %shard_map.123 = (f32[4,24,32,1024]{3,2,1,0:T(8,128)}, bf16[2,4,32,1024]{3,2,1,0:T(8,128)(2,1)}, bf16[2,4,32,1024]{3,2,1,0:T(8,128)(2,1)}, bf16[6,2,24,1024]{3,2...) custom-call(s32[1]{0:T(128)} %bitcast.own_ref.refs_0_, ...), custom_call_target="tpu_custom_call", output_to_operand_aliasing={{0}: (8, {}), {1}: (9, {}), {2}: (10, {})} | custom-call | flops 1 | bytes 1 | tf_op jit(solution)/shard_map/pallas_call | solution.py:175
  30.9 4.4 %collective-permute-start.3 = (bf16[2,4,32,1024]{3,2,1,0:T(8,128)(2,1)}, bf16[2,4,32,1024]{3,2,1,0:T(8,128)(2,1)}, u32[]{:S(2)}, u32[]{:S(2)}) collective-permute-start(bf16[2,4,32,1024]{3,2,1,0:T(8,128)(2,1)} %get-tuple-element.75), channel_id=1, source_target_pairs={{0,1},{1,2},{2,3},{3,4},{4,5},{5,6},{6,7},{8,9},{9,10},{10,11},{11... | collective-permute-start | bytes 1572872 | tf_op jit(solution)/shard_map/ppermute | solution.py:516
  35.3 1.3 collective-permute-start.4
  36.8 1.5 collective-permute-start.6
  38.3 5.6 %collective-permute-done.2.refs_3_ = bf16[6,2,24,1024]{3,2,1,0:T(8,128)(2,1)S(1)} collective-permute-done((bf16[6,2,24,1024]{3,2,1,0:T(8,128)(2,1)}, bf16[6,2,24,1024]{3,2,1,0:T(8,128)(2,1)S(1)}, u32[]{:S(2)}, u32[]{:S(2)}) %collective-permute-start.2) | collective-permute-done | bytes 589856 | tf_op jit(solution)/shard_map/ppermute | solution.py:508
  43.9 2.2 %collective-permute-start.7 = (bf16[6,2,24,1024]{3,2,1,0:T(8,128)(2,1)}, bf16[6,2,24,1024]{3,2,1,0:T(8,128)(2,1)S(1)}, u32[]{:S(2)}, u32[]{:S(2)}) collective-permute-start(bf16[6,2,24,1024]{3,2,1,0:T(8,128)(2,1)} %get-tuple-element.83), channel_id=1, source_target_pairs={{0,24},{8,16},{16,8},{24,0},{1,25},{9,17},{17,9},{25,1},{2,26},{10... | collective-permute-start | bytes 1769480 | tf_op jit(solution)/shard_map/ppermute | solution.py:508
  46.1 0.6 shard_map.124._
  46.7 8.6 %shard_map.125._.state_ref = bf16[8,384,1024]{2,1,0:T(8,128)(2,1)} custom-call(f32[8,128]{1,0:T(8,128)} %shard_map.124._, bf16[384,8,1024]{2,1,0:T(8,128)(2,1)} %state_ref.1), custom_call_target="tpu_custom_call" | custom-call | flops 1 | bytes 1 | tf_op jit(solution)/shard_map/pallas_call | solution.py:319
  55.4 4.1 %shard_map.126 = (bf16[384,1536]{1,0:T(8,128)(2,1)}, bf16[1536,384]{1,0:T(8,128)(2,1)}) custom-call(bf16[8,384,1024]{2,1,0:T(8,128)(2,1)} %shard_map.125._.state_ref, bf16[1536,384]{1,0:T(8,128)(2,1)} %w_in_ref.7, bf16[384,1536]{1,0:T(8,128)(2,1)} %w_out_ref.1), custom_call_target="tpu_custom_call" | custom-call | flops 1 | bytes 1 | tf_op jit(solution)/shard_map/pallas_call | solution.py:341
  59.5 12.9 %shard_map.127 = (f32[4,24,8,1024]{3,2,1,0:T(8,128)}, bf16[2,4,24,1024]{3,2,1,0:T(8,128)(2,1)}, bf16[2,4,24,1024]{3,2,1,0:T(8,128)(2,1)}, bf16[2,4,24,1024]{3,2,1,0:T(8,128)(2,1)}, bf16[2,4,24,1024]{3,2,1,0:T(8,128)(2,1)}) custom-call(s32[1]{0:T(128)} %bitcast.own_ref.refs_0_, s32[2,24]{1,0:T(2,128)} %refs_1_.1, f32[2,24]{1,0:T(2,128)} %constant.9.clone.along_ref.refs_2_, ...), custom_call_target="tpu_custom_call" | custom-call | flops 99999997952 | bytes 104857600 | tf_op jit(solution)/shard_map/pallas_call | solution.py:277
  72.4 1.2 collective-permute-start.9
  73.7 0.6 collective-permute-start.10
  74.3 0.6 broadcast_in_dim.6.wind_ref
  74.9 1.2 broadcast_in_dim.8.weight_ref
  76.1 0.8 copy-done.10
  77.1 19.5 %shard_map.128 = (f32[3,1,1024]{2,1,0:T(1,128)}, bf16[3,4,24,1024]{3,2,1,0:T(8,128)(2,1)}, bf16[3,4,24,1024]{3,2,1,0:T(8,128)(2,1)}, bf16[3,4,24,1024]{3,2,1,0:T(8,128)(2,1)}, bf16[3,4,24,1024]{3,2,1,0:T(8,128)(2,1)}) custom-call(s32[1]{0:T(128)} %bitcast.own_ref.refs_0_, f32[4,24,8,1024]{3,2,1,0:T(8,128)} %get-tuple-element.77._.share_ref, ...), custom_call_target="tpu_custom_call" | custom-call | flops 1 | bytes 1 | tf_op jit(solution)/shard_map/pallas_call | solution.py:407
  96.7 0.7 copy-done.12
  97.7 0.6 shard_map.129
  98.7 1.2 collective-permute-start.12
  100.2 19.6 %shard_map.130 = (f32[3,1,1024]{2,1,0:T(1,128)}, bf16[3,4,24,1024]{3,2,1,0:T(8,128)(2,1)}, bf16[3,4,24,1024]{3,2,1,0:T(8,128)(2,1)}, bf16[3,4,24,1024]{3,2,1,0:T(8,128)(2,1)}, bf16[3,4,24,1024]{3,2,1,0:T(8,128)(2,1)}) custom-call(s32[1]{0:T(128)} %bitcast.own_ref.refs_0_, f32[8,128]{1,0:T(8,128)} %get-tuple-element.91._, ...), custom_call_target="tpu_custom_call" | custom-call | flops 1 | bytes 1 | tf_op jit(solution)/shard_map/pallas_call | solution.py:407
  119.8 0.7 collective-permute-start.14
  120.5 1.2 collective-permute-start.15
  121.9 14.1 %shard_map.131 = (f32[2,1,1024]{2,1,0:T(1,128)}, bf16[2,2,24,1024]{3,2,1,0:T(8,128)(2,1)}, bf16[2,2,24,1024]{3,2,1,0:T(8,128)(2,1)}, bf16[2,2,24,1024]{3,2,1,0:T...) custom-call(s32[1]{0:T(128)} %bitcast.own_ref.refs_0_, ...), custom_call_target="tpu_custom_call" | custom-call | flops 1 | bytes 1 | tf_op jit(solution)/shard_map/pallas_call | solution.py:407
  136.1 0.8 copy-done.1
  137.1 0.6 shard_map.132
  137.7 2.7 %collective-permute-done.15.refs_2_.refs_6_ = bf16[3,4,24,1024]{3,2,1,0:T(8,128)(2,1)S(1)} collective-permute-done((bf16[3,4,24,1024]{3,2,1,0:T(8,128)(2,1)}, bf16[3,4,24,1024]{3,2,1,0:T(8,128)(2,1)S(1)}, u32[]{:S(2)}, u32[]{:S(2)}) %collective-permute-start.15) | collective-permute-done | bytes 589856 | tf_op jit(solution)/shard_map/ppermute | solution.py:508
  140.3 11.1 %collective-permute-done.16.refs_3_.refs_7_ = bf16[3,4,24,1024]{3,2,1,0:T(8,128)(2,1)S(1)} collective-permute-done((bf16[3,4,24,1024]{3,2,1,0:T(8,128)(2,1)}, bf16[3,4,24,1024]{3,2,1,0:T(8,128)(2,1)S(1)}, u32[]{:S(2)}, u32[]{:S(2)}) %collective-permute-start.16) | collective-permute-done | bytes 589856 | tf_op jit(solution)/shard_map/ppermute | solution.py:508
  151.4 0.8 copy-done.5
  152.2 0.6 shard_map.133
  152.8 0.6 collective-permute-start.20
  153.4 1.0 collective-permute-start.18
  154.4 0.8 collective-permute-start.19
  155.3 0.7 copy_bitcast_fusion
  156.0 0.7 copy.45
  156.7 1.0 collective-permute-start.21
  157.7 0.6 collective-permute-start.22
  158.9 2.5 %collective-permute-done.18.refs_10_ = bf16[2,2,24,1024]{3,2,1,0:T(8,128)(2,1)S(1)} collective-permute-done((bf16[2,2,24,1024]{3,2,1,0:T(8,128)(2,1)}, bf16[2,2,24,1024]{3,2,1,0:T(8,128)(2,1)S(1)}, u32[]{:S(2)}, u32[]{:S(2)}) %collective-permute-start.18) | collective-permute-done | bytes 196640 | tf_op jit(solution)/shard_map/ppermute | solution.py:508
  161.3 1.0 collective-permute-start.24
  162.4 2.4 %collective-permute-done.19.refs_11_ = bf16[2,2,24,1024]{3,2,1,0:T(8,128)(2,1)S(1)} collective-permute-done((bf16[2,2,24,1024]{3,2,1,0:T(8,128)(2,1)}, bf16[2,2,24,1024]{3,2,1,0:T(8,128)(2,1)S(1)}, u32[]{:S(2)}, u32[]{:S(2)}) %collective-permute-start.19) | collective-permute-done | bytes 196640 | tf_op jit(solution)/shard_map/ppermute | solution.py:508
  164.8 1.2 collective-permute-start.25
  166.0 0.6 maximum_select_fusion
  166.6 8.7 %shard_map.134._ = f32[4,24,32,1024]{3,2,1,0:T(8,128)} custom-call(s32[1]{0:T(128)} %bitcast.own_ref.refs_0_, f32[8,128]{1,0:T(8,128)} %get-tuple-element.117._, f32[4,24,32,1024]{3,2,1,0:T(8,128)} %get-tuple-element.70.refs_0_.refs_9_.home_ref, f32[4,24,8,1024]{3,2,1,0:T(8,128)} %get-tuple-element.77._.share_ref, ...), custom_call_target="tpu_custom_call" | custom-call | flops 1 | bytes 1 | tf_op jit(solution)/shard_map/pallas_call | solution.py:475
  175.4 0.6 copy-done.21
  176.1 4.7 %shard_map.135._ = f32[4,24,32,1024]{3,2,1,0:T(8,128)} custom-call(s32[1]{0:T(128)} %bitcast.own_ref.refs_0_, f32[4,24,32,1024]{3,2,1,0:T(8,128)} %shard_map.134._, f32[4,24,32,1024]{3,2,1,0:T(8,128)} %get-tuple-element.70.refs_0_.refs_9_.home_ref, f32[4,24,8,1024]{3,2,1,0:T(8,128)} %get-tuple-element.77._.share_ref, ...), custom_call_target="tpu_custom_call", output_to_operand_aliasing={{}: (1, {})} | custom-call | flops 1 | bytes 1 | tf_op jit(solution)/shard_map/pallas_call | solution.py:475
  180.9 0.6 copy-done.19
  181.6 4.7 %shard_map.136 = f32[4,24,32,1024]{3,2,1,0:T(8,128)} custom-call(s32[1]{0:T(128)} %bitcast.own_ref.refs_0_, f32[4,24,32,1024]{3,2,1,0:T(8,128)} %shard_map.135._, f32[4,24,32,1024]{3,2,1,0:T(8,128)} %get-tuple-element.70.refs_0_.refs_9_.home_ref, f32[4,24,8,1024]{3,2,1,0:T(8,128)} %get-tuple-element.77._.share_ref, ...), custom_call_target="tpu_custom_call", output_to_operand_aliasing={{}: (1, {})} | custom-call | flops 1 | bytes 1 | tf_op jit(solution)/shard_map/pallas_call | solution.py:475
  (78 shorter events, 3.1 us)
Async XLA Ops:
  14.2 22.4 %collective-permute-start = (bf16[6,2,24,1024]{3,2,1,0:T(8,128)(2,1)}, bf16[6,2,24,1024]{3,2,1,0:T(8,128)(2,1)S(1)}, u32[]{:S(2)}, u32[]{:S(2)}) collective-permute-start(bf16[6,2,24,1024]{3,2,1,0:T(8,128)(2,1)} %get-tuple-element.71), channel_id=1, source_target_pairs={{0,8},{8,0},{16,24},{24,16},{1,9},{9,1},{17,25},{25,17},{2,10},{10... | collective-permute-start | bytes 1769480 | tf_op jit(solution)/shard_map/ppermute | solution.py:508
  14.7 22.0 %collective-permute-start.1 = (bf16[6,2,24,1024]{3,2,1,0:T(8,128)(2,1)}, bf16[6,2,24,1024]{3,2,1,0:T(8,128)(2,1)S(1)}, u32[]{:S(2)}, u32[]{:S(2)}) collective-permute-start(bf16[6,2,24,1024]{3,2,1,0:T(8,128)(2,1)} %get-tuple-element.72), channel_id=1, source_target_pairs={{0,16},{8,24},{16,0},{24,8},{1,17},{9,25},{17,1},{25,9},{2,18},{10... | collective-permute-start | bytes 1769480 | tf_op jit(solution)/shard_map/ppermute | solution.py:508
  17.3 26.6 %collective-permute-start.2 = (bf16[6,2,24,1024]{3,2,1,0:T(8,128)(2,1)}, bf16[6,2,24,1024]{3,2,1,0:T(8,128)(2,1)S(1)}, u32[]{:S(2)}, u32[]{:S(2)}) collective-permute-start(bf16[6,2,24,1024]{3,2,1,0:T(8,128)(2,1)} %get-tuple-element.73), channel_id=1, source_target_pairs={{0,24},{8,16},{16,8},{24,0},{1,25},{9,17},{17,9},{25,1},{2,26},{10... | collective-permute-start | bytes 1769480 | tf_op jit(solution)/shard_map/ppermute | solution.py:508
  30.9 28.5 %collective-permute-start.3 = (bf16[2,4,32,1024]{3,2,1,0:T(8,128)(2,1)}, bf16[2,4,32,1024]{3,2,1,0:T(8,128)(2,1)}, u32[]{:S(2)}, u32[]{:S(2)}) collective-permute-start(bf16[2,4,32,1024]{3,2,1,0:T(8,128)(2,1)} %get-tuple-element.75), channel_id=1, source_target_pairs={{0,1},{1,2},{2,3},{3,4},{4,5},{5,6},{6,7},{8,9},{9,10},{10,11},{11... | collective-permute-start | bytes 1572872 | tf_op jit(solution)/shard_map/ppermute | solution.py:516
  35.3 24.1 %collective-permute-start.4 = (bf16[2,4,32,1024]{3,2,1,0:T(8,128)(2,1)}, bf16[2,4,32,1024]{3,2,1,0:T(8,128)(2,1)}, u32[]{:S(2)}, u32[]{:S(2)}) collective-permute-start(bf16[2,4,32,1024]{3,2,1,0:T(8,128)(2,1)} %get-tuple-element.76), channel_id=1, source_target_pairs={{1,0},{2,1},{3,2},{4,3},{5,4},{6,5},{7,6},{9,8},{10,9},{11,10},{12... | collective-permute-start | bytes 1572872 | tf_op jit(solution)/shard_map/ppermute | solution.py:516
  36.6 9.5 %copy-start.6 = (bf16[6,2,24,1024]{3,2,1,0:T(8,128)(2,1)}, bf16[6,2,24,1024]{3,2,1,0:T(8,128)(2,1)S(1)}, u32[]{:S(2)}) copy-start(bf16[6,2,24,1024]{3,2,1,0:T(8,128)(2,1)S(1)} %collective-permute-done.refs_1_) | copy-start | bytes 1769476
  36.6 37.0 %collective-permute-start.5 = (bf16[6,2,24,1024]{3,2,1,0:T(8,128)(2,1)}, bf16[6,2,24,1024]{3,2,1,0:T(8,128)(2,1)S(1)}, u32[]{:S(2)}, u32[]{:S(2)}) collective-permute-start(bf16[6,2,24,1024]{3,2,1,0:T(8,128)(2,1)} %get-tuple-element.81), channel_id=1, source_target_pairs={{0,8},{8,0},{16,24},{24,16},{1,9},{9,1},{17,25},{25,17},{2,10},{10... | collective-permute-start | bytes 1769480 | tf_op jit(solution)/shard_map/ppermute | solution.py:508
  36.8 9.4 %copy-start.7 = (bf16[6,2,24,1024]{3,2,1,0:T(8,128)(2,1)}, bf16[6,2,24,1024]{3,2,1,0:T(8,128)(2,1)S(1)}, u32[]{:S(2)}) copy-start(bf16[6,2,24,1024]{3,2,1,0:T(8,128)(2,1)S(1)} %collective-permute-done.1.refs_2_) | copy-start | bytes 1769476
  36.8 39.3 %collective-permute-start.6 = (bf16[6,2,24,1024]{3,2,1,0:T(8,128)(2,1)}, bf16[6,2,24,1024]{3,2,1,0:T(8,128)(2,1)S(1)}, u32[]{:S(2)}, u32[]{:S(2)}) collective-permute-start(bf16[6,2,24,1024]{3,2,1,0:T(8,128)(2,1)} %get-tuple-element.82), channel_id=1, source_target_pairs={{0,16},{8,24},{16,0},{24,8},{1,17},{9,25},{17,1},{25,9},{2,18},{10... | collective-permute-start | bytes 1769480 | tf_op jit(solution)/shard_map/ppermute | solution.py:508
  43.9 2.2 %copy-start.8 = (bf16[6,2,24,1024]{3,2,1,0:T(8,128)(2,1)}, bf16[6,2,24,1024]{3,2,1,0:T(8,128)(2,1)S(1)}, u32[]{:S(2)}) copy-start(bf16[6,2,24,1024]{3,2,1,0:T(8,128)(2,1)S(1)} %collective-permute-done.2.refs_3_) | copy-start | bytes 1769476
  43.9 32.2 %collective-permute-start.7 = (bf16[6,2,24,1024]{3,2,1,0:T(8,128)(2,1)}, bf16[6,2,24,1024]{3,2,1,0:T(8,128)(2,1)S(1)}, u32[]{:S(2)}, u32[]{:S(2)}) collective-permute-start(bf16[6,2,24,1024]{3,2,1,0:T(8,128)(2,1)} %get-tuple-element.83), channel_id=1, source_target_pairs={{0,24},{8,16},{16,8},{24,0},{1,25},{9,17},{17,9},{25,1},{2,26},{10... | collective-permute-start | bytes 1769480 | tf_op jit(solution)/shard_map/ppermute | solution.py:508
  59.4 14.8 %copy-start.25 = (f32[8,1024]{1,0:T(8,128)S(1)}, f32[8,1024]{1,0:T(8,128)}, u32[]{:S(2)}) copy-start(f32[8,1024]{1,0:T(8,128)} %param.13) | copy-start | bytes 98308
  59.5 15.5 %copy-start.26 = (f32[1536]{0:T(1024)S(1)}, f32[1536]{0:T(1024)}, u32[]{:S(2)}) copy-start(f32[1536]{0:T(1024)} %param.20) | copy-start | bytes 18436
  72.4 24.3 %collective-permute-start.8 = (bf16[2,4,24,1024]{3,2,1,0:T(8,128)(2,1)}, bf16[2,4,24,1024]{3,2,1,0:T(8,128)(2,1)S(1)}, u32[]{:S(2)}, u32[]{:S(2)}) collective-permute-start(bf16[2,4,24,1024]{3,2,1,0:T(8,128)(2,1)} %get-tuple-element.85), channel_id=1, source_target_pairs={{0,8},{8,0},{16,24},{24,16},{1,9},{9,1},{17,25},{25,17},{2,10},{10... | collective-permute-start | bytes 1179656 | tf_op jit(solution)/shard_map/ppermute | solution.py:508
  72.4 24.3 %collective-permute-start.9 = (bf16[2,4,24,1024]{3,2,1,0:T(8,128)(2,1)}, bf16[2,4,24,1024]{3,2,1,0:T(8,128)(2,1)S(1)}, u32[]{:S(2)}, u32[]{:S(2)}) collective-permute-start(bf16[2,4,24,1024]{3,2,1,0:T(8,128)(2,1)} %get-tuple-element.86), channel_id=1, source_target_pairs={{0,16},{8,24},{16,0},{24,8},{1,17},{9,25},{17,1},{25,9},{2,18},{10... | collective-permute-start | bytes 1179656 | tf_op jit(solution)/shard_map/ppermute | solution.py:508
  73.7 2.5 %copy-start.9 = (bf16[6,2,24,1024]{3,2,1,0:T(8,128)(2,1)}, bf16[6,2,24,1024]{3,2,1,0:T(8,128)(2,1)S(1)}, u32[]{:S(2)}) copy-start(bf16[6,2,24,1024]{3,2,1,0:T(8,128)(2,1)S(1)} %collective-permute-done.5.refs_5_) | copy-start | bytes 1769476
  73.7 23.0 %collective-permute-start.10 = (bf16[2,4,24,1024]{3,2,1,0:T(8,128)(2,1)}, bf16[2,4,24,1024]{3,2,1,0:T(8,128)(2,1)S(1)}, u32[]{:S(2)}, u32[]{:S(2)}) collective-permute-start(bf16[2,4,24,1024]{3,2,1,0:T(8,128)(2,1)} %get-tuple-element.87), channel_id=1, source_target_pairs={{0,24},{8,16},{16,8},{24,0},{1,25},{9,17},{17,9},{25,1},{2,26},{10... | collective-permute-start | bytes 1179656 | tf_op jit(solution)/shard_map/ppermute | solution.py:508
  76.1 0.8 copy-start.10
  76.1 1.0 copy-start.11
  96.7 0.8 copy-start.12
  96.7 0.9 copy-start.13
  96.7 1.0 copy-start.14
  98.3 23.3 %collective-permute-start.11 = (bf16[3,4,24,1024]{3,2,1,0:T(8,128)(2,1)}, bf16[3,4,24,1024]{3,2,1,0:T(8,128)(2,1)S(1)}, u32[]{:S(2)}, u32[]{:S(2)}) collective-permute-start(bf16[3,4,24,1024]{3,2,1,0:T(8,128)(2,1)} %get-tuple-element.95), channel_id=1, source_target_pairs={{0,8},{8,0},{16,24},{24,16},{1,9},{9,1},{17,25},{25,17},{2,10},{10... | collective-permute-start | bytes 1769480 | tf_op jit(solution)/shard_map/ppermute | solution.py:508
  98.7 37.4 %collective-permute-start.12 = (bf16[3,4,24,1024]{3,2,1,0:T(8,128)(2,1)}, bf16[3,4,24,1024]{3,2,1,0:T(8,128)(2,1)S(1)}, u32[]{:S(2)}, u32[]{:S(2)}) collective-permute-start(bf16[3,4,24,1024]{3,2,1,0:T(8,128)(2,1)} %get-tuple-element.96), channel_id=1, source_target_pairs={{0,16},{8,24},{16,0},{24,8},{1,17},{9,25},{17,1},{25,9},{2,18},{10... | collective-permute-start | bytes 1769480 | tf_op jit(solution)/shard_map/ppermute | solution.py:508
  99.8 36.2 %collective-permute-start.13 = (bf16[3,4,24,1024]{3,2,1,0:T(8,128)(2,1)}, bf16[3,4,24,1024]{3,2,1,0:T(8,128)(2,1)S(1)}, u32[]{:S(2)}, u32[]{:S(2)}) collective-permute-start(bf16[3,4,24,1024]{3,2,1,0:T(8,128)(2,1)} %get-tuple-element.97), channel_id=1, source_target_pairs={{0,24},{8,16},{16,8},{24,0},{1,25},{9,17},{17,9},{25,1},{2,26},{10... | collective-permute-start | bytes 1769480 | tf_op jit(solution)/shard_map/ppermute | solution.py:508
  119.8 17.9 %collective-permute-start.14 = (bf16[3,4,24,1024]{3,2,1,0:T(8,128)(2,1)}, bf16[3,4,24,1024]{3,2,1,0:T(8,128)(2,1)S(1)}, u32[]{:S(2)}, u32[]{:S(2)}) collective-permute-start(bf16[3,4,24,1024]{3,2,1,0:T(8,128)(2,1)} %get-tuple-element.108), channel_id=1, source_target_pairs={{0,8},{8,0},{16,24},{24,16},{1,9},{9,1},{17,25},{25,17},{2,10},{10... | collective-permute-start | bytes 1769480 | tf_op jit(solution)/shard_map/ppermute | solution.py:508
  120.5 19.8 %collective-permute-start.15 = (bf16[3,4,24,1024]{3,2,1,0:T(8,128)(2,1)}, bf16[3,4,24,1024]{3,2,1,0:T(8,128)(2,1)S(1)}, u32[]{:S(2)}, u32[]{:S(2)}) collective-permute-start(bf16[3,4,24,1024]{3,2,1,0:T(8,128)(2,1)} %get-tuple-element.109), channel_id=1, source_target_pairs={{0,16},{8,24},{16,0},{24,8},{1,17},{9,25},{17,1},{25,9},{2,18},{10... | collective-permute-start | bytes 1769480 | tf_op jit(solution)/shard_map/ppermute | solution.py:508
  121.7 14.4 %copy-start = (bf16[3,4,24,1024]{3,2,1,0:T(8,128)(2,1)}, bf16[3,4,24,1024]{3,2,1,0:T(8,128)(2,1)S(1)}, u32[]{:S(2)}) copy-start(bf16[3,4,24,1024]{3,2,1,0:T(8,128)(2,1)S(1)} %collective-permute-done.11.refs_1_) | copy-start | bytes 1769476
  121.7 29.7 %collective-permute-start.16 = (bf16[3,4,24,1024]{3,2,1,0:T(8,128)(2,1)}, bf16[3,4,24,1024]{3,2,1,0:T(8,128)(2,1)S(1)}, u32[]{:S(2)}, u32[]{:S(2)}) collective-permute-start(bf16[3,4,24,1024]{3,2,1,0:T(8,128)(2,1)} %get-tuple-element.110), channel_id=1, source_target_pairs={{0,24},{8,16},{16,8},{24,0},{1,25},{9,17},{17,9},{25,1},{2,26},{10... | collective-permute-start | bytes 1769480 | tf_op jit(solution)/shard_map/ppermute | solution.py:508
  121.9 33.4 %copy-start.24 = (f32[3,1,1024]{2,1,0:T(1,128)S(1)}, f32[3,1,1024]{2,1,0:T(1,128)}, u32[]{:S(2)}) copy-start(f32[3,1,1024]{2,1,0:T(1,128)} %get-tuple-element.84.refs_0_) | copy-start | bytes 36868
  136.1 0.8 copy-start.1
  136.1 1.0 copy-start.2
  137.7 13.8 %copy-start.3 = (bf16[3,4,24,1024]{3,2,1,0:T(8,128)(2,1)}, bf16[3,4,24,1024]{3,2,1,0:T(8,128)(2,1)S(1)}, u32[]{:S(2)}) copy-start(bf16[3,4,24,1024]{3,2,1,0:T(8,128)(2,1)S(1)} %collective-permute-done.14.refs_1_.refs_5_) | copy-start | bytes 1769476
  140.3 11.1 %copy-start.4 = (bf16[3,4,24,1024]{3,2,1,0:T(8,128)(2,1)}, bf16[3,4,24,1024]{3,2,1,0:T(8,128)(2,1)S(1)}, u32[]{:S(2)}) copy-start(bf16[3,4,24,1024]{3,2,1,0:T(8,128)(2,1)S(1)} %collective-permute-done.15.refs_2_.refs_6_) | copy-start | bytes 1769476
  151.4 0.8 copy-start.5
  152.8 4.9 %collective-permute-start.20 = (bf16[2,1,24,1024]{3,2,1,0:T(8,128)(2,1)}, bf16[2,1,24,1024]{3,2,1,0:T(8,128)(2,1)S(1)}, u32[]{:S(2)}, u32[]{:S(2)}) collective-permute-start(bf16[2,1,24,1024]{3,2,1,0:T(8,128)(2,1)} %get-tuple-element.125), channel_id=1, source_target_pairs={{0,8},{8,0},{16,24},{24,16},{1,9},{9,1},{17,25},{25,17},{2,10},{10... | collective-permute-start | bytes 294920 | tf_op jit(solution)/shard_map/ppermute | solution.py:508
  153.4 4.9 %collective-permute-start.17 = (bf16[2,2,24,1024]{3,2,1,0:T(8,128)(2,1)}, bf16[2,2,24,1024]{3,2,1,0:T(8,128)(2,1)S(1)}, u32[]{:S(2)}, u32[]{:S(2)}) collective-permute-start(bf16[2,2,24,1024]{3,2,1,0:T(8,128)(2,1)} %get-tuple-element.121), channel_id=1, source_target_pairs={{0,8},{8,0},{16,24},{24,16},{1,9},{9,1},{17,25},{25,17},{2,10},{10... | collective-permute-start | bytes 589832 | tf_op jit(solution)/shard_map/ppermute | solution.py:508
  153.4 7.9 %collective-permute-start.18 = (bf16[2,2,24,1024]{3,2,1,0:T(8,128)(2,1)}, bf16[2,2,24,1024]{3,2,1,0:T(8,128)(2,1)S(1)}, u32[]{:S(2)}, u32[]{:S(2)}) collective-permute-start(bf16[2,2,24,1024]{3,2,1,0:T(8,128)(2,1)} %get-tuple-element.122), channel_id=1, source_target_pairs={{0,16},{8,24},{16,0},{24,8},{1,17},{9,25},{17,1},{25,9},{2,18},{10... | collective-permute-start | bytes 589832 | tf_op jit(solution)/shard_map/ppermute | solution.py:508
  154.4 10.3 %collective-permute-start.19 = (bf16[2,2,24,1024]{3,2,1,0:T(8,128)(2,1)}, bf16[2,2,24,1024]{3,2,1,0:T(8,128)(2,1)S(1)}, u32[]{:S(2)}, u32[]{:S(2)}) collective-permute-start(bf16[2,2,24,1024]{3,2,1,0:T(8,128)(2,1)} %get-tuple-element.123), channel_id=1, source_target_pairs={{0,24},{8,16},{16,8},{24,0},{1,25},{9,17},{17,9},{25,1},{2,26},{10... | collective-permute-start | bytes 589832 | tf_op jit(solution)/shard_map/ppermute | solution.py:508
  156.7 18.7 %collective-permute-start.21 = (bf16[2,1,24,1024]{3,2,1,0:T(8,128)(2,1)}, bf16[2,1,24,1024]{3,2,1,0:T(8,128)(2,1)S(1)}, u32[]{:S(2)}, u32[]{:S(2)}) collective-permute-start(bf16[2,1,24,1024]{3,2,1,0:T(8,128)(2,1)} %get-tuple-element.126), channel_id=1, source_target_pairs={{0,16},{8,24},{16,0},{24,8},{1,17},{9,25},{17,1},{25,9},{2,18},{10... | collective-permute-start | bytes 294920 | tf_op jit(solution)/shard_map/ppermute | solution.py:508
  157.7 17.7 %copy-start.18 = (bf16[2,1,24,1024]{3,2,1,0:T(8,128)(2,1)}, bf16[2,1,24,1024]{3,2,1,0:T(8,128)(2,1)S(1)}, u32[]{:S(2)}) copy-start(bf16[2,1,24,1024]{3,2,1,0:T(8,128)(2,1)S(1)} %collective-permute-done.20.refs_9_) | copy-start | bytes 294916
  157.7 17.7 %collective-permute-start.22 = (bf16[2,1,24,1024]{3,2,1,0:T(8,128)(2,1)}, bf16[2,1,24,1024]{3,2,1,0:T(8,128)(2,1)S(1)}, u32[]{:S(2)}, u32[]{:S(2)}) collective-permute-start(bf16[2,1,24,1024]{3,2,1,0:T(8,128)(2,1)} %get-tuple-element.127), channel_id=1, source_target_pairs={{0,24},{8,16},{16,8},{24,0},{1,25},{9,17},{17,9},{25,1},{2,26},{10... | collective-permute-start | bytes 294920 | tf_op jit(solution)/shard_map/ppermute | solution.py:508
  158.4 8.3 %copy-start.15 = (bf16[2,2,24,1024]{3,2,1,0:T(8,128)(2,1)}, bf16[2,2,24,1024]{3,2,1,0:T(8,128)(2,1)S(1)}, u32[]{:S(2)}) copy-start(bf16[2,2,24,1024]{3,2,1,0:T(8,128)(2,1)S(1)} %collective-permute-done.17.refs_9_) | copy-start | bytes 589828
  158.4 22.4 %collective-permute-start.23 = (bf16[2,1,24,1024]{3,2,1,0:T(8,128)(2,1)}, bf16[2,1,24,1024]{3,2,1,0:T(8,128)(2,1)S(1)}, u32[]{:S(2)}, u32[]{:S(2)}) collective-permute-start(bf16[2,1,24,1024]{3,2,1,0:T(8,128)(2,1)} %get-tuple-element.129), channel_id=1, source_target_pairs={{0,8},{8,0},{16,24},{24,16},{1,9},{9,1},{17,25},{25,17},{2,10},{10... | collective-permute-start | bytes 294920 | tf_op jit(solution)/shard_map/ppermute | solution.py:508
  161.3 5.3 %copy-start.16 = (bf16[2,2,24,1024]{3,2,1,0:T(8,128)(2,1)}, bf16[2,2,24,1024]{3,2,1,0:T(8,128)(2,1)S(1)}, u32[]{:S(2)}) copy-start(bf16[2,2,24,1024]{3,2,1,0:T(8,128)(2,1)S(1)} %collective-permute-done.18.refs_10_) | copy-start | bytes 589828
  161.3 19.5 %collective-permute-start.24 = (bf16[2,1,24,1024]{3,2,1,0:T(8,128)(2,1)}, bf16[2,1,24,1024]{3,2,1,0:T(8,128)(2,1)S(1)}, u32[]{:S(2)}, u32[]{:S(2)}) collective-permute-start(bf16[2,1,24,1024]{3,2,1,0:T(8,128)(2,1)} %get-tuple-element.130), channel_id=1, source_target_pairs={{0,16},{8,24},{16,0},{24,8},{1,17},{9,25},{17,1},{25,9},{2,18},{10... | collective-permute-start | bytes 294920 | tf_op jit(solution)/shard_map/ppermute | solution.py:508
  164.8 1.9 %copy-start.17 = (bf16[2,2,24,1024]{3,2,1,0:T(8,128)(2,1)}, bf16[2,2,24,1024]{3,2,1,0:T(8,128)(2,1)S(1)}, u32[]{:S(2)}) copy-start(bf16[2,2,24,1024]{3,2,1,0:T(8,128)(2,1)S(1)} %collective-permute-done.19.refs_11_) | copy-start | bytes 589828
  164.8 16.1 %collective-permute-start.25 = (bf16[2,1,24,1024]{3,2,1,0:T(8,128)(2,1)}, bf16[2,1,24,1024]{3,2,1,0:T(8,128)(2,1)S(1)}, u32[]{:S(2)}, u32[]{:S(2)}) collective-permute-start(bf16[2,1,24,1024]{3,2,1,0:T(8,128)(2,1)} %get-tuple-element.131), channel_id=1, source_target_pairs={{0,24},{8,16},{16,8},{24,0},{1,25},{9,17},{17,9},{25,1},{2,26},{10... | collective-permute-start | bytes 294920 | tf_op jit(solution)/shard_map/ppermute | solution.py:508
  (5 other events, 3.3 us)

commit v5 on v4

--- a/solution.py
+++ b/solution.py
@@ -301,31 +301,36 @@
     return outs[0], list(outs[1:])
 
 
-def by_row_kernel(_, state_ref, out_ref, swap_ref):
-    deep, local, _ = state_ref.shape
-    pitch = deep + 1
+def by_row_kernel(*refs):
+    state_ref, out_ref, swap_ref = refs[-3:]
+    some, local, cols = state_ref.shape
+    pitch = some + 1
+    lanes = lane_tiles(cols)
 
     def body(d, carry):
-        swap_ref[pl.ds(d, local, stride=pitch), :] = state_ref[d].astype(jnp.float32)
+        for c, here in enumerate(lanes):
+            swap_ref[c, pl.ds(d, local, stride=pitch), :] = state_ref[d, :, here].astype(jnp.float32)
         return carry
 
-    lax.fori_loop(0, deep, body, 0, unroll=64)
+    lax.fori_loop(0, some, body, 0, unroll=8)
     for r in range(local):
-        out_ref[r] = swap_ref[pl.ds(r * pitch, deep), :].astype(jnp.bfloat16)
+        for c, here in enumerate(lanes):
+            out_ref[r, :, here] = swap_ref[c, pl.ds(r * pitch, some), :].astype(jnp.bfloat16)
 
 
 def by_row(after, state):
     deep, local, cols = state.shape
+    some = 48
     return pl.pallas_call(
         by_row_kernel,
-        grid=(cols // LANES,),
-        in_specs=[UNREAD, pl.BlockSpec((deep, local, LANES), lambda c: (0, 0, c))],
-        out_specs=pl.BlockSpec((local, deep, LANES), lambda c: (0, 0, c)),
+        grid=(deep // some,),
+        in_specs=[UNREAD] * len(after) + [pl.BlockSpec((some, local, cols), lambda d: (d, 0, 0))],
+        out_specs=pl.BlockSpec((local, some, cols), lambda d: (0, d, 0)),
         out_shape=jax.ShapeDtypeStruct((local, deep, cols), jnp.bfloat16),
-        scratch_shapes=[pltpu.VMEM((local * (deep + 1), LANES), jnp.float32)],
+        scratch_shapes=[pltpu.VMEM((cols // LANES, local * (some + 1), LANES), jnp.float32)],
         compiler_params=pltpu.CompilerParams(vmem_limit_bytes=VMEM_LIMIT),
         cost_estimate=COST,
-    )(after, state)
+    )(*after, state)
 
 
 def turned_kernel(_, w_in_ref, w_out_ref, in_t_ref, out_t_ref):
@@ -345,7 +350,7 @@
         out_specs=[wide, tall],
         out_shape=[jax.ShapeDtypeStruct((total, hidden), w_in.dtype), jax.ShapeDtypeStruct((hidden, total), w_in.dtype)],
         compiler_params=pltpu.CompilerParams(vmem_limit_bytes=VMEM_LIMIT),
-        cost_estimate=COST,
+        cost_estimate=LONG,
     )(after, w_in, w_out)
 
 
@@ -434,53 +439,59 @@
     return outs[0], [list(outs[1 + g * parts : 1 + (g + 1) * parts]) for g in range(len(sent))]
 
 
-def join_kernel(parts, spans, own_ref, _, home_ref, share_ref, *refs):
+def join_kernel(parts, local, spans, own_ref, _, home_ref, share_ref, *refs):
     out_ref, swap_ref = refs[-2:]
-    dirs, rows, cols = home_ref.shape[1:]
+    dirs, _, cols = home_ref.shape[1:]
     pitch = dirs + 1
-    local = rows // parts
     own = own_ref[0]
     lanes = lane_tiles(cols)
-    tiles = rows // TILE
-    for i, (first, count, chunk) in enumerate(spans):
-        for k in range(parts):
-            owner = own ^ k
-            for j in range(count):
-                start = (owner * local + chunk_row(owner, first + j, chunk)) * pitch
-                for c, here in enumerate(lanes):
-                    swap_ref[c, pl.ds(start, dirs), :] = refs[i * parts + k][j, 0, :, here].astype(jnp.float32)
+    t = pl.program_id(1)
+    tiles = pl.num_programs(1)
+
+    @pl.when(t == 0)
+    def _():
+        for i, (first, count, chunk) in enumerate(spans):
+            for k in range(parts):
+                owner = own ^ k
+                for j in range(count):
+                    start = (owner * local + chunk_row(owner, first + j, chunk)) * pitch
+                    for c, here in enumerate(lanes):
+                        swap_ref[c, pl.ds(start, dirs), :] = refs[i * parts + k][j, 0, :, here].astype(jnp.float32)
+
+    row = lax.broadcasted_iota(jnp.int32, (TILE, LANES), 0)
+    reached = ((t == 0) & (row < HALO)) | ((t == tiles - 1) & (row >= TILE - HALO))
+    shift = jnp.where(t == 0, TILE - HALO, HALO)
 
     def body(d, carry):
-        for t in range(tiles):
-            for c, here in enumerate(lanes):
-                grown = swap_ref[c, pl.ds(t * TILE * pitch + d, TILE, stride=pitch), :]
-                value = with_share(home_ref[0, d, pl.ds(t * TILE, TILE), here], share_ref, 0, d, here, t, tiles)
-                out_ref[0, d, pl.ds(t * TILE, TILE), here] = value + grown
+        for c, here in enumerate(lanes):
+            grown = swap_ref[c, pl.ds(t * TILE * pitch + d, TILE, stride=pitch), :]
+            shared = jnp.where(reached, pltpu.roll(share_ref[0, d, :, here], shift, 0), 0.0)
+            out_ref[0, d, :, here] = home_ref[0, d, :, here] + shared + grown
         return carry
 
-    lax.fori_loop(0, dirs, body, 0, unroll=12)
+    lax.fori_loop(0, dirs, body, 0, unroll=8)
 
 
 def join(own, into, home, share, early, late, rows_of, chunks, group):
     begin, many = group
     parts = len(late)
     _, dirs, rows, cols = home.shape
+    assert rows > TILE
     last = late[0].shape[0]
     spans = [(*span, chunks[0]) for span in rows_of] + [(0, last, chunks[-1])]
-    width = min(cols, 256)
-    block = pl.BlockSpec((1, dirs, rows, width), lambda f, c: (begin + f, 0, 0, c))
+    block = pl.BlockSpec((1, dirs, TILE, cols), lambda f, t: (begin + f, 0, t, 0))
     specs = [
-        pl.BlockSpec((count, 1, dirs, width), lambda f, c: (0, begin + f, 0, c)) for _, count in rows_of for _ in range(parts)
-    ] + [pl.BlockSpec((last, 1, dirs, width), lambda f, c: (0, f, 0, c))] * parts
+        pl.BlockSpec((count, 1, dirs, cols), lambda f, t: (0, begin + f, 0, 0)) for _, count in rows_of for _ in range(parts)
+    ] + [pl.BlockSpec((last, 1, dirs, cols), lambda f, t: (0, f, 0, 0))] * parts
     return pl.pallas_call(
-        functools.partial(join_kernel, parts, spans),
-        grid=(many, cols // width),
+        functools.partial(join_kernel, parts, rows // parts, spans),
+        grid=(many, rows // TILE),
         in_specs=[pl.BlockSpec(memory_space=pltpu.SMEM), UNREAD, block]
-        + [pl.BlockSpec((1, dirs, TILE, width), lambda f, c: (begin + f, 0, 0, c))]
+        + [pl.BlockSpec((1, dirs, TILE, cols), lambda f, t: (begin + f, 0, 0, 0))]
         + specs,
         out_specs=block,
         out_shape=jax.ShapeDtypeStruct(home.shape, jnp.float32),
-        scratch_shapes=[pltpu.VMEM((width // LANES, rows * (dirs + 1), LANES), jnp.float32)],
+        scratch_shapes=[pltpu.VMEM((cols // LANES, rows * (dirs + 1), LANES), jnp.float32)],
         input_output_aliases={} if begin == 0 else {1: 0},
         compiler_params=pltpu.CompilerParams(vmem_limit_bytes=VMEM_LIMIT),
         cost_estimate=COST,
@@ -549,9 +560,8 @@
     weight = wind_weight[:, None]
     wind = wind_speed[:, None]
     everything = [(0, freqs)]
-    many = freqs // 2 if freqs % 2 == 0 else freqs
-    groups = [(begin, many) for begin in range(0, freqs, many)]
     sent = halves(freqs)
+    groups = [(freqs - begin - many, many) for begin, many in reversed(sent)]
     levels = (cg_index, turn_index, sea_mask)
     if local > HALO:
         chunks = [(HALO, 0, local - HALO), (0, local - HALO, HALO)]
@@ -566,9 +576,14 @@
             early.append(swapped(pieces))
     home, low, high = into
     above, below = across(low, high)
-    after = arrived(home, early[0][1:])[0] if len(early) > 1 else home
-    state = by_row(after, forward_state)
-    in_t, out_t = turned(state, w_in, w_out)
+    after = home
+    for pieces in early[:-2]:
+        after, _ = arrived(after, pieces[1:])
+    state = by_row((after, wind, weight), forward_state)
+    after = state
+    for pieces in early[-2:-1]:
+        after, _ = arrived(after, pieces[1:])
+    in_t, out_t = turned(after, w_in, w_out)
     share, pieces = outer(own, dir_sign, along, in_t, above, below, *levels, home, parts, chunks[-1])
     late = swapped(pieces)
     term = functools.partial(source_term, own)
@@ -581,7 +596,7 @@
         grad, [back] = term(after, *fixed, early, groups, everything, span, ahead)
         after = grad
         if not grads:
-            after, rest = arrived(grad, late[1:], back[1:])
+            after, rest = arrived(grad, late[1:-1], back[1:])
             back = [back[0], *rest]
         grads.append(grad)
         early_back.append(swapped(back))
@@ -590,7 +605,8 @@
     for g, pieces in enumerate(late_back):
         if g < len(early_back):
             rest = [piece for group in late_back[g:] for piece in group[1:]]
-            start, rest = arrived(start, early_back[g][1:], rest)
+            awaited = early_back[g][1:] if g + 1 < len(early_back) else early_back[g][1:-1]
+            start, rest = arrived(start, awaited, rest)
             for n, group in enumerate(late_back[g:]):
                 late_back[g + n] = [group[0], *rest[n * (parts - 1) : (n + 1) * (parts - 1)]]
         returned.append(swapped(late_back[g]))

time: 187 us -> 190 us (1.016)
  Pallas kernels: 127 us -> 134 us
  waiting for transfers between devices: 24.3 us -> 19.1 us
    ppermute x24 -> x27, waiting for transfers between devices: 24.3 us -> 13.2 us  [swapped(): lax.ppermute(pieces[k], 'comp', [(i, i ^ k) for i in range(parts)])]
    ppermute x2, waiting for transfers between devices: 0.01 us -> 5.86 us  [across(): return (lax.ppermute(high, 'space', up), lax.ppermute(low, 'space', down))]
    pallas_call x2 -> x3, Pallas kernels: 27.1 us -> 31.1 us  [inner(): pl.pallas_call(functools.partial(inner_kernel, parts, local, chunk, into...]
    pallas_call x4, Pallas kernels: 26.8 us -> 28.9 us  [the longest x3 20.5 us: join(): pl.pallas_call(functools.partial(join_kernel, parts, rows // parts, spans...]
    unnamed x56 -> x60, local copies, waits for them, and re-layouts: 6.6 us -> 7.87 us
    ppermute x24 -> x27, starting transfers between devices: 19.7 us -> 20.6 us  [swapped(): lax.ppermute(pieces[k], 'comp', [(i, i ^ k) for i in range(parts)])]
  transfers between devices with their start and end apart: 26 -> 29, of which waited for: 5 -> 5; matrix products, arithmetic and copies ran while one was open for 2% -> 2% of each run, Pallas kernels for 57% -> 63%
where the time goes in v5:
time: 190 us; the launch traced here: 189 us
  Pallas kernels  134 us (71%)
  starting transfers between devices  25.3 us (13%)
  waiting for transfers between devices  19.1 us (10%)
  local copies, waits for them, and re-layouts  9.67 us (5%)
    pallas_call x3, Pallas kernels, source_term(): pl.pallas_call(functools.partial(source_kernel, parts, got, sent, dirs, 2...  53.6 us
    pallas_call x3, Pallas kernels, inner(): pl.pallas_call(functools.partial(inner_kernel, parts, local, chunk, into...  31.1 us
    ppermute x27, starting transfers between devices, swapped(): lax.ppermute(pieces[k], 'comp', [(i, i ^ k) for i in range(parts)])  20.6 us
    pallas_call x3, Pallas kernels, join(): pl.pallas_call(functools.partial(join_kernel, parts, rows // parts, spans...  20.5 us
    ppermute x27, waiting for transfers between devices, swapped(): lax.ppermute(pieces[k], 'comp', [(i, i ^ k) for i in range(parts)])  13.2 us
    pallas_call x1, Pallas kernels, outer(): pl.pallas_call(functools.partial(outer_kernel, parts, local, chunk), grid...  12.9 us
    pallas_call x1, Pallas kernels, by_row(): pl.pallas_call(by_row_kernel, grid=(deep // some,), in_specs=[UNREAD] * l...  8.43 us
    unnamed x60, local copies, waits for them, and re-layouts  7.87 us
  transfers between devices with their start and end apart: 29, of which 5 were waited for; matrix products, arithmetic and copies ran while one was open for 2% of the time, Pallas kernels for 63%

profile of v5, /device:TPU:0, one launch (start us, length us, event | category | flops | bytes accessed | tf_op | source)
XLA Modules:
  0.0 189.2 jit_solution(10179881080287405916)
XLA Ops:
  0.6 8.7 %shard_map.122 = (f32[4,24,32,1024]{3,2,1,0:T(8,128)}, bf16[2,4,32,1024]{3,2,1,0:T(8,128)(2,1)}, bf16[2,4,32,1024]{3,2,1,0:T(8,128)(2,1)}, bf16[6,1,24,1024]{3,2...) custom-call(s32[1]{0:T(128)} %bitcast.own_ref.refs_0_, ...), custom_call_target="tpu_custom_call" | custom-call | flops 1 | bytes 1 | tf_op jit(solution)/shard_map/pallas_call | solution.py:175
  9.8 2.6 %collective-permute-start.1 = (bf16[6,1,24,1024]{3,2,1,0:T(8,128)(2,1)}, bf16[6,1,24,1024]{3,2,1,0:T(8,128)(2,1)S(1)}, u32[]{:S(2)}, u32[]{:S(2)}) collective-permute-start(bf16[6,1,24,1024]{3,2,1,0:T(8,128)(2,1)} %get-tuple-element.82), channel_id=1, source_target_pairs={{0,16},{8,24},{16,0},{24,8},{1,17},{9,25},{17,1},{25,9},{2,18},{10... | collective-permute-start | bytes 884744 | tf_op jit(solution)/shard_map/ppermute | solution.py:519
  12.5 8.8 %shard_map.123 = (f32[4,24,32,1024]{3,2,1,0:T(8,128)}, bf16[2,4,32,1024]{3,2,1,0:T(8,128)(2,1)}, bf16[2,4,32,1024]{3,2,1,0:T(8,128)(2,1)}, bf16[6,1,24,1024]{3,2...) custom-call(s32[1]{0:T(128)} %bitcast.own_ref.refs_0_, ...), custom_call_target="tpu_custom_call", output_to_operand_aliasing={{0}: (8, {}), {1}: (9, {}), {2}: (10, {})} | custom-call | flops 1 | bytes 1 | tf_op jit(solution)/shard_map/pallas_call | solution.py:175
  21.4 1.9 %collective-permute-start.4 = (bf16[6,1,24,1024]{3,2,1,0:T(8,128)(2,1)}, bf16[6,1,24,1024]{3,2,1,0:T(8,128)(2,1)S(1)}, u32[]{:S(2)}, u32[]{:S(2)}) collective-permute-start(bf16[6,1,24,1024]{3,2,1,0:T(8,128)(2,1)} %get-tuple-element.85), channel_id=1, source_target_pairs={{0,16},{8,24},{16,0},{24,8},{1,17},{9,25},{17,1},{25,9},{2,18},{10... | collective-permute-start | bytes 884744 | tf_op jit(solution)/shard_map/ppermute | solution.py:519
  23.3 13.6 %shard_map.124 = (f32[4,24,32,1024]{3,2,1,0:T(8,128)}, bf16[2,4,32,1024]{3,2,1,0:T(8,128)(2,1)}, bf16[2,4,32,1024]{3,2,1,0:T(8,128)(2,1)}, bf16[6,2,24,1024]{3,2...) custom-call(s32[1]{0:T(128)} %bitcast.own_ref.refs_0_, ...), custom_call_target="tpu_custom_call", output_to_operand_aliasing={{0}: (8, {}), {1}: (9, {}), {2}: (10, {})} | custom-call | flops 1 | bytes 1 | tf_op jit(solution)/shard_map/pallas_call | solution.py:175
  36.9 0.6 broadcast_in_dim.6.refs_1_.wind_ref
  37.5 1.2 broadcast_in_dim.8.refs_2_.weight_ref
  38.7 3.4 %collective-permute-start.6 = (bf16[2,4,32,1024]{3,2,1,0:T(8,128)(2,1)}, bf16[2,4,32,1024]{3,2,1,0:T(8,128)(2,1)S(1)}, u32[]{:S(2)}, u32[]{:S(2)}) collective-permute-start(bf16[2,4,32,1024]{3,2,1,0:T(8,128)(2,1)} %get-tuple-element.88), channel_id=1, source_target_pairs={{0,1},{1,2},{2,3},{3,4},{4,5},{5,6},{6,7},{8,9},{9,10},{10,11},{11... | collective-permute-start | bytes 1572872 | tf_op jit(solution)/shard_map/ppermute | solution.py:527
  42.1 1.3 collective-permute-start.7
  43.5 0.6 shard_map.125.refs_0_
  44.1 8.4 %shard_map.126.refs_0_.state_ref = bf16[8,384,1024]{2,1,0:T(8,128)(2,1)} custom-call(f32[8,128]{1,0:T(8,128)} %shard_map.125.refs_0_, f32[8,1,1024]{2,1,0:T(1,128)} %broadcast_in_dim.6.refs_1_.wind_ref, f32[1536,1]{1,0:T(8,128)} %broadcast_in_dim.8.refs_2_.weight_ref, bf16[384,8,1024]{2,1,0:T(8,128)(2,1)} %refs_3_.1), custom_call_target="tpu_custom_call" | custom-call | flops 1 | bytes 1 | tf_op jit(solution)/shard_map/pallas_call | solution.py:324
  52.7 1.5 collective-permute-start.9
  54.4 0.6 copy-done.11
  55.0 0.6 shard_map.127._
  55.6 4.1 %shard_map.128 = (bf16[384,1536]{1,0:T(8,128)(2,1)}, bf16[1536,384]{1,0:T(8,128)(2,1)}) custom-call(f32[8,128]{1,0:T(8,128)} %shard_map.127._, bf16[1536,384]{1,0:T(8,128)(2,1)} %w_in_ref.7, bf16[384,1536]{1,0:T(8,128)(2,1)} %w_out_ref.1), custom_call_target="tpu_custom_call" | custom-call | flops 99999997952 | bytes 104857600 | tf_op jit(solution)/shard_map/pallas_call | solution.py:346
  59.6 5.9 %collective-permute-done.6.refs_4_ = bf16[2,4,32,1024]{3,2,1,0:T(8,128)(2,1)S(1)} collective-permute-done((bf16[2,4,32,1024]{3,2,1,0:T(8,128)(2,1)}, bf16[2,4,32,1024]{3,2,1,0:T(8,128)(2,1)S(1)}, u32[]{:S(2)}, u32[]{:S(2)}) %collective-permute-start.6) | collective-permute-done | bytes 524320 | tf_op jit(solution)/shard_map/ppermute | solution.py:527
  65.5 0.8 copy-done.27
  66.5 12.9 %shard_map.129 = (f32[4,24,8,1024]{3,2,1,0:T(8,128)}, bf16[2,4,24,1024]{3,2,1,0:T(8,128)(2,1)}, bf16[2,4,24,1024]{3,2,1,0:T(8,128)(2,1)}, bf16[2,4,24,1024]{3,2,1,0:T(8,128)(2,1)}, bf16[2,4,24,1024]{3,2,1,0:T(8,128)(2,1)}) custom-call(s32[1]{0:T(128)} %bitcast.own_ref.refs_0_, s32[2,24]{1,0:T(2,128)} %refs_1_.1, f32[2,24]{1,0:T(2,128)} %constant.9.clone.along_ref.refs_2_, ...), custom_call_target="tpu_custom_call" | custom-call | flops 99999997952 | bytes 104857600 | tf_op jit(solution)/shard_map/pallas_call | solution.py:277
  79.4 1.6 collective-permute-start.12
  81.3 19.7 %shard_map.130 = (f32[3,1,1024]{2,1,0:T(1,128)}, bf16[3,4,24,1024]{3,2,1,0:T(8,128)(2,1)}, bf16[3,4,24,1024]{3,2,1,0:T(8,128)(2,1)}, bf16[3,4,24,1024]{3,2,1,0:T(8,128)(2,1)}, bf16[3,4,24,1024]{3,2,1,0:T(8,128)(2,1)}) custom-call(s32[1]{0:T(128)} %bitcast.own_ref.refs_0_, f32[4,24,8,1024]{3,2,1,0:T(8,128)} %get-tuple-element.90._.share_ref, ...), custom_call_target="tpu_custom_call" | custom-call | flops 1 | bytes 1 | tf_op jit(solution)/shard_map/pallas_call | solution.py:412
  101.0 0.7 copy-done.12
  101.9 0.6 shard_map.131
  102.8 1.6 collective-permute-start.15
  104.4 19.7 %shard_map.132 = (f32[3,1,1024]{2,1,0:T(1,128)}, bf16[3,4,24,1024]{3,2,1,0:T(8,128)(2,1)}, bf16[3,4,24,1024]{3,2,1,0:T(8,128)(2,1)}, bf16[3,4,24,1024]{3,2,1,0:T(8,128)(2,1)}, bf16[3,4,24,1024]{3,2,1,0:T(8,128)(2,1)}) custom-call(s32[1]{0:T(128)} %bitcast.own_ref.refs_0_, f32[8,128]{1,0:T(8,128)} %get-tuple-element.104._, ...), custom_call_target="tpu_custom_call" | custom-call | flops 1 | bytes 1 | tf_op jit(solution)/shard_map/pallas_call | solution.py:412
  124.1 0.6 collective-permute-start.17
  124.7 0.7 copy-done.14
  125.4 1.6 collective-permute-start.18
  127.0 14.3 %shard_map.133 = (f32[2,1,1024]{2,1,0:T(1,128)}, bf16[2,2,24,1024]{3,2,1,0:T(8,128)(2,1)}, bf16[2,2,24,1024]{3,2,1,0:T(8,128)(2,1)}, bf16[2,2,24,1024]{3,2,1,0:T...) custom-call(s32[1]{0:T(128)} %bitcast.own_ref.refs_0_, ...), custom_call_target="tpu_custom_call" | custom-call | flops 1 | bytes 1 | tf_op jit(solution)/shard_map/pallas_call | solution.py:412
  141.3 0.8 copy-done.3
  142.3 0.6 shard_map.134
  142.9 1.6 collective-permute-done.18.refs_2_.refs_6_
  144.5 0.8 copy-done.1
  145.3 0.6 shard_map.135
  146.4 1.6 collective-permute-start.21
  148.0 0.7 copy_bitcast_fusion
  148.7 0.7 copy.49
  149.4 6.9 %collective-permute-done.19.refs_7_ = bf16[3,4,24,1024]{3,2,1,0:T(8,128)(2,1)S(1)} collective-permute-done((bf16[3,4,24,1024]{3,2,1,0:T(8,128)(2,1)}, bf16[3,4,24,1024]{3,2,1,0:T(8,128)(2,1)S(1)}, u32[]{:S(2)}, u32[]{:S(2)}) %collective-permute-start.19) | collective-permute-done | bytes 589856 | tf_op jit(solution)/shard_map/ppermute | solution.py:519
  156.3 0.8 collective-permute-start.24
  157.1 1.2 collective-permute-start.25
  158.5 2.9 %collective-permute-done.21.refs_10_ = bf16[2,2,24,1024]{3,2,1,0:T(8,128)(2,1)S(1)} collective-permute-done((bf16[2,2,24,1024]{3,2,1,0:T(8,128)(2,1)}, bf16[2,2,24,1024]{3,2,1,0:T(8,128)(2,1)S(1)}, u32[]{:S(2)}, u32[]{:S(2)}) %collective-permute-start.21) | collective-permute-done | bytes 196640 | tf_op jit(solution)/shard_map/ppermute | solution.py:519
  161.3 1.6 collective-permute-start.27
  162.9 1.8 collective-permute-done.22.refs_11_
  164.7 1.8 collective-permute-start.28
  166.5 0.6 maximum_select_fusion
  167.2 10.0 %shard_map.136._ = f32[4,24,32,1024]{3,2,1,0:T(8,128)} custom-call(s32[1]{0:T(128)} %bitcast.own_ref.refs_0_, f32[8,128]{1,0:T(8,128)} %get-tuple-element.130._, f32[4,24,32,1024]{3,2,1,0:T(8,128)} %get-tuple-element.80.refs_0_.refs_9_.home_ref, f32[4,24,8,1024]{3,2,1,0:T(8,128)} %get-tuple-element.90._.share_ref, ...), custom_call_target="tpu_custom_call" | custom-call | flops 1 | bytes 1 | tf_op jit(solution)/shard_map/pallas_call | solution.py:486
  177.2 0.6 copy-done.21
  177.9 5.3 %shard_map.137._ = f32[4,24,32,1024]{3,2,1,0:T(8,128)} custom-call(s32[1]{0:T(128)} %bitcast.own_ref.refs_0_, f32[4,24,32,1024]{3,2,1,0:T(8,128)} %shard_map.136._, f32[4,24,32,1024]{3,2,1,0:T(8,128)} %get-tuple-element.80.refs_0_.refs_9_.home_ref, f32[4,24,8,1024]{3,2,1,0:T(8,128)} %get-tuple-element.90._.share_ref, ...), custom_call_target="tpu_custom_call", output_to_operand_aliasing={{}: (1, {})} | custom-call | flops 1 | bytes 1 | tf_op jit(solution)/shard_map/pallas_call | solution.py:486
  183.9 5.3 %shard_map.138 = f32[4,24,32,1024]{3,2,1,0:T(8,128)} custom-call(s32[1]{0:T(128)} %bitcast.own_ref.refs_0_, f32[4,24,32,1024]{3,2,1,0:T(8,128)} %shard_map.137._, f32[4,24,32,1024]{3,2,1,0:T(8,128)} %get-tuple-element.80.refs_0_.refs_9_.home_ref, f32[4,24,8,1024]{3,2,1,0:T(8,128)} %get-tuple-element.90._.share_ref, ...), custom_call_target="tpu_custom_call", output_to_operand_aliasing={{}: (1, {})} | custom-call | flops 1 | bytes 1 | tf_op jit(solution)/shard_map/pallas_call | solution.py:486
  (90 shorter events, 3.8 us)
Async XLA Ops:
  9.4 13.9 %collective-permute-start = (bf16[6,1,24,1024]{3,2,1,0:T(8,128)(2,1)}, bf16[6,1,24,1024]{3,2,1,0:T(8,128)(2,1)S(1)}, u32[]{:S(2)}, u32[]{:S(2)}) collective-permute-start(bf16[6,1,24,1024]{3,2,1,0:T(8,128)(2,1)} %get-tuple-element.81), channel_id=1, source_target_pairs={{0,8},{8,0},{16,24},{24,16},{1,9},{9,1},{17,25},{25,17},{2,10},{10... | collective-permute-start | bytes 884744 | tf_op jit(solution)/shard_map/ppermute | solution.py:519
  9.8 28.9 %collective-permute-start.1 = (bf16[6,1,24,1024]{3,2,1,0:T(8,128)(2,1)}, bf16[6,1,24,1024]{3,2,1,0:T(8,128)(2,1)S(1)}, u32[]{:S(2)}, u32[]{:S(2)}) collective-permute-start(bf16[6,1,24,1024]{3,2,1,0:T(8,128)(2,1)} %get-tuple-element.82), channel_id=1, source_target_pairs={{0,16},{8,24},{16,0},{24,8},{1,17},{9,25},{17,1},{25,9},{2,18},{10... | collective-permute-start | bytes 884744 | tf_op jit(solution)/shard_map/ppermute | solution.py:519
  12.4 29.8 %collective-permute-start.2 = (bf16[6,1,24,1024]{3,2,1,0:T(8,128)(2,1)}, bf16[6,1,24,1024]{3,2,1,0:T(8,128)(2,1)S(1)}, u32[]{:S(2)}, u32[]{:S(2)}) collective-permute-start(bf16[6,1,24,1024]{3,2,1,0:T(8,128)(2,1)} %get-tuple-element.83), channel_id=1, source_target_pairs={{0,24},{8,16},{16,8},{24,0},{1,25},{9,17},{17,9},{25,1},{2,26},{10... | collective-permute-start | bytes 884744 | tf_op jit(solution)/shard_map/ppermute | solution.py:519
  21.2 31.3 %collective-permute-start.3 = (bf16[6,1,24,1024]{3,2,1,0:T(8,128)(2,1)}, bf16[6,1,24,1024]{3,2,1,0:T(8,128)(2,1)S(1)}, u32[]{:S(2)}, u32[]{:S(2)}) collective-permute-start(bf16[6,1,24,1024]{3,2,1,0:T(8,128)(2,1)} %get-tuple-element.84), channel_id=1, source_target_pairs={{0,8},{8,0},{16,24},{24,16},{1,9},{9,1},{17,25},{25,17},{2,10},{10... | collective-permute-start | bytes 884744 | tf_op jit(solution)/shard_map/ppermute | solution.py:519
  21.4 31.4 %collective-permute-start.4 = (bf16[6,1,24,1024]{3,2,1,0:T(8,128)(2,1)}, bf16[6,1,24,1024]{3,2,1,0:T(8,128)(2,1)S(1)}, u32[]{:S(2)}, u32[]{:S(2)}) collective-permute-start(bf16[6,1,24,1024]{3,2,1,0:T(8,128)(2,1)} %get-tuple-element.85), channel_id=1, source_target_pairs={{0,16},{8,24},{16,0},{24,8},{1,17},{9,25},{17,1},{25,9},{2,18},{10... | collective-permute-start | bytes 884744 | tf_op jit(solution)/shard_map/ppermute | solution.py:519
  23.3 13.6 %copy-start.6 = (bf16[6,1,24,1024]{3,2,1,0:T(8,128)(2,1)}, bf16[6,1,24,1024]{3,2,1,0:T(8,128)(2,1)S(1)}, u32[]{:S(2)}) copy-start(bf16[6,1,24,1024]{3,2,1,0:T(8,128)(2,1)S(1)} %collective-permute-done.refs_1_) | copy-start | bytes 884740
  23.3 31.0 %collective-permute-start.5 = (bf16[6,1,24,1024]{3,2,1,0:T(8,128)(2,1)}, bf16[6,1,24,1024]{3,2,1,0:T(8,128)(2,1)S(1)}, u32[]{:S(2)}, u32[]{:S(2)}) collective-permute-start(bf16[6,1,24,1024]{3,2,1,0:T(8,128)(2,1)} %get-tuple-element.86), channel_id=1, source_target_pairs={{0,24},{8,16},{16,8},{24,0},{1,25},{9,17},{17,9},{25,1},{2,26},{10... | collective-permute-start | bytes 884744 | tf_op jit(solution)/shard_map/ppermute | solution.py:519
  23.3 13.6 %copy-start.25 = (f32[8,1024]{1,0:T(8,128)S(1)}, f32[8,1024]{1,0:T(8,128)}, u32[]{:S(2)}) copy-start(f32[8,1024]{1,0:T(8,128)} %param.13) | copy-start | bytes 98308
  23.3 14.2 %copy-start.26 = (f32[1536]{0:T(1024)S(1)}, f32[1536]{0:T(1024)}, u32[]{:S(2)}) copy-start(f32[1536]{0:T(1024)} %param.20) | copy-start | bytes 18436
  38.7 4.8 %copy-start.7 = (bf16[6,1,24,1024]{3,2,1,0:T(8,128)(2,1)}, bf16[6,1,24,1024]{3,2,1,0:T(8,128)(2,1)S(1)}, u32[]{:S(2)}) copy-start(bf16[6,1,24,1024]{3,2,1,0:T(8,128)(2,1)S(1)} %collective-permute-done.1.refs_2_) | copy-start | bytes 884740
  38.7 26.8 %collective-permute-start.6 = (bf16[2,4,32,1024]{3,2,1,0:T(8,128)(2,1)}, bf16[2,4,32,1024]{3,2,1,0:T(8,128)(2,1)S(1)}, u32[]{:S(2)}, u32[]{:S(2)}) collective-permute-start(bf16[2,4,32,1024]{3,2,1,0:T(8,128)(2,1)} %get-tuple-element.88), channel_id=1, source_target_pairs={{0,1},{1,2},{2,3},{3,4},{4,5},{5,6},{6,7},{8,9},{9,10},{10,11},{11... | collective-permute-start | bytes 1572872 | tf_op jit(solution)/shard_map/ppermute | solution.py:527
  42.1 1.3 copy-start.8
  42.1 23.3 %collective-permute-start.7 = (bf16[2,4,32,1024]{3,2,1,0:T(8,128)(2,1)}, bf16[2,4,32,1024]{3,2,1,0:T(8,128)(2,1)S(1)}, u32[]{:S(2)}, u32[]{:S(2)}) collective-permute-start(bf16[2,4,32,1024]{3,2,1,0:T(8,128)(2,1)} %get-tuple-element.89), channel_id=1, source_target_pairs={{1,0},{2,1},{3,2},{4,3},{5,4},{6,5},{7,6},{9,8},{10,9},{11,10},{12... | collective-permute-start | bytes 1572872 | tf_op jit(solution)/shard_map/ppermute | solution.py:527
  52.5 1.9 copy-start.9
  52.5 28.5 %collective-permute-start.8 = (bf16[6,2,24,1024]{3,2,1,0:T(8,128)(2,1)}, bf16[6,2,24,1024]{3,2,1,0:T(8,128)(2,1)}, u32[]{:S(2)}, u32[]{:S(2)}) collective-permute-start(bf16[6,2,24,1024]{3,2,1,0:T(8,128)(2,1)} %get-tuple-element.95), channel_id=1, source_target_pairs={{0,8},{8,0},{16,24},{24,16},{1,9},{9,1},{17,25},{25,17},{2,10},{10... | collective-permute-start | bytes 1769480 | tf_op jit(solution)/shard_map/ppermute | solution.py:519
  52.7 1.6 copy-start.10
  52.7 28.6 %collective-permute-start.9 = (bf16[6,2,24,1024]{3,2,1,0:T(8,128)(2,1)}, bf16[6,2,24,1024]{3,2,1,0:T(8,128)(2,1)}, u32[]{:S(2)}, u32[]{:S(2)}) collective-permute-start(bf16[6,2,24,1024]{3,2,1,0:T(8,128)(2,1)} %get-tuple-element.96), channel_id=1, source_target_pairs={{0,16},{8,24},{16,0},{24,8},{1,17},{9,25},{17,1},{25,9},{2,18},{10... | collective-permute-start | bytes 1769480 | tf_op jit(solution)/shard_map/ppermute | solution.py:519
  54.3 27.0 %collective-permute-start.10 = (bf16[6,2,24,1024]{3,2,1,0:T(8,128)(2,1)}, bf16[6,2,24,1024]{3,2,1,0:T(8,128)(2,1)}, u32[]{:S(2)}, u32[]{:S(2)}) collective-permute-start(bf16[6,2,24,1024]{3,2,1,0:T(8,128)(2,1)} %get-tuple-element.97), channel_id=1, source_target_pairs={{0,24},{8,16},{16,8},{24,0},{1,25},{9,17},{17,9},{25,1},{2,26},{10... | collective-permute-start | bytes 1769480 | tf_op jit(solution)/shard_map/ppermute | solution.py:519
  65.5 1.0 copy-start.28
  79.4 21.6 %collective-permute-start.11 = (bf16[2,4,24,1024]{3,2,1,0:T(8,128)(2,1)}, bf16[2,4,24,1024]{3,2,1,0:T(8,128)(2,1)S(1)}, u32[]{:S(2)}, u32[]{:S(2)}) collective-permute-start(bf16[2,4,24,1024]{3,2,1,0:T(8,128)(2,1)} %get-tuple-element.99), channel_id=1, source_target_pairs={{0,8},{8,0},{16,24},{24,16},{1,9},{9,1},{17,25},{25,17},{2,10},{10... | collective-permute-start | bytes 1179656 | tf_op jit(solution)/shard_map/ppermute | solution.py:519
  79.4 21.6 %collective-permute-start.12 = (bf16[2,4,24,1024]{3,2,1,0:T(8,128)(2,1)}, bf16[2,4,24,1024]{3,2,1,0:T(8,128)(2,1)S(1)}, u32[]{:S(2)}, u32[]{:S(2)}) collective-permute-start(bf16[2,4,24,1024]{3,2,1,0:T(8,128)(2,1)} %get-tuple-element.100), channel_id=1, source_target_pairs={{0,16},{8,24},{16,0},{24,8},{1,17},{9,25},{17,1},{25,9},{2,18},{10... | collective-permute-start | bytes 1179656 | tf_op jit(solution)/shard_map/ppermute | solution.py:519
  81.0 43.7 %collective-permute-start.13 = (bf16[2,4,24,1024]{3,2,1,0:T(8,128)(2,1)}, bf16[2,4,24,1024]{3,2,1,0:T(8,128)(2,1)S(1)}, u32[]{:S(2)}, u32[]{:S(2)}) collective-permute-start(bf16[2,4,24,1024]{3,2,1,0:T(8,128)(2,1)} %get-tuple-element.107), channel_id=1, source_target_pairs={{0,24},{8,16},{16,8},{24,0},{1,25},{9,17},{17,9},{25,1},{2,26},{10... | collective-permute-start | bytes 1179656 | tf_op jit(solution)/shard_map/ppermute | solution.py:519
  101.0 0.9 copy-start.13
  102.5 24.5 %collective-permute-start.14 = (bf16[3,4,24,1024]{3,2,1,0:T(8,128)(2,1)}, bf16[3,4,24,1024]{3,2,1,0:T(8,128)(2,1)S(1)}, u32[]{:S(2)}, u32[]{:S(2)}) collective-permute-start(bf16[3,4,24,1024]{3,2,1,0:T(8,128)(2,1)} %get-tuple-element.109), channel_id=1, source_target_pairs={{0,8},{8,0},{16,24},{24,16},{1,9},{9,1},{17,25},{25,17},{2,10},{10... | collective-permute-start | bytes 1769480 | tf_op jit(solution)/shard_map/ppermute | solution.py:519
  102.8 38.5 %collective-permute-start.15 = (bf16[3,4,24,1024]{3,2,1,0:T(8,128)(2,1)}, bf16[3,4,24,1024]{3,2,1,0:T(8,128)(2,1)S(1)}, u32[]{:S(2)}, u32[]{:S(2)}) collective-permute-start(bf16[3,4,24,1024]{3,2,1,0:T(8,128)(2,1)} %get-tuple-element.110), channel_id=1, source_target_pairs={{0,16},{8,24},{16,0},{24,8},{1,17},{9,25},{17,1},{25,9},{2,18},{10... | collective-permute-start | bytes 1769480 | tf_op jit(solution)/shard_map/ppermute | solution.py:519
  104.4 36.9 %collective-permute-start.16 = (bf16[3,4,24,1024]{3,2,1,0:T(8,128)(2,1)}, bf16[3,4,24,1024]{3,2,1,0:T(8,128)(2,1)S(1)}, u32[]{:S(2)}, u32[]{:S(2)}) collective-permute-start(bf16[3,4,24,1024]{3,2,1,0:T(8,128)(2,1)} %get-tuple-element.111), channel_id=1, source_target_pairs={{0,24},{8,16},{16,8},{24,0},{1,25},{9,17},{17,9},{25,1},{2,26},{10... | collective-permute-start | bytes 1769480 | tf_op jit(solution)/shard_map/ppermute | solution.py:519
  104.4 43.6 %copy-start.24 = (f32[3,1,1024]{2,1,0:T(1,128)S(1)}, f32[3,1,1024]{2,1,0:T(1,128)}, u32[]{:S(2)}) copy-start(f32[3,1,1024]{2,1,0:T(1,128)} %get-tuple-element.98.refs_0_) | copy-start | bytes 36868
  124.1 18.9 %collective-permute-start.17 = (bf16[3,4,24,1024]{3,2,1,0:T(8,128)(2,1)}, bf16[3,4,24,1024]{3,2,1,0:T(8,128)(2,1)S(1)}, u32[]{:S(2)}, u32[]{:S(2)}) collective-permute-start(bf16[3,4,24,1024]{3,2,1,0:T(8,128)(2,1)} %get-tuple-element.122), channel_id=1, source_target_pairs={{0,8},{8,0},{16,24},{24,16},{1,9},{9,1},{17,25},{25,17},{2,10},{10... | collective-permute-start | bytes 1769480 | tf_op jit(solution)/shard_map/ppermute | solution.py:519
  125.4 19.0 %collective-permute-start.18 = (bf16[3,4,24,1024]{3,2,1,0:T(8,128)(2,1)}, bf16[3,4,24,1024]{3,2,1,0:T(8,128)(2,1)S(1)}, u32[]{:S(2)}, u32[]{:S(2)}) collective-permute-start(bf16[3,4,24,1024]{3,2,1,0:T(8,128)(2,1)} %get-tuple-element.123), channel_id=1, source_target_pairs={{0,16},{8,24},{16,0},{24,8},{1,17},{9,25},{17,1},{25,9},{2,18},{10... | collective-permute-start | bytes 1769480 | tf_op jit(solution)/shard_map/ppermute | solution.py:519
  127.0 14.3 %copy-start.2 = (bf16[3,4,24,1024]{3,2,1,0:T(8,128)(2,1)}, bf16[3,4,24,1024]{3,2,1,0:T(8,128)(2,1)S(1)}, u32[]{:S(2)}) copy-start(bf16[3,4,24,1024]{3,2,1,0:T(8,128)(2,1)S(1)} %collective-permute-done.14.refs_1_) | copy-start | bytes 1769476
  127.0 29.3 %collective-permute-start.19 = (bf16[3,4,24,1024]{3,2,1,0:T(8,128)(2,1)}, bf16[3,4,24,1024]{3,2,1,0:T(8,128)(2,1)S(1)}, u32[]{:S(2)}, u32[]{:S(2)}) collective-permute-start(bf16[3,4,24,1024]{3,2,1,0:T(8,128)(2,1)} %get-tuple-element.133), channel_id=1, source_target_pairs={{0,24},{8,16},{16,8},{24,0},{1,25},{9,17},{17,9},{25,1},{2,26},{10... | collective-permute-start | bytes 1769480 | tf_op jit(solution)/shard_map/ppermute | solution.py:519
  141.3 0.8 copy-start.3
  141.3 1.0 copy-start.4
  142.9 1.6 copy-start
  145.9 11.2 %collective-permute-start.23 = (bf16[2,1,24,1024]{3,2,1,0:T(8,128)(2,1)}, bf16[2,1,24,1024]{3,2,1,0:T(8,128)(2,1)S(1)}, u32[]{:S(2)}, u32[]{:S(2)}) collective-permute-start(bf16[2,1,24,1024]{3,2,1,0:T(8,128)(2,1)} %get-tuple-element.139), channel_id=1, source_target_pairs={{0,8},{8,0},{16,24},{24,16},{1,9},{9,1},{17,25},{25,17},{2,10},{10... | collective-permute-start | bytes 294920 | tf_op jit(solution)/shard_map/ppermute | solution.py:519
  145.9 12.4 %collective-permute-start.20 = (bf16[2,2,24,1024]{3,2,1,0:T(8,128)(2,1)}, bf16[2,2,24,1024]{3,2,1,0:T(8,128)(2,1)S(1)}, u32[]{:S(2)}, u32[]{:S(2)}) collective-permute-start(bf16[2,2,24,1024]{3,2,1,0:T(8,128)(2,1)} %get-tuple-element.135), channel_id=1, source_target_pairs={{0,8},{8,0},{16,24},{24,16},{1,9},{9,1},{17,25},{25,17},{2,10},{10... | collective-permute-start | bytes 589832 | tf_op jit(solution)/shard_map/ppermute | solution.py:519
  146.4 14.9 %collective-permute-start.21 = (bf16[2,2,24,1024]{3,2,1,0:T(8,128)(2,1)}, bf16[2,2,24,1024]{3,2,1,0:T(8,128)(2,1)S(1)}, u32[]{:S(2)}, u32[]{:S(2)}) collective-permute-start(bf16[2,2,24,1024]{3,2,1,0:T(8,128)(2,1)} %get-tuple-element.136), channel_id=1, source_target_pairs={{0,16},{8,24},{16,0},{24,8},{1,17},{9,25},{17,1},{25,9},{2,18},{10... | collective-permute-start | bytes 589832 | tf_op jit(solution)/shard_map/ppermute | solution.py:519
  148.0 16.8 %collective-permute-start.22 = (bf16[2,2,24,1024]{3,2,1,0:T(8,128)(2,1)}, bf16[2,2,24,1024]{3,2,1,0:T(8,128)(2,1)S(1)}, u32[]{:S(2)}, u32[]{:S(2)}) collective-permute-start(bf16[2,2,24,1024]{3,2,1,0:T(8,128)(2,1)} %get-tuple-element.137), channel_id=1, source_target_pairs={{0,24},{8,16},{16,8},{24,0},{1,25},{9,17},{17,9},{25,1},{2,26},{10... | collective-permute-start | bytes 589832 | tf_op jit(solution)/shard_map/ppermute | solution.py:519
  156.3 10.9 %copy-start.5 = (bf16[3,4,24,1024]{3,2,1,0:T(8,128)(2,1)}, bf16[3,4,24,1024]{3,2,1,0:T(8,128)(2,1)S(1)}, u32[]{:S(2)}) copy-start(bf16[3,4,24,1024]{3,2,1,0:T(8,128)(2,1)S(1)} %collective-permute-done.19.refs_7_) | copy-start | bytes 1769476
  156.3 20.8 %collective-permute-start.24 = (bf16[2,1,24,1024]{3,2,1,0:T(8,128)(2,1)}, bf16[2,1,24,1024]{3,2,1,0:T(8,128)(2,1)S(1)}, u32[]{:S(2)}, u32[]{:S(2)}) collective-permute-start(bf16[2,1,24,1024]{3,2,1,0:T(8,128)(2,1)} %get-tuple-element.140), channel_id=1, source_target_pairs={{0,16},{8,24},{16,0},{24,8},{1,17},{9,25},{17,1},{25,9},{2,18},{10... | collective-permute-start | bytes 294920 | tf_op jit(solution)/shard_map/ppermute | solution.py:519
  157.1 20.1 %copy-start.18 = (bf16[2,1,24,1024]{3,2,1,0:T(8,128)(2,1)}, bf16[2,1,24,1024]{3,2,1,0:T(8,128)(2,1)S(1)}, u32[]{:S(2)}) copy-start(bf16[2,1,24,1024]{3,2,1,0:T(8,128)(2,1)S(1)} %collective-permute-done.23.refs_9_) | copy-start | bytes 294916
  157.1 20.1 %collective-permute-start.25 = (bf16[2,1,24,1024]{3,2,1,0:T(8,128)(2,1)}, bf16[2,1,24,1024]{3,2,1,0:T(8,128)(2,1)S(1)}, u32[]{:S(2)}, u32[]{:S(2)}) collective-permute-start(bf16[2,1,24,1024]{3,2,1,0:T(8,128)(2,1)} %get-tuple-element.141), channel_id=1, source_target_pairs={{0,24},{8,16},{16,8},{24,0},{1,25},{9,17},{17,9},{25,1},{2,26},{10... | collective-permute-start | bytes 294920 | tf_op jit(solution)/shard_map/ppermute | solution.py:519
  158.3 8.9 %copy-start.15 = (bf16[2,2,24,1024]{3,2,1,0:T(8,128)(2,1)}, bf16[2,2,24,1024]{3,2,1,0:T(8,128)(2,1)S(1)}, u32[]{:S(2)}) copy-start(bf16[2,2,24,1024]{3,2,1,0:T(8,128)(2,1)S(1)} %collective-permute-done.20.refs_9_) | copy-start | bytes 589828
  158.3 24.9 %collective-permute-start.26 = (bf16[2,1,24,1024]{3,2,1,0:T(8,128)(2,1)}, bf16[2,1,24,1024]{3,2,1,0:T(8,128)(2,1)S(1)}, u32[]{:S(2)}, u32[]{:S(2)}) collective-permute-start(bf16[2,1,24,1024]{3,2,1,0:T(8,128)(2,1)} %get-tuple-element.143), channel_id=1, source_target_pairs={{0,8},{8,0},{16,24},{24,16},{1,9},{9,1},{17,25},{25,17},{2,10},{10... | collective-permute-start | bytes 294920 | tf_op jit(solution)/shard_map/ppermute | solution.py:519
  161.3 5.8 %copy-start.16 = (bf16[2,2,24,1024]{3,2,1,0:T(8,128)(2,1)}, bf16[2,2,24,1024]{3,2,1,0:T(8,128)(2,1)S(1)}, u32[]{:S(2)}) copy-start(bf16[2,2,24,1024]{3,2,1,0:T(8,128)(2,1)S(1)} %collective-permute-done.21.refs_10_) | copy-start | bytes 589828
  161.3 21.9 %collective-permute-start.27 = (bf16[2,1,24,1024]{3,2,1,0:T(8,128)(2,1)}, bf16[2,1,24,1024]{3,2,1,0:T(8,128)(2,1)S(1)}, u32[]{:S(2)}, u32[]{:S(2)}) collective-permute-start(bf16[2,1,24,1024]{3,2,1,0:T(8,128)(2,1)} %get-tuple-element.144), channel_id=1, source_target_pairs={{0,16},{8,24},{16,0},{24,8},{1,17},{9,25},{17,1},{25,9},{2,18},{10... | collective-permute-start | bytes 294920 | tf_op jit(solution)/shard_map/ppermute | solution.py:519
  164.7 2.5 %copy-start.17 = (bf16[2,2,24,1024]{3,2,1,0:T(8,128)(2,1)}, bf16[2,2,24,1024]{3,2,1,0:T(8,128)(2,1)S(1)}, u32[]{:S(2)}) copy-start(bf16[2,2,24,1024]{3,2,1,0:T(8,128)(2,1)S(1)} %collective-permute-done.22.refs_11_) | copy-start | bytes 589828
  164.7 18.5 %collective-permute-start.28 = (bf16[2,1,24,1024]{3,2,1,0:T(8,128)(2,1)}, bf16[2,1,24,1024]{3,2,1,0:T(8,128)(2,1)S(1)}, u32[]{:S(2)}, u32[]{:S(2)}) collective-permute-start(bf16[2,1,24,1024]{3,2,1,0:T(8,128)(2,1)} %get-tuple-element.145), channel_id=1, source_target_pairs={{0,24},{8,16},{16,8},{24,0},{1,25},{9,17},{17,9},{25,1},{2,26},{10... | collective-permute-start | bytes 294920 | tf_op jit(solution)/shard_map/ppermute | solution.py:519
  (10 other events, 7.2 us)

commit v6 on v4

--- a/solution.py
+++ b/solution.py
@@ -13,7 +13,7 @@
 TILE = 8
 LANES = 128
 MIB = 1 << 20
-VMEM_LIMIT = 60 * MIB
+VMEM_LIMIT = 62 * MIB
 COST = pl.CostEstimate(flops=1, bytes_accessed=1, transcendentals=0)
 LONG = pl.CostEstimate(flops=10**11, bytes_accessed=100 * MIB, transcendentals=0)
 
@@ -34,17 +34,27 @@
     return [pl.ds(c * LANES, LANES) for c in range(cols // LANES)]
 
 
-def coefficients(cel_ref, base_ref, trn_ref, here, cg, turn, sea):
+def spreads(dirs):
+    both = direction_factors(dirs).sum(axis=0)
+    values = []
+    for value in both:
+        if not any(abs(value - other) < 1e-5 for other in values):
+            values.append(value)
+    return values, np.array([[int(np.argmin([abs(b - v) for v in values])) for b in both]], np.int32)
+
+
+def coefficients(dirs, cel_ref, kept_ref, trn_ref, here, cg, turn, sea):
     sea = sea.astype(jnp.float32)
     celerity = 0.1 + 0.8 * cg.astype(jnp.float32) / 7.0
     turning = 0.3 * jnp.abs(turn.astype(jnp.float32) - 3.5) / 3.5
     cel_ref[here, :] = celerity * sea
-    base_ref[here, :] = (1.0 - turning) * sea
     trn_ref[here, :] = turning * sea
-
-
-def sweep(dirs, tiles, alone, lanes, sign_ref, along_ref, coefs, turns_up, load, store):
-    cel_ref, base_ref, trn_ref = coefs
+    for n, both in enumerate(spreads(dirs)[0]):
+        kept_ref[n, here, :] = (1.0 - float(both) * celerity - turning) * sea
+
+
+def sweep(dirs, tiles, alone, lanes, sign_ref, along_ref, kind_ref, coefs, turns_up, load, store):
+    cel_ref, kept_ref, trn_ref = coefs
     row = lax.broadcasted_iota(jnp.int32, (TILE, LANES), 0)
     lane = lax.broadcasted_iota(jnp.int32, (TILE, LANES), 1)
     nothing = jnp.zeros((TILE, LANES), jnp.float32)
@@ -57,6 +67,7 @@
         previous = jnp.where(d == 0, dirs - 1, d - 1)
         ax = along_ref[0, d]
         ay = along_ref[1, d]
+        kind = kind_ref[0, d]
         right = sign_ref[0, d] > 0
         high = sign_ref[1, d] > 0
         shift_x = jnp.where(right, LANES - 1, 1)
@@ -89,8 +100,8 @@
                     below = lifted[t - 1] if t > 0 else nothing
                     flow_y = jnp.where(at_high, above, jnp.where(at_low, below, lifted[t]))
                 turned = jnp.where(turns_up(t, c), load(t, following, lanes[c]), load(t, previous, lanes[c]))
-                total = base_ref[span(t), lanes[c]] * here[t] + ax * (flow_x - flow[t])
-                total = total + ay * (flow_y - flow[t]) + trn_ref[span(t), lanes[c]] * turned
+                total = kept_ref[kind, span(t), lanes[c]] * here[t] + ax * flow_x
+                total = total + (ay * flow_y + trn_ref[span(t), lanes[c]] * turned)
                 store(t, d, c, total)
             if c + 1 < len(lanes):
                 before = moved
@@ -109,11 +120,11 @@
                 send_refs[k][j, 0, :, here] = swap_ref[c, pl.ds(start, dirs), :].astype(jnp.bfloat16)
 
 
-def inner_kernel(parts, local, chunk, into, own_ref, sign_ref, along_ref, _, forcing_ref, cg_ref, turn_ref, mask_ref, *refs):
-    refs = refs[3:] if into else refs
-    home_ref, first_out, last_out = refs[:3]
+def inner_kernel(parts, local, chunk, into, own_ref, sign_ref, along_ref, kind_ref, _, forcing_ref, cg_ref, turn_ref, mask_ref, *refs):
+    refs = refs[1:] if into else refs
+    home_ref = refs[0]
     sends = parts if chunk else 0
-    cel_ref, base_ref, trn_ref, first_ref, swap_ref, edge_ref = refs[sends + 3 :]
+    cel_ref, kept_ref, trn_ref, first_ref, swap_ref = refs[sends + 1 :]
     dirs, rows, cols = forcing_ref.shape[1:]
     pitch = dirs + 1
     lanes = lane_tiles(cols)
@@ -124,23 +135,7 @@
 
     for t in range(tiles):
         levels = (cg_ref[0, span(t), :], turn_ref[0, span(t), :], mask_ref[span(t), :])
-        coefficients(cel_ref, base_ref, trn_ref, span(t), *levels)
-
-    def outermost(d, carry):
-        for side, t in enumerate((0, tiles - 1)):
-            for c, here in enumerate(lanes):
-                swap_ref[c, pl.ds(side * TILE * pitch + d, TILE, stride=pitch), :] = forcing_ref[0, d, span(t), here]
-        return carry
-
-    lax.fori_loop(0, dirs, outermost, 0, unroll=8)
-    edge_ref[...] = jnp.zeros_like(edge_ref)
-    for out_ref, low, at in ((first_out, 0, 0), (last_out, rows - HALO, 2 * TILE - HALO)):
-        for r in range(HALO):
-            for c, here in enumerate(lanes):
-                edge_ref[:dirs, here] = swap_ref[c, pl.ds((at + r) * pitch, dirs), :]
-            for n, level in enumerate((cg_ref[0], turn_ref[0], mask_ref[...])):
-                edge_ref[dirs + n : dirs + n + 1, :] = level[low + r : low + r + 1].astype(jnp.float32)
-            out_ref[r, 0] = edge_ref[...].astype(jnp.bfloat16)
+        coefficients(dirs, cel_ref, kept_ref, trn_ref, span(t), *levels)
 
     def turns_up(t, c):
         return turn_ref[0, span(t), lanes[c]] >= 4
@@ -153,11 +148,12 @@
         if chunk:
             swap_ref[c, pl.ds(t * TILE * pitch + d, TILE, stride=pitch), :] = value
 
-    step = functools.partial(sweep, dirs, tiles, False, lanes, sign_ref, along_ref, (cel_ref, base_ref, trn_ref), turns_up)
+    coefs = (cel_ref, kept_ref, trn_ref)
+    step = functools.partial(sweep, dirs, tiles, False, lanes, sign_ref, along_ref, kind_ref, coefs, turns_up)
     step(lambda t, d, here: forcing_ref[0, d, span(t), here], store_first)
     step(lambda t, d, here: first_ref[d, span(t), here], store_last)
     if chunk:
-        emit(own_ref[0], parts, local, chunk, dirs, lanes, swap_ref, refs[3 : sends + 3])
+        emit(own_ref[0], parts, local, chunk, dirs, lanes, swap_ref, refs[1 : sends + 1])
 
 
 def inner(own, signs, along, after, forcing, cg, turn, mask, into, parts, chunk, group):
@@ -167,38 +163,87 @@
     smem = pl.BlockSpec(memory_space=pltpu.SMEM)
     levels = pl.BlockSpec((1, rows, cols), lambda f: (begin + f, 0, 0))
     block = pl.BlockSpec((1, dirs, rows, cols), lambda f: (begin + f, 0, 0, 0))
-    edge = pl.BlockSpec((HALO, 1, dirs + TILE, cols), lambda f: (0, begin + f, 0, 0))
-    edge_shape = jax.ShapeDtypeStruct((HALO, freqs, dirs + TILE, cols), jnp.bfloat16)
     coefs = pltpu.VMEM((rows, cols), jnp.float32)
     sends = parts if chunk else 0
     count = chunk[2] if chunk else 0
     outs = pl.pallas_call(
         functools.partial(inner_kernel, parts, local, chunk, into is not None),
         grid=(many,),
-        in_specs=[smem, smem, smem, UNREAD, block, levels, levels, pl.BlockSpec((rows, cols), lambda f: (0, 0))]
-        + ([] if into is None else [UNREAD] * 3),
-        out_specs=[block, edge, edge] + [pl.BlockSpec((count, 1, dirs, cols), lambda f: (0, f, 0, 0))] * sends,
-        out_shape=[jax.ShapeDtypeStruct(forcing.shape, jnp.float32), edge_shape, edge_shape]
+        in_specs=[smem, smem, smem, smem, UNREAD, block, levels, levels, pl.BlockSpec((rows, cols), lambda f: (0, 0))]
+        + ([] if into is None else [UNREAD]),
+        out_specs=[block] + [pl.BlockSpec((count, 1, dirs, cols), lambda f: (0, f, 0, 0))] * sends,
+        out_shape=[jax.ShapeDtypeStruct(forcing.shape, jnp.float32)]
         + [jax.ShapeDtypeStruct((count, many, dirs, cols), jnp.bfloat16)] * sends,
         scratch_shapes=[
             coefs,
-            coefs,
+            pltpu.VMEM((len(spreads(dirs)[0]), rows, cols), jnp.float32),
             coefs,
             pltpu.VMEM((dirs, rows, cols), jnp.float32),
             pltpu.VMEM((cols // LANES, rows * (dirs + 1), LANES), jnp.float32),
+        ],
+        input_output_aliases={} if into is None else {9: 0},
+        compiler_params=pltpu.CompilerParams(vmem_limit_bytes=VMEM_LIMIT),
+        cost_estimate=COST,
+    )(own, signs, *along, after, forcing, cg, turn, mask, *([] if into is None else [into]))
+    return outs[0], list(outs[1:])
+
+
+def edges_kernel(_, *refs):
+    swap_ref, edge_ref = refs[-2:]
+    dirs, _, cols = refs[0].shape[1:]
+    pitch = dirs + 1
+    lanes = lane_tiles(cols)
+    edge_ref[...] = jnp.zeros_like(edge_ref)
+    for side, low in ((0, 0), (1, TILE - HALO)):
+        forcing_ref, cg_ref, turn_ref, mask_ref = refs[4 * side : 4 * side + 4]
+        out_ref = refs[8 + side]
+
+        def body(d, carry, forcing_ref=forcing_ref):
+            for c, here in enumerate(lanes):
+                swap_ref[c, pl.ds(d, TILE, stride=pitch), :] = forcing_ref[0, d, :, here]
+            return carry
+
+        lax.fori_loop(0, dirs, body, 0, unroll=12)
+        for r in range(HALO):
+            for c, here in enumerate(lanes):
+                edge_ref[:dirs, here] = swap_ref[c, pl.ds((low + r) * pitch, dirs), :]
+            for n, level in enumerate((cg_ref[0], turn_ref[0], mask_ref[...])):
+                edge_ref[dirs + n : dirs + n + 1, :] = level[low + r : low + r + 1].astype(jnp.float32)
+            out_ref[r, 0] = edge_ref[...].astype(jnp.bfloat16)
+
+
+def edges(after, forcing, cg, turn, mask):
+    freqs, dirs, rows, cols = forcing.shape
+    out = pl.BlockSpec((HALO, 1, dirs + TILE, cols), lambda f: (0, f, 0, 0))
+    shape = jax.ShapeDtypeStruct((HALO, freqs, dirs + TILE, cols), jnp.bfloat16)
+    in_specs = [UNREAD]
+    for t in (0, rows // TILE - 1):
+        in_specs += [
+            pl.BlockSpec((1, dirs, TILE, cols), lambda f, t=t: (f, 0, t, 0)),
+            pl.BlockSpec((1, TILE, cols), lambda f, t=t: (f, t, 0)),
+            pl.BlockSpec((1, TILE, cols), lambda f, t=t: (f, t, 0)),
+            pl.BlockSpec((TILE, cols), lambda f, t=t: (t, 0)),
+        ]
+    return pl.pallas_call(
+        edges_kernel,
+        grid=(freqs,),
+        in_specs=in_specs,
+        out_specs=[out, out],
+        out_shape=[shape, shape],
+        scratch_shapes=[
+            pltpu.VMEM((cols // LANES, TILE * (dirs + 1), LANES), jnp.float32),
             pltpu.VMEM((dirs + TILE, cols), jnp.float32),
         ],
-        input_output_aliases={} if into is None else {8: 0, 9: 1, 10: 2},
         compiler_params=pltpu.CompilerParams(vmem_limit_bytes=VMEM_LIMIT),
         cost_estimate=COST,
-    )(own, signs, along, after, forcing, cg, turn, mask, *([] if into is None else into))
-    return outs[:3], list(outs[3:])
+    )(after, *(2 * [forcing, cg, turn, mask]))
 
 
 def outer_kernel(parts, local, chunk, *refs):
-    own_ref, sign_ref, along_ref, _, above_ref, below_ref, cg_ref, turn_ref, mask_ref, home_ref, share_ref = refs[:11]
-    send_refs = refs[11 : 11 + parts]
-    cel_ref, base_ref, trn_ref, up_ref, lev_ref, near_ref, first_ref, side_ref, edge_ref, swap_ref = refs[11 + parts :]
+    own_ref, sign_ref, along_ref, kind_ref, _, above_ref, below_ref = refs[:7]
+    cg_ref, turn_ref, mask_ref, home_ref, share_ref = refs[7:12]
+    send_refs = refs[12 : 12 + parts]
+    cel_ref, kept_ref, trn_ref, up_ref, lev_ref, near_ref, first_ref, side_ref, edge_ref, swap_ref = refs[12 + parts :]
     dirs, rows, cols = home_ref.shape[1:]
     freqs = share_ref.shape[0]
     pitch = dirs + 1
@@ -231,7 +276,7 @@
                     near_ref[q * TILE + low : q * TILE + low + 1, :] = lev_ref[i * TILE + q : i * TILE + q + 1, :]
                 near_ref[q * TILE + HALO : q * TILE + 2 * HALO, :] = mine[:HALO].astype(jnp.float32)
                 near_ref[q * TILE + 2 * HALO : q * TILE + 3 * HALO, :] = mine[rows - HALO :].astype(jnp.float32)
-            coefficients(cel_ref, base_ref, trn_ref, span(n), *[near_ref[span(q), :] for q in range(3)])
+            coefficients(dirs, cel_ref, kept_ref, trn_ref, span(n), *[near_ref[span(q), :] for q in range(3)])
             up_ref[span(n), :] = near_ref[span(1), :]
 
         def turns_up(t, c):
@@ -243,7 +288,8 @@
         def store_last(t, d, c, value):
             share_ref[t, d, :, lanes[c]] = value
 
-        step = functools.partial(sweep, dirs, freqs, True, lanes, sign_ref, along_ref, (cel_ref, base_ref, trn_ref), turns_up)
+        coefs = (cel_ref, kept_ref, trn_ref)
+        step = functools.partial(sweep, dirs, freqs, True, lanes, sign_ref, along_ref, kind_ref, coefs, turns_up)
         step(lambda t, d, here: side_ref[d, span(t), here], store_first)
         step(lambda t, d, here: first_ref[d, span(t), here], store_last)
 
@@ -277,7 +323,7 @@
     outs = pl.pallas_call(
         functools.partial(outer_kernel, parts, local, chunk),
         grid=(freqs,),
-        in_specs=[smem, smem, smem, UNREAD, edge, edge, levels, levels]
+        in_specs=[smem, smem, smem, smem, UNREAD, edge, edge, levels, levels]
         + [pl.BlockSpec((rows, cols), lambda f: (0, 0)), pl.BlockSpec((1, dirs, rows, cols), lambda f: (f, 0, 0, 0))],
         out_specs=[pl.BlockSpec((freqs, dirs, TILE, cols), lambda f: (0, 0, 0, 0))]
         + [pl.BlockSpec((chunk[2], 1, dirs, cols), lambda f: (0, f, 0, 0))] * parts,
@@ -285,7 +331,7 @@
         + [jax.ShapeDtypeStruct((chunk[2], freqs, dirs, cols), jnp.bfloat16)] * parts,
         scratch_shapes=[
             tall,
-            tall,
+            pltpu.VMEM((len(spreads(dirs)[0]), freqs * TILE, cols), jnp.float32),
             tall,
             tall,
             pltpu.VMEM((2 * HALO * TILE, cols), jnp.float32),
@@ -297,43 +343,49 @@
         ],
         compiler_params=pltpu.CompilerParams(vmem_limit_bytes=VMEM_LIMIT),
         cost_estimate=LONG,
-    )(own, signs, along, after, above, below, cg, turn, mask, home)
+    )(own, signs, *along, after, above, below, cg, turn, mask, home)
     return outs[0], list(outs[1:])
 
 
-def by_row_kernel(_, state_ref, out_ref, swap_ref):
-    deep, local, _ = state_ref.shape
-    pitch = deep + 1
+def by_row_kernel(*refs):
+    state_ref, out_ref, swap_ref = refs[-3:]
+    some, local, cols = state_ref.shape
+    pitch = some + 1
+    lanes = lane_tiles(cols)
 
     def body(d, carry):
-        swap_ref[pl.ds(d, local, stride=pitch), :] = state_ref[d].astype(jnp.float32)
+        for c, here in enumerate(lanes):
+            swap_ref[c, pl.ds(d, local, stride=pitch), :] = state_ref[d, :, here].astype(jnp.float32)
         return carry
 
-    lax.fori_loop(0, deep, body, 0, unroll=64)
+    lax.fori_loop(0, some, body, 0, unroll=8)
     for r in range(local):
-        out_ref[r] = swap_ref[pl.ds(r * pitch, deep), :].astype(jnp.bfloat16)
+        for c, here in enumerate(lanes):
+            out_ref[r, :, here] = swap_ref[c, pl.ds(r * pitch, some), :].astype(jnp.bfloat16)
 
 
 def by_row(after, state):
     deep, local, cols = state.shape
+    some = 48
     return pl.pallas_call(
         by_row_kernel,
-        grid=(cols // LANES,),
-        in_specs=[UNREAD, pl.BlockSpec((deep, local, LANES), lambda c: (0, 0, c))],
-        out_specs=pl.BlockSpec((local, deep, LANES), lambda c: (0, 0, c)),
+        grid=(deep // some,),
+        in_specs=[UNREAD] * len(after) + [pl.BlockSpec((some, local, cols), lambda d: (d, 0, 0))],
+        out_specs=pl.BlockSpec((local, some, cols), lambda d: (0, d, 0)),
         out_shape=jax.ShapeDtypeStruct((local, deep, cols), jnp.bfloat16),
-        scratch_shapes=[pltpu.VMEM((local * (deep + 1), LANES), jnp.float32)],
+        scratch_shapes=[pltpu.VMEM((cols // LANES, local * (some + 1), LANES), jnp.float32)],
         compiler_params=pltpu.CompilerParams(vmem_limit_bytes=VMEM_LIMIT),
         cost_estimate=COST,
-    )(after, state)
-
-
-def turned_kernel(_, w_in_ref, w_out_ref, in_t_ref, out_t_ref):
+    )(*after, state)
+
+
+def turned_kernel(_, w_in_ref, w_out_ref, weight_ref, in_t_ref, out_t_ref, column_ref):
     in_t_ref[...] = w_in_ref[...].T
     out_t_ref[...] = w_out_ref[...].T
-
-
-def turned(after, w_in, w_out):
+    column_ref[...] = jnp.broadcast_to(weight_ref[...], (LANES, weight_ref.shape[1])).T
+
+
+def turned(after, w_in, w_out, weight):
     hidden, total = w_in.shape
     step = 512
     tall = pl.BlockSpec((step, total), lambda h: (h, 0))
@@ -341,15 +393,19 @@
     return pl.pallas_call(
         turned_kernel,
         grid=(hidden // step,),
-        in_specs=[UNREAD, tall, wide],
-        out_specs=[wide, tall],
-        out_shape=[jax.ShapeDtypeStruct((total, hidden), w_in.dtype), jax.ShapeDtypeStruct((hidden, total), w_in.dtype)],
+        in_specs=[UNREAD, tall, wide, pl.BlockSpec((1, step), lambda h: (0, h))],
+        out_specs=[wide, tall, pl.BlockSpec((step, LANES), lambda h: (h, 0))],
+        out_shape=[
+            jax.ShapeDtypeStruct((total, hidden), w_in.dtype),
+            jax.ShapeDtypeStruct((hidden, total), w_in.dtype),
+            jax.ShapeDtypeStruct((hidden, LANES), jnp.float32),
+        ],
         compiler_params=pltpu.CompilerParams(vmem_limit_bytes=VMEM_LIMIT),
-        cost_estimate=COST,
-    )(after, w_in, w_out)
-
-
-def source_kernel(parts, got, sent, dirs, step, own_ref, _, state_ref, wind_ref, w_in_ref, out_t_ref, in_t_ref, weight_ref, *refs):
+        cost_estimate=LONG,
+    )(after, w_in, w_out, weight.reshape(1, hidden))
+
+
+def source_kernel(parts, got, sent, dirs, step, first, chunk, own_ref, _, state_ref, wind_ref, w_in_ref, out_t_ref, in_t_ref, weight_ref, *refs):
     cell_refs = refs[: parts * len(got)]
     grad_ref = refs[parts * len(got)]
     back_refs = refs[parts * len(got) + 1 : -3]
@@ -368,11 +424,11 @@
             cell_ref[place(k, group), :] = piece.reshape(group[1] * dirs, width)
     cell = cell_ref[...].astype(jnp.bfloat16)
     state = state_ref[0]
-    wind = wind_ref[0]
+    wind = wind_ref[pl.ds(chunk_row(own, first + pl.program_id(0), chunk), 1), :]
     grad = jnp.zeros((TILE, width), jnp.float32)
     for h in range(0, hidden, step):
         some = pl.ds(h, step)
-        weight = weight_ref[some, :]
+        weight = weight_ref[some, :1]
         forward = jnp.dot(w_in_ref[some, :], state, preferred_element_type=jnp.float32) + weight * wind
         squash = jnp.tanh(forward)
         pulled = jnp.dot(out_t_ref[some, :], cell, preferred_element_type=jnp.float32)
@@ -405,18 +461,18 @@
     ]
     back_specs = [pl.BlockSpec((1, many, dirs, width), lambda j, c, own_ref: (j, 0, 0, c)) for _, many in sent for _ in range(parts)]
     outs = pl.pallas_call(
-        functools.partial(source_kernel, parts, got, sent, dirs, 256),
+        functools.partial(source_kernel, parts, got, sent, dirs, 256, first, chunk),
         grid_spec=pltpu.PrefetchScalarGridSpec(
             num_scalar_prefetch=1,
             grid=(count, cols // width),
             in_specs=[
                 UNREAD,
                 pl.BlockSpec((1, total, width), lambda j, c, own_ref: (row_of(j, own_ref), 0, c)),
-                pl.BlockSpec((1, 1, width), lambda j, c, own_ref: (row_of(j, own_ref), 0, c)),
+                pl.BlockSpec((wind.shape[0], width), lambda j, c, own_ref: (0, c)),
                 whole((hidden, total)),
                 whole((hidden, total)),
                 whole((total, hidden)),
-                whole((hidden, 1)),
+                whole((hidden, LANES)),
             ]
             + cell_specs,
             out_specs=[pl.BlockSpec((1, 1, width), lambda j, c, own_ref: (j, 0, c))] + back_specs,
@@ -458,7 +514,7 @@
                 out_ref[0, d, pl.ds(t * TILE, TILE), here] = value + grown
         return carry
 
-    lax.fori_loop(0, dirs, body, 0, unroll=12)
+    lax.fori_loop(0, dirs, body, 0, unroll=2)
 
 
 def join(own, into, home, share, early, late, rows_of, chunks, group):
@@ -467,20 +523,19 @@
     _, dirs, rows, cols = home.shape
     last = late[0].shape[0]
     spans = [(*span, chunks[0]) for span in rows_of] + [(0, last, chunks[-1])]
-    width = min(cols, 256)
-    block = pl.BlockSpec((1, dirs, rows, width), lambda f, c: (begin + f, 0, 0, c))
+    block = pl.BlockSpec((1, dirs, rows, cols), lambda f: (begin + f, 0, 0, 0))
     specs = [
-        pl.BlockSpec((count, 1, dirs, width), lambda f, c: (0, begin + f, 0, c)) for _, count in rows_of for _ in range(parts)
-    ] + [pl.BlockSpec((last, 1, dirs, width), lambda f, c: (0, f, 0, c))] * parts
+        pl.BlockSpec((count, 1, dirs, cols), lambda f: (0, begin + f, 0, 0)) for _, count in rows_of for _ in range(parts)
+    ] + [pl.BlockSpec((last, 1, dirs, cols), lambda f: (0, f, 0, 0))] * parts
     return pl.pallas_call(
         functools.partial(join_kernel, parts, spans),
-        grid=(many, cols // width),
+        grid=(many,),
         in_specs=[pl.BlockSpec(memory_space=pltpu.SMEM), UNREAD, block]
-        + [pl.BlockSpec((1, dirs, TILE, width), lambda f, c: (begin + f, 0, 0, c))]
+        + [pl.BlockSpec((1, dirs, TILE, cols), lambda f: (begin + f, 0, 0, 0))]
         + specs,
         out_specs=block,
         out_shape=jax.ShapeDtypeStruct(home.shape, jnp.float32),
-        scratch_shapes=[pltpu.VMEM((width // LANES, rows * (dirs + 1), LANES), jnp.float32)],
+        scratch_shapes=[pltpu.VMEM((cols // LANES, rows * (dirs + 1), LANES), jnp.float32)],
         input_output_aliases={} if begin == 0 else {1: 0},
         compiler_params=pltpu.CompilerParams(vmem_limit_bytes=VMEM_LIMIT),
         cost_estimate=COST,
@@ -514,15 +569,6 @@
     up = [(i, i + 1) for i in range(count - 1)]
     down = [(i + 1, i) for i in range(count - 1)]
     return lax.ppermute(high, "space", up), lax.ppermute(low, "space", down)
-
-
-def halves(count):
-    spans, begin = [], 0
-    while begin < count:
-        many = max(1, (count - begin) // 2)
-        spans.append((begin, many))
-        begin += many
-    return spans
 
 
 def shards(
@@ -544,14 +590,12 @@
     comps, rows, cols = adjoint_forcing.shape
     freqs = comps // dirs
     local = rows // parts
-    along = jnp.asarray(direction_factors(dirs))
+    along = (jnp.asarray(direction_factors(dirs)), jnp.asarray(spreads(dirs)[1]))
     forcing = adjoint_forcing.reshape(freqs, dirs, rows, cols)
-    weight = wind_weight[:, None]
-    wind = wind_speed[:, None]
     everything = [(0, freqs)]
     many = freqs // 2 if freqs % 2 == 0 else freqs
     groups = [(begin, many) for begin in range(0, freqs, many)]
-    sent = halves(freqs)
+    sent = groups
     levels = (cg_index, turn_index, sea_mask)
     if local > HALO:
         chunks = [(HALO, 0, local - HALO), (0, local - HALO, HALO)]
@@ -559,24 +603,29 @@
         chunks = [(0, 0, local)]
     ahead = chunks[0] if len(chunks) > 1 else None
 
-    early, into, after = [], None, sea_mask
-    for group in groups:
-        into, pieces = inner(own, dir_sign, along, after, forcing, *levels, into, parts, ahead, group)
+    early, home, after = [], None, sea_mask
+    for g, group in enumerate(groups):
+        home, pieces = inner(own, dir_sign, along, after, forcing, *levels, home, parts, ahead, group)
         if ahead:
             early.append(swapped(pieces))
-    home, low, high = into
+        if g == 0:
+            low, high = edges(pieces[-1] if ahead else home, forcing, *levels)
+            after = high
     above, below = across(low, high)
-    after = arrived(home, early[0][1:])[0] if len(early) > 1 else home
-    state = by_row(after, forward_state)
-    in_t, out_t = turned(state, w_in, w_out)
-    share, pieces = outer(own, dir_sign, along, in_t, above, below, *levels, home, parts, chunks[-1])
+    after = home
+    for pieces in early[:-1]:
+        after, _ = arrived(after, pieces[1:])
+    state = by_row((after,), forward_state)
+    share, pieces = outer(own, dir_sign, along, state, above, below, *levels, home, parts, chunks[-1])
     late = swapped(pieces)
+    in_t, out_t, weight = turned(share, w_in, w_out, wind_weight)
     term = functools.partial(source_term, own)
-    fixed = (state, wind, w_in, out_t, in_t, weight)
-    after, grads, early_back, rows_of = share, [], [], []
+    fixed = (state, wind_speed, w_in, out_t, in_t, weight)
+    after, grads, early_back, rows_of = in_t, [], [], []
     if ahead:
         count = ahead[2]
-        rows_of = [(0, count // 2), (count // 2, count - count // 2)] if count > 1 else [(0, count)]
+        some = 2 if count % 2 == 0 else 1
+        rows_of = [(first, some) for first in range(0, count, some)]
     for span in rows_of:
         grad, [back] = term(after, *fixed, early, groups, everything, span, ahead)
         after = grad
@@ -586,15 +635,12 @@
         grads.append(grad)
         early_back.append(swapped(back))
     late_grad, late_back = term(after, *fixed, [late], everything, sent, (0, chunks[-1][2]), chunks[-1])
-    start, returned = late_grad, []
-    for g, pieces in enumerate(late_back):
-        if g < len(early_back):
-            rest = [piece for group in late_back[g:] for piece in group[1:]]
-            start, rest = arrived(start, early_back[g][1:], rest)
-            for n, group in enumerate(late_back[g:]):
-                late_back[g + n] = [group[0], *rest[n * (parts - 1) : (n + 1) * (parts - 1)]]
-        returned.append(swapped(late_back[g]))
-    late_back = returned
+    start = late_grad
+    if early_back:
+        start, rest = arrived(start, early_back[0][1:], [piece for pieces in late_back for piece in pieces[1:]])
+        step = parts - 1
+        late_back = [[pieces[0], *rest[g * step : (g + 1) * step]] for g, pieces in enumerate(late_back)]
+    late_back = [swapped(pieces) for pieces in late_back]
     for group, back in zip(sent, late_back, strict=True):
         start = join(own, start, home, share, early_back, back, rows_of, chunks, group)
     gradient = jnp.where(

time: 187 us -> 173 us (0.925)
  waiting for transfers between devices: 24.3 us -> 15.2 us
  local copies, waits for them, and re-layouts: 8.4 us -> 3.67 us
    ppermute x24, waiting for transfers between devices: 24.3 us -> 15.2 us  [swapped(): lax.ppermute(pieces[k], 'comp', [(i, i ^ k) for i in range(parts)])]
    unnamed x56 -> x44, local copies, waits for them, and re-layouts: 6.6 us -> 3.07 us
    pallas_call x3 -> x4, Pallas kernels: 53.3 us -> 56.5 us  [source_term(): pl.pallas_call(functools.partial(source_kernel, parts, got, sent, dirs, 2...]
    pallas_call x2, Pallas kernels: 27.1 us -> 24.2 us  [inner(): pl.pallas_call(functools.partial(inner_kernel, parts, local, chunk, into...]
  transfers between devices with their start and end apart: 26 -> 26, of which waited for: 5 -> 5; matrix products, arithmetic and copies ran while one was open for 2% -> 1% of each run, Pallas kernels for 57% -> 62%
where the time goes in v6:
time: 173 us; the launch traced here: 172 us
  Pallas kernels  126 us (73%)
  starting transfers between devices  25.6 us (15%)
  waiting for transfers between devices  15.2 us (9%)
  local copies, waits for them, and re-layouts  3.67 us (2%)
    pallas_call x4, Pallas kernels, source_term(): pl.pallas_call(functools.partial(source_kernel, parts, got, sent, dirs, 2...  56.5 us
    pallas_call x2, Pallas kernels, inner(): pl.pallas_call(functools.partial(inner_kernel, parts, local, chunk, into...  24.2 us
    ppermute x24, starting transfers between devices, swapped(): lax.ppermute(pieces[k], 'comp', [(i, i ^ k) for i in range(parts)])  19 us
    ppermute x24, waiting for transfers between devices, swapped(): lax.ppermute(pieces[k], 'comp', [(i, i ^ k) for i in range(parts)])  15.2 us
    pallas_call x2, Pallas kernels, join(): pl.pallas_call(functools.partial(join_kernel, parts, spans), grid=(many,)...  13.1 us
    pallas_call x1, Pallas kernels, outer(): pl.pallas_call(functools.partial(outer_kernel, parts, local, chunk), grid...  12.6 us
    pallas_call x1, Pallas kernels, by_row(): pl.pallas_call(by_row_kernel, grid=(deep // some,), in_specs=[UNREAD] * l...  8.43 us
    ppermute x2, starting transfers between devices, across(): return (lax.ppermute(high, 'space', up), lax.ppermute(low, 'space', down))  6.65 us
  transfers between devices with their start and end apart: 26, of which 5 were waited for; matrix products, arithmetic and copies ran while one was open for 1% of the time, Pallas kernels for 62%

profile of v6, /device:TPU:0, one launch (start us, length us, event | category | flops | bytes accessed | tf_op | source)
XLA Modules:
  0.0 172.1 jit_solution(15610850654238203763)
XLA Ops:
  0.6 12.1 %shard_map.131 = (f32[4,24,32,1024]{3,2,1,0:T(8,128)}, bf16[6,2,24,1024]{3,2,1,0:T(8,128)(2,1)}, bf16[6,2,24,1024]{3,2,1,0:T(8,128)(2,1)}, bf16[6,2,24,1024]{3,2,1,0:T(8,128)(2,1)}, bf16[6,2,24,1024]{3,2,1,0:T(8,128)(2,1)}) custom-call(s32[1]{0:T(128)} %bitcast.own_ref.refs_0_, s32[2,24]{1,0:T(2,128)} %refs_1_.5, f32[2,24]{1,0:T(2,128)} %constant.11.clone.along_ref.refs_2_, ...), custom_call_target="tpu_custom_call" | custom-call | flops 1 | bytes 1 | tf_op jit(solution)/shard_map/pallas_call | solution.py:169
  12.8 0.5 collective-permute-start
  13.2 2.6 %collective-permute-start.1 = (bf16[6,2,24,1024]{3,2,1,0:T(8,128)(2,1)}, bf16[6,2,24,1024]{3,2,1,0:T(8,128)(2,1)S(1)}, u32[]{:S(2)}, u32[]{:S(2)}) collective-permute-start(bf16[6,2,24,1024]{3,2,1,0:T(8,128)(2,1)} %get-tuple-element.62), channel_id=1, source_target_pairs={{0,16},{8,24},{16,0},{24,8},{1,17},{9,25},{17,1},{25,9},{2,18},{10... | collective-permute-start | bytes 1769480 | tf_op jit(solution)/shard_map/ppermute | solution.py:563
  15.9 4.9 %shard_map.132 = (bf16[2,4,32,1024]{3,2,1,0:T(8,128)(2,1)}, bf16[2,4,32,1024]{3,2,1,0:T(8,128)(2,1)}) custom-call(bf16[6,2,24,1024]{3,2,1,0:T(8,128)(2,1)} %get-tuple-element.57._, f32[4,24,32,1024]{3,2,1,0:T(8,128)} %bitcast.12, s32[4,32,1024]{2,1,0:T(8,128)} %refs_7_.3, s32[4,32,1024]{2,1,0:T(8,128)} %refs_8_.1, s32[32,1024]{1,0:T(8,128)} %refs_9_.1, ...), custom_call_target="tpu_custom_call" | custom-call | flops 1 | bytes 1 | tf_op jit(solution)/shard_map/pallas_call | solution.py:227
  20.8 1.3 collective-permute-start.4
  22.1 5.4 %collective-permute-start.3 = (bf16[2,4,32,1024]{3,2,1,0:T(8,128)(2,1)}, bf16[2,4,32,1024]{3,2,1,0:T(8,128)(2,1)}, u32[]{:S(2)}, u32[]{:S(2)}) collective-permute-start(bf16[2,4,32,1024]{3,2,1,0:T(8,128)(2,1)} %get-tuple-element.58._), channel_id=1, source_target_pairs={{0,1},{1,2},{2,3},{3,4},{4,5},{5,6},{6,7},{8,9},{9,10},{10,11},{11... | collective-permute-start | bytes 1572872 | tf_op jit(solution)/shard_map/ppermute | solution.py:571
  27.5 12.1 %shard_map.133 = (f32[4,24,32,1024]{3,2,1,0:T(8,128)}, bf16[6,2,24,1024]{3,2,1,0:T(8,128)(2,1)}, bf16[6,2,24,1024]{3,2,1,0:T(8,128)(2,1)}, bf16[6,2,24,1024]{3,2,1,0:T(8,128)(2,1)}, bf16[6,2,24,1024]{3,2,1,0:T(8,128)(2,1)}) custom-call(s32[1]{0:T(128)} %bitcast.own_ref.refs_0_, s32[2,24]{1,0:T(2,128)} %refs_1_.5, ...), custom_call_target="tpu_custom_call", output_to_operand_aliasing={{0}: (9, {})} | custom-call | flops 1 | bytes 1 | tf_op jit(solution)/shard_map/pallas_call | solution.py:169
  39.6 0.6 reshape.60.weight_ref
  40.2 1.8 %collective-permute-start.6 = (bf16[6,2,24,1024]{3,2,1,0:T(8,128)(2,1)}, bf16[6,2,24,1024]{3,2,1,0:T(8,128)(2,1)}, u32[]{:S(2)}, u32[]{:S(2)}) collective-permute-start(bf16[6,2,24,1024]{3,2,1,0:T(8,128)(2,1)} %get-tuple-element.71), channel_id=1, source_target_pairs={{0,16},{8,24},{16,0},{24,8},{1,17},{9,25},{17,1},{25,9},{2,18},{10... | collective-permute-start | bytes 1769480 | tf_op jit(solution)/shard_map/ppermute | solution.py:563
  42.3 1.4 collective-permute-start.7
  43.8 0.6 shard_map.134.refs_0_
  44.4 8.4 %shard_map.135.refs_4_.state_ref = bf16[8,384,1024]{2,1,0:T(8,128)(2,1)} custom-call(f32[8,128]{1,0:T(8,128)} %shard_map.134.refs_0_, bf16[384,8,1024]{2,1,0:T(8,128)(2,1)} %refs_1_.4), custom_call_target="tpu_custom_call" | custom-call | flops 1 | bytes 1 | tf_op jit(solution)/shard_map/pallas_call | solution.py:370
  52.8 12.6 %shard_map.136 = (f32[4,24,8,1024]{3,2,1,0:T(8,128)}, bf16[2,4,24,1024]{3,2,1,0:T(8,128)(2,1)}, bf16[2,4,24,1024]{3,2,1,0:T(8,128)(2,1)}, bf16[2,4,24,1024]{3,2,1,0:T(8,128)(2,1)}, bf16[2,4,24,1024]{3,2,1,0:T(8,128)(2,1)}) custom-call(s32[1]{0:T(128)} %bitcast.own_ref.refs_0_, s32[2,24]{1,0:T(2,128)} %refs_1_.5, f32[2,24]{1,0:T(2,128)} %constant.11.clone.along_ref.refs_2_, ...), custom_call_target="tpu_custom_call" | custom-call | flops 99999997952 | bytes 104857600 | tf_op jit(solution)/shard_map/pallas_call | solution.py:323
  65.7 1.0 collective-permute-start.9
  66.6 0.7 collective-permute-start.10
  67.3 4.4 %shard_map.137 = (bf16[384,1536]{1,0:T(8,128)(2,1)}, bf16[1536,384]{1,0:T(8,128)(2,1)}, f32[1536,128]{1,0:T(8,128)}) custom-call(f32[4,24,8,1024]{3,2,1,0:T(8,128)} %get-tuple-element.64._.share_ref, bf16[1536,384]{1,0:T(8,128)(2,1)} %w_in_ref.9, bf16[384,1536]{1,0:T(8,128)(2,1)} %w_out_ref.1, f32[1,1536]{1,0:T(1,128)} %reshape.60.weight_ref), custom_call_target="tpu_custom_call" | custom-call | flops 99999997952 | bytes 104857600 | tf_op jit(solution)/shard_map/pallas_call | solution.py:393
  71.7 14.1 %shard_map.138 = (f32[2,1,1024]{2,1,0:T(1,128)}, bf16[2,4,24,1024]{3,2,1,0:T(8,128)(2,1)}, bf16[2,4,24,1024]{3,2,1,0:T(8,128)(2,1)}, bf16[2,4,24,1024]{3,2,1,0:T(8,128)(2,1)}, bf16[2,4,24,1024]{3,2,1,0:T(8,128)(2,1)}) custom-call(s32[1]{0:T(128)} %bitcast.own_ref.refs_0_, bf16[384,1536]{1,0:T(8,128)(2,1)} %get-tuple-element.65._.in_t_ref, ...), custom_call_target="tpu_custom_call" | custom-call | flops 1 | bytes 1 | tf_op jit(solution)/shard_map/pallas_call | solution.py:463
  85.9 0.7 copy-done.8
  86.9 0.6 shard_map.139
  87.5 0.5 collective-permute-start.11
  88.0 1.0 collective-permute-start.12
  89.0 0.4 collective-permute-start.13
  89.3 14.1 %shard_map.140 = (f32[2,1,1024]{2,1,0:T(1,128)}, bf16[2,4,24,1024]{3,2,1,0:T(8,128)(2,1)}, bf16[2,4,24,1024]{3,2,1,0:T(8,128)(2,1)}, bf16[2,4,24,1024]{3,2,1,0:T(8,128)(2,1)}, bf16[2,4,24,1024]{3,2,1,0:T(8,128)(2,1)}) custom-call(s32[1]{0:T(128)} %bitcast.own_ref.refs_0_, f32[8,128]{1,0:T(8,128)} %get-tuple-element.80._, ...), custom_call_target="tpu_custom_call" | custom-call | flops 1 | bytes 1 | tf_op jit(solution)/shard_map/pallas_call | solution.py:463
  103.4 0.9 collective-permute-start.14
  104.3 1.0 collective-permute-start.15
  105.3 14.1 %shard_map.141 = (f32[2,1,1024]{2,1,0:T(1,128)}, bf16[2,4,24,1024]{3,2,1,0:T(8,128)(2,1)}, bf16[2,4,24,1024]{3,2,1,0:T(8,128)(2,1)}, bf16[2,4,24,1024]{3,2,1,0:T(8,128)(2,1)}, bf16[2,4,24,1024]{3,2,1,0:T(8,128)(2,1)}) custom-call(s32[1]{0:T(128)} %bitcast.own_ref.refs_0_, f32[2,1,1024]{2,1,0:T(1,128)} %get-tuple-element.81._, ...), custom_call_target="tpu_custom_call" | custom-call | flops 1 | bytes 1 | tf_op jit(solution)/shard_map/pallas_call | solution.py:463
  119.4 0.5 collective-permute-start.16
  119.9 0.7 collective-permute-start.17
  120.7 1.0 collective-permute-start.18
  121.7 0.5 collective-permute-start.19
  122.1 14.2 %shard_map.142 = (f32[2,1,1024]{2,1,0:T(1,128)}, bf16[2,2,24,1024]{3,2,1,0:T(8,128)(2,1)}, bf16[2,2,24,1024]{3,2,1,0:T(8,128)(2,1)}, bf16[2,2,24,1024]{3,2,1,0:T...) custom-call(s32[1]{0:T(128)} %bitcast.own_ref.refs_0_, ...), custom_call_target="tpu_custom_call" | custom-call | flops 1 | bytes 1 | tf_op jit(solution)/shard_map/pallas_call | solution.py:463
  136.3 0.6 shard_map.143
  136.9 0.8 collective-permute-start.20
  137.7 0.7 copy_bitcast_fusion.2
  138.4 1.0 collective-permute-start.21
  139.4 0.4 collective-permute-start.22
  139.9 0.7 collective-permute-start.23
  140.6 7.5 %collective-permute-done.19.refs_11_ = bf16[2,4,24,1024]{3,2,1,0:T(8,128)(2,1)} collective-permute-done((bf16[2,4,24,1024]{3,2,1,0:T(8,128)(2,1)}, bf16[2,4,24,1024]{3,2,1,0:T(8,128)(2,1)}, u32[]{:S(2)}, u32[]{:S(2)}) %collective-permute-start.19) | collective-permute-done | bytes 393248 | tf_op jit(solution)/shard_map/ppermute | solution.py:563
  148.1 1.0 collective-permute-start.24
  149.1 0.4 collective-permute-start.25
  149.5 0.7 maximum_select_fusion
  150.2 2.0 %collective-permute-done.21.refs_14_ = bf16[2,2,24,1024]{3,2,1,0:T(8,128)(2,1)S(1)} collective-permute-done((bf16[2,2,24,1024]{3,2,1,0:T(8,128)(2,1)}, bf16[2,2,24,1024]{3,2,1,0:T(8,128)(2,1)S(1)}, u32[]{:S(2)}, u32[]{:S(2)}) %collective-permute-start.21) | collective-permute-done | bytes 196640 | tf_op jit(solution)/shard_map/ppermute | solution.py:563
  152.1 4.2 %collective-permute-done.22.refs_15_ = bf16[2,2,24,1024]{3,2,1,0:T(8,128)(2,1)S(1)} collective-permute-done((bf16[2,2,24,1024]{3,2,1,0:T(8,128)(2,1)}, bf16[2,2,24,1024]{3,2,1,0:T(8,128)(2,1)S(1)}, u32[]{:S(2)}, u32[]{:S(2)}) %collective-permute-start.22) | collective-permute-done | bytes 196640 | tf_op jit(solution)/shard_map/ppermute | solution.py:563
  156.4 0.7 copy-done.16
  157.1 6.6 %shard_map.144._ = f32[4,24,32,1024]{3,2,1,0:T(8,128)} custom-call(s32[1]{0:T(128)} %bitcast.own_ref.refs_0_, f32[8,128]{1,0:T(8,128)} %get-tuple-element.94._, f32[4,24,32,1024]{3,2,1,0:T(8,128)} %get-tuple-element.60.refs_0_.refs_10_.home_ref, f32[4,24,8,1024]{3,2,1,0:T(8,128)} %get-tuple-element.64._.share_ref, ...), custom_call_target="tpu_custom_call" | custom-call | flops 1 | bytes 1 | tf_op jit(solution)/shard_map/pallas_call | solution.py:530
  163.7 1.1 collective-permute-done.25.refs_15_
  164.8 0.7 copy-done.14
  165.5 6.5 %shard_map.145 = f32[4,24,32,1024]{3,2,1,0:T(8,128)} custom-call(s32[1]{0:T(128)} %bitcast.own_ref.refs_0_, f32[4,24,32,1024]{3,2,1,0:T(8,128)} %shard_map.144._, f32[4,24,32,1024]{3,2,1,0:T(8,128)} %get-tuple-element.60.refs_0_.refs_10_.home_ref, f32[4,24,8,1024]{3,2,1,0:T(8,128)} %get-tuple-element.64._.share_ref, ...), custom_call_target="tpu_custom_call", output_to_operand_aliasing={{}: (1, {})} | custom-call | flops 1 | bytes 1 | tf_op jit(solution)/shard_map/pallas_call | solution.py:530
  (65 shorter events, 1.1 us)
Async XLA Ops:
  12.8 27.4 %collective-permute-start = (bf16[6,2,24,1024]{3,2,1,0:T(8,128)(2,1)}, bf16[6,2,24,1024]{3,2,1,0:T(8,128)(2,1)S(1)}, u32[]{:S(2)}, u32[]{:S(2)}) collective-permute-start(bf16[6,2,24,1024]{3,2,1,0:T(8,128)(2,1)} %get-tuple-element.61), channel_id=1, source_target_pairs={{0,8},{8,0},{16,24},{24,16},{1,9},{9,1},{17,25},{25,17},{2,10},{10... | collective-permute-start | bytes 1769480 | tf_op jit(solution)/shard_map/ppermute | solution.py:563
  13.2 27.0 %collective-permute-start.1 = (bf16[6,2,24,1024]{3,2,1,0:T(8,128)(2,1)}, bf16[6,2,24,1024]{3,2,1,0:T(8,128)(2,1)S(1)}, u32[]{:S(2)}, u32[]{:S(2)}) collective-permute-start(bf16[6,2,24,1024]{3,2,1,0:T(8,128)(2,1)} %get-tuple-element.62), channel_id=1, source_target_pairs={{0,16},{8,24},{16,0},{24,8},{1,17},{9,25},{17,1},{25,9},{2,18},{10... | collective-permute-start | bytes 1769480 | tf_op jit(solution)/shard_map/ppermute | solution.py:563
  15.8 26.5 %collective-permute-start.2 = (bf16[6,2,24,1024]{3,2,1,0:T(8,128)(2,1)}, bf16[6,2,24,1024]{3,2,1,0:T(8,128)(2,1)S(1)}, u32[]{:S(2)}, u32[]{:S(2)}) collective-permute-start(bf16[6,2,24,1024]{3,2,1,0:T(8,128)(2,1)} %get-tuple-element.57._), channel_id=1, source_target_pairs={{0,24},{8,16},{16,8},{24,0},{1,25},{9,17},{17,9},{25,1},{2,26},{10... | collective-permute-start | bytes 1769480 | tf_op jit(solution)/shard_map/ppermute | solution.py:563
  20.8 32.0 %collective-permute-start.4 = (bf16[2,4,32,1024]{3,2,1,0:T(8,128)(2,1)}, bf16[2,4,32,1024]{3,2,1,0:T(8,128)(2,1)}, u32[]{:S(2)}, u32[]{:S(2)}) collective-permute-start(bf16[2,4,32,1024]{3,2,1,0:T(8,128)(2,1)} %get-tuple-element.63), channel_id=1, source_target_pairs={{1,0},{2,1},{3,2},{4,3},{5,4},{6,5},{7,6},{9,8},{10,9},{11,10},{12... | collective-permute-start | bytes 1572872 | tf_op jit(solution)/shard_map/ppermute | solution.py:571
  22.1 30.7 %collective-permute-start.3 = (bf16[2,4,32,1024]{3,2,1,0:T(8,128)(2,1)}, bf16[2,4,32,1024]{3,2,1,0:T(8,128)(2,1)}, u32[]{:S(2)}, u32[]{:S(2)}) collective-permute-start(bf16[2,4,32,1024]{3,2,1,0:T(8,128)(2,1)} %get-tuple-element.58._), channel_id=1, source_target_pairs={{0,1},{1,2},{2,3},{3,4},{4,5},{5,6},{6,7},{8,9},{9,10},{10,11},{11... | collective-permute-start | bytes 1572872 | tf_op jit(solution)/shard_map/ppermute | solution.py:571
  27.5 12.1 %copy-start.20 = (f32[1536]{0:T(1024)S(1)}, f32[1536]{0:T(1024)}, u32[]{:S(2)}) copy-start(f32[1536]{0:T(1024)} %param.21) | copy-start | bytes 18436
  40.2 3.6 %copy-start = (bf16[6,2,24,1024]{3,2,1,0:T(8,128)(2,1)}, bf16[6,2,24,1024]{3,2,1,0:T(8,128)(2,1)S(1)}, u32[]{:S(2)}) copy-start(bf16[6,2,24,1024]{3,2,1,0:T(8,128)(2,1)S(1)} %collective-permute-done.refs_1_) | copy-start | bytes 1769476
  40.2 26.5 %collective-permute-start.5 = (bf16[6,2,24,1024]{3,2,1,0:T(8,128)(2,1)}, bf16[6,2,24,1024]{3,2,1,0:T(8,128)(2,1)}, u32[]{:S(2)}, u32[]{:S(2)}) collective-permute-start(bf16[6,2,24,1024]{3,2,1,0:T(8,128)(2,1)} %get-tuple-element.70), channel_id=1, source_target_pairs={{0,8},{8,0},{16,24},{24,16},{1,9},{9,1},{17,25},{25,17},{2,10},{10... | collective-permute-start | bytes 1769480 | tf_op jit(solution)/shard_map/ppermute | solution.py:563
  40.2 3.6 %copy-start.1 = (bf16[6,2,24,1024]{3,2,1,0:T(8,128)(2,1)}, bf16[6,2,24,1024]{3,2,1,0:T(8,128)(2,1)S(1)}, u32[]{:S(2)}) copy-start(bf16[6,2,24,1024]{3,2,1,0:T(8,128)(2,1)S(1)} %collective-permute-done.1.refs_2_) | copy-start | bytes 1769476
  40.2 31.5 %collective-permute-start.6 = (bf16[6,2,24,1024]{3,2,1,0:T(8,128)(2,1)}, bf16[6,2,24,1024]{3,2,1,0:T(8,128)(2,1)}, u32[]{:S(2)}, u32[]{:S(2)}) collective-permute-start(bf16[6,2,24,1024]{3,2,1,0:T(8,128)(2,1)} %get-tuple-element.71), channel_id=1, source_target_pairs={{0,16},{8,24},{16,0},{24,8},{1,17},{9,25},{17,1},{25,9},{2,18},{10... | collective-permute-start | bytes 1769480 | tf_op jit(solution)/shard_map/ppermute | solution.py:563
  42.3 1.4 copy-start.2
  42.3 29.4 %collective-permute-start.7 = (bf16[6,2,24,1024]{3,2,1,0:T(8,128)(2,1)}, bf16[6,2,24,1024]{3,2,1,0:T(8,128)(2,1)}, u32[]{:S(2)}, u32[]{:S(2)}) collective-permute-start(bf16[6,2,24,1024]{3,2,1,0:T(8,128)(2,1)} %get-tuple-element.72), channel_id=1, source_target_pairs={{0,24},{8,16},{16,8},{24,0},{1,25},{9,17},{17,9},{25,1},{2,26},{10... | collective-permute-start | bytes 1769480 | tf_op jit(solution)/shard_map/ppermute | solution.py:563
  65.4 20.5 %collective-permute-start.8 = (bf16[2,4,24,1024]{3,2,1,0:T(8,128)(2,1)}, bf16[2,4,24,1024]{3,2,1,0:T(8,128)(2,1)S(1)}, u32[]{:S(2)}, u32[]{:S(2)}) collective-permute-start(bf16[2,4,24,1024]{3,2,1,0:T(8,128)(2,1)} %get-tuple-element.74), channel_id=1, source_target_pairs={{0,8},{8,0},{16,24},{24,16},{1,9},{9,1},{17,25},{25,17},{2,10},{10... | collective-permute-start | bytes 1179656 | tf_op jit(solution)/shard_map/ppermute | solution.py:563
  65.7 20.2 %collective-permute-start.9 = (bf16[2,4,24,1024]{3,2,1,0:T(8,128)(2,1)}, bf16[2,4,24,1024]{3,2,1,0:T(8,128)(2,1)S(1)}, u32[]{:S(2)}, u32[]{:S(2)}) collective-permute-start(bf16[2,4,24,1024]{3,2,1,0:T(8,128)(2,1)} %get-tuple-element.75), channel_id=1, source_target_pairs={{0,16},{8,24},{16,0},{24,8},{1,17},{9,25},{17,1},{25,9},{2,18},{10... | collective-permute-start | bytes 1179656 | tf_op jit(solution)/shard_map/ppermute | solution.py:563
  66.6 19.3 %collective-permute-start.10 = (bf16[2,4,24,1024]{3,2,1,0:T(8,128)(2,1)}, bf16[2,4,24,1024]{3,2,1,0:T(8,128)(2,1)S(1)}, u32[]{:S(2)}, u32[]{:S(2)}) collective-permute-start(bf16[2,4,24,1024]{3,2,1,0:T(8,128)(2,1)} %get-tuple-element.76), channel_id=1, source_target_pairs={{0,24},{8,16},{16,8},{24,0},{1,25},{9,17},{17,9},{25,1},{2,26},{10... | collective-permute-start | bytes 1179656 | tf_op jit(solution)/shard_map/ppermute | solution.py:563
  85.9 0.7 copy-start.8
  85.9 0.8 copy-start.9
  85.9 1.0 copy-start.10
  87.5 31.9 %collective-permute-start.11 = (bf16[2,4,24,1024]{3,2,1,0:T(8,128)(2,1)}, bf16[2,4,24,1024]{3,2,1,0:T(8,128)(2,1)S(1)}, u32[]{:S(2)}, u32[]{:S(2)}) collective-permute-start(bf16[2,4,24,1024]{3,2,1,0:T(8,128)(2,1)} %get-tuple-element.85), channel_id=1, source_target_pairs={{0,8},{8,0},{16,24},{24,16},{1,9},{9,1},{17,25},{25,17},{2,10},{10... | collective-permute-start | bytes 1179656 | tf_op jit(solution)/shard_map/ppermute | solution.py:563
  88.0 32.0 %collective-permute-start.12 = (bf16[2,4,24,1024]{3,2,1,0:T(8,128)(2,1)}, bf16[2,4,24,1024]{3,2,1,0:T(8,128)(2,1)S(1)}, u32[]{:S(2)}, u32[]{:S(2)}) collective-permute-start(bf16[2,4,24,1024]{3,2,1,0:T(8,128)(2,1)} %get-tuple-element.86), channel_id=1, source_target_pairs={{0,16},{8,24},{16,0},{24,8},{1,17},{9,25},{17,1},{25,9},{2,18},{10... | collective-permute-start | bytes 1179656 | tf_op jit(solution)/shard_map/ppermute | solution.py:563
  89.0 31.7 %collective-permute-start.13 = (bf16[2,4,24,1024]{3,2,1,0:T(8,128)(2,1)}, bf16[2,4,24,1024]{3,2,1,0:T(8,128)(2,1)S(1)}, u32[]{:S(2)}, u32[]{:S(2)}) collective-permute-start(bf16[2,4,24,1024]{3,2,1,0:T(8,128)(2,1)} %get-tuple-element.87), channel_id=1, source_target_pairs={{0,24},{8,16},{16,8},{24,0},{1,25},{9,17},{17,9},{25,1},{2,26},{10... | collective-permute-start | bytes 1179656 | tf_op jit(solution)/shard_map/ppermute | solution.py:563
  103.4 18.2 %collective-permute-start.14 = (bf16[2,4,24,1024]{3,2,1,0:T(8,128)(2,1)}, bf16[2,4,24,1024]{3,2,1,0:T(8,128)(2,1)S(1)}, u32[]{:S(2)}, u32[]{:S(2)}) collective-permute-start(bf16[2,4,24,1024]{3,2,1,0:T(8,128)(2,1)} %get-tuple-element.97), channel_id=1, source_target_pairs={{0,8},{8,0},{16,24},{24,16},{1,9},{9,1},{17,25},{25,17},{2,10},{10... | collective-permute-start | bytes 1179656 | tf_op jit(solution)/shard_map/ppermute | solution.py:563
  104.3 32.6 %collective-permute-start.15 = (bf16[2,4,24,1024]{3,2,1,0:T(8,128)(2,1)}, bf16[2,4,24,1024]{3,2,1,0:T(8,128)(2,1)S(1)}, u32[]{:S(2)}, u32[]{:S(2)}) collective-permute-start(bf16[2,4,24,1024]{3,2,1,0:T(8,128)(2,1)} %get-tuple-element.98), channel_id=1, source_target_pairs={{0,16},{8,24},{16,0},{24,8},{1,17},{9,25},{17,1},{25,9},{2,18},{10... | collective-permute-start | bytes 1179656 | tf_op jit(solution)/shard_map/ppermute | solution.py:563
  119.4 16.9 %copy-start.3 = (bf16[2,4,24,1024]{3,2,1,0:T(8,128)(2,1)}, bf16[2,4,24,1024]{3,2,1,0:T(8,128)(2,1)S(1)}, u32[]{:S(2)}) copy-start(bf16[2,4,24,1024]{3,2,1,0:T(8,128)(2,1)S(1)} %collective-permute-done.11.refs_1_) | copy-start | bytes 1179652
  119.4 19.0 %collective-permute-start.16 = (bf16[2,4,24,1024]{3,2,1,0:T(8,128)(2,1)}, bf16[2,4,24,1024]{3,2,1,0:T(8,128)(2,1)}, u32[]{:S(2)}, u32[]{:S(2)}) collective-permute-start(bf16[2,4,24,1024]{3,2,1,0:T(8,128)(2,1)} %get-tuple-element.99), channel_id=1, source_target_pairs={{0,24},{8,16},{16,8},{24,0},{1,25},{9,17},{17,9},{25,1},{2,26},{10... | collective-permute-start | bytes 1179656 | tf_op jit(solution)/shard_map/ppermute | solution.py:563
  119.9 16.3 %copy-start.4 = (bf16[2,4,24,1024]{3,2,1,0:T(8,128)(2,1)}, bf16[2,4,24,1024]{3,2,1,0:T(8,128)(2,1)S(1)}, u32[]{:S(2)}) copy-start(bf16[2,4,24,1024]{3,2,1,0:T(8,128)(2,1)S(1)} %collective-permute-done.12.refs_2_) | copy-start | bytes 1179652
  119.9 19.5 %collective-permute-start.17 = (bf16[2,4,24,1024]{3,2,1,0:T(8,128)(2,1)}, bf16[2,4,24,1024]{3,2,1,0:T(8,128)(2,1)}, u32[]{:S(2)}, u32[]{:S(2)}) collective-permute-start(bf16[2,4,24,1024]{3,2,1,0:T(8,128)(2,1)} %get-tuple-element.101), channel_id=1, source_target_pairs={{0,8},{8,0},{16,24},{24,16},{1,9},{9,1},{17,25},{25,17},{2,10},{10... | collective-permute-start | bytes 1179656 | tf_op jit(solution)/shard_map/ppermute | solution.py:563
  120.7 15.6 %copy-start.5 = (bf16[2,4,24,1024]{3,2,1,0:T(8,128)(2,1)}, bf16[2,4,24,1024]{3,2,1,0:T(8,128)(2,1)S(1)}, u32[]{:S(2)}) copy-start(bf16[2,4,24,1024]{3,2,1,0:T(8,128)(2,1)S(1)} %collective-permute-done.13.refs_3_) | copy-start | bytes 1179652
  120.7 19.2 %collective-permute-start.18 = (bf16[2,4,24,1024]{3,2,1,0:T(8,128)(2,1)}, bf16[2,4,24,1024]{3,2,1,0:T(8,128)(2,1)}, u32[]{:S(2)}, u32[]{:S(2)}) collective-permute-start(bf16[2,4,24,1024]{3,2,1,0:T(8,128)(2,1)} %get-tuple-element.102), channel_id=1, source_target_pairs={{0,16},{8,24},{16,0},{24,8},{1,17},{9,25},{17,1},{25,9},{2,18},{10... | collective-permute-start | bytes 1179656 | tf_op jit(solution)/shard_map/ppermute | solution.py:563
  121.6 15.3 %copy-start.6 = (bf16[2,4,24,1024]{3,2,1,0:T(8,128)(2,1)}, bf16[2,4,24,1024]{3,2,1,0:T(8,128)(2,1)S(1)}, u32[]{:S(2)}) copy-start(bf16[2,4,24,1024]{3,2,1,0:T(8,128)(2,1)S(1)} %collective-permute-done.14.refs_5_) | copy-start | bytes 1179652
  121.7 26.4 %collective-permute-start.19 = (bf16[2,4,24,1024]{3,2,1,0:T(8,128)(2,1)}, bf16[2,4,24,1024]{3,2,1,0:T(8,128)(2,1)}, u32[]{:S(2)}, u32[]{:S(2)}) collective-permute-start(bf16[2,4,24,1024]{3,2,1,0:T(8,128)(2,1)} %get-tuple-element.103), channel_id=1, source_target_pairs={{0,24},{8,16},{16,8},{24,0},{1,25},{9,17},{17,9},{25,1},{2,26},{10... | collective-permute-start | bytes 1179656 | tf_op jit(solution)/shard_map/ppermute | solution.py:563
  122.1 15.6 %copy-start.18 = (f32[2,1,1024]{2,1,0:T(1,128)S(1)}, f32[2,1,1024]{2,1,0:T(1,128)}, u32[]{:S(2)}) copy-start(f32[2,1,1024]{2,1,0:T(1,128)} %get-tuple-element.73.refs_0_) | copy-start | bytes 24580
  122.1 27.4 %copy-start.17 = (f32[2,1,1024]{2,1,0:T(1,128)S(1)}, f32[2,1,1024]{2,1,0:T(1,128)}, u32[]{:S(2)}) copy-start(f32[2,1,1024]{2,1,0:T(1,128)} %get-tuple-element.81._) | copy-start | bytes 24580
  122.1 27.4 %copy-start.19 = (f32[2,1,1024]{2,1,0:T(1,128)S(1)}, f32[2,1,1024]{2,1,0:T(1,128)}, u32[]{:S(2)}) copy-start(f32[2,1,1024]{2,1,0:T(1,128)} %get-tuple-element.82._) | copy-start | bytes 24580
  136.9 19.5 %copy-start.7 = (bf16[2,4,24,1024]{3,2,1,0:T(8,128)(2,1)}, bf16[2,4,24,1024]{3,2,1,0:T(8,128)(2,1)S(1)}, u32[]{:S(2)}) copy-start(bf16[2,4,24,1024]{3,2,1,0:T(8,128)(2,1)S(1)} %collective-permute-done.15.refs_6_) | copy-start | bytes 1179652
  136.9 12.2 %collective-permute-start.20 = (bf16[2,2,24,1024]{3,2,1,0:T(8,128)(2,1)}, bf16[2,2,24,1024]{3,2,1,0:T(8,128)(2,1)S(1)}, u32[]{:S(2)}, u32[]{:S(2)}) collective-permute-start(bf16[2,2,24,1024]{3,2,1,0:T(8,128)(2,1)} %get-tuple-element.105), channel_id=1, source_target_pairs={{0,8},{8,0},{16,24},{24,16},{1,9},{9,1},{17,25},{25,17},{2,10},{10... | collective-permute-start | bytes 589832 | tf_op jit(solution)/shard_map/ppermute | solution.py:563
  138.4 13.7 %collective-permute-start.21 = (bf16[2,2,24,1024]{3,2,1,0:T(8,128)(2,1)}, bf16[2,2,24,1024]{3,2,1,0:T(8,128)(2,1)S(1)}, u32[]{:S(2)}, u32[]{:S(2)}) collective-permute-start(bf16[2,2,24,1024]{3,2,1,0:T(8,128)(2,1)} %get-tuple-element.106), channel_id=1, source_target_pairs={{0,16},{8,24},{16,0},{24,8},{1,17},{9,25},{17,1},{25,9},{2,18},{10... | collective-permute-start | bytes 589832 | tf_op jit(solution)/shard_map/ppermute | solution.py:563
  139.4 17.0 %collective-permute-start.22 = (bf16[2,2,24,1024]{3,2,1,0:T(8,128)(2,1)}, bf16[2,2,24,1024]{3,2,1,0:T(8,128)(2,1)S(1)}, u32[]{:S(2)}, u32[]{:S(2)}) collective-permute-start(bf16[2,2,24,1024]{3,2,1,0:T(8,128)(2,1)} %get-tuple-element.107), channel_id=1, source_target_pairs={{0,24},{8,16},{16,8},{24,0},{1,25},{9,17},{17,9},{25,1},{2,26},{10... | collective-permute-start | bytes 589832 | tf_op jit(solution)/shard_map/ppermute | solution.py:563
  139.9 23.8 %collective-permute-start.23 = (bf16[2,2,24,1024]{3,2,1,0:T(8,128)(2,1)}, bf16[2,2,24,1024]{3,2,1,0:T(8,128)(2,1)S(1)}, u32[]{:S(2)}, u32[]{:S(2)}) collective-permute-start(bf16[2,2,24,1024]{3,2,1,0:T(8,128)(2,1)} %get-tuple-element.109), channel_id=1, source_target_pairs={{0,8},{8,0},{16,24},{24,16},{1,9},{9,1},{17,25},{25,17},{2,10},{10... | collective-permute-start | bytes 589832 | tf_op jit(solution)/shard_map/ppermute | solution.py:563
  148.1 15.6 %collective-permute-start.24 = (bf16[2,2,24,1024]{3,2,1,0:T(8,128)(2,1)}, bf16[2,2,24,1024]{3,2,1,0:T(8,128)(2,1)S(1)}, u32[]{:S(2)}, u32[]{:S(2)}) collective-permute-start(bf16[2,2,24,1024]{3,2,1,0:T(8,128)(2,1)} %get-tuple-element.110), channel_id=1, source_target_pairs={{0,16},{8,24},{16,0},{24,8},{1,17},{9,25},{17,1},{25,9},{2,18},{10... | collective-permute-start | bytes 589832 | tf_op jit(solution)/shard_map/ppermute | solution.py:563
  149.1 7.3 %copy-start.12 = (bf16[2,2,24,1024]{3,2,1,0:T(8,128)(2,1)}, bf16[2,2,24,1024]{3,2,1,0:T(8,128)(2,1)S(1)}, u32[]{:S(2)}) copy-start(bf16[2,2,24,1024]{3,2,1,0:T(8,128)(2,1)S(1)} %collective-permute-done.20.refs_13_) | copy-start | bytes 589828
  149.1 15.7 %collective-permute-start.25 = (bf16[2,2,24,1024]{3,2,1,0:T(8,128)(2,1)}, bf16[2,2,24,1024]{3,2,1,0:T(8,128)(2,1)S(1)}, u32[]{:S(2)}, u32[]{:S(2)}) collective-permute-start(bf16[2,2,24,1024]{3,2,1,0:T(8,128)(2,1)} %get-tuple-element.111), channel_id=1, source_target_pairs={{0,24},{8,16},{16,8},{24,0},{1,25},{9,17},{17,9},{25,1},{2,26},{10... | collective-permute-start | bytes 589832 | tf_op jit(solution)/shard_map/ppermute | solution.py:563
  152.1 4.3 %copy-start.15 = (bf16[2,2,24,1024]{3,2,1,0:T(8,128)(2,1)}, bf16[2,2,24,1024]{3,2,1,0:T(8,128)(2,1)S(1)}, u32[]{:S(2)}) copy-start(bf16[2,2,24,1024]{3,2,1,0:T(8,128)(2,1)S(1)} %collective-permute-done.21.refs_14_) | copy-start | bytes 589828
  156.4 0.7 copy-start.16
  163.6 1.2 copy-start.11
  163.7 1.2 copy-start.13
  164.8 0.7 copy-start.14

commit v7 on v6

--- a/solution.py
+++ b/solution.py
@@ -626,11 +626,15 @@
         count = ahead[2]
         some = 2 if count % 2 == 0 else 1
         rows_of = [(first, some) for first in range(0, count, some)]
-    for span in rows_of:
+    for n, span in enumerate(rows_of):
+        if n == 1:
+            after, _ = arrived(after, late[-1:])
+        if n > 1:
+            after, _ = arrived(after, early_back[n - 2][1:2])
         grad, [back] = term(after, *fixed, early, groups, everything, span, ahead)
         after = grad
         if not grads:
-            after, rest = arrived(grad, late[1:], back[1:])
+            after, rest = arrived(grad, late[1:-1] if len(rows_of) > 1 else late[1:], back[1:])
             back = [back[0], *rest]
         grads.append(grad)
         early_back.append(swapped(back))
@@ -641,6 +645,8 @@
         step = parts - 1
         late_back = [[pieces[0], *rest[g * step : (g + 1) * step]] for g, pieces in enumerate(late_back)]
     late_back = [swapped(pieces) for pieces in late_back]
+    if early_back:
+        start, _ = arrived(start, early_back[-1][1:])
     for group, back in zip(sent, late_back, strict=True):
         start = join(own, start, home, share, early_back, back, rows_of, chunks, group)
     gradient = jnp.where(

time: 173 us -> 167 us (0.965)
  waiting for transfers between devices: 15.2 us -> 6.76 us
  Pallas kernels: 126 us -> 128 us
    ppermute x24, waiting for transfers between devices: 15.2 us -> 6.75 us  [swapped(): lax.ppermute(pieces[k], 'comp', [(i, i ^ k) for i in range(parts)])]
    pallas_call x3 -> x6, Pallas kernels: 1.78 us -> 3.56 us  [arrived(): pl.pallas_call(functools.partial(arrived_kernel, len(held)), in_specs=[UN...]
  transfers between devices with their start and end apart: 26 -> 26, of which waited for: 5 -> 5; matrix products, arithmetic and copies ran while one was open for 1% -> 1% of each run, Pallas kernels for 62% -> 66%
where the time goes in v7:
time: 167 us; the launch traced here: 166 us
  Pallas kernels  128 us (77%)
  starting transfers between devices  25.4 us (15%)
  waiting for transfers between devices  6.76 us (4%)
  local copies, waits for them, and re-layouts  4.74 us (3%)
    pallas_call x4, Pallas kernels, source_term(): pl.pallas_call(functools.partial(source_kernel, parts, got, sent, dirs, 2...  56.5 us
    pallas_call x2, Pallas kernels, inner(): pl.pallas_call(functools.partial(inner_kernel, parts, local, chunk, into...  24.2 us
    ppermute x24, starting transfers between devices, swapped(): lax.ppermute(pieces[k], 'comp', [(i, i ^ k) for i in range(parts)])  18.8 us
    pallas_call x2, Pallas kernels, join(): pl.pallas_call(functools.partial(join_kernel, parts, spans), grid=(many,)...  13.1 us
    pallas_call x1, Pallas kernels, outer(): pl.pallas_call(functools.partial(outer_kernel, parts, local, chunk), grid...  12.6 us
    pallas_call x1, Pallas kernels, by_row(): pl.pallas_call(by_row_kernel, grid=(deep // some,), in_specs=[UNREAD] * l...  8.43 us
    ppermute x24, waiting for transfers between devices, swapped(): lax.ppermute(pieces[k], 'comp', [(i, i ^ k) for i in range(parts)])  6.75 us
    ppermute x2, starting transfers between devices, across(): return (lax.ppermute(high, 'space', up), lax.ppermute(low, 'space', down))  6.65 us
  transfers between devices with their start and end apart: 26, of which 5 were waited for; matrix products, arithmetic and copies ran while one was open for 1% of the time, Pallas kernels for 66%

profile of v7, /device:TPU:0, one launch (start us, length us, event | category | flops | bytes accessed | tf_op | source)
XLA Modules:
  0.0 166.3 jit_solution(17141933957261646779)
XLA Ops:
  0.6 12.1 %shard_map.131 = (f32[4,24,32,1024]{3,2,1,0:T(8,128)}, bf16[6,2,24,1024]{3,2,1,0:T(8,128)(2,1)}, bf16[6,2,24,1024]{3,2,1,0:T(8,128)(2,1)}, bf16[6,2,24,1024]{3,2,1,0:T(8,128)(2,1)}, bf16[6,2,24,1024]{3,2,1,0:T(8,128)(2,1)}) custom-call(s32[1]{0:T(128)} %bitcast.own_ref.refs_0_, s32[2,24]{1,0:T(2,128)} %refs_1_.5, f32[2,24]{1,0:T(2,128)} %constant.11.clone.along_ref.refs_2_, ...), custom_call_target="tpu_custom_call" | custom-call | flops 1 | bytes 1 | tf_op jit(solution)/shard_map/pallas_call | solution.py:169
  12.8 0.5 collective-permute-start
  13.2 2.6 %collective-permute-start.1 = (bf16[6,2,24,1024]{3,2,1,0:T(8,128)(2,1)}, bf16[6,2,24,1024]{3,2,1,0:T(8,128)(2,1)S(1)}, u32[]{:S(2)}, u32[]{:S(2)}) collective-permute-start(bf16[6,2,24,1024]{3,2,1,0:T(8,128)(2,1)} %get-tuple-element.62), channel_id=1, source_target_pairs={{0,16},{8,24},{16,0},{24,8},{1,17},{9,25},{17,1},{25,9},{2,18},{10... | collective-permute-start | bytes 1769480 | tf_op jit(solution)/shard_map/ppermute | solution.py:563
  15.9 4.9 %shard_map.132 = (bf16[2,4,32,1024]{3,2,1,0:T(8,128)(2,1)}, bf16[2,4,32,1024]{3,2,1,0:T(8,128)(2,1)}) custom-call(bf16[6,2,24,1024]{3,2,1,0:T(8,128)(2,1)} %get-tuple-element.57._, f32[4,24,32,1024]{3,2,1,0:T(8,128)} %bitcast.12, s32[4,32,1024]{2,1,0:T(8,128)} %refs_7_.3, s32[4,32,1024]{2,1,0:T(8,128)} %refs_8_.1, s32[32,1024]{1,0:T(8,128)} %refs_9_.1, ...), custom_call_target="tpu_custom_call" | custom-call | flops 1 | bytes 1 | tf_op jit(solution)/shard_map/pallas_call | solution.py:227
  20.8 1.3 collective-permute-start.4
  22.1 5.4 %collective-permute-start.3 = (bf16[2,4,32,1024]{3,2,1,0:T(8,128)(2,1)}, bf16[2,4,32,1024]{3,2,1,0:T(8,128)(2,1)}, u32[]{:S(2)}, u32[]{:S(2)}) collective-permute-start(bf16[2,4,32,1024]{3,2,1,0:T(8,128)(2,1)} %get-tuple-element.58._), channel_id=1, source_target_pairs={{0,1},{1,2},{2,3},{3,4},{4,5},{5,6},{6,7},{8,9},{9,10},{10,11},{11... | collective-permute-start | bytes 1572872 | tf_op jit(solution)/shard_map/ppermute | solution.py:571
  27.5 12.1 %shard_map.133 = (f32[4,24,32,1024]{3,2,1,0:T(8,128)}, bf16[6,2,24,1024]{3,2,1,0:T(8,128)(2,1)}, bf16[6,2,24,1024]{3,2,1,0:T(8,128)(2,1)}, bf16[6,2,24,1024]{3,2,1,0:T(8,128)(2,1)}, bf16[6,2,24,1024]{3,2,1,0:T(8,128)(2,1)}) custom-call(s32[1]{0:T(128)} %bitcast.own_ref.refs_0_, s32[2,24]{1,0:T(2,128)} %refs_1_.5, ...), custom_call_target="tpu_custom_call", output_to_operand_aliasing={{0}: (9, {})} | custom-call | flops 1 | bytes 1 | tf_op jit(solution)/shard_map/pallas_call | solution.py:169
  39.6 0.6 reshape.60.weight_ref
  40.2 1.8 %collective-permute-start.6 = (bf16[6,2,24,1024]{3,2,1,0:T(8,128)(2,1)}, bf16[6,2,24,1024]{3,2,1,0:T(8,128)(2,1)}, u32[]{:S(2)}, u32[]{:S(2)}) collective-permute-start(bf16[6,2,24,1024]{3,2,1,0:T(8,128)(2,1)} %get-tuple-element.71), channel_id=1, source_target_pairs={{0,16},{8,24},{16,0},{24,8},{1,17},{9,25},{17,1},{25,9},{2,18},{10... | collective-permute-start | bytes 1769480 | tf_op jit(solution)/shard_map/ppermute | solution.py:563
  42.3 1.4 collective-permute-start.7
  43.8 0.6 shard_map.134.refs_0_
  44.4 8.4 %shard_map.135.refs_4_.state_ref = bf16[8,384,1024]{2,1,0:T(8,128)(2,1)} custom-call(f32[8,128]{1,0:T(8,128)} %shard_map.134.refs_0_, bf16[384,8,1024]{2,1,0:T(8,128)(2,1)} %refs_1_.4), custom_call_target="tpu_custom_call" | custom-call | flops 1 | bytes 1 | tf_op jit(solution)/shard_map/pallas_call | solution.py:370
  52.8 12.6 %shard_map.136 = (f32[4,24,8,1024]{3,2,1,0:T(8,128)}, bf16[2,4,24,1024]{3,2,1,0:T(8,128)(2,1)}, bf16[2,4,24,1024]{3,2,1,0:T(8,128)(2,1)}, bf16[2,4,24,1024]{3,2,1,0:T(8,128)(2,1)}, bf16[2,4,24,1024]{3,2,1,0:T(8,128)(2,1)}) custom-call(s32[1]{0:T(128)} %bitcast.own_ref.refs_0_, s32[2,24]{1,0:T(2,128)} %refs_1_.5, f32[2,24]{1,0:T(2,128)} %constant.11.clone.along_ref.refs_2_, ...), custom_call_target="tpu_custom_call" | custom-call | flops 99999997952 | bytes 104857600 | tf_op jit(solution)/shard_map/pallas_call | solution.py:323
  65.6 1.0 collective-permute-start.9
  66.6 0.7 collective-permute-start.10
  67.3 4.4 %shard_map.137 = (bf16[384,1536]{1,0:T(8,128)(2,1)}, bf16[1536,384]{1,0:T(8,128)(2,1)}, f32[1536,128]{1,0:T(8,128)}) custom-call(f32[4,24,8,1024]{3,2,1,0:T(8,128)} %get-tuple-element.64._.share_ref, bf16[1536,384]{1,0:T(8,128)(2,1)} %w_in_ref.9, bf16[384,1536]{1,0:T(8,128)(2,1)} %w_out_ref.1, f32[1,1536]{1,0:T(1,128)} %reshape.60.weight_ref), custom_call_target="tpu_custom_call" | custom-call | flops 99999997952 | bytes 104857600 | tf_op jit(solution)/shard_map/pallas_call | solution.py:393
  71.7 14.1 %shard_map.138 = (f32[2,1,1024]{2,1,0:T(1,128)}, bf16[2,4,24,1024]{3,2,1,0:T(8,128)(2,1)}, bf16[2,4,24,1024]{3,2,1,0:T(8,128)(2,1)}, bf16[2,4,24,1024]{3,2,1,0:T(8,128)(2,1)}, bf16[2,4,24,1024]{3,2,1,0:T(8,128)(2,1)}) custom-call(s32[1]{0:T(128)} %bitcast.own_ref.refs_0_, bf16[384,1536]{1,0:T(8,128)(2,1)} %get-tuple-element.65._.in_t_ref, ...), custom_call_target="tpu_custom_call" | custom-call | flops 1 | bytes 1 | tf_op jit(solution)/shard_map/pallas_call | solution.py:463
  85.9 0.7 copy-done.11
  86.7 0.6 shard_map.139
  87.3 0.5 collective-permute-start.11
  87.8 1.0 collective-permute-start.12
  89.2 0.8 copy-done.10
  89.9 0.6 shard_map.140._
  90.5 14.1 %shard_map.141 = (f32[2,1,1024]{2,1,0:T(1,128)}, bf16[2,4,24,1024]{3,2,1,0:T(8,128)(2,1)}, bf16[2,4,24,1024]{3,2,1,0:T(8,128)(2,1)}, bf16[2,4,24,1024]{3,2,1,0:T(8,128)(2,1)}, bf16[2,4,24,1024]{3,2,1,0:T(8,128)(2,1)}) custom-call(s32[1]{0:T(128)} %bitcast.own_ref.refs_0_, f32[8,128]{1,0:T(8,128)} %shard_map.140._, ...), custom_call_target="tpu_custom_call" | custom-call | flops 1 | bytes 1 | tf_op jit(solution)/shard_map/pallas_call | solution.py:463
  104.6 0.8 collective-permute-start.17
  105.5 1.0 collective-permute-start.18
  106.5 0.4 collective-permute-start.19
  107.3 0.6 shard_map.142._
  107.9 14.1 %shard_map.143 = (f32[2,1,1024]{2,1,0:T(1,128)}, bf16[2,4,24,1024]{3,2,1,0:T(8,128)(2,1)}, bf16[2,4,24,1024]{3,2,1,0:T(8,128)(2,1)}, bf16[2,4,24,1024]{3,2,1,0:T(8,128)(2,1)}, bf16[2,4,24,1024]{3,2,1,0:T(8,128)(2,1)}) custom-call(s32[1]{0:T(128)} %bitcast.own_ref.refs_0_, f32[8,128]{1,0:T(8,128)} %shard_map.142._, ...), custom_call_target="tpu_custom_call" | custom-call | flops 1 | bytes 1 | tf_op jit(solution)/shard_map/pallas_call | solution.py:463
  122.5 1.0 collective-permute-start.15
  123.4 0.7 copy-done.9
  124.2 0.5 collective-permute-start.16
  124.7 14.1 %shard_map.144 = (f32[2,1,1024]{2,1,0:T(1,128)}, bf16[2,2,24,1024]{3,2,1,0:T(8,128)(2,1)}, bf16[2,2,24,1024]{3,2,1,0:T(8,128)(2,1)}, bf16[2,2,24,1024]{3,2,1,0:T...) custom-call(s32[1]{0:T(128)} %bitcast.own_ref.refs_0_, ...), custom_call_target="tpu_custom_call" | custom-call | flops 1 | bytes 1 | tf_op jit(solution)/shard_map/pallas_call | solution.py:463
  138.8 0.6 shard_map.145
  139.4 0.7 collective-permute-start.20
  140.1 1.0 collective-permute-start.21
  141.4 0.9 collective-permute-start.22
  142.5 1.1 collective-permute-start.24
  143.6 0.6 collective-permute-start.25
  144.2 0.7 copy_bitcast_fusion
  144.9 0.7 maximum_select_fusion
  145.6 0.6 shard_map.146._
  146.2 2.1 %collective-permute-done.21.refs_14_ = bf16[2,2,24,1024]{3,2,1,0:T(8,128)(2,1)} collective-permute-done((bf16[2,2,24,1024]{3,2,1,0:T(8,128)(2,1)}, bf16[2,2,24,1024]{3,2,1,0:T(8,128)(2,1)}, u32[]{:S(2)}, u32[]{:S(2)}) %collective-permute-start.21) | collective-permute-done | bytes 196640 | tf_op jit(solution)/shard_map/ppermute | solution.py:563
  148.3 2.7 %collective-permute-done.22.refs_15_ = bf16[2,2,24,1024]{3,2,1,0:T(8,128)(2,1)} collective-permute-done((bf16[2,2,24,1024]{3,2,1,0:T(8,128)(2,1)}, bf16[2,2,24,1024]{3,2,1,0:T(8,128)(2,1)}, u32[]{:S(2)}, u32[]{:S(2)}) %collective-permute-start.22) | collective-permute-done | bytes 196640 | tf_op jit(solution)/shard_map/ppermute | solution.py:563
  151.0 6.6 %shard_map.147._ = f32[4,24,32,1024]{3,2,1,0:T(8,128)} custom-call(s32[1]{0:T(128)} %bitcast.own_ref.refs_0_, f32[8,128]{1,0:T(8,128)} %shard_map.146._, f32[4,24,32,1024]{3,2,1,0:T(8,128)} %get-tuple-element.60.refs_0_.refs_10_.home_ref, f32[4,24,8,1024]{3,2,1,0:T(8,128)} %get-tuple-element.64._.share_ref, ...), custom_call_target="tpu_custom_call" | custom-call | flops 1 | bytes 1 | tf_op jit(solution)/shard_map/pallas_call | solution.py:530
  157.6 1.3 collective-permute-done.25.refs_15_
  158.9 0.7 copy-done.16
  159.6 6.6 %shard_map.148 = f32[4,24,32,1024]{3,2,1,0:T(8,128)} custom-call(s32[1]{0:T(128)} %bitcast.own_ref.refs_0_, f32[4,24,32,1024]{3,2,1,0:T(8,128)} %shard_map.147._, f32[4,24,32,1024]{3,2,1,0:T(8,128)} %get-tuple-element.60.refs_0_.refs_10_.home_ref, f32[4,24,8,1024]{3,2,1,0:T(8,128)} %get-tuple-element.64._.share_ref, ...), custom_call_target="tpu_custom_call", output_to_operand_aliasing={{}: (1, {})} | custom-call | flops 1 | bytes 1 | tf_op jit(solution)/shard_map/pallas_call | solution.py:530
  (68 shorter events, 2.4 us)
Async XLA Ops:
  12.8 27.4 %collective-permute-start = (bf16[6,2,24,1024]{3,2,1,0:T(8,128)(2,1)}, bf16[6,2,24,1024]{3,2,1,0:T(8,128)(2,1)S(1)}, u32[]{:S(2)}, u32[]{:S(2)}) collective-permute-start(bf16[6,2,24,1024]{3,2,1,0:T(8,128)(2,1)} %get-tuple-element.61), channel_id=1, source_target_pairs={{0,8},{8,0},{16,24},{24,16},{1,9},{9,1},{17,25},{25,17},{2,10},{10... | collective-permute-start | bytes 1769480 | tf_op jit(solution)/shard_map/ppermute | solution.py:563
  13.2 27.0 %collective-permute-start.1 = (bf16[6,2,24,1024]{3,2,1,0:T(8,128)(2,1)}, bf16[6,2,24,1024]{3,2,1,0:T(8,128)(2,1)S(1)}, u32[]{:S(2)}, u32[]{:S(2)}) collective-permute-start(bf16[6,2,24,1024]{3,2,1,0:T(8,128)(2,1)} %get-tuple-element.62), channel_id=1, source_target_pairs={{0,16},{8,24},{16,0},{24,8},{1,17},{9,25},{17,1},{25,9},{2,18},{10... | collective-permute-start | bytes 1769480 | tf_op jit(solution)/shard_map/ppermute | solution.py:563
  15.8 26.5 %collective-permute-start.2 = (bf16[6,2,24,1024]{3,2,1,0:T(8,128)(2,1)}, bf16[6,2,24,1024]{3,2,1,0:T(8,128)(2,1)S(1)}, u32[]{:S(2)}, u32[]{:S(2)}) collective-permute-start(bf16[6,2,24,1024]{3,2,1,0:T(8,128)(2,1)} %get-tuple-element.57._), channel_id=1, source_target_pairs={{0,24},{8,16},{16,8},{24,0},{1,25},{9,17},{17,9},{25,1},{2,26},{10... | collective-permute-start | bytes 1769480 | tf_op jit(solution)/shard_map/ppermute | solution.py:563
  20.8 32.0 %collective-permute-start.4 = (bf16[2,4,32,1024]{3,2,1,0:T(8,128)(2,1)}, bf16[2,4,32,1024]{3,2,1,0:T(8,128)(2,1)}, u32[]{:S(2)}, u32[]{:S(2)}) collective-permute-start(bf16[2,4,32,1024]{3,2,1,0:T(8,128)(2,1)} %get-tuple-element.63), channel_id=1, source_target_pairs={{1,0},{2,1},{3,2},{4,3},{5,4},{6,5},{7,6},{9,8},{10,9},{11,10},{12... | collective-permute-start | bytes 1572872 | tf_op jit(solution)/shard_map/ppermute | solution.py:571
  22.1 30.7 %collective-permute-start.3 = (bf16[2,4,32,1024]{3,2,1,0:T(8,128)(2,1)}, bf16[2,4,32,1024]{3,2,1,0:T(8,128)(2,1)}, u32[]{:S(2)}, u32[]{:S(2)}) collective-permute-start(bf16[2,4,32,1024]{3,2,1,0:T(8,128)(2,1)} %get-tuple-element.58._), channel_id=1, source_target_pairs={{0,1},{1,2},{2,3},{3,4},{4,5},{5,6},{6,7},{8,9},{9,10},{10,11},{11... | collective-permute-start | bytes 1572872 | tf_op jit(solution)/shard_map/ppermute | solution.py:571
  27.5 12.1 %copy-start.20 = (f32[1536]{0:T(1024)S(1)}, f32[1536]{0:T(1024)}, u32[]{:S(2)}) copy-start(f32[1536]{0:T(1024)} %param.21) | copy-start | bytes 18436
  40.2 3.6 %copy-start = (bf16[6,2,24,1024]{3,2,1,0:T(8,128)(2,1)}, bf16[6,2,24,1024]{3,2,1,0:T(8,128)(2,1)S(1)}, u32[]{:S(2)}) copy-start(bf16[6,2,24,1024]{3,2,1,0:T(8,128)(2,1)S(1)} %collective-permute-done.refs_1_) | copy-start | bytes 1769476
  40.2 26.4 %collective-permute-start.5 = (bf16[6,2,24,1024]{3,2,1,0:T(8,128)(2,1)}, bf16[6,2,24,1024]{3,2,1,0:T(8,128)(2,1)}, u32[]{:S(2)}, u32[]{:S(2)}) collective-permute-start(bf16[6,2,24,1024]{3,2,1,0:T(8,128)(2,1)} %get-tuple-element.70), channel_id=1, source_target_pairs={{0,8},{8,0},{16,24},{24,16},{1,9},{9,1},{17,25},{25,17},{2,10},{10... | collective-permute-start | bytes 1769480 | tf_op jit(solution)/shard_map/ppermute | solution.py:563
  40.2 3.6 %copy-start.1 = (bf16[6,2,24,1024]{3,2,1,0:T(8,128)(2,1)}, bf16[6,2,24,1024]{3,2,1,0:T(8,128)(2,1)S(1)}, u32[]{:S(2)}) copy-start(bf16[6,2,24,1024]{3,2,1,0:T(8,128)(2,1)S(1)} %collective-permute-done.1.refs_2_) | copy-start | bytes 1769476
  40.2 31.5 %collective-permute-start.6 = (bf16[6,2,24,1024]{3,2,1,0:T(8,128)(2,1)}, bf16[6,2,24,1024]{3,2,1,0:T(8,128)(2,1)}, u32[]{:S(2)}, u32[]{:S(2)}) collective-permute-start(bf16[6,2,24,1024]{3,2,1,0:T(8,128)(2,1)} %get-tuple-element.71), channel_id=1, source_target_pairs={{0,16},{8,24},{16,0},{24,8},{1,17},{9,25},{17,1},{25,9},{2,18},{10... | collective-permute-start | bytes 1769480 | tf_op jit(solution)/shard_map/ppermute | solution.py:563
  42.3 1.4 copy-start.2
  42.3 29.4 %collective-permute-start.7 = (bf16[6,2,24,1024]{3,2,1,0:T(8,128)(2,1)}, bf16[6,2,24,1024]{3,2,1,0:T(8,128)(2,1)}, u32[]{:S(2)}, u32[]{:S(2)}) collective-permute-start(bf16[6,2,24,1024]{3,2,1,0:T(8,128)(2,1)} %get-tuple-element.72), channel_id=1, source_target_pairs={{0,24},{8,16},{16,8},{24,0},{1,25},{9,17},{17,9},{25,1},{2,26},{10... | collective-permute-start | bytes 1769480 | tf_op jit(solution)/shard_map/ppermute | solution.py:563
  65.4 20.5 %collective-permute-start.8 = (bf16[2,4,24,1024]{3,2,1,0:T(8,128)(2,1)}, bf16[2,4,24,1024]{3,2,1,0:T(8,128)(2,1)S(1)}, u32[]{:S(2)}, u32[]{:S(2)}) collective-permute-start(bf16[2,4,24,1024]{3,2,1,0:T(8,128)(2,1)} %get-tuple-element.74), channel_id=1, source_target_pairs={{0,8},{8,0},{16,24},{24,16},{1,9},{9,1},{17,25},{25,17},{2,10},{10... | collective-permute-start | bytes 1179656 | tf_op jit(solution)/shard_map/ppermute | solution.py:563
  65.6 20.3 %collective-permute-start.9 = (bf16[2,4,24,1024]{3,2,1,0:T(8,128)(2,1)}, bf16[2,4,24,1024]{3,2,1,0:T(8,128)(2,1)S(1)}, u32[]{:S(2)}, u32[]{:S(2)}) collective-permute-start(bf16[2,4,24,1024]{3,2,1,0:T(8,128)(2,1)} %get-tuple-element.75), channel_id=1, source_target_pairs={{0,16},{8,24},{16,0},{24,8},{1,17},{9,25},{17,1},{25,9},{2,18},{10... | collective-permute-start | bytes 1179656 | tf_op jit(solution)/shard_map/ppermute | solution.py:563
  66.6 22.6 %collective-permute-start.10 = (bf16[2,4,24,1024]{3,2,1,0:T(8,128)(2,1)}, bf16[2,4,24,1024]{3,2,1,0:T(8,128)(2,1)S(1)}, u32[]{:S(2)}, u32[]{:S(2)}) collective-permute-start(bf16[2,4,24,1024]{3,2,1,0:T(8,128)(2,1)} %get-tuple-element.80), channel_id=1, source_target_pairs={{0,24},{8,16},{16,8},{24,0},{1,25},{9,17},{17,9},{25,1},{2,26},{10... | collective-permute-start | bytes 1179656 | tf_op jit(solution)/shard_map/ppermute | solution.py:563
  85.9 0.8 copy-start.11
  85.9 0.9 copy-start.12
  87.3 19.2 %collective-permute-start.11 = (bf16[2,4,24,1024]{3,2,1,0:T(8,128)(2,1)}, bf16[2,4,24,1024]{3,2,1,0:T(8,128)(2,1)S(1)}, u32[]{:S(2)}, u32[]{:S(2)}) collective-permute-start(bf16[2,4,24,1024]{3,2,1,0:T(8,128)(2,1)} %get-tuple-element.82), channel_id=1, source_target_pairs={{0,8},{8,0},{16,24},{24,16},{1,9},{9,1},{17,25},{25,17},{2,10},{10... | collective-permute-start | bytes 1179656 | tf_op jit(solution)/shard_map/ppermute | solution.py:563
  87.8 34.2 %collective-permute-start.12 = (bf16[2,4,24,1024]{3,2,1,0:T(8,128)(2,1)}, bf16[2,4,24,1024]{3,2,1,0:T(8,128)(2,1)S(1)}, u32[]{:S(2)}, u32[]{:S(2)}) collective-permute-start(bf16[2,4,24,1024]{3,2,1,0:T(8,128)(2,1)} %get-tuple-element.86), channel_id=1, source_target_pairs={{0,16},{8,24},{16,0},{24,8},{1,17},{9,25},{17,1},{25,9},{2,18},{10... | collective-permute-start | bytes 1179656 | tf_op jit(solution)/shard_map/ppermute | solution.py:563
  88.8 33.7 %collective-permute-start.13 = (bf16[2,4,24,1024]{3,2,1,0:T(8,128)(2,1)}, bf16[2,4,24,1024]{3,2,1,0:T(8,128)(2,1)S(1)}, u32[]{:S(2)}, u32[]{:S(2)}) collective-permute-start(bf16[2,4,24,1024]{3,2,1,0:T(8,128)(2,1)} %get-tuple-element.87), channel_id=1, source_target_pairs={{0,24},{8,16},{16,8},{24,0},{1,25},{9,17},{17,9},{25,1},{2,26},{10... | collective-permute-start | bytes 1179656 | tf_op jit(solution)/shard_map/ppermute | solution.py:563
  89.2 0.8 copy-start.10
  104.6 18.8 %collective-permute-start.17 = (bf16[2,4,24,1024]{3,2,1,0:T(8,128)(2,1)}, bf16[2,4,24,1024]{3,2,1,0:T(8,128)(2,1)S(1)}, u32[]{:S(2)}, u32[]{:S(2)}) collective-permute-start(bf16[2,4,24,1024]{3,2,1,0:T(8,128)(2,1)} %get-tuple-element.100), channel_id=1, source_target_pairs={{0,8},{8,0},{16,24},{24,16},{1,9},{9,1},{17,25},{25,17},{2,10},{10... | collective-permute-start | bytes 1179656 | tf_op jit(solution)/shard_map/ppermute | solution.py:563
  105.5 34.0 %collective-permute-start.18 = (bf16[2,4,24,1024]{3,2,1,0:T(8,128)(2,1)}, bf16[2,4,24,1024]{3,2,1,0:T(8,128)(2,1)}, u32[]{:S(2)}, u32[]{:S(2)}) collective-permute-start(bf16[2,4,24,1024]{3,2,1,0:T(8,128)(2,1)} %get-tuple-element.101), channel_id=1, source_target_pairs={{0,16},{8,24},{16,0},{24,8},{1,17},{9,25},{17,1},{25,9},{2,18},{10... | collective-permute-start | bytes 1179656 | tf_op jit(solution)/shard_map/ppermute | solution.py:563
  106.5 0.8 copy-start.3
  106.5 33.6 %collective-permute-start.19 = (bf16[2,4,24,1024]{3,2,1,0:T(8,128)(2,1)}, bf16[2,4,24,1024]{3,2,1,0:T(8,128)(2,1)}, u32[]{:S(2)}, u32[]{:S(2)}) collective-permute-start(bf16[2,4,24,1024]{3,2,1,0:T(8,128)(2,1)} %get-tuple-element.102), channel_id=1, source_target_pairs={{0,24},{8,16},{16,8},{24,0},{1,25},{9,17},{17,9},{25,1},{2,26},{10... | collective-permute-start | bytes 1179656 | tf_op jit(solution)/shard_map/ppermute | solution.py:563
  122.0 16.8 %copy-start.4 = (bf16[2,4,24,1024]{3,2,1,0:T(8,128)(2,1)}, bf16[2,4,24,1024]{3,2,1,0:T(8,128)(2,1)S(1)}, u32[]{:S(2)}) copy-start(bf16[2,4,24,1024]{3,2,1,0:T(8,128)(2,1)S(1)} %collective-permute-done.12.refs_2_) | copy-start | bytes 1179652
  122.0 20.3 %collective-permute-start.14 = (bf16[2,4,24,1024]{3,2,1,0:T(8,128)(2,1)}, bf16[2,4,24,1024]{3,2,1,0:T(8,128)(2,1)S(1)}, u32[]{:S(2)}, u32[]{:S(2)}) collective-permute-start(bf16[2,4,24,1024]{3,2,1,0:T(8,128)(2,1)} %get-tuple-element.95), channel_id=1, source_target_pairs={{0,8},{8,0},{16,24},{24,16},{1,9},{9,1},{17,25},{25,17},{2,10},{10... | collective-permute-start | bytes 1179656 | tf_op jit(solution)/shard_map/ppermute | solution.py:563
  122.5 16.4 %copy-start.5 = (bf16[2,4,24,1024]{3,2,1,0:T(8,128)(2,1)}, bf16[2,4,24,1024]{3,2,1,0:T(8,128)(2,1)S(1)}, u32[]{:S(2)}) copy-start(bf16[2,4,24,1024]{3,2,1,0:T(8,128)(2,1)S(1)} %collective-permute-done.13.refs_3_) | copy-start | bytes 1179652
  122.5 20.0 %collective-permute-start.15 = (bf16[2,4,24,1024]{3,2,1,0:T(8,128)(2,1)}, bf16[2,4,24,1024]{3,2,1,0:T(8,128)(2,1)S(1)}, u32[]{:S(2)}, u32[]{:S(2)}) collective-permute-start(bf16[2,4,24,1024]{3,2,1,0:T(8,128)(2,1)} %get-tuple-element.96), channel_id=1, source_target_pairs={{0,16},{8,24},{16,0},{24,8},{1,17},{9,25},{17,1},{25,9},{2,18},{10... | collective-permute-start | bytes 1179656 | tf_op jit(solution)/shard_map/ppermute | solution.py:563
  123.4 0.7 copy-start.9
  124.2 19.4 %collective-permute-start.16 = (bf16[2,4,24,1024]{3,2,1,0:T(8,128)(2,1)}, bf16[2,4,24,1024]{3,2,1,0:T(8,128)(2,1)S(1)}, u32[]{:S(2)}, u32[]{:S(2)}) collective-permute-start(bf16[2,4,24,1024]{3,2,1,0:T(8,128)(2,1)} %get-tuple-element.97), channel_id=1, source_target_pairs={{0,24},{8,16},{16,8},{24,0},{1,25},{9,17},{17,9},{25,1},{2,26},{10... | collective-permute-start | bytes 1179656 | tf_op jit(solution)/shard_map/ppermute | solution.py:563
  124.7 15.4 %copy-start.17 = (f32[2,1,1024]{2,1,0:T(1,128)S(1)}, f32[2,1,1024]{2,1,0:T(1,128)}, u32[]{:S(2)}) copy-start(f32[2,1,1024]{2,1,0:T(1,128)} %get-tuple-element.73.refs_0_) | copy-start | bytes 24580
  124.7 15.4 %copy-start.18 = (f32[2,1,1024]{2,1,0:T(1,128)S(1)}, f32[2,1,1024]{2,1,0:T(1,128)}, u32[]{:S(2)}) copy-start(f32[2,1,1024]{2,1,0:T(1,128)} %get-tuple-element.81.refs_0_) | copy-start | bytes 24580
  124.7 19.5 %copy-start.19 = (f32[2,1,1024]{2,1,0:T(1,128)S(1)}, f32[2,1,1024]{2,1,0:T(1,128)}, u32[]{:S(2)}) copy-start(f32[2,1,1024]{2,1,0:T(1,128)} %get-tuple-element.83._) | copy-start | bytes 24580
  139.4 1.9 %collective-permute-start.20 = (bf16[2,2,24,1024]{3,2,1,0:T(8,128)(2,1)}, bf16[2,2,24,1024]{3,2,1,0:T(8,128)(2,1)S(1)}, u32[]{:S(2)}, u32[]{:S(2)}) collective-permute-start(bf16[2,2,24,1024]{3,2,1,0:T(8,128)(2,1)} %get-tuple-element.105), channel_id=1, source_target_pairs={{0,8},{8,0},{16,24},{24,16},{1,9},{9,1},{17,25},{25,17},{2,10},{10... | collective-permute-start | bytes 589832 | tf_op jit(solution)/shard_map/ppermute | solution.py:563
  140.1 8.1 %collective-permute-start.21 = (bf16[2,2,24,1024]{3,2,1,0:T(8,128)(2,1)}, bf16[2,2,24,1024]{3,2,1,0:T(8,128)(2,1)}, u32[]{:S(2)}, u32[]{:S(2)}) collective-permute-start(bf16[2,2,24,1024]{3,2,1,0:T(8,128)(2,1)} %get-tuple-element.106), channel_id=1, source_target_pairs={{0,16},{8,24},{16,0},{24,8},{1,17},{9,25},{17,1},{25,9},{2,18},{10... | collective-permute-start | bytes 589832 | tf_op jit(solution)/shard_map/ppermute | solution.py:563
  141.4 9.6 %copy-start.14 = (bf16[2,2,24,1024]{3,2,1,0:T(8,128)(2,1)}, bf16[2,2,24,1024]{3,2,1,0:T(8,128)(2,1)S(1)}, u32[]{:S(2)}) copy-start(bf16[2,2,24,1024]{3,2,1,0:T(8,128)(2,1)S(1)} %collective-permute-done.20.refs_13_) | copy-start | bytes 589828
  141.4 9.6 %collective-permute-start.22 = (bf16[2,2,24,1024]{3,2,1,0:T(8,128)(2,1)}, bf16[2,2,24,1024]{3,2,1,0:T(8,128)(2,1)}, u32[]{:S(2)}, u32[]{:S(2)}) collective-permute-start(bf16[2,2,24,1024]{3,2,1,0:T(8,128)(2,1)} %get-tuple-element.107), channel_id=1, source_target_pairs={{0,24},{8,16},{16,8},{24,0},{1,25},{9,17},{17,9},{25,1},{2,26},{10... | collective-permute-start | bytes 589832 | tf_op jit(solution)/shard_map/ppermute | solution.py:563
  142.3 3.2 %copy-start.6 = (bf16[2,4,24,1024]{3,2,1,0:T(8,128)(2,1)}, bf16[2,4,24,1024]{3,2,1,0:T(8,128)(2,1)S(1)}, u32[]{:S(2)}) copy-start(bf16[2,4,24,1024]{3,2,1,0:T(8,128)(2,1)S(1)} %collective-permute-done.14.refs_1_.refs_9_) | copy-start | bytes 1179652
  142.3 15.2 %collective-permute-start.23 = (bf16[2,2,24,1024]{3,2,1,0:T(8,128)(2,1)}, bf16[2,2,24,1024]{3,2,1,0:T(8,128)(2,1)S(1)}, u32[]{:S(2)}, u32[]{:S(2)}) collective-permute-start(bf16[2,2,24,1024]{3,2,1,0:T(8,128)(2,1)} %get-tuple-element.109), channel_id=1, source_target_pairs={{0,8},{8,0},{16,24},{24,16},{1,9},{9,1},{17,25},{25,17},{2,10},{10... | collective-permute-start | bytes 589832 | tf_op jit(solution)/shard_map/ppermute | solution.py:563
  142.5 3.1 %copy-start.7 = (bf16[2,4,24,1024]{3,2,1,0:T(8,128)(2,1)}, bf16[2,4,24,1024]{3,2,1,0:T(8,128)(2,1)S(1)}, u32[]{:S(2)}) copy-start(bf16[2,4,24,1024]{3,2,1,0:T(8,128)(2,1)S(1)} %collective-permute-done.15.refs_2_.refs_10_) | copy-start | bytes 1179652
  142.5 15.1 %collective-permute-start.24 = (bf16[2,2,24,1024]{3,2,1,0:T(8,128)(2,1)}, bf16[2,2,24,1024]{3,2,1,0:T(8,128)(2,1)S(1)}, u32[]{:S(2)}, u32[]{:S(2)}) collective-permute-start(bf16[2,2,24,1024]{3,2,1,0:T(8,128)(2,1)} %get-tuple-element.110), channel_id=1, source_target_pairs={{0,16},{8,24},{16,0},{24,8},{1,17},{9,25},{17,1},{25,9},{2,18},{10... | collective-permute-start | bytes 589832 | tf_op jit(solution)/shard_map/ppermute | solution.py:563
  143.6 2.0 %copy-start.8 = (bf16[2,4,24,1024]{3,2,1,0:T(8,128)(2,1)}, bf16[2,4,24,1024]{3,2,1,0:T(8,128)(2,1)S(1)}, u32[]{:S(2)}) copy-start(bf16[2,4,24,1024]{3,2,1,0:T(8,128)(2,1)S(1)} %collective-permute-done.16.refs_3_.refs_11_) | copy-start | bytes 1179652
  143.6 15.4 %collective-permute-start.25 = (bf16[2,2,24,1024]{3,2,1,0:T(8,128)(2,1)}, bf16[2,2,24,1024]{3,2,1,0:T(8,128)(2,1)S(1)}, u32[]{:S(2)}, u32[]{:S(2)}) collective-permute-start(bf16[2,2,24,1024]{3,2,1,0:T(8,128)(2,1)} %get-tuple-element.111), channel_id=1, source_target_pairs={{0,24},{8,16},{16,8},{24,0},{1,25},{9,17},{17,9},{25,1},{2,26},{10... | collective-permute-start | bytes 589832 | tf_op jit(solution)/shard_map/ppermute | solution.py:563
  157.6 1.4 copy-start.13
  157.6 1.4 copy-start.15
  158.9 0.7 copy-start.16

commit v8 on v7

--- a/solution.py
+++ b/solution.py
@@ -13,7 +13,7 @@
 TILE = 8
 LANES = 128
 MIB = 1 << 20
-VMEM_LIMIT = 62 * MIB
+VMEM_LIMIT = 64 * MIB
 COST = pl.CostEstimate(flops=1, bytes_accessed=1, transcendentals=0)
 LONG = pl.CostEstimate(flops=10**11, bytes_accessed=100 * MIB, transcendentals=0)
 
@@ -514,7 +514,7 @@
                 out_ref[0, d, pl.ds(t * TILE, TILE), here] = value + grown
         return carry
 
-    lax.fori_loop(0, dirs, body, 0, unroll=2)
+    lax.fori_loop(0, dirs, body, 0, unroll=4)
 
 
 def join(own, into, home, share, early, late, rows_of, chunks, group):
@@ -523,19 +523,20 @@
     _, dirs, rows, cols = home.shape
     last = late[0].shape[0]
     spans = [(*span, chunks[0]) for span in rows_of] + [(0, last, chunks[-1])]
-    block = pl.BlockSpec((1, dirs, rows, cols), lambda f: (begin + f, 0, 0, 0))
+    width = cols // 2 if cols % (2 * LANES) == 0 else cols
+    block = pl.BlockSpec((1, dirs, rows, width), lambda f, c: (begin + f, 0, 0, c))
     specs = [
-        pl.BlockSpec((count, 1, dirs, cols), lambda f: (0, begin + f, 0, 0)) for _, count in rows_of for _ in range(parts)
-    ] + [pl.BlockSpec((last, 1, dirs, cols), lambda f: (0, f, 0, 0))] * parts
+        pl.BlockSpec((count, 1, dirs, width), lambda f, c: (0, begin + f, 0, c)) for _, count in rows_of for _ in range(parts)
+    ] + [pl.BlockSpec((last, 1, dirs, width), lambda f, c: (0, f, 0, c))] * parts
     return pl.pallas_call(
         functools.partial(join_kernel, parts, spans),
-        grid=(many,),
+        grid=(many, cols // width),
         in_specs=[pl.BlockSpec(memory_space=pltpu.SMEM), UNREAD, block]
-        + [pl.BlockSpec((1, dirs, TILE, cols), lambda f: (begin + f, 0, 0, 0))]
+        + [pl.BlockSpec((1, dirs, TILE, width), lambda f, c: (begin + f, 0, 0, c))]
         + specs,
         out_specs=block,
         out_shape=jax.ShapeDtypeStruct(home.shape, jnp.float32),
-        scratch_shapes=[pltpu.VMEM((cols // LANES, rows * (dirs + 1), LANES), jnp.float32)],
+        scratch_shapes=[pltpu.VMEM((width // LANES, rows * (dirs + 1), LANES), jnp.float32)],
         input_output_aliases={} if begin == 0 else {1: 0},
         compiler_params=pltpu.CompilerParams(vmem_limit_bytes=VMEM_LIMIT),
         cost_estimate=COST,

time: 167 us -> 166 us (level)
  local copies, waits for them, and re-layouts: 4.74 us -> 2.74 us
    unnamed x44 -> x2, local copies, waits for them, and re-layouts: 4.14 us -> 1.45 us
  transfers between devices with their start and end apart: 26 -> 26, of which waited for: 5 -> 3; matrix products, arithmetic and copies ran while one was open for 1% -> 2% of each run, Pallas kernels for 66% -> 67%
where the time goes in v8:
time: 166 us; the launch traced here: 165 us
  Pallas kernels  129 us (78%)
  starting transfers between devices  25.4 us (15%)
  waiting for transfers between devices  6.23 us (4%)
  local copies, waits for them, and re-layouts  2.74 us (2%)
    pallas_call x4, Pallas kernels, source_term(): pl.pallas_call(functools.partial(source_kernel, parts, got, sent, dirs, 2...  56.5 us
    pallas_call x2, Pallas kernels, inner(): pl.pallas_call(functools.partial(inner_kernel, parts, local, chunk, into...  24.2 us
    ppermute x24, starting transfers between devices, swapped(): lax.ppermute(pieces[k], 'comp', [(i, i ^ k) for i in range(parts)])  18.7 us
    pallas_call x2, Pallas kernels, join(): pl.pallas_call(functools.partial(join_kernel, parts, spans), grid=(many,...  14.1 us
    pallas_call x1, Pallas kernels, outer(): pl.pallas_call(functools.partial(outer_kernel, parts, local, chunk), grid...  12.6 us
    pallas_call x1, Pallas kernels, by_row(): pl.pallas_call(by_row_kernel, grid=(deep // some,), in_specs=[UNREAD] * l...  8.43 us
    ppermute x2, starting transfers between devices, across(): return (lax.ppermute(high, 'space', up), lax.ppermute(low, 'space', down))  6.64 us
    ppermute x24, waiting for transfers between devices, swapped(): lax.ppermute(pieces[k], 'comp', [(i, i ^ k) for i in range(parts)])  6.23 us
  transfers between devices with their start and end apart: 26, of which 3 were waited for; matrix products, arithmetic and copies ran while one was open for 2% of the time, Pallas kernels for 67%

profile of v8, /device:TPU:0, one launch (start us, length us, event | category | flops | bytes accessed | tf_op | source)
XLA Modules:
  0.0 164.6 jit_solution(9554201134544817721)
XLA Ops:
  0.6 12.1 %shard_map.131 = (f32[4,24,32,1024]{3,2,1,0:T(8,128)}, bf16[6,2,24,1024]{3,2,1,0:T(8,128)(2,1)}, bf16[6,2,24,1024]{3,2,1,0:T(8,128)(2,1)}, bf16[6,2,24,1024]{3,2,1,0:T(8,128)(2,1)}, bf16[6,2,24,1024]{3,2,1,0:T(8,128)(2,1)}) custom-call(s32[1]{0:T(128)} %bitcast.own_ref.refs_0_, s32[2,24]{1,0:T(2,128)} %refs_1_.5, f32[2,24]{1,0:T(2,128)} %constant.11.clone.along_ref.refs_2_, ...), custom_call_target="tpu_custom_call" | custom-call | flops 1 | bytes 1 | tf_op jit(solution)/shard_map/pallas_call | solution.py:169
  12.8 0.5 collective-permute-start
  13.2 2.6 %collective-permute-start.1 = (bf16[6,2,24,1024]{3,2,1,0:T(8,128)(2,1)}, bf16[6,2,24,1024]{3,2,1,0:T(8,128)(2,1)}, u32[]{:S(2)}, u32[]{:S(2)}) collective-permute-start(bf16[6,2,24,1024]{3,2,1,0:T(8,128)(2,1)} %get-tuple-element.62), channel_id=1, source_target_pairs={{0,16},{8,24},{16,0},{24,8},{1,17},{9,25},{17,1},{25,9},{2,18},{10... | collective-permute-start | bytes 1769480 | tf_op jit(solution)/shard_map/ppermute | solution.py:564
  15.9 4.9 %shard_map.132 = (bf16[2,4,32,1024]{3,2,1,0:T(8,128)(2,1)}, bf16[2,4,32,1024]{3,2,1,0:T(8,128)(2,1)}) custom-call(bf16[6,2,24,1024]{3,2,1,0:T(8,128)(2,1)} %get-tuple-element.57._, f32[4,24,32,1024]{3,2,1,0:T(8,128)} %bitcast.12, s32[4,32,1024]{2,1,0:T(8,128)} %refs_7_.3, s32[4,32,1024]{2,1,0:T(8,128)} %refs_8_.1, s32[32,1024]{1,0:T(8,128)} %refs_9_.1, ...), custom_call_target="tpu_custom_call" | custom-call | flops 1 | bytes 1 | tf_op jit(solution)/shard_map/pallas_call | solution.py:227
  20.8 1.3 collective-permute-start.4
  22.1 5.4 %collective-permute-start.3 = (bf16[2,4,32,1024]{3,2,1,0:T(8,128)(2,1)}, bf16[2,4,32,1024]{3,2,1,0:T(8,128)(2,1)}, u32[]{:S(2)}, u32[]{:S(2)}) collective-permute-start(bf16[2,4,32,1024]{3,2,1,0:T(8,128)(2,1)} %get-tuple-element.58._), channel_id=1, source_target_pairs={{0,1},{1,2},{2,3},{3,4},{4,5},{5,6},{6,7},{8,9},{9,10},{10,11},{11... | collective-permute-start | bytes 1572872 | tf_op jit(solution)/shard_map/ppermute | solution.py:572
  27.4 12.1 %shard_map.133 = (f32[4,24,32,1024]{3,2,1,0:T(8,128)}, bf16[6,2,24,1024]{3,2,1,0:T(8,128)(2,1)}, bf16[6,2,24,1024]{3,2,1,0:T(8,128)(2,1)}, bf16[6,2,24,1024]{3,2,1,0:T(8,128)(2,1)}, bf16[6,2,24,1024]{3,2,1,0:T(8,128)(2,1)}) custom-call(s32[1]{0:T(128)} %bitcast.own_ref.refs_0_, s32[2,24]{1,0:T(2,128)} %refs_1_.5, ...), custom_call_target="tpu_custom_call", output_to_operand_aliasing={{0}: (9, {})} | custom-call | flops 1 | bytes 1 | tf_op jit(solution)/shard_map/pallas_call | solution.py:169
  39.5 1.3 reshape.60.weight_ref
  40.8 1.8 %collective-permute-start.6 = (bf16[6,2,24,1024]{3,2,1,0:T(8,128)(2,1)}, bf16[6,2,24,1024]{3,2,1,0:T(8,128)(2,1)}, u32[]{:S(2)}, u32[]{:S(2)}) collective-permute-start(bf16[6,2,24,1024]{3,2,1,0:T(8,128)(2,1)} %get-tuple-element.71), channel_id=1, source_target_pairs={{0,16},{8,24},{16,0},{24,8},{1,17},{9,25},{17,1},{25,9},{2,18},{10... | collective-permute-start | bytes 1769480 | tf_op jit(solution)/shard_map/ppermute | solution.py:564
  42.6 1.2 collective-permute-start.7
  43.9 0.6 shard_map.134.refs_0_
  44.5 8.4 %shard_map.135.refs_4_.state_ref = bf16[8,384,1024]{2,1,0:T(8,128)(2,1)} custom-call(f32[8,128]{1,0:T(8,128)} %shard_map.134.refs_0_, bf16[384,8,1024]{2,1,0:T(8,128)(2,1)} %refs_1_.4), custom_call_target="tpu_custom_call" | custom-call | flops 1 | bytes 1 | tf_op jit(solution)/shard_map/pallas_call | solution.py:370
  52.9 12.6 %shard_map.136 = (f32[4,24,8,1024]{3,2,1,0:T(8,128)}, bf16[2,4,24,1024]{3,2,1,0:T(8,128)(2,1)}, bf16[2,4,24,1024]{3,2,1,0:T(8,128)(2,1)}, bf16[2,4,24,1024]{3,2,1,0:T(8,128)(2,1)}, bf16[2,4,24,1024]{3,2,1,0:T(8,128)(2,1)}) custom-call(s32[1]{0:T(128)} %bitcast.own_ref.refs_0_, s32[2,24]{1,0:T(2,128)} %refs_1_.5, f32[2,24]{1,0:T(2,128)} %constant.11.clone.along_ref.refs_2_, ...), custom_call_target="tpu_custom_call" | custom-call | flops 99999997952 | bytes 104857600 | tf_op jit(solution)/shard_map/pallas_call | solution.py:323
  65.7 0.7 collective-permute-start.9
  66.4 1.0 collective-permute-start.10
  67.4 4.4 %shard_map.137 = (bf16[384,1536]{1,0:T(8,128)(2,1)}, bf16[1536,384]{1,0:T(8,128)(2,1)}, f32[1536,128]{1,0:T(8,128)}) custom-call(f32[4,24,8,1024]{3,2,1,0:T(8,128)} %get-tuple-element.64._.share_ref, bf16[1536,384]{1,0:T(8,128)(2,1)} %w_in_ref.9, bf16[384,1536]{1,0:T(8,128)(2,1)} %w_out_ref.1, f32[1,1536]{1,0:T(1,128)} %reshape.60.weight_ref), custom_call_target="tpu_custom_call" | custom-call | flops 99999997952 | bytes 104857600 | tf_op jit(solution)/shard_map/pallas_call | solution.py:393
  71.8 14.1 %shard_map.138 = (f32[2,1,1024]{2,1,0:T(1,128)}, bf16[2,4,24,1024]{3,2,1,0:T(8,128)(2,1)}, bf16[2,4,24,1024]{3,2,1,0:T(8,128)(2,1)}, bf16[2,4,24,1024]{3,2,1,0:T(8,128)(2,1)}, bf16[2,4,24,1024]{3,2,1,0:T(8,128)(2,1)}) custom-call(s32[1]{0:T(128)} %bitcast.own_ref.refs_0_, bf16[384,1536]{1,0:T(8,128)(2,1)} %get-tuple-element.65._.in_t_ref, ...), custom_call_target="tpu_custom_call" | custom-call | flops 1 | bytes 1 | tf_op jit(solution)/shard_map/pallas_call | solution.py:463
  86.0 0.6 shard_map.139
  86.6 0.5 collective-permute-start.11
  87.1 0.7 collective-permute-start.12
  87.7 0.7 collective-permute-start.13
  88.4 0.6 shard_map.140._
  89.0 14.1 %shard_map.141 = (f32[2,1,1024]{2,1,0:T(1,128)}, bf16[2,4,24,1024]{3,2,1,0:T(8,128)(2,1)}, bf16[2,4,24,1024]{3,2,1,0:T(8,128)(2,1)}, bf16[2,4,24,1024]{3,2,1,0:T(8,128)(2,1)}, bf16[2,4,24,1024]{3,2,1,0:T(8,128)(2,1)}) custom-call(s32[1]{0:T(128)} %bitcast.own_ref.refs_0_, f32[8,128]{1,0:T(8,128)} %shard_map.140._, ...), custom_call_target="tpu_custom_call" | custom-call | flops 1 | bytes 1 | tf_op jit(solution)/shard_map/pallas_call | solution.py:463
  103.2 0.8 collective-permute-start.17
  104.0 0.7 collective-permute-start.18
  104.7 0.8 collective-permute-start.19
  105.4 0.6 shard_map.142._
  106.0 14.1 %shard_map.143 = (f32[2,1,1024]{2,1,0:T(1,128)}, bf16[2,4,24,1024]{3,2,1,0:T(8,128)(2,1)}, bf16[2,4,24,1024]{3,2,1,0:T(8,128)(2,1)}, bf16[2,4,24,1024]{3,2,1,0:T(8,128)(2,1)}, bf16[2,4,24,1024]{3,2,1,0:T(8,128)(2,1)}) custom-call(s32[1]{0:T(128)} %bitcast.own_ref.refs_0_, f32[8,128]{1,0:T(8,128)} %shard_map.142._, ...), custom_call_target="tpu_custom_call" | custom-call | flops 1 | bytes 1 | tf_op jit(solution)/shard_map/pallas_call | solution.py:463
  120.1 0.8 collective-permute-start.14
  120.9 0.7 collective-permute-start.15
  121.6 0.8 collective-permute-start.16
  122.4 14.1 %shard_map.144 = (f32[2,1,1024]{2,1,0:T(1,128)}, bf16[2,2,24,1024]{3,2,1,0:T(8,128)(2,1)}, bf16[2,2,24,1024]{3,2,1,0:T(8,128)(2,1)}, bf16[2,2,24,1024]{3,2,1,0:T...) custom-call(s32[1]{0:T(128)} %bitcast.own_ref.refs_0_, ...), custom_call_target="tpu_custom_call" | custom-call | flops 1 | bytes 1 | tf_op jit(solution)/shard_map/pallas_call | solution.py:463
  136.5 0.6 shard_map.145
  137.1 0.7 collective-permute-start.20
  137.8 0.7 copy_bitcast_fusion.1
  138.5 0.7 collective-permute-start.21
  139.3 0.7 collective-permute-start.22
  140.0 0.8 collective-permute-start.23
  140.8 0.7 collective-permute-start.24
  141.4 0.7 collective-permute-start.25
  142.2 0.7 copy_bitcast_fusion
  142.9 0.7 maximum_select_fusion
  143.6 0.6 shard_map.146._
  144.1 2.5 %collective-permute-done.21.refs_14_ = bf16[2,2,24,1024]{3,2,1,0:T(8,128)(2,1)} collective-permute-done((bf16[2,2,24,1024]{3,2,1,0:T(8,128)(2,1)}, bf16[2,2,24,1024]{3,2,1,0:T(8,128)(2,1)}, u32[]{:S(2)}, u32[]{:S(2)}) %collective-permute-start.21) | collective-permute-done | bytes 196640 | tf_op jit(solution)/shard_map/ppermute | solution.py:564
  146.7 2.4 %collective-permute-done.22.refs_15_ = bf16[2,2,24,1024]{3,2,1,0:T(8,128)(2,1)} collective-permute-done((bf16[2,2,24,1024]{3,2,1,0:T(8,128)(2,1)}, bf16[2,2,24,1024]{3,2,1,0:T(8,128)(2,1)}, u32[]{:S(2)}, u32[]{:S(2)}) %collective-permute-start.22) | collective-permute-done | bytes 196640 | tf_op jit(solution)/shard_map/ppermute | solution.py:564
  149.1 7.1 %shard_map.147._ = f32[4,24,32,1024]{3,2,1,0:T(8,128)} custom-call(s32[1]{0:T(128)} %bitcast.own_ref.refs_0_, f32[8,128]{1,0:T(8,128)} %shard_map.146._, f32[4,24,32,1024]{3,2,1,0:T(8,128)} %get-tuple-element.60.refs_0_.refs_10_.home_ref, f32[4,24,8,1024]{3,2,1,0:T(8,128)} %get-tuple-element.64._.share_ref, ...), custom_call_target="tpu_custom_call" | custom-call | flops 1 | bytes 1 | tf_op jit(solution)/shard_map/pallas_call | solution.py:531
  156.2 1.2 collective-permute-done.25.refs_15_
  157.4 7.1 %shard_map.148 = f32[4,24,32,1024]{3,2,1,0:T(8,128)} custom-call(s32[1]{0:T(128)} %bitcast.own_ref.refs_0_, f32[4,24,32,1024]{3,2,1,0:T(8,128)} %shard_map.147._, f32[4,24,32,1024]{3,2,1,0:T(8,128)} %get-tuple-element.60.refs_0_.refs_10_.home_ref, f32[4,24,8,1024]{3,2,1,0:T(8,128)} %get-tuple-element.64._.share_ref, ...), custom_call_target="tpu_custom_call", output_to_operand_aliasing={{}: (1, {})} | custom-call | flops 1 | bytes 1 | tf_op jit(solution)/shard_map/pallas_call | solution.py:531
  (26 shorter events, 0.4 us)
Async XLA Ops:
  12.8 28.1 %collective-permute-start = (bf16[6,2,24,1024]{3,2,1,0:T(8,128)(2,1)}, bf16[6,2,24,1024]{3,2,1,0:T(8,128)(2,1)}, u32[]{:S(2)}, u32[]{:S(2)}) collective-permute-start(bf16[6,2,24,1024]{3,2,1,0:T(8,128)(2,1)} %get-tuple-element.61), channel_id=1, source_target_pairs={{0,8},{8,0},{16,24},{24,16},{1,9},{9,1},{17,25},{25,17},{2,10},{10... | collective-permute-start | bytes 1769480 | tf_op jit(solution)/shard_map/ppermute | solution.py:564
  13.2 27.6 %collective-permute-start.1 = (bf16[6,2,24,1024]{3,2,1,0:T(8,128)(2,1)}, bf16[6,2,24,1024]{3,2,1,0:T(8,128)(2,1)}, u32[]{:S(2)}, u32[]{:S(2)}) collective-permute-start(bf16[6,2,24,1024]{3,2,1,0:T(8,128)(2,1)} %get-tuple-element.62), channel_id=1, source_target_pairs={{0,16},{8,24},{16,0},{24,8},{1,17},{9,25},{17,1},{25,9},{2,18},{10... | collective-permute-start | bytes 1769480 | tf_op jit(solution)/shard_map/ppermute | solution.py:564
  15.8 26.8 %collective-permute-start.2 = (bf16[6,2,24,1024]{3,2,1,0:T(8,128)(2,1)}, bf16[6,2,24,1024]{3,2,1,0:T(8,128)(2,1)}, u32[]{:S(2)}, u32[]{:S(2)}) collective-permute-start(bf16[6,2,24,1024]{3,2,1,0:T(8,128)(2,1)} %get-tuple-element.57._), channel_id=1, source_target_pairs={{0,24},{8,16},{16,8},{24,0},{1,25},{9,17},{17,9},{25,1},{2,26},{10... | collective-permute-start | bytes 1769480 | tf_op jit(solution)/shard_map/ppermute | solution.py:564
  20.8 32.1 %collective-permute-start.4 = (bf16[2,4,32,1024]{3,2,1,0:T(8,128)(2,1)}, bf16[2,4,32,1024]{3,2,1,0:T(8,128)(2,1)}, u32[]{:S(2)}, u32[]{:S(2)}) collective-permute-start(bf16[2,4,32,1024]{3,2,1,0:T(8,128)(2,1)} %get-tuple-element.63), channel_id=1, source_target_pairs={{1,0},{2,1},{3,2},{4,3},{5,4},{6,5},{7,6},{9,8},{10,9},{11,10},{12... | collective-permute-start | bytes 1572872 | tf_op jit(solution)/shard_map/ppermute | solution.py:572
  22.1 30.8 %collective-permute-start.3 = (bf16[2,4,32,1024]{3,2,1,0:T(8,128)(2,1)}, bf16[2,4,32,1024]{3,2,1,0:T(8,128)(2,1)}, u32[]{:S(2)}, u32[]{:S(2)}) collective-permute-start(bf16[2,4,32,1024]{3,2,1,0:T(8,128)(2,1)} %get-tuple-element.58._), channel_id=1, source_target_pairs={{0,1},{1,2},{2,3},{3,4},{4,5},{5,6},{6,7},{8,9},{9,10},{10,11},{11... | collective-permute-start | bytes 1572872 | tf_op jit(solution)/shard_map/ppermute | solution.py:572
  40.8 25.6 %collective-permute-start.5 = (bf16[6,2,24,1024]{3,2,1,0:T(8,128)(2,1)}, bf16[6,2,24,1024]{3,2,1,0:T(8,128)(2,1)}, u32[]{:S(2)}, u32[]{:S(2)}) collective-permute-start(bf16[6,2,24,1024]{3,2,1,0:T(8,128)(2,1)} %get-tuple-element.70), channel_id=1, source_target_pairs={{0,8},{8,0},{16,24},{24,16},{1,9},{9,1},{17,25},{25,17},{2,10},{10... | collective-permute-start | bytes 1769480 | tf_op jit(solution)/shard_map/ppermute | solution.py:564
  40.8 31.0 %collective-permute-start.6 = (bf16[6,2,24,1024]{3,2,1,0:T(8,128)(2,1)}, bf16[6,2,24,1024]{3,2,1,0:T(8,128)(2,1)}, u32[]{:S(2)}, u32[]{:S(2)}) collective-permute-start(bf16[6,2,24,1024]{3,2,1,0:T(8,128)(2,1)} %get-tuple-element.71), channel_id=1, source_target_pairs={{0,16},{8,24},{16,0},{24,8},{1,17},{9,25},{17,1},{25,9},{2,18},{10... | collective-permute-start | bytes 1769480 | tf_op jit(solution)/shard_map/ppermute | solution.py:564
  42.6 29.2 %collective-permute-start.7 = (bf16[6,2,24,1024]{3,2,1,0:T(8,128)(2,1)}, bf16[6,2,24,1024]{3,2,1,0:T(8,128)(2,1)}, u32[]{:S(2)}, u32[]{:S(2)}) collective-permute-start(bf16[6,2,24,1024]{3,2,1,0:T(8,128)(2,1)} %get-tuple-element.72), channel_id=1, source_target_pairs={{0,24},{8,16},{16,8},{24,0},{1,25},{9,17},{17,9},{25,1},{2,26},{10... | collective-permute-start | bytes 1769480 | tf_op jit(solution)/shard_map/ppermute | solution.py:564
  65.5 20.4 %collective-permute-start.8 = (bf16[2,4,24,1024]{3,2,1,0:T(8,128)(2,1)}, bf16[2,4,24,1024]{3,2,1,0:T(8,128)(2,1)}, u32[]{:S(2)}, u32[]{:S(2)}) collective-permute-start(bf16[2,4,24,1024]{3,2,1,0:T(8,128)(2,1)} %get-tuple-element.74), channel_id=1, source_target_pairs={{0,8},{8,0},{16,24},{24,16},{1,9},{9,1},{17,25},{25,17},{2,10},{10... | collective-permute-start | bytes 1179656 | tf_op jit(solution)/shard_map/ppermute | solution.py:564
  65.7 20.2 %collective-permute-start.9 = (bf16[2,4,24,1024]{3,2,1,0:T(8,128)(2,1)}, bf16[2,4,24,1024]{3,2,1,0:T(8,128)(2,1)}, u32[]{:S(2)}, u32[]{:S(2)}) collective-permute-start(bf16[2,4,24,1024]{3,2,1,0:T(8,128)(2,1)} %get-tuple-element.75), channel_id=1, source_target_pairs={{0,16},{8,24},{16,0},{24,8},{1,17},{9,25},{17,1},{25,9},{2,18},{10... | collective-permute-start | bytes 1179656 | tf_op jit(solution)/shard_map/ppermute | solution.py:564
  66.4 22.0 %collective-permute-start.10 = (bf16[2,4,24,1024]{3,2,1,0:T(8,128)(2,1)}, bf16[2,4,24,1024]{3,2,1,0:T(8,128)(2,1)}, u32[]{:S(2)}, u32[]{:S(2)}) collective-permute-start(bf16[2,4,24,1024]{3,2,1,0:T(8,128)(2,1)} %get-tuple-element.80), channel_id=1, source_target_pairs={{0,24},{8,16},{16,8},{24,0},{1,25},{9,17},{17,9},{25,1},{2,26},{10... | collective-permute-start | bytes 1179656 | tf_op jit(solution)/shard_map/ppermute | solution.py:564
  86.6 18.1 %collective-permute-start.11 = (bf16[2,4,24,1024]{3,2,1,0:T(8,128)(2,1)}, bf16[2,4,24,1024]{3,2,1,0:T(8,128)(2,1)}, u32[]{:S(2)}, u32[]{:S(2)}) collective-permute-start(bf16[2,4,24,1024]{3,2,1,0:T(8,128)(2,1)} %get-tuple-element.82), channel_id=1, source_target_pairs={{0,8},{8,0},{16,24},{24,16},{1,9},{9,1},{17,25},{25,17},{2,10},{10... | collective-permute-start | bytes 1179656 | tf_op jit(solution)/shard_map/ppermute | solution.py:564
  87.1 33.1 %collective-permute-start.12 = (bf16[2,4,24,1024]{3,2,1,0:T(8,128)(2,1)}, bf16[2,4,24,1024]{3,2,1,0:T(8,128)(2,1)}, u32[]{:S(2)}, u32[]{:S(2)}) collective-permute-start(bf16[2,4,24,1024]{3,2,1,0:T(8,128)(2,1)} %get-tuple-element.86), channel_id=1, source_target_pairs={{0,16},{8,24},{16,0},{24,8},{1,17},{9,25},{17,1},{25,9},{2,18},{10... | collective-permute-start | bytes 1179656 | tf_op jit(solution)/shard_map/ppermute | solution.py:564
  87.7 33.2 %collective-permute-start.13 = (bf16[2,4,24,1024]{3,2,1,0:T(8,128)(2,1)}, bf16[2,4,24,1024]{3,2,1,0:T(8,128)(2,1)}, u32[]{:S(2)}, u32[]{:S(2)}) collective-permute-start(bf16[2,4,24,1024]{3,2,1,0:T(8,128)(2,1)} %get-tuple-element.87), channel_id=1, source_target_pairs={{0,24},{8,16},{16,8},{24,0},{1,25},{9,17},{17,9},{25,1},{2,26},{10... | collective-permute-start | bytes 1179656 | tf_op jit(solution)/shard_map/ppermute | solution.py:564
  103.2 18.5 %collective-permute-start.17 = (bf16[2,4,24,1024]{3,2,1,0:T(8,128)(2,1)}, bf16[2,4,24,1024]{3,2,1,0:T(8,128)(2,1)}, u32[]{:S(2)}, u32[]{:S(2)}) collective-permute-start(bf16[2,4,24,1024]{3,2,1,0:T(8,128)(2,1)} %get-tuple-element.100), channel_id=1, source_target_pairs={{0,8},{8,0},{16,24},{24,16},{1,9},{9,1},{17,25},{25,17},{2,10},{10... | collective-permute-start | bytes 1179656 | tf_op jit(solution)/shard_map/ppermute | solution.py:564
  104.0 33.1 %collective-permute-start.18 = (bf16[2,4,24,1024]{3,2,1,0:T(8,128)(2,1)}, bf16[2,4,24,1024]{3,2,1,0:T(8,128)(2,1)}, u32[]{:S(2)}, u32[]{:S(2)}) collective-permute-start(bf16[2,4,24,1024]{3,2,1,0:T(8,128)(2,1)} %get-tuple-element.101), channel_id=1, source_target_pairs={{0,16},{8,24},{16,0},{24,8},{1,17},{9,25},{17,1},{25,9},{2,18},{10... | collective-permute-start | bytes 1179656 | tf_op jit(solution)/shard_map/ppermute | solution.py:564
  104.7 33.8 %collective-permute-start.19 = (bf16[2,4,24,1024]{3,2,1,0:T(8,128)(2,1)}, bf16[2,4,24,1024]{3,2,1,0:T(8,128)(2,1)}, u32[]{:S(2)}, u32[]{:S(2)}) collective-permute-start(bf16[2,4,24,1024]{3,2,1,0:T(8,128)(2,1)} %get-tuple-element.102), channel_id=1, source_target_pairs={{0,24},{8,16},{16,8},{24,0},{1,25},{9,17},{17,9},{25,1},{2,26},{10... | collective-permute-start | bytes 1179656 | tf_op jit(solution)/shard_map/ppermute | solution.py:564
  120.1 19.8 %collective-permute-start.14 = (bf16[2,4,24,1024]{3,2,1,0:T(8,128)(2,1)}, bf16[2,4,24,1024]{3,2,1,0:T(8,128)(2,1)}, u32[]{:S(2)}, u32[]{:S(2)}) collective-permute-start(bf16[2,4,24,1024]{3,2,1,0:T(8,128)(2,1)} %get-tuple-element.95), channel_id=1, source_target_pairs={{0,8},{8,0},{16,24},{24,16},{1,9},{9,1},{17,25},{25,17},{2,10},{10... | collective-permute-start | bytes 1179656 | tf_op jit(solution)/shard_map/ppermute | solution.py:564
  120.9 19.8 %collective-permute-start.15 = (bf16[2,4,24,1024]{3,2,1,0:T(8,128)(2,1)}, bf16[2,4,24,1024]{3,2,1,0:T(8,128)(2,1)}, u32[]{:S(2)}, u32[]{:S(2)}) collective-permute-start(bf16[2,4,24,1024]{3,2,1,0:T(8,128)(2,1)} %get-tuple-element.96), channel_id=1, source_target_pairs={{0,16},{8,24},{16,0},{24,8},{1,17},{9,25},{17,1},{25,9},{2,18},{10... | collective-permute-start | bytes 1179656 | tf_op jit(solution)/shard_map/ppermute | solution.py:564
  121.6 19.8 %collective-permute-start.16 = (bf16[2,4,24,1024]{3,2,1,0:T(8,128)(2,1)}, bf16[2,4,24,1024]{3,2,1,0:T(8,128)(2,1)}, u32[]{:S(2)}, u32[]{:S(2)}) collective-permute-start(bf16[2,4,24,1024]{3,2,1,0:T(8,128)(2,1)} %get-tuple-element.97), channel_id=1, source_target_pairs={{0,24},{8,16},{16,8},{24,0},{1,25},{9,17},{17,9},{25,1},{2,26},{10... | collective-permute-start | bytes 1179656 | tf_op jit(solution)/shard_map/ppermute | solution.py:564
  137.1 2.2 %collective-permute-start.20 = (bf16[2,2,24,1024]{3,2,1,0:T(8,128)(2,1)}, bf16[2,2,24,1024]{3,2,1,0:T(8,128)(2,1)}, u32[]{:S(2)}, u32[]{:S(2)}) collective-permute-start(bf16[2,2,24,1024]{3,2,1,0:T(8,128)(2,1)} %get-tuple-element.105), channel_id=1, source_target_pairs={{0,8},{8,0},{16,24},{24,16},{1,9},{9,1},{17,25},{25,17},{2,10},{10... | collective-permute-start | bytes 589832 | tf_op jit(solution)/shard_map/ppermute | solution.py:564
  138.5 8.2 %collective-permute-start.21 = (bf16[2,2,24,1024]{3,2,1,0:T(8,128)(2,1)}, bf16[2,2,24,1024]{3,2,1,0:T(8,128)(2,1)}, u32[]{:S(2)}, u32[]{:S(2)}) collective-permute-start(bf16[2,2,24,1024]{3,2,1,0:T(8,128)(2,1)} %get-tuple-element.106), channel_id=1, source_target_pairs={{0,16},{8,24},{16,0},{24,8},{1,17},{9,25},{17,1},{25,9},{2,18},{10... | collective-permute-start | bytes 589832 | tf_op jit(solution)/shard_map/ppermute | solution.py:564
  139.3 9.8 %collective-permute-start.22 = (bf16[2,2,24,1024]{3,2,1,0:T(8,128)(2,1)}, bf16[2,2,24,1024]{3,2,1,0:T(8,128)(2,1)}, u32[]{:S(2)}, u32[]{:S(2)}) collective-permute-start(bf16[2,2,24,1024]{3,2,1,0:T(8,128)(2,1)} %get-tuple-element.107), channel_id=1, source_target_pairs={{0,24},{8,16},{16,8},{24,0},{1,25},{9,17},{17,9},{25,1},{2,26},{10... | collective-permute-start | bytes 589832 | tf_op jit(solution)/shard_map/ppermute | solution.py:564
  140.0 16.2 %collective-permute-start.23 = (bf16[2,2,24,1024]{3,2,1,0:T(8,128)(2,1)}, bf16[2,2,24,1024]{3,2,1,0:T(8,128)(2,1)}, u32[]{:S(2)}, u32[]{:S(2)}) collective-permute-start(bf16[2,2,24,1024]{3,2,1,0:T(8,128)(2,1)} %get-tuple-element.109), channel_id=1, source_target_pairs={{0,8},{8,0},{16,24},{24,16},{1,9},{9,1},{17,25},{25,17},{2,10},{10... | collective-permute-start | bytes 589832 | tf_op jit(solution)/shard_map/ppermute | solution.py:564
  140.8 15.4 %collective-permute-start.24 = (bf16[2,2,24,1024]{3,2,1,0:T(8,128)(2,1)}, bf16[2,2,24,1024]{3,2,1,0:T(8,128)(2,1)}, u32[]{:S(2)}, u32[]{:S(2)}) collective-permute-start(bf16[2,2,24,1024]{3,2,1,0:T(8,128)(2,1)} %get-tuple-element.110), channel_id=1, source_target_pairs={{0,16},{8,24},{16,0},{24,8},{1,17},{9,25},{17,1},{25,9},{2,18},{10... | collective-permute-start | bytes 589832 | tf_op jit(solution)/shard_map/ppermute | solution.py:564
  141.4 16.0 %collective-permute-start.25 = (bf16[2,2,24,1024]{3,2,1,0:T(8,128)(2,1)}, bf16[2,2,24,1024]{3,2,1,0:T(8,128)(2,1)}, u32[]{:S(2)}, u32[]{:S(2)}) collective-permute-start(bf16[2,2,24,1024]{3,2,1,0:T(8,128)(2,1)} %get-tuple-element.111), channel_id=1, source_target_pairs={{0,24},{8,16},{16,8},{24,0},{1,25},{9,17},{17,9},{25,1},{2,26},{10... | collective-permute-start | bytes 589832 | tf_op jit(solution)/shard_map/ppermute | solution.py:564

commit v9 on v7

--- a/solution.py
+++ b/solution.py
@@ -13,7 +13,7 @@
 TILE = 8
 LANES = 128
 MIB = 1 << 20
-VMEM_LIMIT = 62 * MIB
+VMEM_LIMIT = 64 * MIB
 COST = pl.CostEstimate(flops=1, bytes_accessed=1, transcendentals=0)
 LONG = pl.CostEstimate(flops=10**11, bytes_accessed=100 * MIB, transcendentals=0)
 
@@ -382,7 +382,10 @@
 def turned_kernel(_, w_in_ref, w_out_ref, weight_ref, in_t_ref, out_t_ref, column_ref):
     in_t_ref[...] = w_in_ref[...].T
     out_t_ref[...] = w_out_ref[...].T
-    column_ref[...] = jnp.broadcast_to(weight_ref[...], (LANES, weight_ref.shape[1])).T
+
+    @pl.when(pl.program_id(0) == 0)
+    def _():
+        column_ref[...] = jnp.broadcast_to(weight_ref[...][None, :], (LANES, weight_ref.shape[0])).T
 
 
 def turned(after, w_in, w_out, weight):
@@ -393,8 +396,8 @@
     return pl.pallas_call(
         turned_kernel,
         grid=(hidden // step,),
-        in_specs=[UNREAD, tall, wide, pl.BlockSpec((1, step), lambda h: (0, h))],
-        out_specs=[wide, tall, pl.BlockSpec((step, LANES), lambda h: (h, 0))],
+        in_specs=[UNREAD, tall, wide, pl.BlockSpec(memory_space=pltpu.VMEM)],
+        out_specs=[wide, tall, pl.BlockSpec((hidden, LANES), lambda h: (0, 0))],
         out_shape=[
             jax.ShapeDtypeStruct((total, hidden), w_in.dtype),
             jax.ShapeDtypeStruct((hidden, total), w_in.dtype),
@@ -402,7 +405,7 @@
         ],
         compiler_params=pltpu.CompilerParams(vmem_limit_bytes=VMEM_LIMIT),
         cost_estimate=LONG,
-    )(after, w_in, w_out, weight.reshape(1, hidden))
+    )(after, w_in, w_out, weight)
 
 
 def source_kernel(parts, got, sent, dirs, step, first, chunk, own_ref, _, state_ref, wind_ref, w_in_ref, out_t_ref, in_t_ref, weight_ref, *refs):

time: 167 us -> 166 us (level)
  local copies, waits for them, and re-layouts: 4.74 us -> 1.45 us
    unnamed x44 -> x2, local copies, waits for them, and re-layouts: 4.14 us -> 1.45 us
  transfers between devices with their start and end apart: 26 -> 26, of which waited for: 5 -> 5; matrix products, arithmetic and copies ran while one was open for 1% -> 1% of each run, Pallas kernels for 66% -> 67%
where the time goes in v9:
time: 166 us; the launch traced here: 165 us
  Pallas kernels  128 us (77%)
  starting transfers between devices  25.5 us (15%)
  waiting for transfers between devices  7.86 us (5%)
    pallas_call x4, Pallas kernels, source_term(): pl.pallas_call(functools.partial(source_kernel, parts, got, sent, dirs, 2...  56.7 us
    pallas_call x2, Pallas kernels, inner(): pl.pallas_call(functools.partial(inner_kernel, parts, local, chunk, into...  24.2 us
    ppermute x24, starting transfers between devices, swapped(): lax.ppermute(pieces[k], 'comp', [(i, i ^ k) for i in range(parts)])  18.9 us
    pallas_call x2, Pallas kernels, join(): pl.pallas_call(functools.partial(join_kernel, parts, spans), grid=(many,)...  13.1 us
    pallas_call x1, Pallas kernels, outer(): pl.pallas_call(functools.partial(outer_kernel, parts, local, chunk), grid...  12.6 us
    pallas_call x1, Pallas kernels, by_row(): pl.pallas_call(by_row_kernel, grid=(deep // some,), in_specs=[UNREAD] * l...  8.43 us
    ppermute x24, waiting for transfers between devices, swapped(): lax.ppermute(pieces[k], 'comp', [(i, i ^ k) for i in range(parts)])  7.86 us
    ppermute x2, starting transfers between devices, across(): return (lax.ppermute(high, 'space', up), lax.ppermute(low, 'space', down))  6.64 us
  transfers between devices with their start and end apart: 26, of which 5 were waited for; matrix products, arithmetic and copies ran while one was open for 1% of the time, Pallas kernels for 67%

profile of v9, /device:TPU:0, one launch (start us, length us, event | category | flops | bytes accessed | tf_op | source)
XLA Modules:
  0.0 164.6 jit_solution(11240812141028785032)
XLA Ops:
  0.6 12.1 %shard_map.131 = (f32[4,24,32,1024]{3,2,1,0:T(8,128)}, bf16[6,2,24,1024]{3,2,1,0:T(8,128)(2,1)}, bf16[6,2,24,1024]{3,2,1,0:T(8,128)(2,1)}, bf16[6,2,24,1024]{3,2,1,0:T(8,128)(2,1)}, bf16[6,2,24,1024]{3,2,1,0:T(8,128)(2,1)}) custom-call(s32[1]{0:T(128)} %bitcast.own_ref.refs_0_, s32[2,24]{1,0:T(2,128)} %refs_1_.5, f32[2,24]{1,0:T(2,128)} %constant.11.clone.along_ref.refs_2_, ...), custom_call_target="tpu_custom_call" | custom-call | flops 1 | bytes 1 | tf_op jit(solution)/shard_map/pallas_call | solution.py:169
  12.8 0.5 collective-permute-start
  13.2 2.6 %collective-permute-start.1 = (bf16[6,2,24,1024]{3,2,1,0:T(8,128)(2,1)}, bf16[6,2,24,1024]{3,2,1,0:T(8,128)(2,1)}, u32[]{:S(2)}, u32[]{:S(2)}) collective-permute-start(bf16[6,2,24,1024]{3,2,1,0:T(8,128)(2,1)} %get-tuple-element.62), channel_id=1, source_target_pairs={{0,16},{8,24},{16,0},{24,8},{1,17},{9,25},{17,1},{25,9},{2,18},{10... | collective-permute-start | bytes 1769480 | tf_op jit(solution)/shard_map/ppermute | solution.py:566
  15.9 4.9 %shard_map.132 = (bf16[2,4,32,1024]{3,2,1,0:T(8,128)(2,1)}, bf16[2,4,32,1024]{3,2,1,0:T(8,128)(2,1)}) custom-call(bf16[6,2,24,1024]{3,2,1,0:T(8,128)(2,1)} %get-tuple-element.57._, f32[4,24,32,1024]{3,2,1,0:T(8,128)} %bitcast.12, s32[4,32,1024]{2,1,0:T(8,128)} %refs_7_.3, s32[4,32,1024]{2,1,0:T(8,128)} %refs_8_.1, s32[32,1024]{1,0:T(8,128)} %refs_9_.1, ...), custom_call_target="tpu_custom_call" | custom-call | flops 1 | bytes 1 | tf_op jit(solution)/shard_map/pallas_call | solution.py:227
  20.8 1.3 collective-permute-start.4
  22.1 5.4 %collective-permute-start.3 = (bf16[2,4,32,1024]{3,2,1,0:T(8,128)(2,1)}, bf16[2,4,32,1024]{3,2,1,0:T(8,128)(2,1)}, u32[]{:S(2)}, u32[]{:S(2)}) collective-permute-start(bf16[2,4,32,1024]{3,2,1,0:T(8,128)(2,1)} %get-tuple-element.58._), channel_id=1, source_target_pairs={{0,1},{1,2},{2,3},{3,4},{4,5},{5,6},{6,7},{8,9},{9,10},{10,11},{11... | collective-permute-start | bytes 1572872 | tf_op jit(solution)/shard_map/ppermute | solution.py:574
  27.4 12.1 %shard_map.133 = (f32[4,24,32,1024]{3,2,1,0:T(8,128)}, bf16[6,2,24,1024]{3,2,1,0:T(8,128)(2,1)}, bf16[6,2,24,1024]{3,2,1,0:T(8,128)(2,1)}, bf16[6,2,24,1024]{3,2,1,0:T(8,128)(2,1)}, bf16[6,2,24,1024]{3,2,1,0:T(8,128)(2,1)}) custom-call(s32[1]{0:T(128)} %bitcast.own_ref.refs_0_, s32[2,24]{1,0:T(2,128)} %refs_1_.5, ...), custom_call_target="tpu_custom_call", output_to_operand_aliasing={{0}: (9, {})} | custom-call | flops 1 | bytes 1 | tf_op jit(solution)/shard_map/pallas_call | solution.py:169
  39.6 1.8 %collective-permute-start.6 = (bf16[6,2,24,1024]{3,2,1,0:T(8,128)(2,1)}, bf16[6,2,24,1024]{3,2,1,0:T(8,128)(2,1)}, u32[]{:S(2)}, u32[]{:S(2)}) collective-permute-start(bf16[6,2,24,1024]{3,2,1,0:T(8,128)(2,1)} %get-tuple-element.71), channel_id=1, source_target_pairs={{0,16},{8,24},{16,0},{24,8},{1,17},{9,25},{17,1},{25,9},{2,18},{10... | collective-permute-start | bytes 1769480 | tf_op jit(solution)/shard_map/ppermute | solution.py:566
  41.4 1.0 collective-permute-done.2.refs_3_
  42.4 1.4 collective-permute-start.7
  43.9 0.6 shard_map.134.refs_0_
  44.5 8.4 %shard_map.135.refs_4_.state_ref = bf16[8,384,1024]{2,1,0:T(8,128)(2,1)} custom-call(f32[8,128]{1,0:T(8,128)} %shard_map.134.refs_0_, bf16[384,8,1024]{2,1,0:T(8,128)(2,1)} %refs_1_.4), custom_call_target="tpu_custom_call" | custom-call | flops 1 | bytes 1 | tf_op jit(solution)/shard_map/pallas_call | solution.py:370
  52.9 12.6 %shard_map.136 = (f32[4,24,8,1024]{3,2,1,0:T(8,128)}, bf16[2,4,24,1024]{3,2,1,0:T(8,128)(2,1)}, bf16[2,4,24,1024]{3,2,1,0:T(8,128)(2,1)}, bf16[2,4,24,1024]{3,2,1,0:T(8,128)(2,1)}, bf16[2,4,24,1024]{3,2,1,0:T(8,128)(2,1)}) custom-call(s32[1]{0:T(128)} %bitcast.own_ref.refs_0_, s32[2,24]{1,0:T(2,128)} %refs_1_.5, f32[2,24]{1,0:T(2,128)} %constant.11.clone.along_ref.refs_2_, ...), custom_call_target="tpu_custom_call" | custom-call | flops 99999997952 | bytes 104857600 | tf_op jit(solution)/shard_map/pallas_call | solution.py:323
  65.8 0.5 collective-permute-start.9
  66.2 1.2 collective-permute-start.10
  67.4 4.7 %shard_map.137 = (bf16[384,1536]{1,0:T(8,128)(2,1)}, bf16[1536,384]{1,0:T(8,128)(2,1)}, f32[1536,128]{1,0:T(8,128)}) custom-call(f32[4,24,8,1024]{3,2,1,0:T(8,128)} %get-tuple-element.64._.share_ref, bf16[1536,384]{1,0:T(8,128)(2,1)} %w_in_ref.9, bf16[384,1536]{1,0:T(8,128)(2,1)} %w_out_ref.1, f32[1536]{0:T(1024)} %weight_ref.1), custom_call_target="tpu_custom_call" | custom-call | flops 99999997952 | bytes 104857600 | tf_op jit(solution)/shard_map/pallas_call | solution.py:396
  72.2 14.1 %shard_map.138 = (f32[2,1,1024]{2,1,0:T(1,128)}, bf16[2,4,24,1024]{3,2,1,0:T(8,128)(2,1)}, bf16[2,4,24,1024]{3,2,1,0:T(8,128)(2,1)}, bf16[2,4,24,1024]{3,2,1,0:T(8,128)(2,1)}, bf16[2,4,24,1024]{3,2,1,0:T(8,128)(2,1)}) custom-call(s32[1]{0:T(128)} %bitcast.own_ref.refs_0_, bf16[384,1536]{1,0:T(8,128)(2,1)} %get-tuple-element.65._.in_t_ref, ...), custom_call_target="tpu_custom_call" | custom-call | flops 1 | bytes 1 | tf_op jit(solution)/shard_map/pallas_call | solution.py:466
  86.3 0.6 shard_map.139
  86.9 0.5 collective-permute-start.11
  87.4 0.5 collective-permute-start.12
  87.9 0.9 collective-permute-start.13
  88.8 0.6 shard_map.140._
  89.3 14.1 %shard_map.141 = (f32[2,1,1024]{2,1,0:T(1,128)}, bf16[2,4,24,1024]{3,2,1,0:T(8,128)(2,1)}, bf16[2,4,24,1024]{3,2,1,0:T(8,128)(2,1)}, bf16[2,4,24,1024]{3,2,1,0:T(8,128)(2,1)}, bf16[2,4,24,1024]{3,2,1,0:T(8,128)(2,1)}) custom-call(s32[1]{0:T(128)} %bitcast.own_ref.refs_0_, f32[8,128]{1,0:T(8,128)} %shard_map.140._, ...), custom_call_target="tpu_custom_call" | custom-call | flops 1 | bytes 1 | tf_op jit(solution)/shard_map/pallas_call | solution.py:466
  103.5 0.8 collective-permute-start.17
  104.3 0.5 collective-permute-start.18
  104.8 0.9 collective-permute-start.19
  105.8 0.6 shard_map.142._
  106.4 14.3 %shard_map.143 = (f32[2,1,1024]{2,1,0:T(1,128)}, bf16[2,4,24,1024]{3,2,1,0:T(8,128)(2,1)}, bf16[2,4,24,1024]{3,2,1,0:T(8,128)(2,1)}, bf16[2,4,24,1024]{3,2,1,0:T(8,128)(2,1)}, bf16[2,4,24,1024]{3,2,1,0:T(8,128)(2,1)}) custom-call(s32[1]{0:T(128)} %bitcast.own_ref.refs_0_, f32[8,128]{1,0:T(8,128)} %shard_map.142._, ...), custom_call_target="tpu_custom_call" | custom-call | flops 1 | bytes 1 | tf_op jit(solution)/shard_map/pallas_call | solution.py:466
  120.7 0.8 collective-permute-start.14
  121.4 0.5 collective-permute-start.15
  121.9 0.9 collective-permute-start.16
  122.9 14.1 %shard_map.144 = (f32[2,1,1024]{2,1,0:T(1,128)}, bf16[2,2,24,1024]{3,2,1,0:T(8,128)(2,1)}, bf16[2,2,24,1024]{3,2,1,0:T(8,128)(2,1)}, bf16[2,2,24,1024]{3,2,1,0:T...) custom-call(s32[1]{0:T(128)} %bitcast.own_ref.refs_0_, ...), custom_call_target="tpu_custom_call" | custom-call | flops 1 | bytes 1 | tf_op jit(solution)/shard_map/pallas_call | solution.py:466
  137.0 0.6 shard_map.145
  137.6 0.7 collective-permute-start.20
  138.3 0.7 copy_bitcast_fusion.1
  139.0 0.6 collective-permute-start.21
  139.7 0.7 collective-permute-start.22
  140.5 0.8 collective-permute-start.23
  141.3 0.6 collective-permute-start.24
  141.9 0.8 collective-permute-start.25
  142.7 0.7 copy_bitcast_fusion
  143.4 0.7 maximum_select_fusion
  144.1 0.6 shard_map.146._
  144.7 2.5 %collective-permute-done.21.refs_14_ = bf16[2,2,24,1024]{3,2,1,0:T(8,128)(2,1)} collective-permute-done((bf16[2,2,24,1024]{3,2,1,0:T(8,128)(2,1)}, bf16[2,2,24,1024]{3,2,1,0:T(8,128)(2,1)}, u32[]{:S(2)}, u32[]{:S(2)}) %collective-permute-start.21) | collective-permute-done | bytes 196640 | tf_op jit(solution)/shard_map/ppermute | solution.py:566
  147.2 2.3 %collective-permute-done.22.refs_15_ = bf16[2,2,24,1024]{3,2,1,0:T(8,128)(2,1)} collective-permute-done((bf16[2,2,24,1024]{3,2,1,0:T(8,128)(2,1)}, bf16[2,2,24,1024]{3,2,1,0:T(8,128)(2,1)}, u32[]{:S(2)}, u32[]{:S(2)}) %collective-permute-start.22) | collective-permute-done | bytes 196640 | tf_op jit(solution)/shard_map/ppermute | solution.py:566
  149.5 6.6 %shard_map.147._ = f32[4,24,32,1024]{3,2,1,0:T(8,128)} custom-call(s32[1]{0:T(128)} %bitcast.own_ref.refs_0_, f32[8,128]{1,0:T(8,128)} %shard_map.146._, f32[4,24,32,1024]{3,2,1,0:T(8,128)} %get-tuple-element.60.refs_0_.refs_10_.home_ref, f32[4,24,8,1024]{3,2,1,0:T(8,128)} %get-tuple-element.64._.share_ref, ...), custom_call_target="tpu_custom_call" | custom-call | flops 1 | bytes 1 | tf_op jit(solution)/shard_map/pallas_call | solution.py:533
  156.1 1.8 %collective-permute-done.25.refs_15_ = bf16[2,2,24,1024]{3,2,1,0:T(8,128)(2,1)} collective-permute-done((bf16[2,2,24,1024]{3,2,1,0:T(8,128)(2,1)}, bf16[2,2,24,1024]{3,2,1,0:T(8,128)(2,1)}, u32[]{:S(2)}, u32[]{:S(2)}) %collective-permute-start.25) | collective-permute-done | bytes 196640 | tf_op jit(solution)/shard_map/ppermute | solution.py:566
  157.9 6.6 %shard_map.148 = f32[4,24,32,1024]{3,2,1,0:T(8,128)} custom-call(s32[1]{0:T(128)} %bitcast.own_ref.refs_0_, f32[4,24,32,1024]{3,2,1,0:T(8,128)} %shard_map.147._, f32[4,24,32,1024]{3,2,1,0:T(8,128)} %get-tuple-element.60.refs_0_.refs_10_.home_ref, f32[4,24,8,1024]{3,2,1,0:T(8,128)} %get-tuple-element.64._.share_ref, ...), custom_call_target="tpu_custom_call", output_to_operand_aliasing={{}: (1, {})} | custom-call | flops 1 | bytes 1 | tf_op jit(solution)/shard_map/pallas_call | solution.py:533
  (25 shorter events, 0.6 us)
Async XLA Ops:
  12.8 26.8 %collective-permute-start = (bf16[6,2,24,1024]{3,2,1,0:T(8,128)(2,1)}, bf16[6,2,24,1024]{3,2,1,0:T(8,128)(2,1)}, u32[]{:S(2)}, u32[]{:S(2)}) collective-permute-start(bf16[6,2,24,1024]{3,2,1,0:T(8,128)(2,1)} %get-tuple-element.61), channel_id=1, source_target_pairs={{0,8},{8,0},{16,24},{24,16},{1,9},{9,1},{17,25},{25,17},{2,10},{10... | collective-permute-start | bytes 1769480 | tf_op jit(solution)/shard_map/ppermute | solution.py:566
  13.2 26.4 %collective-permute-start.1 = (bf16[6,2,24,1024]{3,2,1,0:T(8,128)(2,1)}, bf16[6,2,24,1024]{3,2,1,0:T(8,128)(2,1)}, u32[]{:S(2)}, u32[]{:S(2)}) collective-permute-start(bf16[6,2,24,1024]{3,2,1,0:T(8,128)(2,1)} %get-tuple-element.62), channel_id=1, source_target_pairs={{0,16},{8,24},{16,0},{24,8},{1,17},{9,25},{17,1},{25,9},{2,18},{10... | collective-permute-start | bytes 1769480 | tf_op jit(solution)/shard_map/ppermute | solution.py:566
  15.8 26.6 %collective-permute-start.2 = (bf16[6,2,24,1024]{3,2,1,0:T(8,128)(2,1)}, bf16[6,2,24,1024]{3,2,1,0:T(8,128)(2,1)}, u32[]{:S(2)}, u32[]{:S(2)}) collective-permute-start(bf16[6,2,24,1024]{3,2,1,0:T(8,128)(2,1)} %get-tuple-element.57._), channel_id=1, source_target_pairs={{0,24},{8,16},{16,8},{24,0},{1,25},{9,17},{17,9},{25,1},{2,26},{10... | collective-permute-start | bytes 1769480 | tf_op jit(solution)/shard_map/ppermute | solution.py:566
  20.8 32.1 %collective-permute-start.4 = (bf16[2,4,32,1024]{3,2,1,0:T(8,128)(2,1)}, bf16[2,4,32,1024]{3,2,1,0:T(8,128)(2,1)}, u32[]{:S(2)}, u32[]{:S(2)}) collective-permute-start(bf16[2,4,32,1024]{3,2,1,0:T(8,128)(2,1)} %get-tuple-element.63), channel_id=1, source_target_pairs={{1,0},{2,1},{3,2},{4,3},{5,4},{6,5},{7,6},{9,8},{10,9},{11,10},{12... | collective-permute-start | bytes 1572872 | tf_op jit(solution)/shard_map/ppermute | solution.py:574
  22.1 30.8 %collective-permute-start.3 = (bf16[2,4,32,1024]{3,2,1,0:T(8,128)(2,1)}, bf16[2,4,32,1024]{3,2,1,0:T(8,128)(2,1)}, u32[]{:S(2)}, u32[]{:S(2)}) collective-permute-start(bf16[2,4,32,1024]{3,2,1,0:T(8,128)(2,1)} %get-tuple-element.58._), channel_id=1, source_target_pairs={{0,1},{1,2},{2,3},{3,4},{4,5},{5,6},{6,7},{8,9},{9,10},{10,11},{11... | collective-permute-start | bytes 1572872 | tf_op jit(solution)/shard_map/ppermute | solution.py:574
  39.5 26.7 %collective-permute-start.5 = (bf16[6,2,24,1024]{3,2,1,0:T(8,128)(2,1)}, bf16[6,2,24,1024]{3,2,1,0:T(8,128)(2,1)}, u32[]{:S(2)}, u32[]{:S(2)}) collective-permute-start(bf16[6,2,24,1024]{3,2,1,0:T(8,128)(2,1)} %get-tuple-element.70), channel_id=1, source_target_pairs={{0,8},{8,0},{16,24},{24,16},{1,9},{9,1},{17,25},{25,17},{2,10},{10... | collective-permute-start | bytes 1769480 | tf_op jit(solution)/shard_map/ppermute | solution.py:566
  39.6 32.5 %collective-permute-start.6 = (bf16[6,2,24,1024]{3,2,1,0:T(8,128)(2,1)}, bf16[6,2,24,1024]{3,2,1,0:T(8,128)(2,1)}, u32[]{:S(2)}, u32[]{:S(2)}) collective-permute-start(bf16[6,2,24,1024]{3,2,1,0:T(8,128)(2,1)} %get-tuple-element.71), channel_id=1, source_target_pairs={{0,16},{8,24},{16,0},{24,8},{1,17},{9,25},{17,1},{25,9},{2,18},{10... | collective-permute-start | bytes 1769480 | tf_op jit(solution)/shard_map/ppermute | solution.py:566
  42.4 29.7 %collective-permute-start.7 = (bf16[6,2,24,1024]{3,2,1,0:T(8,128)(2,1)}, bf16[6,2,24,1024]{3,2,1,0:T(8,128)(2,1)}, u32[]{:S(2)}, u32[]{:S(2)}) collective-permute-start(bf16[6,2,24,1024]{3,2,1,0:T(8,128)(2,1)} %get-tuple-element.72), channel_id=1, source_target_pairs={{0,24},{8,16},{16,8},{24,0},{1,25},{9,17},{17,9},{25,1},{2,26},{10... | collective-permute-start | bytes 1769480 | tf_op jit(solution)/shard_map/ppermute | solution.py:566
  65.5 20.8 %collective-permute-start.8 = (bf16[2,4,24,1024]{3,2,1,0:T(8,128)(2,1)}, bf16[2,4,24,1024]{3,2,1,0:T(8,128)(2,1)}, u32[]{:S(2)}, u32[]{:S(2)}) collective-permute-start(bf16[2,4,24,1024]{3,2,1,0:T(8,128)(2,1)} %get-tuple-element.74), channel_id=1, source_target_pairs={{0,8},{8,0},{16,24},{24,16},{1,9},{9,1},{17,25},{25,17},{2,10},{10... | collective-permute-start | bytes 1179656 | tf_op jit(solution)/shard_map/ppermute | solution.py:566
  65.8 20.5 %collective-permute-start.9 = (bf16[2,4,24,1024]{3,2,1,0:T(8,128)(2,1)}, bf16[2,4,24,1024]{3,2,1,0:T(8,128)(2,1)}, u32[]{:S(2)}, u32[]{:S(2)}) collective-permute-start(bf16[2,4,24,1024]{3,2,1,0:T(8,128)(2,1)} %get-tuple-element.75), channel_id=1, source_target_pairs={{0,16},{8,24},{16,0},{24,8},{1,17},{9,25},{17,1},{25,9},{2,18},{10... | collective-permute-start | bytes 1179656 | tf_op jit(solution)/shard_map/ppermute | solution.py:566
  66.2 22.5 %collective-permute-start.10 = (bf16[2,4,24,1024]{3,2,1,0:T(8,128)(2,1)}, bf16[2,4,24,1024]{3,2,1,0:T(8,128)(2,1)}, u32[]{:S(2)}, u32[]{:S(2)}) collective-permute-start(bf16[2,4,24,1024]{3,2,1,0:T(8,128)(2,1)} %get-tuple-element.80), channel_id=1, source_target_pairs={{0,24},{8,16},{16,8},{24,0},{1,25},{9,17},{17,9},{25,1},{2,26},{10... | collective-permute-start | bytes 1179656 | tf_op jit(solution)/shard_map/ppermute | solution.py:566
  86.9 17.9 %collective-permute-start.11 = (bf16[2,4,24,1024]{3,2,1,0:T(8,128)(2,1)}, bf16[2,4,24,1024]{3,2,1,0:T(8,128)(2,1)}, u32[]{:S(2)}, u32[]{:S(2)}) collective-permute-start(bf16[2,4,24,1024]{3,2,1,0:T(8,128)(2,1)} %get-tuple-element.82), channel_id=1, source_target_pairs={{0,8},{8,0},{16,24},{24,16},{1,9},{9,1},{17,25},{25,17},{2,10},{10... | collective-permute-start | bytes 1179656 | tf_op jit(solution)/shard_map/ppermute | solution.py:566
  87.4 33.3 %collective-permute-start.12 = (bf16[2,4,24,1024]{3,2,1,0:T(8,128)(2,1)}, bf16[2,4,24,1024]{3,2,1,0:T(8,128)(2,1)}, u32[]{:S(2)}, u32[]{:S(2)}) collective-permute-start(bf16[2,4,24,1024]{3,2,1,0:T(8,128)(2,1)} %get-tuple-element.86), channel_id=1, source_target_pairs={{0,16},{8,24},{16,0},{24,8},{1,17},{9,25},{17,1},{25,9},{2,18},{10... | collective-permute-start | bytes 1179656 | tf_op jit(solution)/shard_map/ppermute | solution.py:566
  87.9 33.6 %collective-permute-start.13 = (bf16[2,4,24,1024]{3,2,1,0:T(8,128)(2,1)}, bf16[2,4,24,1024]{3,2,1,0:T(8,128)(2,1)}, u32[]{:S(2)}, u32[]{:S(2)}) collective-permute-start(bf16[2,4,24,1024]{3,2,1,0:T(8,128)(2,1)} %get-tuple-element.87), channel_id=1, source_target_pairs={{0,24},{8,16},{16,8},{24,0},{1,25},{9,17},{17,9},{25,1},{2,26},{10... | collective-permute-start | bytes 1179656 | tf_op jit(solution)/shard_map/ppermute | solution.py:566
  103.5 18.4 %collective-permute-start.17 = (bf16[2,4,24,1024]{3,2,1,0:T(8,128)(2,1)}, bf16[2,4,24,1024]{3,2,1,0:T(8,128)(2,1)}, u32[]{:S(2)}, u32[]{:S(2)}) collective-permute-start(bf16[2,4,24,1024]{3,2,1,0:T(8,128)(2,1)} %get-tuple-element.100), channel_id=1, source_target_pairs={{0,8},{8,0},{16,24},{24,16},{1,9},{9,1},{17,25},{25,17},{2,10},{10... | collective-permute-start | bytes 1179656 | tf_op jit(solution)/shard_map/ppermute | solution.py:566
  104.3 33.3 %collective-permute-start.18 = (bf16[2,4,24,1024]{3,2,1,0:T(8,128)(2,1)}, bf16[2,4,24,1024]{3,2,1,0:T(8,128)(2,1)}, u32[]{:S(2)}, u32[]{:S(2)}) collective-permute-start(bf16[2,4,24,1024]{3,2,1,0:T(8,128)(2,1)} %get-tuple-element.101), channel_id=1, source_target_pairs={{0,16},{8,24},{16,0},{24,8},{1,17},{9,25},{17,1},{25,9},{2,18},{10... | collective-permute-start | bytes 1179656 | tf_op jit(solution)/shard_map/ppermute | solution.py:566
  104.8 34.2 %collective-permute-start.19 = (bf16[2,4,24,1024]{3,2,1,0:T(8,128)(2,1)}, bf16[2,4,24,1024]{3,2,1,0:T(8,128)(2,1)}, u32[]{:S(2)}, u32[]{:S(2)}) collective-permute-start(bf16[2,4,24,1024]{3,2,1,0:T(8,128)(2,1)} %get-tuple-element.102), channel_id=1, source_target_pairs={{0,24},{8,16},{16,8},{24,0},{1,25},{9,17},{17,9},{25,1},{2,26},{10... | collective-permute-start | bytes 1179656 | tf_op jit(solution)/shard_map/ppermute | solution.py:566
  120.7 19.8 %collective-permute-start.14 = (bf16[2,4,24,1024]{3,2,1,0:T(8,128)(2,1)}, bf16[2,4,24,1024]{3,2,1,0:T(8,128)(2,1)}, u32[]{:S(2)}, u32[]{:S(2)}) collective-permute-start(bf16[2,4,24,1024]{3,2,1,0:T(8,128)(2,1)} %get-tuple-element.95), channel_id=1, source_target_pairs={{0,8},{8,0},{16,24},{24,16},{1,9},{9,1},{17,25},{25,17},{2,10},{10... | collective-permute-start | bytes 1179656 | tf_op jit(solution)/shard_map/ppermute | solution.py:566
  121.4 19.8 %collective-permute-start.15 = (bf16[2,4,24,1024]{3,2,1,0:T(8,128)(2,1)}, bf16[2,4,24,1024]{3,2,1,0:T(8,128)(2,1)}, u32[]{:S(2)}, u32[]{:S(2)}) collective-permute-start(bf16[2,4,24,1024]{3,2,1,0:T(8,128)(2,1)} %get-tuple-element.96), channel_id=1, source_target_pairs={{0,16},{8,24},{16,0},{24,8},{1,17},{9,25},{17,1},{25,9},{2,18},{10... | collective-permute-start | bytes 1179656 | tf_op jit(solution)/shard_map/ppermute | solution.py:566
  121.9 20.0 %collective-permute-start.16 = (bf16[2,4,24,1024]{3,2,1,0:T(8,128)(2,1)}, bf16[2,4,24,1024]{3,2,1,0:T(8,128)(2,1)}, u32[]{:S(2)}, u32[]{:S(2)}) collective-permute-start(bf16[2,4,24,1024]{3,2,1,0:T(8,128)(2,1)} %get-tuple-element.97), channel_id=1, source_target_pairs={{0,24},{8,16},{16,8},{24,0},{1,25},{9,17},{17,9},{25,1},{2,26},{10... | collective-permute-start | bytes 1179656 | tf_op jit(solution)/shard_map/ppermute | solution.py:566
  137.6 2.1 %collective-permute-start.20 = (bf16[2,2,24,1024]{3,2,1,0:T(8,128)(2,1)}, bf16[2,2,24,1024]{3,2,1,0:T(8,128)(2,1)}, u32[]{:S(2)}, u32[]{:S(2)}) collective-permute-start(bf16[2,2,24,1024]{3,2,1,0:T(8,128)(2,1)} %get-tuple-element.105), channel_id=1, source_target_pairs={{0,8},{8,0},{16,24},{24,16},{1,9},{9,1},{17,25},{25,17},{2,10},{10... | collective-permute-start | bytes 589832 | tf_op jit(solution)/shard_map/ppermute | solution.py:566
  139.0 8.2 %collective-permute-start.21 = (bf16[2,2,24,1024]{3,2,1,0:T(8,128)(2,1)}, bf16[2,2,24,1024]{3,2,1,0:T(8,128)(2,1)}, u32[]{:S(2)}, u32[]{:S(2)}) collective-permute-start(bf16[2,2,24,1024]{3,2,1,0:T(8,128)(2,1)} %get-tuple-element.106), channel_id=1, source_target_pairs={{0,16},{8,24},{16,0},{24,8},{1,17},{9,25},{17,1},{25,9},{2,18},{10... | collective-permute-start | bytes 589832 | tf_op jit(solution)/shard_map/ppermute | solution.py:566
  139.7 9.8 %collective-permute-start.22 = (bf16[2,2,24,1024]{3,2,1,0:T(8,128)(2,1)}, bf16[2,2,24,1024]{3,2,1,0:T(8,128)(2,1)}, u32[]{:S(2)}, u32[]{:S(2)}) collective-permute-start(bf16[2,2,24,1024]{3,2,1,0:T(8,128)(2,1)} %get-tuple-element.107), channel_id=1, source_target_pairs={{0,24},{8,16},{16,8},{24,0},{1,25},{9,17},{17,9},{25,1},{2,26},{10... | collective-permute-start | bytes 589832 | tf_op jit(solution)/shard_map/ppermute | solution.py:566
  140.5 15.6 %collective-permute-start.23 = (bf16[2,2,24,1024]{3,2,1,0:T(8,128)(2,1)}, bf16[2,2,24,1024]{3,2,1,0:T(8,128)(2,1)}, u32[]{:S(2)}, u32[]{:S(2)}) collective-permute-start(bf16[2,2,24,1024]{3,2,1,0:T(8,128)(2,1)} %get-tuple-element.109), channel_id=1, source_target_pairs={{0,8},{8,0},{16,24},{24,16},{1,9},{9,1},{17,25},{25,17},{2,10},{10... | collective-permute-start | bytes 589832 | tf_op jit(solution)/shard_map/ppermute | solution.py:566
  141.3 14.8 %collective-permute-start.24 = (bf16[2,2,24,1024]{3,2,1,0:T(8,128)(2,1)}, bf16[2,2,24,1024]{3,2,1,0:T(8,128)(2,1)}, u32[]{:S(2)}, u32[]{:S(2)}) collective-permute-start(bf16[2,2,24,1024]{3,2,1,0:T(8,128)(2,1)} %get-tuple-element.110), channel_id=1, source_target_pairs={{0,16},{8,24},{16,0},{24,8},{1,17},{9,25},{17,1},{25,9},{2,18},{10... | collective-permute-start | bytes 589832 | tf_op jit(solution)/shard_map/ppermute | solution.py:566
  141.9 16.0 %collective-permute-start.25 = (bf16[2,2,24,1024]{3,2,1,0:T(8,128)(2,1)}, bf16[2,2,24,1024]{3,2,1,0:T(8,128)(2,1)}, u32[]{:S(2)}, u32[]{:S(2)}) collective-permute-start(bf16[2,2,24,1024]{3,2,1,0:T(8,128)(2,1)} %get-tuple-element.111), channel_id=1, source_target_pairs={{0,24},{8,16},{16,8},{24,0},{1,25},{9,17},{17,9},{25,1},{2,26},{10... | collective-permute-start | bytes 589832 | tf_op jit(solution)/shard_map/ppermute | solution.py:566

commit v10 on v9

--- a/solution.py
+++ b/solution.py
@@ -108,7 +108,7 @@
                 here, flow, moved = later
         return carry
 
-    lax.fori_loop(0, dirs, one, 0, unroll=6)
+    lax.fori_loop(0, dirs, one, 0, unroll=12)
 
 
 def emit(own, parts, local, chunk, dirs, lanes, swap_ref, send_refs):
@@ -617,7 +617,7 @@
     above, below = across(low, high)
     after = home
     for pieces in early[:-1]:
-        after, _ = arrived(after, pieces[1:])
+        after, _ = arrived(after, pieces[:0:-1])
     state = by_row((after,), forward_state)
     share, pieces = outer(own, dir_sign, along, state, above, below, *levels, home, parts, chunks[-1])
     late = swapped(pieces)

time: 166 us -> 165 us (level)
  transfers between devices with their start and end apart: 26 -> 26, of which waited for: 5 -> 3; matrix products, arithmetic and copies ran while one was open for 1% -> 1% of each run, Pallas kernels for 67% -> 67%
where the time goes in v10:
time: 165 us; the launch traced here: 164 us
  Pallas kernels  128 us (78%)
  starting transfers between devices  25.7 us (16%)
  waiting for transfers between devices  6.72 us (4%)
    pallas_call x4, Pallas kernels, source_term(): pl.pallas_call(functools.partial(source_kernel, parts, got, sent, dirs, 2...  56.7 us
    pallas_call x2, Pallas kernels, inner(): pl.pallas_call(functools.partial(inner_kernel, parts, local, chunk, into...  24.3 us
    ppermute x24, starting transfers between devices, swapped(): lax.ppermute(pieces[k], 'comp', [(i, i ^ k) for i in range(parts)])  19.1 us
    pallas_call x2, Pallas kernels, join(): pl.pallas_call(functools.partial(join_kernel, parts, spans), grid=(many,)...  13.1 us
    pallas_call x1, Pallas kernels, outer(): pl.pallas_call(functools.partial(outer_kernel, parts, local, chunk), grid...  12.5 us
    pallas_call x1, Pallas kernels, by_row(): pl.pallas_call(by_row_kernel, grid=(deep // some,), in_specs=[UNREAD] * l...  8.43 us
    ppermute x24, waiting for transfers between devices, swapped(): lax.ppermute(pieces[k], 'comp', [(i, i ^ k) for i in range(parts)])  6.72 us
    ppermute x2, starting transfers between devices, across(): return (lax.ppermute(high, 'space', up), lax.ppermute(low, 'space', down))  6.64 us
  transfers between devices with their start and end apart: 26, of which 3 were waited for; matrix products, arithmetic and copies ran while one was open for 1% of the time, Pallas kernels for 67%

profile of v10, /device:TPU:0, one launch (start us, length us, event | category | flops | bytes accessed | tf_op | source)
XLA Modules:
  0.0 163.9 jit_solution(3493737496101171399)
XLA Ops:
  0.6 12.2 %shard_map.131 = (f32[4,24,32,1024]{3,2,1,0:T(8,128)}, bf16[6,2,24,1024]{3,2,1,0:T(8,128)(2,1)}, bf16[6,2,24,1024]{3,2,1,0:T(8,128)(2,1)}, bf16[6,2,24,1024]{3,2,1,0:T(8,128)(2,1)}, bf16[6,2,24,1024]{3,2,1,0:T(8,128)(2,1)}) custom-call(s32[1]{0:T(128)} %bitcast.own_ref.refs_0_, s32[2,24]{1,0:T(2,128)} %refs_1_.5, f32[2,24]{1,0:T(2,128)} %constant.11.clone.along_ref.refs_2_, ...), custom_call_target="tpu_custom_call" | custom-call | flops 1 | bytes 1 | tf_op jit(solution)/shard_map/pallas_call | solution.py:169
  12.8 3.0 %collective-permute-start.1 = (bf16[6,2,24,1024]{3,2,1,0:T(8,128)(2,1)}, bf16[6,2,24,1024]{3,2,1,0:T(8,128)(2,1)}, u32[]{:S(2)}, u32[]{:S(2)}) collective-permute-start(bf16[6,2,24,1024]{3,2,1,0:T(8,128)(2,1)} %get-tuple-element.61), channel_id=1, source_target_pairs={{0,16},{8,24},{16,0},{24,8},{1,17},{9,25},{17,1},{25,9},{2,18},{10... | collective-permute-start | bytes 1769480 | tf_op jit(solution)/shard_map/ppermute | solution.py:566
  15.8 0.2 collective-permute-start
  16.0 4.9 %shard_map.132 = (bf16[2,4,32,1024]{3,2,1,0:T(8,128)(2,1)}, bf16[2,4,32,1024]{3,2,1,0:T(8,128)(2,1)}) custom-call(bf16[6,2,24,1024]{3,2,1,0:T(8,128)(2,1)} %get-tuple-element.57._, f32[4,24,32,1024]{3,2,1,0:T(8,128)} %bitcast.12, s32[4,32,1024]{2,1,0:T(8,128)} %refs_7_.3, s32[4,32,1024]{2,1,0:T(8,128)} %refs_8_.1, s32[32,1024]{1,0:T(8,128)} %refs_9_.1, ...), custom_call_target="tpu_custom_call" | custom-call | flops 1 | bytes 1 | tf_op jit(solution)/shard_map/pallas_call | solution.py:227
  20.9 1.3 collective-permute-start.4
  22.2 5.4 %collective-permute-start.3 = (bf16[2,4,32,1024]{3,2,1,0:T(8,128)(2,1)}, bf16[2,4,32,1024]{3,2,1,0:T(8,128)(2,1)}, u32[]{:S(2)}, u32[]{:S(2)}) collective-permute-start(bf16[2,4,32,1024]{3,2,1,0:T(8,128)(2,1)} %get-tuple-element.58._), channel_id=1, source_target_pairs={{0,1},{1,2},{2,3},{3,4},{4,5},{5,6},{6,7},{8,9},{9,10},{10,11},{11... | collective-permute-start | bytes 1572872 | tf_op jit(solution)/shard_map/ppermute | solution.py:574
  27.5 12.1 %shard_map.133 = (f32[4,24,32,1024]{3,2,1,0:T(8,128)}, bf16[6,2,24,1024]{3,2,1,0:T(8,128)(2,1)}, bf16[6,2,24,1024]{3,2,1,0:T(8,128)(2,1)}, bf16[6,2,24,1024]{3,2,1,0:T(8,128)(2,1)}, bf16[6,2,24,1024]{3,2,1,0:T(8,128)(2,1)}) custom-call(s32[1]{0:T(128)} %bitcast.own_ref.refs_0_, s32[2,24]{1,0:T(2,128)} %refs_1_.5, ...), custom_call_target="tpu_custom_call", output_to_operand_aliasing={{0}: (9, {})} | custom-call | flops 1 | bytes 1 | tf_op jit(solution)/shard_map/pallas_call | solution.py:169
  39.7 0.1 collective-permute-start.5
  39.8 2.0 %collective-permute-start.6 = (bf16[6,2,24,1024]{3,2,1,0:T(8,128)(2,1)}, bf16[6,2,24,1024]{3,2,1,0:T(8,128)(2,1)}, u32[]{:S(2)}, u32[]{:S(2)}) collective-permute-start(bf16[6,2,24,1024]{3,2,1,0:T(8,128)(2,1)} %get-tuple-element.71), channel_id=1, source_target_pairs={{0,16},{8,24},{16,0},{24,8},{1,17},{9,25},{17,1},{25,9},{2,18},{10... | collective-permute-start | bytes 1769480 | tf_op jit(solution)/shard_map/ppermute | solution.py:566
  41.8 1.4 collective-permute-start.7
  43.2 0.6 shard_map.134.refs_0_
  43.8 8.4 %shard_map.135.refs_4_.state_ref = bf16[8,384,1024]{2,1,0:T(8,128)(2,1)} custom-call(f32[8,128]{1,0:T(8,128)} %shard_map.134.refs_0_, bf16[384,8,1024]{2,1,0:T(8,128)(2,1)} %refs_1_.4), custom_call_target="tpu_custom_call" | custom-call | flops 1 | bytes 1 | tf_op jit(solution)/shard_map/pallas_call | solution.py:370
  52.3 12.5 %shard_map.136 = (f32[4,24,8,1024]{3,2,1,0:T(8,128)}, bf16[2,4,24,1024]{3,2,1,0:T(8,128)(2,1)}, bf16[2,4,24,1024]{3,2,1,0:T(8,128)(2,1)}, bf16[2,4,24,1024]{3,2,1,0:T(8,128)(2,1)}, bf16[2,4,24,1024]{3,2,1,0:T(8,128)(2,1)}) custom-call(s32[1]{0:T(128)} %bitcast.own_ref.refs_0_, s32[2,24]{1,0:T(2,128)} %refs_1_.5, f32[2,24]{1,0:T(2,128)} %constant.11.clone.along_ref.refs_2_, ...), custom_call_target="tpu_custom_call" | custom-call | flops 99999997952 | bytes 104857600 | tf_op jit(solution)/shard_map/pallas_call | solution.py:323
  64.8 0.7 collective-permute-start.9
  65.5 1.2 collective-permute-start.10
  66.7 4.7 %shard_map.137 = (bf16[384,1536]{1,0:T(8,128)(2,1)}, bf16[1536,384]{1,0:T(8,128)(2,1)}, f32[1536,128]{1,0:T(8,128)}) custom-call(f32[4,24,8,1024]{3,2,1,0:T(8,128)} %get-tuple-element.64._.share_ref, bf16[1536,384]{1,0:T(8,128)(2,1)} %w_in_ref.9, bf16[384,1536]{1,0:T(8,128)(2,1)} %w_out_ref.1, f32[1536]{0:T(1024)} %weight_ref.1), custom_call_target="tpu_custom_call" | custom-call | flops 99999997952 | bytes 104857600 | tf_op jit(solution)/shard_map/pallas_call | solution.py:396
  71.5 14.1 %shard_map.138 = (f32[2,1,1024]{2,1,0:T(1,128)}, bf16[2,4,24,1024]{3,2,1,0:T(8,128)(2,1)}, bf16[2,4,24,1024]{3,2,1,0:T(8,128)(2,1)}, bf16[2,4,24,1024]{3,2,1,0:T(8,128)(2,1)}, bf16[2,4,24,1024]{3,2,1,0:T(8,128)(2,1)}) custom-call(s32[1]{0:T(128)} %bitcast.own_ref.refs_0_, bf16[384,1536]{1,0:T(8,128)(2,1)} %get-tuple-element.65._.in_t_ref, ...), custom_call_target="tpu_custom_call" | custom-call | flops 1 | bytes 1 | tf_op jit(solution)/shard_map/pallas_call | solution.py:466
  85.6 0.6 shard_map.139
  86.2 0.3 collective-permute-start.11
  86.6 0.6 collective-permute-start.12
  87.2 0.9 collective-permute-start.13
  88.1 0.6 shard_map.140._
  88.7 14.1 %shard_map.141 = (f32[2,1,1024]{2,1,0:T(1,128)}, bf16[2,4,24,1024]{3,2,1,0:T(8,128)(2,1)}, bf16[2,4,24,1024]{3,2,1,0:T(8,128)(2,1)}, bf16[2,4,24,1024]{3,2,1,0:T(8,128)(2,1)}, bf16[2,4,24,1024]{3,2,1,0:T(8,128)(2,1)}) custom-call(s32[1]{0:T(128)} %bitcast.own_ref.refs_0_, f32[8,128]{1,0:T(8,128)} %shard_map.140._, ...), custom_call_target="tpu_custom_call" | custom-call | flops 1 | bytes 1 | tf_op jit(solution)/shard_map/pallas_call | solution.py:466
  102.8 0.7 collective-permute-start.17
  103.5 0.6 collective-permute-start.18
  104.1 0.8 collective-permute-start.19
  104.9 0.6 shard_map.142._
  105.5 14.3 %shard_map.143 = (f32[2,1,1024]{2,1,0:T(1,128)}, bf16[2,4,24,1024]{3,2,1,0:T(8,128)(2,1)}, bf16[2,4,24,1024]{3,2,1,0:T(8,128)(2,1)}, bf16[2,4,24,1024]{3,2,1,0:T(8,128)(2,1)}, bf16[2,4,24,1024]{3,2,1,0:T(8,128)(2,1)}) custom-call(s32[1]{0:T(128)} %bitcast.own_ref.refs_0_, f32[8,128]{1,0:T(8,128)} %shard_map.142._, ...), custom_call_target="tpu_custom_call" | custom-call | flops 1 | bytes 1 | tf_op jit(solution)/shard_map/pallas_call | solution.py:466
  119.9 0.8 collective-permute-start.14
  120.6 0.6 collective-permute-start.15
  121.3 0.8 collective-permute-start.16
  122.1 14.1 %shard_map.144 = (f32[2,1,1024]{2,1,0:T(1,128)}, bf16[2,2,24,1024]{3,2,1,0:T(8,128)(2,1)}, bf16[2,2,24,1024]{3,2,1,0:T(8,128)(2,1)}, bf16[2,2,24,1024]{3,2,1,0:T...) custom-call(s32[1]{0:T(128)} %bitcast.own_ref.refs_0_, ...), custom_call_target="tpu_custom_call" | custom-call | flops 1 | bytes 1 | tf_op jit(solution)/shard_map/pallas_call | solution.py:466
  136.2 0.6 shard_map.145
  136.8 0.7 collective-permute-start.20
  137.5 0.7 copy_bitcast_fusion.1
  138.2 0.7 collective-permute-start.21
  138.9 0.7 collective-permute-start.22
  139.7 0.8 collective-permute-start.23
  140.5 0.6 collective-permute-start.24
  141.1 0.8 collective-permute-start.25
  141.9 0.7 copy_bitcast_fusion
  142.6 0.7 maximum_select_fusion
  143.3 0.6 shard_map.146._
  143.9 2.5 %collective-permute-done.21.refs_14_ = bf16[2,2,24,1024]{3,2,1,0:T(8,128)(2,1)} collective-permute-done((bf16[2,2,24,1024]{3,2,1,0:T(8,128)(2,1)}, bf16[2,2,24,1024]{3,2,1,0:T(8,128)(2,1)}, u32[]{:S(2)}, u32[]{:S(2)}) %collective-permute-start.21) | collective-permute-done | bytes 196640 | tf_op jit(solution)/shard_map/ppermute | solution.py:566
  146.4 2.3 %collective-permute-done.22.refs_15_ = bf16[2,2,24,1024]{3,2,1,0:T(8,128)(2,1)} collective-permute-done((bf16[2,2,24,1024]{3,2,1,0:T(8,128)(2,1)}, bf16[2,2,24,1024]{3,2,1,0:T(8,128)(2,1)}, u32[]{:S(2)}, u32[]{:S(2)}) %collective-permute-start.22) | collective-permute-done | bytes 196640 | tf_op jit(solution)/shard_map/ppermute | solution.py:566
  148.7 6.6 %shard_map.147._ = f32[4,24,32,1024]{3,2,1,0:T(8,128)} custom-call(s32[1]{0:T(128)} %bitcast.own_ref.refs_0_, f32[8,128]{1,0:T(8,128)} %shard_map.146._, f32[4,24,32,1024]{3,2,1,0:T(8,128)} %get-tuple-element.60.refs_0_.refs_10_.home_ref, f32[4,24,8,1024]{3,2,1,0:T(8,128)} %get-tuple-element.64._.share_ref, ...), custom_call_target="tpu_custom_call" | custom-call | flops 1 | bytes 1 | tf_op jit(solution)/shard_map/pallas_call | solution.py:533
  155.3 1.8 %collective-permute-done.25.refs_15_ = bf16[2,2,24,1024]{3,2,1,0:T(8,128)(2,1)} collective-permute-done((bf16[2,2,24,1024]{3,2,1,0:T(8,128)(2,1)}, bf16[2,2,24,1024]{3,2,1,0:T(8,128)(2,1)}, u32[]{:S(2)}, u32[]{:S(2)}) %collective-permute-start.25) | collective-permute-done | bytes 196640 | tf_op jit(solution)/shard_map/ppermute | solution.py:566
  157.1 6.6 %shard_map.148 = f32[4,24,32,1024]{3,2,1,0:T(8,128)} custom-call(s32[1]{0:T(128)} %bitcast.own_ref.refs_0_, f32[4,24,32,1024]{3,2,1,0:T(8,128)} %shard_map.147._, f32[4,24,32,1024]{3,2,1,0:T(8,128)} %get-tuple-element.60.refs_0_.refs_10_.home_ref, f32[4,24,8,1024]{3,2,1,0:T(8,128)} %get-tuple-element.64._.share_ref, ...), custom_call_target="tpu_custom_call", output_to_operand_aliasing={{}: (1, {})} | custom-call | flops 1 | bytes 1 | tf_op jit(solution)/shard_map/pallas_call | solution.py:533
  (25 shorter events, 0.1 us)
Async XLA Ops:
  12.8 26.9 %collective-permute-start.1 = (bf16[6,2,24,1024]{3,2,1,0:T(8,128)(2,1)}, bf16[6,2,24,1024]{3,2,1,0:T(8,128)(2,1)}, u32[]{:S(2)}, u32[]{:S(2)}) collective-permute-start(bf16[6,2,24,1024]{3,2,1,0:T(8,128)(2,1)} %get-tuple-element.61), channel_id=1, source_target_pairs={{0,16},{8,24},{16,0},{24,8},{1,17},{9,25},{17,1},{25,9},{2,18},{10... | collective-permute-start | bytes 1769480 | tf_op jit(solution)/shard_map/ppermute | solution.py:566
  15.8 24.0 %collective-permute-start.2 = (bf16[6,2,24,1024]{3,2,1,0:T(8,128)(2,1)}, bf16[6,2,24,1024]{3,2,1,0:T(8,128)(2,1)}, u32[]{:S(2)}, u32[]{:S(2)}) collective-permute-start(bf16[6,2,24,1024]{3,2,1,0:T(8,128)(2,1)} %get-tuple-element.62), channel_id=1, source_target_pairs={{0,8},{8,0},{16,24},{24,16},{1,9},{9,1},{17,25},{25,17},{2,10},{10... | collective-permute-start | bytes 1769480 | tf_op jit(solution)/shard_map/ppermute | solution.py:566
  15.8 26.0 %collective-permute-start = (bf16[6,2,24,1024]{3,2,1,0:T(8,128)(2,1)}, bf16[6,2,24,1024]{3,2,1,0:T(8,128)(2,1)}, u32[]{:S(2)}, u32[]{:S(2)}) collective-permute-start(bf16[6,2,24,1024]{3,2,1,0:T(8,128)(2,1)} %get-tuple-element.57._), channel_id=1, source_target_pairs={{0,24},{8,16},{16,8},{24,0},{1,25},{9,17},{17,9},{25,1},{2,26},{10... | collective-permute-start | bytes 1769480 | tf_op jit(solution)/shard_map/ppermute | solution.py:566
  20.9 31.4 %collective-permute-start.4 = (bf16[2,4,32,1024]{3,2,1,0:T(8,128)(2,1)}, bf16[2,4,32,1024]{3,2,1,0:T(8,128)(2,1)}, u32[]{:S(2)}, u32[]{:S(2)}) collective-permute-start(bf16[2,4,32,1024]{3,2,1,0:T(8,128)(2,1)} %get-tuple-element.63), channel_id=1, source_target_pairs={{1,0},{2,1},{3,2},{4,3},{5,4},{6,5},{7,6},{9,8},{10,9},{11,10},{12... | collective-permute-start | bytes 1572872 | tf_op jit(solution)/shard_map/ppermute | solution.py:574
  22.2 30.1 %collective-permute-start.3 = (bf16[2,4,32,1024]{3,2,1,0:T(8,128)(2,1)}, bf16[2,4,32,1024]{3,2,1,0:T(8,128)(2,1)}, u32[]{:S(2)}, u32[]{:S(2)}) collective-permute-start(bf16[2,4,32,1024]{3,2,1,0:T(8,128)(2,1)} %get-tuple-element.58._), channel_id=1, source_target_pairs={{0,1},{1,2},{2,3},{3,4},{4,5},{5,6},{6,7},{8,9},{9,10},{10,11},{11... | collective-permute-start | bytes 1572872 | tf_op jit(solution)/shard_map/ppermute | solution.py:574
  39.7 25.8 %collective-permute-start.5 = (bf16[6,2,24,1024]{3,2,1,0:T(8,128)(2,1)}, bf16[6,2,24,1024]{3,2,1,0:T(8,128)(2,1)}, u32[]{:S(2)}, u32[]{:S(2)}) collective-permute-start(bf16[6,2,24,1024]{3,2,1,0:T(8,128)(2,1)} %get-tuple-element.70), channel_id=1, source_target_pairs={{0,8},{8,0},{16,24},{24,16},{1,9},{9,1},{17,25},{25,17},{2,10},{10... | collective-permute-start | bytes 1769480 | tf_op jit(solution)/shard_map/ppermute | solution.py:566
  39.8 31.7 %collective-permute-start.6 = (bf16[6,2,24,1024]{3,2,1,0:T(8,128)(2,1)}, bf16[6,2,24,1024]{3,2,1,0:T(8,128)(2,1)}, u32[]{:S(2)}, u32[]{:S(2)}) collective-permute-start(bf16[6,2,24,1024]{3,2,1,0:T(8,128)(2,1)} %get-tuple-element.71), channel_id=1, source_target_pairs={{0,16},{8,24},{16,0},{24,8},{1,17},{9,25},{17,1},{25,9},{2,18},{10... | collective-permute-start | bytes 1769480 | tf_op jit(solution)/shard_map/ppermute | solution.py:566
  41.8 29.7 %collective-permute-start.7 = (bf16[6,2,24,1024]{3,2,1,0:T(8,128)(2,1)}, bf16[6,2,24,1024]{3,2,1,0:T(8,128)(2,1)}, u32[]{:S(2)}, u32[]{:S(2)}) collective-permute-start(bf16[6,2,24,1024]{3,2,1,0:T(8,128)(2,1)} %get-tuple-element.72), channel_id=1, source_target_pairs={{0,24},{8,16},{16,8},{24,0},{1,25},{9,17},{17,9},{25,1},{2,26},{10... | collective-permute-start | bytes 1769480 | tf_op jit(solution)/shard_map/ppermute | solution.py:566
  64.8 20.8 %collective-permute-start.8 = (bf16[2,4,24,1024]{3,2,1,0:T(8,128)(2,1)}, bf16[2,4,24,1024]{3,2,1,0:T(8,128)(2,1)}, u32[]{:S(2)}, u32[]{:S(2)}) collective-permute-start(bf16[2,4,24,1024]{3,2,1,0:T(8,128)(2,1)} %get-tuple-element.74), channel_id=1, source_target_pairs={{0,8},{8,0},{16,24},{24,16},{1,9},{9,1},{17,25},{25,17},{2,10},{10... | collective-permute-start | bytes 1179656 | tf_op jit(solution)/shard_map/ppermute | solution.py:566
  64.8 20.8 %collective-permute-start.9 = (bf16[2,4,24,1024]{3,2,1,0:T(8,128)(2,1)}, bf16[2,4,24,1024]{3,2,1,0:T(8,128)(2,1)}, u32[]{:S(2)}, u32[]{:S(2)}) collective-permute-start(bf16[2,4,24,1024]{3,2,1,0:T(8,128)(2,1)} %get-tuple-element.75), channel_id=1, source_target_pairs={{0,16},{8,24},{16,0},{24,8},{1,17},{9,25},{17,1},{25,9},{2,18},{10... | collective-permute-start | bytes 1179656 | tf_op jit(solution)/shard_map/ppermute | solution.py:566
  65.5 22.5 %collective-permute-start.10 = (bf16[2,4,24,1024]{3,2,1,0:T(8,128)(2,1)}, bf16[2,4,24,1024]{3,2,1,0:T(8,128)(2,1)}, u32[]{:S(2)}, u32[]{:S(2)}) collective-permute-start(bf16[2,4,24,1024]{3,2,1,0:T(8,128)(2,1)} %get-tuple-element.80), channel_id=1, source_target_pairs={{0,24},{8,16},{16,8},{24,0},{1,25},{9,17},{17,9},{25,1},{2,26},{10... | collective-permute-start | bytes 1179656 | tf_op jit(solution)/shard_map/ppermute | solution.py:566
  86.2 17.9 %collective-permute-start.11 = (bf16[2,4,24,1024]{3,2,1,0:T(8,128)(2,1)}, bf16[2,4,24,1024]{3,2,1,0:T(8,128)(2,1)}, u32[]{:S(2)}, u32[]{:S(2)}) collective-permute-start(bf16[2,4,24,1024]{3,2,1,0:T(8,128)(2,1)} %get-tuple-element.82), channel_id=1, source_target_pairs={{0,8},{8,0},{16,24},{24,16},{1,9},{9,1},{17,25},{25,17},{2,10},{10... | collective-permute-start | bytes 1179656 | tf_op jit(solution)/shard_map/ppermute | solution.py:566
  86.6 33.3 %collective-permute-start.12 = (bf16[2,4,24,1024]{3,2,1,0:T(8,128)(2,1)}, bf16[2,4,24,1024]{3,2,1,0:T(8,128)(2,1)}, u32[]{:S(2)}, u32[]{:S(2)}) collective-permute-start(bf16[2,4,24,1024]{3,2,1,0:T(8,128)(2,1)} %get-tuple-element.86), channel_id=1, source_target_pairs={{0,16},{8,24},{16,0},{24,8},{1,17},{9,25},{17,1},{25,9},{2,18},{10... | collective-permute-start | bytes 1179656 | tf_op jit(solution)/shard_map/ppermute | solution.py:566
  87.2 33.5 %collective-permute-start.13 = (bf16[2,4,24,1024]{3,2,1,0:T(8,128)(2,1)}, bf16[2,4,24,1024]{3,2,1,0:T(8,128)(2,1)}, u32[]{:S(2)}, u32[]{:S(2)}) collective-permute-start(bf16[2,4,24,1024]{3,2,1,0:T(8,128)(2,1)} %get-tuple-element.87), channel_id=1, source_target_pairs={{0,24},{8,16},{16,8},{24,0},{1,25},{9,17},{17,9},{25,1},{2,26},{10... | collective-permute-start | bytes 1179656 | tf_op jit(solution)/shard_map/ppermute | solution.py:566
  102.8 18.5 %collective-permute-start.17 = (bf16[2,4,24,1024]{3,2,1,0:T(8,128)(2,1)}, bf16[2,4,24,1024]{3,2,1,0:T(8,128)(2,1)}, u32[]{:S(2)}, u32[]{:S(2)}) collective-permute-start(bf16[2,4,24,1024]{3,2,1,0:T(8,128)(2,1)} %get-tuple-element.100), channel_id=1, source_target_pairs={{0,8},{8,0},{16,24},{24,16},{1,9},{9,1},{17,25},{25,17},{2,10},{10... | collective-permute-start | bytes 1179656 | tf_op jit(solution)/shard_map/ppermute | solution.py:566
  103.5 33.3 %collective-permute-start.18 = (bf16[2,4,24,1024]{3,2,1,0:T(8,128)(2,1)}, bf16[2,4,24,1024]{3,2,1,0:T(8,128)(2,1)}, u32[]{:S(2)}, u32[]{:S(2)}) collective-permute-start(bf16[2,4,24,1024]{3,2,1,0:T(8,128)(2,1)} %get-tuple-element.101), channel_id=1, source_target_pairs={{0,16},{8,24},{16,0},{24,8},{1,17},{9,25},{17,1},{25,9},{2,18},{10... | collective-permute-start | bytes 1179656 | tf_op jit(solution)/shard_map/ppermute | solution.py:566
  104.1 34.1 %collective-permute-start.19 = (bf16[2,4,24,1024]{3,2,1,0:T(8,128)(2,1)}, bf16[2,4,24,1024]{3,2,1,0:T(8,128)(2,1)}, u32[]{:S(2)}, u32[]{:S(2)}) collective-permute-start(bf16[2,4,24,1024]{3,2,1,0:T(8,128)(2,1)} %get-tuple-element.102), channel_id=1, source_target_pairs={{0,24},{8,16},{16,8},{24,0},{1,25},{9,17},{17,9},{25,1},{2,26},{10... | collective-permute-start | bytes 1179656 | tf_op jit(solution)/shard_map/ppermute | solution.py:566
  119.9 19.8 %collective-permute-start.14 = (bf16[2,4,24,1024]{3,2,1,0:T(8,128)(2,1)}, bf16[2,4,24,1024]{3,2,1,0:T(8,128)(2,1)}, u32[]{:S(2)}, u32[]{:S(2)}) collective-permute-start(bf16[2,4,24,1024]{3,2,1,0:T(8,128)(2,1)} %get-tuple-element.95), channel_id=1, source_target_pairs={{0,8},{8,0},{16,24},{24,16},{1,9},{9,1},{17,25},{25,17},{2,10},{10... | collective-permute-start | bytes 1179656 | tf_op jit(solution)/shard_map/ppermute | solution.py:566
  120.6 19.8 %collective-permute-start.15 = (bf16[2,4,24,1024]{3,2,1,0:T(8,128)(2,1)}, bf16[2,4,24,1024]{3,2,1,0:T(8,128)(2,1)}, u32[]{:S(2)}, u32[]{:S(2)}) collective-permute-start(bf16[2,4,24,1024]{3,2,1,0:T(8,128)(2,1)} %get-tuple-element.96), channel_id=1, source_target_pairs={{0,16},{8,24},{16,0},{24,8},{1,17},{9,25},{17,1},{25,9},{2,18},{10... | collective-permute-start | bytes 1179656 | tf_op jit(solution)/shard_map/ppermute | solution.py:566
  121.3 19.8 %collective-permute-start.16 = (bf16[2,4,24,1024]{3,2,1,0:T(8,128)(2,1)}, bf16[2,4,24,1024]{3,2,1,0:T(8,128)(2,1)}, u32[]{:S(2)}, u32[]{:S(2)}) collective-permute-start(bf16[2,4,24,1024]{3,2,1,0:T(8,128)(2,1)} %get-tuple-element.97), channel_id=1, source_target_pairs={{0,24},{8,16},{16,8},{24,0},{1,25},{9,17},{17,9},{25,1},{2,26},{10... | collective-permute-start | bytes 1179656 | tf_op jit(solution)/shard_map/ppermute | solution.py:566
  136.8 2.1 %collective-permute-start.20 = (bf16[2,2,24,1024]{3,2,1,0:T(8,128)(2,1)}, bf16[2,2,24,1024]{3,2,1,0:T(8,128)(2,1)}, u32[]{:S(2)}, u32[]{:S(2)}) collective-permute-start(bf16[2,2,24,1024]{3,2,1,0:T(8,128)(2,1)} %get-tuple-element.105), channel_id=1, source_target_pairs={{0,8},{8,0},{16,24},{24,16},{1,9},{9,1},{17,25},{25,17},{2,10},{10... | collective-permute-start | bytes 589832 | tf_op jit(solution)/shard_map/ppermute | solution.py:566
  138.2 8.2 %collective-permute-start.21 = (bf16[2,2,24,1024]{3,2,1,0:T(8,128)(2,1)}, bf16[2,2,24,1024]{3,2,1,0:T(8,128)(2,1)}, u32[]{:S(2)}, u32[]{:S(2)}) collective-permute-start(bf16[2,2,24,1024]{3,2,1,0:T(8,128)(2,1)} %get-tuple-element.106), channel_id=1, source_target_pairs={{0,16},{8,24},{16,0},{24,8},{1,17},{9,25},{17,1},{25,9},{2,18},{10... | collective-permute-start | bytes 589832 | tf_op jit(solution)/shard_map/ppermute | solution.py:566
  138.9 9.8 %collective-permute-start.22 = (bf16[2,2,24,1024]{3,2,1,0:T(8,128)(2,1)}, bf16[2,2,24,1024]{3,2,1,0:T(8,128)(2,1)}, u32[]{:S(2)}, u32[]{:S(2)}) collective-permute-start(bf16[2,2,24,1024]{3,2,1,0:T(8,128)(2,1)} %get-tuple-element.107), channel_id=1, source_target_pairs={{0,24},{8,16},{16,8},{24,0},{1,25},{9,17},{17,9},{25,1},{2,26},{10... | collective-permute-start | bytes 589832 | tf_op jit(solution)/shard_map/ppermute | solution.py:566
  139.7 15.6 %collective-permute-start.23 = (bf16[2,2,24,1024]{3,2,1,0:T(8,128)(2,1)}, bf16[2,2,24,1024]{3,2,1,0:T(8,128)(2,1)}, u32[]{:S(2)}, u32[]{:S(2)}) collective-permute-start(bf16[2,2,24,1024]{3,2,1,0:T(8,128)(2,1)} %get-tuple-element.109), channel_id=1, source_target_pairs={{0,8},{8,0},{16,24},{24,16},{1,9},{9,1},{17,25},{25,17},{2,10},{10... | collective-permute-start | bytes 589832 | tf_op jit(solution)/shard_map/ppermute | solution.py:566
  140.5 14.9 %collective-permute-start.24 = (bf16[2,2,24,1024]{3,2,1,0:T(8,128)(2,1)}, bf16[2,2,24,1024]{3,2,1,0:T(8,128)(2,1)}, u32[]{:S(2)}, u32[]{:S(2)}) collective-permute-start(bf16[2,2,24,1024]{3,2,1,0:T(8,128)(2,1)} %get-tuple-element.110), channel_id=1, source_target_pairs={{0,16},{8,24},{16,0},{24,8},{1,17},{9,25},{17,1},{25,9},{2,18},{10... | collective-permute-start | bytes 589832 | tf_op jit(solution)/shard_map/ppermute | solution.py:566
  141.1 16.0 %collective-permute-start.25 = (bf16[2,2,24,1024]{3,2,1,0:T(8,128)(2,1)}, bf16[2,2,24,1024]{3,2,1,0:T(8,128)(2,1)}, u32[]{:S(2)}, u32[]{:S(2)}) collective-permute-start(bf16[2,2,24,1024]{3,2,1,0:T(8,128)(2,1)} %get-tuple-element.111), channel_id=1, source_target_pairs={{0,24},{8,16},{16,8},{24,0},{1,25},{9,17},{17,9},{25,1},{2,26},{10... | collective-permute-start | bytes 589832 | tf_op jit(solution)/shard_map/ppermute | solution.py:566
